TPU v7x, 32 devices: a whole 2x2x4 slice. The times are simulated.
32 devices in a mesh: dp: 8 (over y, x, core), chan: 4 (over z).
Axes of the slice: x: 2, y: 2, z: 4, core: 2. Of those that a mesh axis runs over, the one named last changes fastest.
Arguments:
- latents_in: bfloat16 [16, 16, 16, 512], P('dp', None, None, 'chan'), may hold values from -6 to 6
- norm_gains: float32 [3, 512], P(None, 'chan'), may hold values from 0.1 to 1.9
- norm_shifts: float32 [3, 512], P(None, 'chan'), may hold values from -3 to 3
- conv_weights: bfloat16 [2, 3, 3, 512, 512], P(None, None, None, None, 'chan'), may hold values from -0.09375 to 0.09375
- conv_biases: float32 [2, 512], P(None, 'chan'), may hold values from -3 to 3
- qkv_weights: bfloat16 [3, 512, 512], P(None, None, 'chan'), may hold values from -0.375 to 0.375
- attn_biases: float32 [3, 512], P(None, 'chan'), may hold values from -3 to 3
- out_weight: bfloat16 [512, 512], P(None, 'chan'), may hold values from -0.75 to 0.75
- proj_weight: bfloat16 [512, 256], P(None, 'chan'), may hold values from -0.25 to 0.25
- proj_bias: float32 [256], P('chan'), may hold values from -3 to 3
- codebook: float32 [1024, 256], P(None, 'chan'), may hold values from -6 to 6
- codes: int32 [16, 16, 16], P('dp'), may hold values from 0 to 1023, as said below
- reset_src: int32 [1024], replicated, may hold values from 0 to 4095
- cotangent: bfloat16 [16, 16, 16, 256], P('dp', None, None, 'chan'), may hold values from -6 to 6
Outputs:
- latents_out: float32 [16, 16, 16, 256], P('dp', None, None, 'chan')
- commitment: float32 [256], P('chan')
- perplexity: float32 [], replicated
- new_codebook: float32 [1024, 256], P(None, 'chan')
- grad_latents: float32 [16, 16, 16, 512], P('dp', None, None, 'chan')
- grad_norm_gains: float32 [3, 512], P(None, 'chan')
- grad_norm_shifts: float32 [3, 512], P(None, 'chan')
- grad_conv_weights: float32 [2, 3, 3, 512, 512], P(None, None, None, None, 'chan')
- grad_conv_biases: float32 [2, 512], P(None, 'chan')
- grad_qkv_weights: float32 [3, 512, 512], P(None, None, 'chan')
- grad_attn_biases: float32 [3, 512], P(None, 'chan')
- grad_out_weight: float32 [512, 512], P(None, 'chan')
- grad_proj_weight: float32 [512, 256], P(None, 'chan')
- grad_proj_bias: float32 [256], P('chan')
- grad_codebook: float32 [1024, 256], P(None, 'chan')
Inputs may be any that keep to these rules, and one draw needn't show every extreme that they name: All code indices lie in one set of 768 codes chosen by the seed. `reset_src`: a position number (image × 16 + row) × 16 + column.
All inputs are finite; a program needn't handle non-finite values.
Results may differ from a plain program's by a relative error of at most 0.02.
Values may be sent and summed in bfloat16 or wider, within the bound.
No kernel may reach another device: no remote copies, remote signals or barrier semaphores. Data moves between devices by JAX's collectives and lax.ppermute only.
A program may use at most 128 MiB of HBM per device.

v0:
```python
import jax
import jax.numpy as jnp
from jax import lax
from jax.sharding import PartitionSpec as P

C = 512
CODES = 1024
GROUPS = 32
LAT = 16


EPSILON = 1e-06
BETA = 0.25


def swish_slope(values):
    sigmoid_v = jax.nn.sigmoid(values)
    return (values * sigmoid_v, sigmoid_v * (1.0 + values * (1.0 - sigmoid_v)))


def group_shape(values):
    dims_in = values.shape
    group_width = C // GROUPS
    return (dims_in[0], dims_in[1] * dims_in[2], dims_in[3] // group_width, group_width)


def norm_forward(values, gain_vec, shift_vec):
    grouped = values.reshape(group_shape(values))
    mean_value = jnp.mean(grouped, axis=(1, 3), keepdims=True)
    centred = grouped - mean_value
    variance = jnp.mean(centred * centred, axis=(1, 3), keepdims=True)
    inverse = lax.rsqrt(variance + EPSILON)
    normed = (centred * inverse).reshape(values.shape)
    return (normed * gain_vec + shift_vec, normed, inverse)


def norm_backward(upstream, normed, inverse, gain_vec):
    gain_grad = jnp.sum(upstream * normed, axis=(0, 1, 2))
    shift_grad = jnp.sum(upstream, axis=(0, 1, 2))
    scaled = (upstream * gain_vec).reshape(group_shape(upstream))
    normed_groups = normed.reshape(group_shape(normed))
    projected = jnp.mean(scaled * normed_groups, axis=(1, 3), keepdims=True)
    source = inverse * (
        scaled - jnp.mean(scaled, axis=(1, 3), keepdims=True) - normed_groups * projected
    )
    return (source.reshape(upstream.shape), gain_grad, shift_grad)


def conv_taps(full_input, kernel):
    padded = jnp.pad(full_input, ((0, 0), (1, 1), (1, 1), (0, 0)))
    result = None
    for row_tap in range(3):
        for col_tap in range(3):
            window = padded[:, row_tap : row_tap + LAT, col_tap : col_tap + LAT, :]
            tap_term = jnp.einsum(
                "bhwc,cd->bhwd",
                window,
                kernel[row_tap, col_tap],
                preferred_element_type=jnp.float32,
            )
            result = tap_term if result is None else result + tap_term
    return result


def conv_kernel_grad(full_input, upstream):
    padded = jnp.pad(full_input, ((0, 0), (1, 1), (1, 1), (0, 0)))
    tap_rows = []
    for row_tap in range(3):
        columns = []
        for col_tap in range(3):
            window = padded[:, row_tap : row_tap + LAT, col_tap : col_tap + LAT, :]
            columns.append(
                jnp.einsum("bhwc,bhwd->cd", window, upstream, preferred_element_type=jnp.float32)
            )
        tap_rows.append(jnp.stack(columns))
    return jnp.stack(tap_rows)


def conv_input_grad(upstream, kernel):
    padded = jnp.pad(upstream, ((0, 0), (1, 1), (1, 1), (0, 0)))
    result = None
    for row_tap in range(3):
        for col_tap in range(3):
            window = padded[:, 2 - row_tap : 2 - row_tap + LAT, 2 - col_tap : 2 - col_tap + LAT, :]
            tap_term = jnp.einsum(
                "bhwd,cd->bhwc",
                window,
                kernel[row_tap, col_tap],
                preferred_element_type=jnp.float32,
            )
            result = tap_term if result is None else result + tap_term
    return result


def shards(
    latents_in,
    norm_gains,
    norm_shifts,
    conv_weights,
    conv_biases,
    qkv_weights,
    attn_biases,
    out_weight,
    proj_weight,
    proj_bias,
    codebook,
    codes,
    reset_src,
    cotangent,
):
    images = latents_in.shape[0]
    positions = LAT * LAT
    tokens = images * positions
    tokens_all = tokens * lax.axis_size("dp")
    local_width = latents_in.shape[3]
    scores_scale_factor = float(C) ** (-0.5)
    blocks = images // 2
    inputs = latents_in.astype(jnp.float32)

    def blocked(array):
        return array.reshape(blocks, 2, positions, array.shape[-1])

    pre_first, normed_first, inverse_first = norm_forward(inputs, norm_gains[0], norm_shifts[0])
    act_first, slope_first = swish_slope(pre_first)
    full_first = lax.all_gather(act_first.astype(jnp.bfloat16), "chan", axis=3, tiled=True)
    hidden = conv_taps(full_first, conv_weights[0]) + conv_biases[0]
    pre_second, normed_second, inverse_second = norm_forward(hidden, norm_gains[1], norm_shifts[1])
    act_second, slope_second = swish_slope(pre_second)
    full_second = lax.all_gather(act_second.astype(jnp.bfloat16), "chan", axis=3, tiled=True)
    residual = inputs + conv_taps(full_second, conv_weights[1]) + conv_biases[1]
    pre_third, normed_third, inverse_third = norm_forward(residual, norm_gains[2], norm_shifts[2])
    full_third = lax.all_gather(
        pre_third.astype(jnp.bfloat16).reshape(tokens, local_width), "chan", axis=1, tiled=True
    )
    query_input = (
        jnp.dot(full_third, qkv_weights[0], preferred_element_type=jnp.float32) + attn_biases[0]
    ).astype(jnp.bfloat16)
    key_part = jnp.dot(full_third, qkv_weights[1], preferred_element_type=jnp.float32).astype(
        jnp.bfloat16
    )
    value_part = (
        jnp.dot(full_third, qkv_weights[2], preferred_element_type=jnp.float32) + attn_biases[1]
    ).astype(jnp.bfloat16)
    query_full, key_full = (
        lax.all_gather(query_input, "chan", axis=1, tiled=True),
        lax.all_gather(key_part, "chan", axis=1, tiled=True),
    )

    def attend(pieces):
        query_tile_rows, key_tile_rows, value_tile_rows = pieces
        attention_scores = (
            jnp.einsum(
                "ulp,ugp->ulg", query_tile_rows, key_tile_rows, preferred_element_type=jnp.float32
            )
            * scores_scale_factor
        )
        row_max = jnp.max(attention_scores, axis=-1, keepdims=True)
        shifted = jnp.exp(attention_scores - row_max)
        row_sum = jnp.sum(shifted, axis=-1, keepdims=True)
        attention_weights = (shifted / row_sum).astype(jnp.bfloat16)
        mixed_block = jnp.einsum(
            "pth,phz->ptz", attention_weights, value_tile_rows, preferred_element_type=jnp.float32
        )
        return (mixed_block, row_max + jnp.log(row_sum))

    mixed_output, log_sums = lax.map(
        attend, (blocked(query_full), blocked(key_full), blocked(value_part))
    )
    mixed_low = mixed_output.astype(jnp.bfloat16).reshape(tokens, local_width)
    full_mixed = lax.all_gather(mixed_low, "chan", axis=1, tiled=True)
    attended = jnp.dot(full_mixed, out_weight, preferred_element_type=jnp.float32) + attn_biases[2]
    output_low = (residual.reshape(tokens, local_width) + attended).astype(jnp.bfloat16)
    full_output = lax.all_gather(output_low, "chan", axis=1, tiled=True)
    latents = jnp.dot(full_output, proj_weight, preferred_element_type=jnp.float32) + proj_bias
    code_index = codes.reshape(tokens)
    quantized = jnp.take(codebook, code_index, axis=0)
    difference = latents - quantized
    commit_sq = jnp.sum(difference * difference, axis=0)
    usage = jax.ops.segment_sum(jnp.ones((tokens,), jnp.float32), code_index, num_segments=CODES)
    book_grad = jax.ops.segment_sum(-difference, code_index, num_segments=CODES) * (
        2.0 * CODES / tokens_all
    )
    local_rows = reset_src - lax.axis_index("dp") * tokens
    inside = ((local_rows >= 0) & (local_rows < tokens)).astype(jnp.float32)
    picked = jnp.take(latents, jnp.clip(local_rows, 0, tokens - 1), axis=0) * inside[:, None]
    latent_grad = (
        cotangent.reshape(tokens, -1).astype(jnp.float32) + 2.0 * BETA * difference
    ).astype(jnp.bfloat16)
    proj_grad = jnp.einsum(
        "tc,te->ce", full_output, latent_grad, preferred_element_type=jnp.float32
    )
    proj_bias_grad = jnp.sum(latent_grad, axis=0, dtype=jnp.float32)
    output_part = jnp.einsum(
        "te,ce->tc", latent_grad, proj_weight, preferred_element_type=jnp.float32
    )
    output_grad = lax.psum_scatter(
        output_part.astype(jnp.bfloat16), "chan", scatter_dimension=1, tiled=True
    ).astype(jnp.float32)
    attended_grad = output_grad.astype(jnp.bfloat16)
    mixed_part = jnp.einsum(
        "td,cd->tc", attended_grad, out_weight, preferred_element_type=jnp.float32
    )
    mixed_grad = lax.psum_scatter(
        mixed_part.astype(jnp.bfloat16), "chan", scatter_dimension=1, tiled=True
    )
    mixed_grad_full, value_full = (
        lax.all_gather(mixed_grad, "chan", axis=1, tiled=True),
        lax.all_gather(value_part, "chan", axis=1, tiled=True),
    )
    out_grad = jnp.einsum(
        "tc,td->cd", full_mixed, attended_grad, preferred_element_type=jnp.float32
    )
    out_bias_grad = jnp.sum(attended_grad, axis=0, dtype=jnp.float32)

    def attend_back(pieces):
        (
            query_tile_rows,
            key_tile_rows,
            sums_block,
            gradient_tile_rows,
            value_tile_rows,
            query_shard_rows,
            key_shard_rows,
            grad_local,
        ) = pieces
        attention_scores = (
            jnp.einsum(
                "ulp,ugp->ulg", query_tile_rows, key_tile_rows, preferred_element_type=jnp.float32
            )
            * scores_scale_factor
        )
        attention_weights = jnp.exp(attention_scores - sums_block)
        weight_grad = jnp.einsum(
            "ulp,ugp->ulg", gradient_tile_rows, value_tile_rows, preferred_element_type=jnp.float32
        )
        row_dot = jnp.sum(attention_weights * weight_grad, axis=-1, keepdims=True)
        scores_gradient = (attention_weights * (weight_grad - row_dot)).astype(jnp.bfloat16)
        query_grad_block = (
            jnp.einsum(
                "pth,phz->ptz", scores_gradient, key_shard_rows, preferred_element_type=jnp.float32
            )
            * scores_scale_factor
        )
        key_grad_block = (
            jnp.einsum(
                "dxg,dxf->dgf",
                scores_gradient,
                query_shard_rows,
                preferred_element_type=jnp.float32,
            )
            * scores_scale_factor
        )
        value_grad_block = jnp.einsum(
            "dxg,dxf->dgf",
            attention_weights.astype(jnp.bfloat16),
            grad_local,
            preferred_element_type=jnp.float32,
        )
        return (query_grad_block, key_grad_block, value_grad_block)

    grads_qkv = lax.map(
        attend_back,
        (
            blocked(query_full),
            blocked(key_full),
            log_sums,
            blocked(mixed_grad_full),
            blocked(value_full),
            blocked(query_input),
            blocked(key_part),
            blocked(mixed_grad),
        ),
    )
    query_grad, key_grad, value_grad = (
        member.reshape(tokens, local_width).astype(jnp.bfloat16) for member in grads_qkv
    )
    qkv_grad = jnp.stack(
        [
            jnp.einsum("tc,td->cd", full_third, member, preferred_element_type=jnp.float32)
            for member in (query_grad, key_grad, value_grad)
        ]
    )
    attn_bias_grad = jnp.stack(
        [
            jnp.sum(query_grad, axis=0, dtype=jnp.float32),
            jnp.sum(value_grad, axis=0, dtype=jnp.float32),
            out_bias_grad,
        ]
    )
    third_part = jnp.einsum(
        "td,cd->tc", query_grad, qkv_weights[0], preferred_element_type=jnp.float32
    )
    third_part = third_part + jnp.einsum(
        "td,cd->tc", key_grad, qkv_weights[1], preferred_element_type=jnp.float32
    )
    third_part = third_part + jnp.einsum(
        "td,cd->tc", value_grad, qkv_weights[2], preferred_element_type=jnp.float32
    )
    third_grad = lax.psum_scatter(
        third_part.astype(jnp.bfloat16), "chan", scatter_dimension=1, tiled=True
    ).astype(jnp.float32)
    source_third, gain_third, shift_third = norm_backward(
        third_grad.reshape(residual.shape), normed_third, inverse_third, norm_gains[2]
    )
    residual_grad = output_grad.reshape(residual.shape) + source_third
    branch_grad = residual_grad.astype(jnp.bfloat16)
    kernel_second = conv_kernel_grad(full_second, branch_grad)
    bias_second = jnp.sum(branch_grad, axis=(0, 1, 2), dtype=jnp.float32)
    second_grad = lax.psum_scatter(
        conv_input_grad(branch_grad, conv_weights[1]).astype(jnp.bfloat16),
        "chan",
        scatter_dimension=3,
        tiled=True,
    ).astype(jnp.float32)
    source_second, gain_second, shift_second = norm_backward(
        second_grad * slope_second, normed_second, inverse_second, norm_gains[1]
    )
    hidden_grad = source_second.astype(jnp.bfloat16)
    kernel_first = conv_kernel_grad(full_first, hidden_grad)
    bias_first = jnp.sum(hidden_grad, axis=(0, 1, 2), dtype=jnp.float32)
    first_grad = lax.psum_scatter(
        conv_input_grad(hidden_grad, conv_weights[0]).astype(jnp.bfloat16),
        "chan",
        scatter_dimension=3,
        tiled=True,
    ).astype(jnp.float32)
    source_first, gain_first, shift_first = norm_backward(
        first_grad * slope_first, normed_first, inverse_first, norm_gains[0]
    )
    input_grad = residual_grad + source_first
    conv_grad = jnp.stack([kernel_first, kernel_second])
    conv_bias_grad = jnp.stack([bias_first, bias_second])
    (
        qkv_grad,
        attn_bias_grad,
        out_grad,
        proj_grad,
        proj_bias_grad,
        book_grad,
        usage,
        picked,
        commit_sq,
        gain_third,
        shift_third,
        conv_grad,
        conv_bias_grad,
        gain_first,
        gain_second,
        shift_first,
        shift_second,
    ) = lax.psum(
        (
            qkv_grad,
            attn_bias_grad,
            out_grad,
            proj_grad,
            proj_bias_grad,
            book_grad,
            usage,
            picked,
            commit_sq,
            gain_third,
            shift_third,
            conv_grad,
            conv_bias_grad,
            gain_first,
            gain_second,
            shift_first,
            shift_second,
        ),
        "dp",
    )
    share = usage / tokens_all
    perplexity = jnp.exp(-jnp.sum(share * jnp.log(jnp.maximum(share, 1.0 / tokens_all))))
    new_codebook = jnp.where(usage[:, None] > 0.5, codebook, picked)
    commitment = commit_sq / tokens_all
    gains_grad = jnp.stack([gain_first, gain_second, gain_third])
    shifts_grad = jnp.stack([shift_first, shift_second, shift_third])
    return (
        latents.reshape(images, LAT, LAT, -1),
        commitment,
        perplexity,
        new_codebook,
        input_grad,
        gains_grad,
        shifts_grad,
        conv_grad,
        conv_bias_grad,
        qkv_grad,
        attn_bias_grad,
        out_grad,
        proj_grad,
        proj_bias_grad,
        book_grad,
    )


def solution(mesh):
    return jax.shard_map(
        shards,
        mesh=mesh,
        in_specs=(
            P("dp", None, None, "chan"),
            P(None, "chan"),
            P(None, "chan"),
            P(None, None, None, None, "chan"),
            P(None, "chan"),
            P(None, None, "chan"),
            P(None, "chan"),
            P(None, "chan"),
            P(None, "chan"),
            P("chan"),
            P(None, "chan"),
            P("dp", None, None),
            P(),
            P("dp", None, None, "chan"),
        ),
        out_specs=(
            P("dp", None, None, "chan"),
            P("chan"),
            P(),
            P(None, "chan"),
            P("dp", None, None, "chan"),
            P(None, "chan"),
            P(None, "chan"),
            P(None, None, None, None, "chan"),
            P(None, "chan"),
            P(None, None, "chan"),
            P(None, "chan"),
            P(None, "chan"),
            P(None, "chan"),
            P("chan"),
            P(None, "chan"),
        ),
        check_vma=False,
    )
```

profile of v0, /device:TPU:0, one launch (start us, length us, event | category | flops | bytes accessed | tf_op | source)
XLA Modules:
  0.0 478.6 jit_solution(6326328118566964244)
XLA Ops:
  15.8 16.7 %all_gather.27 = bf16[2,16,16,512]{3,2,1,0:T(8,128)(2,1)S(1)} all-gather(bf16[2,16,16,128]{3,2,1,0:T(8,128)(2,1)S(1)} %fusion.29), channel_id=1, replica_groups=mesh['dp'=8,'chan'=4] {'chan'}, dimensions={3}, use_global_device_ids=true | all-gather | bytes 655360 | tf_op jit(solution)/shard_map/all_gather | solution.py:125
  38.0 14.6 %all_gather.28 = bf16[2,16,16,512]{3,2,1,0:T(8,128)(2,1)S(1)} all-gather(bf16[2,16,16,128]{3,2,1,0:T(8,128)(2,1)S(1)} %multiply_convert_fusion.2), channel_id=1, replica_groups=mesh['dp'=8,'chan'=4] {'chan'}, dimensions={3}, use_global_device_ids=true | all-gather | bytes 655360 | tf_op jit(solution)/shard_map/all_gather | solution.py:129
  57.0 14.3 %all_gather.29 = bf16[512,512]{1,0:T(8,128)(2,1)S(1)} all-gather(bf16[512,128]{1,0:T(8,128)(2,1)S(1)} %bitcast.456), channel_id=1, replica_groups=mesh['dp'=8,'chan'=4] {'chan'}, dimensions={1}, use_global_device_ids=true | all-gather | bytes 655360 | tf_op jit(solution)/shard_map/all_gather | solution.py:132
  71.9 15.8 %all_gather.30 = bf16[512,512]{1,0:T(8,128)(2,1)S(1)} all-gather(bf16[512,128]{1,0:T(8,128)(2,1)S(1)} %fusion.7), channel_id=1, replica_groups=mesh['dp'=8,'chan'=4] {'chan'}, dimensions={1}, use_global_device_ids=true | all-gather | bytes 655360 | tf_op jit(solution)/shard_map/all_gather | solution.py:145
  87.8 15.1 %all_gather.31 = bf16[512,512]{1,0:T(8,128)(2,1)S(1)} all-gather(bf16[512,128]{1,0:T(8,128)(2,1)S(1)} %convolution_convert_fusion.4), channel_id=1, replica_groups=mesh['dp'=8,'chan'=4] {'chan'}, dimensions={1}, use_global_device_ids=true | all-gather | bytes 655360 | tf_op jit(solution)/shard_map/all_gather | solution.py:146
  105.2 15.4 %all_gather.32 = bf16[512,512]{1,0:T(8,128)(2,1)S(1)} all-gather(bf16[512,128]{1,0:T(8,128)(2,1)S(1)} %bitcast.458), channel_id=1, replica_groups=mesh['dp'=8,'chan'=4] {'chan'}, dimensions={1}, use_global_device_ids=true | all-gather | bytes 655360 | tf_op jit(solution)/shard_map/all_gather | solution.py:170
  120.9 14.5 %all_gather.33 = bf16[512,512]{1,0:T(8,128)(2,1)} all-gather(bf16[512,128]{1,0:T(8,128)(2,1)S(1)} %fusion.11), channel_id=1, replica_groups=mesh['dp'=8,'chan'=4] {'chan'}, dimensions={1}, use_global_device_ids=true | all-gather | bytes 655360 | tf_op jit(solution)/shard_map/all_gather | solution.py:173
  141.1 2.1 fusion.112
  145.6 2.0 copy.158
  151.2 3.0 copy.114
  157.7 3.4 scatter_custom_fusion.1
  162.4 4.3 gather_fusion.1
  168.1 2.1 convolution_convert_fusion
  170.1 2.1 copy.160
  172.3 19.0 %all_gather.35 = bf16[512,512]{1,0:T(8,128)(2,1)} all-gather(bf16[512,128]{1,0:T(8,128)(2,1)S(1)} %copy-done.27), channel_id=1, replica_groups=mesh['dp'=8,'chan'=4] {'chan'}, dimensions={1}, use_global_device_ids=true | all-gather | bytes 655360 | tf_op jit(solution)/shard_map/all_gather | solution.py:208
  195.8 15.3 %all_gather.34 = bf16[512,512]{1,0:T(8,128)(2,1)S(1)} all-gather(bf16[512,128]{1,0:T(8,128)(2,1)S(1)} %copy.161), channel_id=1, replica_groups=mesh['dp'=8,'chan'=4] {'chan'}, dimensions={1}, use_global_device_ids=true | all-gather | bytes 655360 | tf_op jit(solution)/shard_map/all_gather | solution.py:207
  215.9 2.1 copy.162
  226.0 12.5 %reduce-scatter.20.cloned.1.call-done = bf16[128,512]{1,0:T(8,128)(2,1)} async-done(((bf16[512,512]{1,0:T(8,128)(2,1)}), bf16[128,512]{1,0:T(8,128)(2,1)}) %reduce-scatter.20.cloned.1.call-update) | async-done | bytes 131088
  246.7 2.4 convert_reduce_fusion.3
  258.2 7.2 %copy.164 = bf16[2,16,16,512]{2,1,0,3:T(8,128)(2,1)} copy(bf16[2,16,16,512]{3,2,1,0:T(8,128)(2,1)} %fusion.1) | data formatting | bytes 1048576
  265.4 8.5 %reshape.360 = bf16[512,512]{1,0:T(8,128)(2,1)} reshape(bf16[512,2,16,16]{3,2,1,0:T(8,128)(2,1)} %bitcast.434) | data formatting | bytes 1048576
  277.7 16.3 %reduce-scatter.22.cloned.1.call-done = bf16[128,512]{1,0:T(8,128)(2,1)} async-done(((bf16[512,512]{1,0:T(8,128)(2,1)}), bf16[128,512]{1,0:T(8,128)(2,1)}) %reduce-scatter.22.cloned.1.call-update) | async-done | bytes 131088
  294.0 2.7 reshape.361
  296.7 2.3 copy.165
  309.2 6.4 %copy.166 = bf16[2,16,16,512]{2,1,0,3:T(8,128)(2,1)} copy(bf16[2,16,16,512]{3,2,1,0:T(8,128)(2,1)S(1)} %fusion.2) | data formatting | bytes 1048576
  315.6 8.5 %reshape.362 = bf16[512,512]{1,0:T(8,128)(2,1)} reshape(bf16[512,2,16,16]{3,2,1,0:T(8,128)(2,1)} %bitcast.435) | data formatting | bytes 1048576
  327.7 2.6 pad_maximum_fusion
  330.3 4.4 scatter_custom_fusion
  335.0 9.1 %reduce-scatter.24.cloned.1.call-done = bf16[128,512]{1,0:T(8,128)(2,1)} async-done(((bf16[512,512]{1,0:T(8,128)(2,1)}), bf16[128,512]{1,0:T(8,128)(2,1)}) %reduce-scatter.24.cloned.1.call-update) | async-done | bytes 131088
  348.0 23.3 %all-reduce.4 = (f32[64]{0:T(128)S(1)}, f32[1024]{0:T(1024)S(1)}, f32[1,128]{1,0:T(1,128)S(1)}, f32[1,128]{1,0:T(1,128)S(1)}, f32[1,128]{1,0:T(1,128)S(1)}, /*in...) all-reduce(f32[64]{0:T(128)S(1)} %copy-done.70, ...), channel_id=1, replica_groups=mesh['dp'=8,'chan'=4] {'dp'}, use_global_device_ids=true, to_apply=%region_15.16 | all-reduce | flops 2560 | bytes 20480 | tf_op jit(solution)/shard_map/psum | solution.py:351
  374.4 85.5 %all-reduce.8.cloned.1.call-done = (f32[1024,64]{1,0:T(8,128)}, f32[2,3,3,512,128]{4,3,2,1,0:T(8,128)}, f32[3,512,128]{2,1,0:T(8,128)}, f32[512,128]{1,0:T(8,128...) async-done(((f32[1024,64]{1,0:T(8,128)}, f32[2,3,3,512,128]{4,3,2,1,0:T(8,128)}, f32[3,512,128]{2,1,0:T(8,128)}, f32[512,128]{1,0:T(8,128)}, f32[512,64]{0,1:T(8,128)}, ...) | async-done | bytes 6422544 | tf_op jit(solution)/shard_map/psum | solution.py:351
  463.0 5.0 %copy.174 = f32[2,3,3,512,128]{4,3,2,1,0:T(8,128)} copy(f32[2,3,3,512,128]{4,3,2,1,0:T(8,128)} %get-tuple-element.227) | data formatting | bytes 9437184
  (372 shorter events, 103.0 us)
Async XLA Ops:
  7.2 113.4 %copy-start = (bf16[512,128]{1,0:T(8,128)(2,1)S(1)}, bf16[512,128]{1,0:T(8,128)(2,1)}, u32[]{:S(2)}) copy-start(bf16[512,128]{1,0:T(8,128)(2,1)} %param.21) | copy-start | bytes 393220
  7.2 160.9 %reduce-scatter.16.cloned.1.call-start = ((), (), s32[]{:S(2)}) async-start(), calls=%async_computation.5 | async-start | bytes 655360
  12.6 21.6 %copy-start.42 = (f32[2,128]{1,0:T(2,128)}, f32[2,128]{1,0:T(2,128)S(1)}, u32[]{:S(2)}) copy-start(f32[2,128]{1,0:T(2,128)S(1)} %mul.273) | copy-start | bytes 3076
  13.9 20.3 %copy-start.61 = (f32[128]{0:T(128)}, f32[128]{0:T(128)S(1)}, u32[]{:S(2)}) copy-start(f32[128]{0:T(128)S(1)} %get-tuple-element.190) | copy-start | bytes 1540
  13.9 24.0 %copy-start.56 = (f32[128]{0:T(128)}, f32[128]{0:T(128)S(1)}, u32[]{:S(2)}) copy-start(f32[128]{0:T(128)S(1)} %get-tuple-element.192) | copy-start | bytes 1540
  14.0 42.9 %copy-start.63 = (f32[128]{0:T(128)}, f32[128]{0:T(128)S(1)}, u32[]{:S(2)}) copy-start(f32[128]{0:T(128)S(1)} %get-tuple-element.191) | copy-start | bytes 1540
  14.7 19.5 %copy-start.66 = (f32[128]{0:T(128)}, f32[128]{0:T(128)S(1)}, u32[]{:S(2)}) copy-start(f32[128]{0:T(128)S(1)} %get-tuple-element.197) | copy-start | bytes 1540
  14.8 23.2 %copy-start.64 = (f32[128]{0:T(128)}, f32[128]{0:T(128)S(1)}, u32[]{:S(2)}) copy-start(f32[128]{0:T(128)S(1)} %get-tuple-element.198) | copy-start | bytes 1540
  34.3 20.8 %copy-start.5 = (bf16[3,3,512,128]{3,2,1,0:T(8,128)(2,1)}, bf16[3,3,512,128]{3,2,1,0:T(8,128)(2,1)S(1)}, u32[]{:S(2)}) copy-start(bf16[3,3,512,128]{3,2,1,0:T(8,128)(2,1)S(1)} %get-tuple-element.184) | copy-start | bytes 3538948
  55.4 15.9 %copy-start.76 = (f32[3,128]{1,0:T(4,128)S(1)}, f32[3,128]{1,0:T(4,128)}, u32[]{:S(2)}) copy-start(f32[3,128]{1,0:T(4,128)} %param.20) | copy-start | bytes 4612
  55.4 15.9 %copy-start.14 = (bf16[3,512,128]{2,1,0:T(8,128)(2,1)S(1)}, bf16[3,512,128]{2,1,0:T(8,128)(2,1)}, u32[]{:S(2)}) copy-start(bf16[3,512,128]{2,1,0:T(8,128)(2,1)} %param.19) | copy-start | bytes 1179652
  71.6 32.5 %copy-start.17 = (bf16[512,128]{1,0:T(8,128)(2,1)}, bf16[512,128]{1,0:T(8,128)(2,1)S(1)}, u32[]{:S(2)}) copy-start(bf16[512,128]{1,0:T(8,128)(2,1)S(1)} %convolution_convert_fusion.4) | copy-start | bytes 393220
  71.9 32.2 %copy-start.19 = (bf16[512,128]{1,0:T(8,128)(2,1)}, bf16[512,128]{1,0:T(8,128)(2,1)S(1)}, u32[]{:S(2)}) copy-start(bf16[512,128]{1,0:T(8,128)(2,1)S(1)} %fusion.7) | copy-start | bytes 393220
  105.2 30.2 %copy-start.60 = (s32[512]{0:T(512)S(1)}, s32[512]{0:T(512)}, u32[]{:S(2)}) copy-start(s32[512]{0:T(512)} %reshape.276) | copy-start | bytes 6148
  105.2 30.8 %copy-start.28 = (f32[1024,64]{0,1:T(8,128)S(1)}, f32[1024,64]{0,1:T(8,128)}, u32[]{:S(2)}) copy-start(f32[1024,64]{0,1:T(8,128)} %param.24) | copy-start | bytes 786436
  147.7 47.1 %reduce-scatter.18.cloned.1.call-start = ((), (), s32[]{:S(2)}) async-start(), calls=%async_computation.6 | async-start | bytes 655360
  170.1 21.1 %copy-start.59 = (f32[2,256]{1,0:T(2,128)S(1)}, f32[2,256]{1,0:T(2,128)}, u32[]{:S(2)}) copy-start(f32[2,256]{1,0:T(2,128)} %copy-done.58) | copy-start | bytes 6148
  170.1 21.2 %copy-start.51 = (s32[1024]{0:T(1024)S(1)}, s32[1024]{0:T(1024)}, u32[]{:S(2)}) copy-start(s32[1024]{0:T(1024)} %param.26) | copy-start | bytes 12292
  172.2 66.3 %reduce-scatter.20.cloned.1.call-start = ((), (), s32[]{:S(2)}) async-start(), calls=%async_computation.7 | async-start | bytes 655360
  172.3 20.9 %copy-start.13 = (f32[1024,64]{1,0:T(8,128)S(1)}, f32[1024,64]{1,0:T(8,128)}, u32[]{:S(2)}) copy-start(f32[1024,64]{1,0:T(8,128)} %gather_fusion.1) | copy-start | bytes 786436
  195.8 16.1 %copy-start.12 = (bf16[512,512]{1,0:T(8,128)(2,1)S(1)}, bf16[512,512]{1,0:T(8,128)(2,1)}, u32[]{:S(2)}) copy-start(bf16[512,512]{1,0:T(8,128)(2,1)} %all_gather.35) | copy-start | bytes 1572868
  218.0 76.0 %reduce-scatter.22.cloned.1.call-start = ((), (), s32[]{:S(2)}) async-start(), calls=%async_computation.8 | async-start | bytes 655360
  225.1 15.3 %copy-start.47 = (f32[2,128]{1,0:T(2,128)S(1)}, f32[2,128]{1,0:T(2,128)}, u32[]{:S(2)}) copy-start(f32[2,128]{1,0:T(2,128)} %copy-done.46) | copy-start | bytes 3076
  226.0 17.6 %copy-start.48 = (f32[2,8]{0,1:T(8,128)S(1)}, f32[2,8]{0,1:T(8,128)}, u32[]{:S(2)}) copy-start(f32[2,8]{0,1:T(8,128)} %copy.115) | copy-start | bytes 196
  226.0 17.6 %copy-start.49 = (f32[2,8]{0,1:T(8,128)S(1)}, f32[2,8]{0,1:T(8,128)}, u32[]{:S(2)}) copy-start(f32[2,8]{0,1:T(8,128)} %copy.113) | copy-start | bytes 196
  226.0 17.6 %copy-start.50 = (f32[8,16]{1,0:T(8,128)S(1)}, f32[8,16]{1,0:T(8,128)}, u32[]{:S(2)}) copy-start(f32[8,16]{1,0:T(8,128)} %mul.310) | copy-start | bytes 1540
  273.9 70.1 %reduce-scatter.24.cloned.1.call-start = ((), (), s32[]{:S(2)}) async-start(), calls=%async_computation.9 | async-start | bytes 655360
  277.7 21.3 %copy-start.45 = (f32[2,128]{1,0:T(2,128)S(1)}, f32[2,128]{1,0:T(2,128)}, u32[]{:S(2)}) copy-start(f32[2,128]{1,0:T(2,128)} %copy-done.44) | copy-start | bytes 3076
  277.7 21.3 %copy-start.57 = (f32[128]{0:T(128)S(1)}, f32[128]{0:T(128)}, u32[]{:S(2)}) copy-start(f32[128]{0:T(128)} %copy-done.56) | copy-start | bytes 1540
  277.7 21.3 %copy-start.65 = (f32[128]{0:T(128)S(1)}, f32[128]{0:T(128)}, u32[]{:S(2)}) copy-start(f32[128]{0:T(128)} %copy-done.64) | copy-start | bytes 1540
  324.1 135.8 %all-reduce.8.cloned.1.call-start = ((), (), s32[]{:S(2)}) async-start(), calls=%async_computation.10 | async-start | bytes 13893632 | tf_op jit(solution)/shard_map/psum | solution.py:351
  345.9 27.7 %copy-start.21 = (f32[2,16,16,128]{3,2,1,0:T(8,128)S(1)}, f32[2,16,16,128]{3,2,1,0:T(8,128)}, u32[]{:S(2)}) copy-start(f32[2,16,16,128]{3,2,1,0:T(8,128)} %get-tuple-element.179) | copy-start | bytes 786436
  (52 other events, 232.6 us)
Sparse Core Ops, SparseCore 0:
  147.8 20.2 reduce-scatter.15
  172.3 22.3 reduce-scatter.17
  218.1 20.3 reduce-scatter.19
  274.1 19.9 reduce-scatter.21
  324.2 19.7 reduce-scatter.23
  349.0 110.8 all-reduce.7
where the time goes:
time: 487 us; the launch traced here: 479 us
  blocking collectives  164 us (34%)
  waiting for transfers between devices  125 us (26%)
  local copies, waits for them, and re-layouts  93.7 us (19%)
  matrix products  41.6 us (9%)
  other arithmetic  35.7 us (7%)
  between operations  17.3 us (4%)
    psum x1, waiting for transfers between devices, shards(): lax.psum((qkv_grad, attn_bias_grad, out_grad, proj_grad, proj_bias_grad,...  85.5 us
    unnamed x177, local copies, waits for them, and re-layouts  63.5 us
    unnamed x11, waiting for transfers between devices  39.7 us
    psum x1, blocking collectives, shards(): lax.psum((qkv_grad, attn_bias_grad, out_grad, proj_grad, proj_bias_grad,...  23.3 us
    all_gather x1, blocking collectives, shards(): lax.all_gather(value_part, 'chan', axis=1, tiled=True)  19 us
    all_gather x1, blocking collectives, shards(): lax.all_gather(act_first.astype(jnp.bfloat16), 'chan', axis=3, tiled=True)  16.7 us
    all_gather x1, blocking collectives, shards(): lax.all_gather(query_input, 'chan', axis=1, tiled=True)  15.8 us
    all_gather x1, blocking collectives, shards(): full_mixed = lax.all_gather(mixed_low, 'chan', axis=1, tiled=True)  15.4 us
  transfers between devices with their start and end apart: 6, of which 6 were waited for; matrix products, arithmetic and copies ran while one was open for 10% of the time, Pallas kernels for 0%

commit v1 on v0

v1 whole, which is shorter than its diff:
```python
import jax
import jax.numpy as jnp
from jax import lax
from jax.experimental import pallas as pl
from jax.experimental.pallas import tpu as pltpu
from jax.sharding import PartitionSpec as P

F32 = jnp.float32
BF = jnp.bfloat16
C = 512
CODES = 1024
LAT = 16
POS = LAT * LAT
EPSILON = 1e-06
BETA = 0.25
SCORE_SCALE = float(C) ** (-0.5)
GROUP_COUNT = float(POS * 16)
WIDE = 1152
VMEM = 20
HEAVY = 10**11
PARTS = 8


def call(body, outs, *args, scratch=(), flops=0, name=None, space=pltpu.VMEM):
    result = pl.pallas_call(
        body,
        out_shape=list(outs),
        in_specs=[pl.BlockSpec(memory_space=pltpu.SMEM)]
        + [pl.BlockSpec(memory_space=space)] * (len(args) - 1),
        out_specs=[pl.BlockSpec(memory_space=pltpu.VMEM)] * len(outs),
        scratch_shapes=list(scratch),
        compiler_params=pltpu.CompilerParams(vmem_limit_bytes=VMEM * 2**20),
        cost_estimate=pl.CostEstimate(flops=flops, bytes_accessed=1, transcendentals=0),
        name=name,
    )(*args)
    return result


def sds(shape, dtype):
    return jax.ShapeDtypeStruct(shape, dtype)


def dot(a, b):
    return jnp.dot(a, b, preferred_element_type=F32)


def dot_nt(a, b):
    return lax.dot_general(a, b, (((1,), (1,)), ((), ())), preferred_element_type=F32)


def dot_tn(a, b):
    return lax.dot_general(a, b, (((0,), (0,)), ((), ())), preferred_element_type=F32)


def lanes(parts):
    return jnp.concatenate(parts, axis=1)


def rows_of(parts):
    return jnp.concatenate(parts, axis=0)


def pack_rows(vectors, height=8):
    width = vectors[0].shape[1]
    spot = lax.broadcasted_iota(jnp.int32, (height, width), 0)
    result = jnp.zeros((height, width), F32)
    for index, vector in enumerate(vectors):
        result = jnp.where(spot == index, vector, result)
    return result


def split_low(values):
    high = values.astype(BF).astype(F32)
    return high, values - high


def group_sums(rows):
    first = lax.broadcasted_iota(jnp.int32, (128, 128), 0) >> 4
    second = lax.broadcasted_iota(jnp.int32, (128, 128), 1) >> 4
    ones = (first == second).astype(F32).astype(BF)
    high, rest = split_low(rows)
    middle, low = split_low(rest)
    stacked = rows_of([high, middle, low, jnp.zeros_like(high)]).astype(BF)
    summed = dot(stacked, ones)
    return summed[0:8] + summed[8:16] + summed[16:24]


def col_sum(values):
    return jnp.sum(values, axis=0, keepdims=True)


def moments(values):
    one, two = values[:POS], values[POS:]
    mean = group_sums(pack_rows([col_sum(one), col_sum(two)])) * (1.0 / GROUP_COUNT)
    one, two = one - mean[0:1], two - mean[1:2]
    variance = group_sums(pack_rows([col_sum(one * one), col_sum(two * two)])) * (
        1.0 / GROUP_COUNT
    )
    inverse = lax.rsqrt(variance + EPSILON)
    deviation = jnp.sqrt(variance + EPSILON)
    normed = rows_of([one * inverse[0:1], two * inverse[1:2]])
    stats = pack_rows(
        [mean[0:1], mean[1:2], inverse[0:1], inverse[1:2], deviation[0:1], deviation[1:2]]
    )
    return normed, stats


def renormed(values, stats):
    return rows_of(
        [
            (values[:POS] - stats[0:1]) * stats[2:3],
            (values[POS:] - stats[1:2]) * stats[3:4],
        ]
    )


def norm_back(upstream, normed, stats, gain):
    sides = [(upstream[:POS], normed[:POS]), (upstream[POS:], normed[POS:])]
    plain = [col_sum(u) for u, _ in sides]
    weighted = [col_sum(u * n) for u, n in sides]
    means = group_sums(
        pack_rows([plain[0] * gain, plain[1] * gain, weighted[0] * gain, weighted[1] * gain])
    ) * (1.0 / GROUP_COUNT)
    parts = [
        stats[2 + m : 3 + m] * (u * gain - means[m : m + 1] - n * means[2 + m : 3 + m])
        for m, (u, n) in enumerate(sides)
    ]
    return rows_of(parts), weighted[0] + weighted[1], plain[0] + plain[1]


GAIN, SHIFT, CONV_BIAS, ATTN_BIAS, PROJ_BIAS = 0, 3, 6, 8, 11


def param(ref, index):
    return ref[index : index + 1]


def column_masks(height):
    column = lax.broadcasted_iota(jnp.int32, (height, 128), 0) & (LAT - 1)
    return column >= 1, column <= LAT - 2


def later_rows(values):
    blank = jnp.zeros((LAT, values.shape[1]), values.dtype)
    return rows_of([values[LAT:POS], blank, values[POS + LAT :], blank])


def earlier_rows(values):
    blank = jnp.zeros((LAT, values.shape[1]), values.dtype)
    return rows_of([blank, values[: POS - LAT], blank, values[POS : 2 * POS - LAT]])


def conv_forward(pieces, w_ref):
    full = lanes(pieces)
    height = full.shape[0]
    inner, outer = column_masks(height)
    sums = []
    for col_tap in range(3):
        total = None
        for row_tap in range(3):
            tap = 3 * row_tap + col_tap
            part = dot(full, w_ref[0, :, 128 * tap : 128 * tap + 128])
            if row_tap == 0:
                part = earlier_rows(part)
            elif row_tap == 2:
                part = later_rows(part)
            total = part if total is None else total + part
        sums.append(total)
    left = jnp.where(inner, pltpu.roll(sums[0], 1, 0), 0.0)
    right = jnp.where(outer, pltpu.roll(sums[2], height - 1, 0), 0.0)
    return sums[1] + left + right


def spread_taps(gradient):
    height = gradient.shape[0]
    inner, outer = column_masks(height)
    by_column = [
        jnp.where(outer, pltpu.roll(gradient, height - 1, 0), 0.0),
        gradient,
        jnp.where(inner, pltpu.roll(gradient, 1, 0), 0.0),
    ]
    copies = [None] * 9
    for col_tap in range(3):
        copies[col_tap] = later_rows(by_column[col_tap])
        copies[3 + col_tap] = by_column[col_tap]
        copies[6 + col_tap] = earlier_rows(by_column[col_tap])
    return lanes([c.astype(BF) for c in copies])


def part_row(scalars, part):
    place = scalars[1] ^ part
    block = (place >> 1) ^ scalars[0]
    return place, pl.multiple_of(block * 128 + (place & 1) * 64, 64)


def first_norm_kernel(scalars, x_ref, gain_ref, shift_ref, act_ref, stats_ref):
    normed, stats = moments(x_ref[...].astype(F32))
    pre = normed * gain_ref[0:1] + shift_ref[0:1]
    act_ref[...] = (pre * jax.nn.sigmoid(pre)).astype(BF)
    stats_ref[...] = stats


def code_column(codes):
    grid = rows_of([codes[m] for m in range(codes.shape[0])])
    height = grid.shape[0] * LAT
    high = grid >> 5
    both = lanes([high.astype(F32), (grid - (high << 5)).astype(F32)]).astype(BF)
    lines = lax.broadcasted_iota(jnp.int32, (height, grid.shape[0]), 0) >> 4
    own = (lines == lax.broadcasted_iota(jnp.int32, lines.shape, 1)).astype(F32).astype(BF)
    spread = dot(own, both)
    column = lax.broadcasted_iota(jnp.int32, (height, LAT), 0) & (LAT - 1)
    here = column == lax.broadcasted_iota(jnp.int32, (height, LAT), 1)
    merged = 32.0 * spread[:, :LAT] + spread[:, LAT:]
    return jnp.sum(jnp.where(here, merged, 0.0), axis=1, keepdims=True).astype(jnp.int32)


def start_kernel(scalars, codes_ref, book_ref, cot_ref, _, hot_ref, quant_ref, usage_ref, fixed_ref, start):
    tokens = hot_ref.shape[0]
    hot32 = (
        code_column(codes_ref[...]) == lax.broadcasted_iota(jnp.int32, (tokens, CODES), 1)
    ).astype(F32)
    hot = hot32.astype(BF)
    hot_ref[...] = hot
    counts = col_sum(hot32)
    usage_ref[...] = pack_rows([counts[:, 128 * i : 128 * i + 128] for i in range(8)])
    high, rest = split_low(book_ref[...])
    middle, low = split_low(rest)
    picked = dot_nt(hot, rows_of([high, middle, low]).astype(BF))
    width = book_ref.shape[0]
    quantized = picked[:, :width] + picked[:, width : 2 * width] + picked[:, 2 * width :]
    quant_ref[...] = quantized
    start[...] = cot_ref[...].astype(F32) - 2.0 * BETA * quantized
    for k in range(4):
        row = (scalars[0] ^ k) * 128
        one = start[pl.ds(pl.multiple_of(row, 64), 64), :]
        two = start[pl.ds(pl.multiple_of(row + 64, 64), 64), :]
        high, low = split_low(lanes([one, two]))
        fixed_ref[k, 0:64] = high.astype(BF)
        fixed_ref[k, 64:128] = low.astype(BF)


def conv_weight_kernel(scalars, w_ref, o_ref):
    for k in range(4):
        own = pl.ds(pl.multiple_of((scalars[0] ^ k) * 128, 128), 128)
        for tap in range(9):
            o_ref[0, 128 * k : 128 * k + 128, 128 * tap : 128 * tap + 128] = w_ref[0, tap, own, :]


def attn_weight_kernel(scalars, own_ref, other_ref, o_ref):
    for part in range(PARTS):
        source = (own_ref if part % 2 == 0 else other_ref).at[part // 2]
        _, row = part_row(scalars, part)
        spot = pl.ds(row, 64)
        for k in range(4):
            for m in range(4):
                o_ref[spot, 512 * m + 128 * k : 512 * m + 128 * k + 128] = source[
                    k, :, 128 * m : 128 * m + 128
                ]
        for pair in range(2):
            o_ref[spot, 2048 + 128 * pair : 2176 + 128 * pair] = lanes(
                [source[2 * pair + i, :, 512:576] for i in range(2)]
            )


def conv_one_kernel(
    scalars, a0, a1, a2, a3, w_ref, param_ref, _, hidden_ref, stats_ref, act_ref
):
    hidden = conv_forward([a0[...], a1[...], a2[...], a3[...]], w_ref) + param(
        param_ref, CONV_BIAS
    )
    hidden_ref[...] = hidden
    normed, stats = moments(hidden)
    stats_ref[...] = stats
    pre = normed * param(param_ref, GAIN + 1) + param(param_ref, SHIFT + 1)
    act_ref[...] = (pre * jax.nn.sigmoid(pre)).astype(BF)


def conv_two_kernel(
    scalars, a0, a1, a2, a3, w_ref, param_ref, x_ref, fixed_ref, normed_ref, stats_ref, *pay_refs
):
    residual = x_ref[...].astype(F32) + (
        conv_forward([a0[...], a1[...], a2[...], a3[...]], w_ref) + param(param_ref, CONV_BIAS + 1)
    )
    normed, stats = moments(residual)
    normed_ref[...] = normed
    stats_ref[...] = stats
    gain, shift = param(param_ref, GAIN + 2), param(param_ref, SHIFT + 2)
    for k, ref in enumerate(pay_refs):
        target = scalars[0] ^ k
        own, other = target * 128, (target ^ 1) * 128
        ref[0:128] = (
            normed_ref[pl.ds(pl.multiple_of(other, 128), 128), :] * gain + shift
        ).astype(BF)
        high, low = split_low(normed_ref[pl.ds(pl.multiple_of(own, 128), 128), :])
        ref[128:256] = high.astype(BF)
        ref[256:384] = low.astype(BF)
        is_two = jnp.broadcast_to(target >> 1, (1, 128)) == 1
        mean = jnp.where(is_two, stats[1:2], stats[0:1])
        deviation = jnp.where(is_two, stats[5:6], stats[4:5])
        rows = list(split_low(mean)) + list(split_low(deviation))
        for index in (GAIN + 2, SHIFT + 2, ATTN_BIAS, ATTN_BIAS + 1, ATTN_BIAS + 2, PROJ_BIAS):
            rows.extend(split_low(param(param_ref, index)))
        ref[384:400] = pack_rows(rows, 16).astype(BF)
        ref[400:528] = fixed_ref[k]


def attn_in_kernel(scalars, n0, n1, n2, n3, norm_ref, residual_ref, bias_ref):
    pieces = [n0, n1, n2, n3]
    tails = [n[384:400].astype(F32) for n in pieces]

    def vector(index, width=128):
        row = 2 * index
        return lanes([t[row : row + 1, :width] + t[row + 1 : row + 2, :width] for t in tails])

    mean, deviation, gain, shift = [vector(index) for index in range(4)]
    empty = jnp.zeros((1, 256), F32)
    bias_ref[...] = pack_rows([vector(4), vector(5), vector(6), lanes([vector(7, 64), empty])])
    own = lanes([n[128:256].astype(F32) + n[256:384].astype(F32) for n in pieces])
    residual_ref[...] = own * deviation + mean
    norm_ref[0:128] = (own * gain + shift).astype(BF)
    norm_ref[128:POS] = lanes([n[0:128] for n in pieces])


def attention_kernel(
    scalars, norm_ref, residual_ref, bias_ref, n0, n1, n2, n3, w_ref, *refs
):
    pay_refs = refs[:4]
    out_ref, lat_grad_ref, mixed_ref, att_grad_ref, qg_ref, kg_ref, vg_ref, sums_ref = refs[4:]
    query_bias, value_bias, out_bias = [bias_ref[m : m + 1] for m in range(3)]
    proj_bias = bias_ref[3:4, 0:256]
    pieces = [n0, n1, n2, n3]
    normed = norm_ref[...]
    query = (dot(norm_ref[0:128], w_ref[:, 0:512]) + query_bias).astype(BF)
    keys = dot(normed, w_ref[:, 512:1024]).astype(BF)
    values = (dot(normed, w_ref[:, 1024:1536]) + value_bias).astype(BF)
    scores = dot_nt(query, keys) * SCORE_SCALE
    weights = jnp.exp(scores - jnp.max(scores, axis=1, keepdims=True))
    probs = weights / jnp.sum(weights, axis=1, keepdims=True)
    probs_low = probs.astype(BF)
    mixed = dot(probs_low, values).astype(BF)
    mixed_ref[...] = mixed
    attended = dot(mixed, w_ref[:, 1536:2048]) + out_bias
    output = (residual_ref[...] + attended).astype(BF)
    out_ref[...] = output
    latents = dot(output, w_ref[:, 2048:2304]) + proj_bias
    fixed = []
    for n in pieces:
        both = n[400:464].astype(F32) + n[464:528].astype(F32)
        fixed.append(rows_of([both[:, :64], both[:, 64:]]))
    lat_grad = (lanes(fixed) + 2.0 * BETA * latents).astype(BF)
    blank = jnp.zeros((128, 64), BF)
    for k in range(4):
        lat_grad_ref[:, 128 * k : 128 * k + 128] = lanes([lat_grad[:, 64 * k : 64 * k + 64], blank])
    out_grad = dot_nt(lat_grad, w_ref[:, 2048:2304])
    att_grad = out_grad.astype(BF)
    att_grad_ref[...] = att_grad
    mixed_grad = dot_nt(att_grad, w_ref[:, 1536:2048]).astype(BF)
    probs_grad = dot_nt(mixed_grad, values)
    row_dot = jnp.sum(probs * probs_grad, axis=1, keepdims=True)
    score_grad = (probs * (probs_grad - row_dot)).astype(BF)
    query_grad = (dot(score_grad, keys) * SCORE_SCALE).astype(BF)
    key_grad = (dot_tn(score_grad, query) * SCORE_SCALE).astype(BF)
    value_grad = dot_tn(probs_low, mixed_grad).astype(BF)
    qg_ref[...] = query_grad
    kg_ref[...] = key_grad
    vg_ref[...] = value_grad
    upstream = dot_nt(key_grad, w_ref[:, 512:1024]) + dot_nt(value_grad, w_ref[:, 1024:1536])
    upstream_own = upstream[:128] + dot_nt(query_grad, w_ref[:, 0:512])
    for k in range(4):
        ref = pay_refs[k]
        ref[0:128] = upstream_own[:, 128 * k : 128 * k + 128].astype(ref.dtype)
        ref[128:POS] = upstream[128:, 128 * k : 128 * k + 128].astype(ref.dtype)
        ref[POS : POS + 128] = out_grad[:, 128 * k : 128 * k + 128].astype(ref.dtype)
        piece = latents[:, 64 * k : 64 * k + 64]
        ref[POS + 128 : POS + 192] = lanes([piece[:64], piece[64:]]).astype(ref.dtype)
    sums_ref[...] = pack_rows(
        [
            col_sum(query_grad.astype(F32)),
            col_sum(value_grad.astype(F32)),
            col_sum(att_grad.astype(F32)),
            lanes(
                [
                    part
                    for k in range(4)
                    for part in (
                        col_sum(lat_grad[:, 64 * k : 64 * k + 64].astype(F32)),
                        jnp.zeros((1, 64), F32),
                    )
                ]
            ),
        ]
    )


def attn_grad_kernel(
    scalars,
    norm_ref,
    out_ref,
    lat_grad_ref,
    mixed_ref,
    att_grad_ref,
    qg_ref,
    kg_ref,
    vg_ref,
    sums_ref,
    usage_ref,
    *refs,
):
    keep_refs, send_ref, grads = refs[:4], refs[4], refs[5]
    grads[:, 0:512] = dot_tn(norm_ref[0:128], qg_ref[...]).astype(BF)
    grads[:, 512:1024] = dot_tn(norm_ref[...], kg_ref[...]).astype(BF)
    grads[:, 1024:1536] = dot_tn(norm_ref[...], vg_ref[...]).astype(BF)
    grads[:, 1536:2048] = dot_tn(mixed_ref[...], att_grad_ref[...]).astype(BF)
    grads[:, 2048:2560] = dot_tn(out_ref[...], lat_grad_ref[...]).astype(BF)
    right = lax.broadcasted_iota(jnp.int32, (16, 128), 1) >= 64

    def halves(vectors, offset):
        blank = jnp.zeros((1, 128), F32)
        entries = [blank] * offset
        for vector in vectors:
            entries += [pltpu.roll(vector, 64, 1), vector]
        return jnp.where(right, pack_rows(entries, 16), 0.0)

    biases = []
    for k in range(4):
        vectors = [sums_ref[m : m + 1, 128 * k : 128 * k + 128] for m in range(4)]
        biases.append(halves(vectors, 4))
    tens = jnp.floor(usage_ref[...] * (1.0 / 16.0))
    ones = usage_ref[...] - 16.0 * tens
    for part in range(PARTS):
        place, row = part_row(scalars, part)
        is_first = (jnp.broadcast_to(place, (16, 128)) == 0).astype(F32)
        here = jnp.broadcast_to(place, (8, 128)) == lax.broadcasted_iota(jnp.int32, (8, 128), 0)
        counts = [col_sum(jnp.where(here, digit, 0.0)) for digit in (tens, ones)]
        for k in range(4):
            ref = keep_refs[part // 2].at[k] if part % 2 == 0 else send_ref.at[part // 2, k]
            for m in range(4):
                ref[:, 128 * m : 128 * m + 128] = grads[
                    pl.ds(row, 64), 512 * m + 128 * k : 512 * m + 128 * k + 128
                ]
            extra = biases[k] * is_first
            if k == 0:
                extra = extra + halves(counts, 0)
            block = slice(2048 + 128 * k, 2176 + 128 * k)
            ref[0:16, 512:640] = (grads[pl.ds(row, 16), block].astype(F32) + extra).astype(BF)
            ref[16:64, 512:640] = grads[pl.ds(row + 16, 48), block]


def third_back_kernel(
    scalars,
    p0,
    p1,
    p2,
    p3,
    normed_ref,
    stats_ref,
    param_ref,
    _,
    w_ref,
    residual_ref,
    taps_ref,
    lat_ref,
    small_ref,
    q0,
    q1,
    q2,
    q3,
    up_ref,
    out_ref,
):
    z = scalars[0]
    for near, far, base in ((p0, p1, z), (p2, p3, z ^ 2)):
        first, second = near[0:POS].astype(F32), far[0:POS].astype(F32)
        up_ref[pl.ds(pl.multiple_of(base * 128, 128), 128), :] = first[:128] + second[128:]
        up_ref[pl.ds(pl.multiple_of((base ^ 1) * 128, 128), 128), :] = first[128:] + second[:128]
    for k, ref in enumerate((p0, p1, p2, p3)):
        row = (z ^ k) * 128
        out_ref[pl.ds(pl.multiple_of(row, 128), 128), :] = ref[POS : POS + 128].astype(F32)
        piece = ref[POS + 128 : POS + 192].astype(F32)
        lat_ref[pl.ds(pl.multiple_of(row, 64), 64), :] = piece[:, :64]
        lat_ref[pl.ds(pl.multiple_of(row + 64, 64), 64), :] = piece[:, 64:]
    source, gain_grad, shift_grad = norm_back(
        up_ref[...], normed_ref[...], stats_ref[...], param(param_ref, GAIN + 2)
    )
    residual = out_ref[...] + source
    residual_ref[...] = residual
    low = residual.astype(BF).astype(F32)
    small_ref[...] = pack_rows([gain_grad, shift_grad, col_sum(low)])
    send_taps(low, w_ref, taps_ref, (q0, q1, q2, q3))


def send_taps(gradient, w_ref, taps_ref, piece_refs):
    taps = spread_taps(gradient)
    taps_ref[...] = taps
    for k, ref in enumerate(piece_refs):
        ref[...] = dot_nt(taps, w_ref[0, 128 * k : 128 * k + 128, :]).astype(ref.dtype)


def swish_back(gradient, normed, gain, shift):
    pre = normed * gain + shift
    gate = jax.nn.sigmoid(pre)
    return gradient * (gate * (1.0 + pre * (1.0 - gate)))


def second_back_kernel(
    scalars,
    p0,
    p1,
    p2,
    p3,
    hidden_ref,
    stats_ref,
    param_ref,
    _,
    __,
    w_ref,
    taps_ref,
    small_ref,
    q0,
    q1,
    q2,
    q3,
):
    gradient = p0[...] + p1[...].astype(F32) + p2[...].astype(F32) + p3[...].astype(F32)
    stats = stats_ref[...]
    normed = renormed(hidden_ref[...], stats)
    gain = param(param_ref, GAIN + 1)
    upstream = swish_back(gradient, normed, gain, param(param_ref, SHIFT + 1))
    source, gain_grad, shift_grad = norm_back(upstream, normed, stats, gain)
    low = source.astype(BF).astype(F32)
    small_ref[...] = pack_rows([gain_grad, shift_grad, col_sum(low)])
    send_taps(low, w_ref, taps_ref, (q0, q1, q2, q3))


def first_back_kernel(
    scalars,
    p0,
    p1,
    p2,
    p3,
    x_ref,
    stats_ref,
    param_ref,
    residual_ref,
    _,
    __,
    ___,
    grad_ref,
    small_ref,
):
    gradient = p0[...] + p1[...].astype(F32) + p2[...].astype(F32) + p3[...].astype(F32)
    stats = stats_ref[...]
    normed = renormed(x_ref[...].astype(F32), stats)
    gain = param(param_ref, GAIN)
    upstream = swish_back(gradient, normed, gain, param(param_ref, SHIFT))
    source, gain_grad, shift_grad = norm_back(upstream, normed, stats, gain)
    grad_ref[...] = residual_ref[...] + source
    small_ref[...] = pack_rows([gain_grad, shift_grad])


def conv_one_grad_kernel(scalars, a0, a1, a2, a3, taps_ref, *refs):
    keep_refs, send_ref, grads = refs[:4], refs[4], refs[5]
    full = lanes([a0[...], a1[...], a2[...], a3[...]])
    grads[...] = dot_tn(full, taps_ref[...]).astype(BF)
    for part in range(PARTS):
        _, row = part_row(scalars, part)
        value = grads[pl.ds(row, 64), :]
        if part % 2 == 0:
            keep_refs[part // 2][...] = value
        else:
            send_ref[part // 2] = value


def conv_two_grad_kernel(
    scalars, a0, a1, a2, a3, taps_ref, hot_ref, lat_ref, quant_ref, reset_ref, scale, *refs
):
    keep_refs, send_ref, commit_ref, grads, book = refs[:4], refs[4], refs[5], refs[6], refs[7]
    full = lanes([a0[...], a1[...], a2[...], a3[...]])
    grads[...] = dot_tn(full, taps_ref[...]).astype(BF)
    latents = lat_ref[...]
    difference = latents - quant_ref[...]
    commit_ref[...] = pack_rows([lanes([col_sum(difference * difference), jnp.zeros((1, 64), F32)])])
    high, low = split_low(difference * (-scale))
    sums = dot_tn(lanes([high, low]).astype(BF), hot_ref[...])
    tokens = latents.shape[0]
    where = reset_ref[...] - scalars[2] * tokens
    chosen = (where == lax.broadcasted_iota(jnp.int32, (tokens, CODES), 0)).astype(F32).astype(BF)
    picked = dot_tn(latents.astype(BF), chosen)
    book[0:64] = (sums[:64] + sums[64:]).astype(BF)
    book[64:128] = picked.astype(BF)
    for part in range(PARTS):
        place, row = part_row(scalars, part)
        ref = keep_refs[part // 2] if part % 2 == 0 else send_ref.at[part // 2]
        ref[:, 0:WIDE] = grads[pl.ds(row, 64), :]
        column = pl.ds(pl.multiple_of(place * 128, 128), 128)
        ref[:, WIDE : WIDE + 128] = book[0:64, column]
        ref[:, WIDE + 128 : WIDE + 256] = book[64:128, column]


def finish_two_kernel(
    tokens_all,
    scalars,
    own_ref,
    other_ref,
    book_ref,
    conv_ref,
    gain_ref,
    shift_ref,
    bias_ref,
    commit_ref,
    qkv_ref,
    out_w_ref,
    proj_ref,
    book_grad_ref,
    new_book_ref,
    perplexity_ref,
    attn_bias_ref,
    proj_bias_ref,
    usage,
    proj,
    picked,
):
    extra_sum = jnp.zeros((16, 128), F32)
    total = jnp.zeros((16, 128), F32)
    for part in range(PARTS):
        source = (own_ref if part % 2 == 0 else other_ref).at[part // 2]
        place = scalars[1] ^ part
        rows = pl.ds(pl.multiple_of(place * 64, 64), 64)
        for tap in range(9):
            conv_ref[0, tap, rows, :] = source[:, 128 * tap : 128 * tap + 128].astype(F32)
        column = pl.ds(pl.multiple_of(place * 128, 128), 128)
        book_grad_ref[:, column] = source[:, WIDE : WIDE + 128].astype(F32)
        picked[:, column] = source[:, WIDE + 128 : WIDE + 256].astype(F32)
        for m in range(3):
            qkv_ref[m, rows, :] = source[:, 1408 + 128 * m : 1536 + 128 * m].astype(F32)
        out_w_ref[rows, :] = source[:, 1792:1920].astype(F32)
        proj[rows, :] = source[:, 1920:2048].astype(F32)
        extra = source[0:16, 1920:2048].astype(F32)
        extra_sum = extra_sum + extra
        usage[pl.ds(place, 1), :] = lanes(
            [
                16.0 * extra[0:1, 64:] + extra[2:3, 64:],
                16.0 * extra[1:2, 64:] + extra[3:4, 64:],
            ]
        )
        both = source[0:32, 2048:2176].astype(F32)
        total = total + (both[0:16] + both[16:32])
    for index, row in enumerate((0, 2, 5)):
        gain_ref[index : index + 1] = total[row : row + 1]
        shift_ref[index : index + 1] = total[row + 1 : row + 2]
    bias_ref[0:1] = total[4:5]
    bias_ref[1:2] = total[7:8]
    commit_ref[...] = total[8:9, :64] * (1.0 / tokens_all)
    proj_ref[...] = jnp.transpose(proj[...])[0:64]
    counts = usage[...]
    share = counts * (1.0 / tokens_all)
    terms = share * jnp.log(jnp.maximum(share, 1.0 / tokens_all))
    entropy = jnp.sum(jnp.sum(terms, axis=1, keepdims=True), axis=0, keepdims=True)
    perplexity_ref[...] = jnp.exp(-entropy)
    for block in range(8):
        spot = slice(128 * block, 128 * block + 128)
        new_book_ref[:, spot] = jnp.where(
            counts[block : block + 1] > 0.5, book_ref[:, spot], picked[:, spot]
        )
    for m in range(3):
        attn_bias_ref[m : m + 1] = lanes(
            [extra_sum[4 + 2 * m : 5 + 2 * m, 64:], extra_sum[5 + 2 * m : 6 + 2 * m, 64:]]
        )
    proj_bias_ref[...] = extra_sum[10:11, 64:]


def finish_one_kernel(scalars, own_ref, other_ref, held_ref, conv_ref):
    for part in range(PARTS):
        source = (own_ref if part % 2 == 0 else other_ref).at[part // 2]
        rows = pl.ds(pl.multiple_of((scalars[1] ^ part) * 64, 64), 64)
        for tap in range(9):
            conv_ref[0, tap, rows, :] = source[:, 128 * tap : 128 * tap + 128].astype(F32)


def pair_add_kernel(scalars, k0, k1, k2, k3, get_ref, _, keep_ref, send_ref):
    for i, ref in enumerate((k0, k1, k2, k3)):
        target = (send_ref if i % 2 else keep_ref).at[i // 2]
        target[...] = plus(ref[...], get_ref[i])


def plus(first, second):
    return (first.astype(F32) + second.astype(F32)).astype(BF)


def half_add_kernel(scalars, keep_ref, get_ref, _, own_ref, send_ref):
    own_ref[...] = plus(keep_ref[0], get_ref[0])
    send_ref[...] = plus(keep_ref[1], get_ref[1])


def attn_sum_kernel(scalars, a0, a1, _, keep_ref, send_ref):
    for k in range(2):
        keep_ref[k] = plus(a0[k], a1[k])
        send_ref[k] = plus(a0[2 + k], a1[2 + k])


def tail_first_kernel(
    scalars,
    k0,
    k1,
    k2,
    k3,
    one_get,
    two_keep,
    two_get,
    att_keep,
    att_get,
    _,
    o0,
    o1,
    o2,
    o3,
    two_own,
    two_send,
    att_own,
    att_send,
):
    for i, (ref, out) in enumerate(((k0, o0), (k1, o1), (k2, o2), (k3, o3))):
        out[...] = plus(ref[...], one_get[i])
    two_own[...] = plus(two_keep[0], two_get[0])
    two_send[...] = plus(two_keep[1], two_get[1])
    att_own[...] = plus(att_keep[0], att_get[0])
    att_send[...] = plus(att_keep[1], att_get[1])


def tail_second_kernel(
    scalars,
    o0,
    o1,
    o2,
    o3,
    two_own,
    two_get,
    att_own,
    att_get,
    small_one,
    small_two,
    small_three,
    commit,
    two_ref,
    one_ref,
):
    total = o0[...].astype(F32)
    for ref in (o1, o2, o3):
        total = total + ref[...].astype(F32)
    one_ref[...] = total.astype(BF)
    two_ref[:, 0:1408] = plus(two_own[...], two_get[...])
    two_ref[:, 1408:2048] = plus(att_own[...], att_get[...])
    rows = [small_one[0:1], small_one[1:2]]
    rows += [small_two[m : m + 1] for m in range(3)]
    rows += [small_three[m : m + 1] for m in range(3)]
    rows += [commit[0:1]]
    high, low = split_low(pack_rows(rows, 16))
    two_ref[:, 2048:2176] = rows_of([high, low, jnp.zeros((32, 128), F32)]).astype(BF)


def stack_kernel(scalars, *refs):
    out_ref = refs[-1]
    for k in range(out_ref.shape[0]):
        out_ref[k] = refs[k][...]


def join_kernel(scalars, a0, a1, out_ref):
    out_ref[0:2] = a0[...]
    out_ref[2:4] = a1[...]


def over(axis, array, flip):
    size = lax.axis_size(axis)
    return lax.ppermute(array, axis, [(i, i ^ flip) for i in range(size)])


def flips(array):
    return [over("chan", array, k) for k in (1, 2, 3)]


def plane(array):
    return [array] + [over("dp", array, k) for k in (2, 4, 6)]


def add(*arrays):
    total = arrays[0].astype(F32)
    for array in arrays[1:]:
        total = total + array.astype(F32)
    return total.astype(BF)


def shards(
    latents_in,
    norm_gains,
    norm_shifts,
    conv_weights,
    conv_biases,
    qkv_weights,
    attn_biases,
    out_weight,
    proj_weight,
    proj_bias,
    codebook,
    codes,
    reset_src,
    cotangent,
):
    images = latents_in.shape[0]
    tokens = images * POS
    quarter = tokens // 4
    devices = lax.axis_size("dp")
    tokens_all = tokens * devices
    by_hand = devices == PARTS
    z = lax.axis_index("chan").astype(jnp.int32)
    dp = lax.axis_index("dp").astype(jnp.int32)
    scalars = jnp.stack([z, dp if by_hand else jnp.zeros_like(dp), dp, jnp.zeros_like(dp)])
    x = latents_in.reshape(tokens, 128)
    conv_w = conv_weights.reshape(2, 9, C, 128)

    def whole(shape):
        return pl.BlockSpec(shape, lambda i, n=len(shape): (0,) * n)

    def blocks_call(body, in_specs, out_specs, outs, name, *args, scratch=(), aliases={}):
        return pl.pallas_call(
            body,
            grid=(1,),
            out_shape=outs,
            in_specs=[pl.BlockSpec(memory_space=pltpu.SMEM)] + in_specs,
            out_specs=out_specs,
            scratch_shapes=scratch,
            input_output_aliases=aliases,
            compiler_params=pltpu.CompilerParams(vmem_limit_bytes=VMEM * 2**20),
            cost_estimate=pl.CostEstimate(flops=HEAVY, bytes_accessed=1, transcendentals=0),
            name=name,
        )(scalars, *args)

    act_one, stats_one = call(
        first_norm_kernel,
        [sds((tokens, 128), BF), sds((8, 128), F32)],
        scalars,
        x,
        norm_gains,
        norm_shifts,
        flops=HEAVY,
        name="first_norm",
    )
    pieces_one = [act_one] + flips(act_one)
    rows = scalars[1] * 64
    pack = jnp.concatenate(
        [lax.dynamic_slice(qkv_weights[m], (rows, 0), (64, 128)) for m in range(3)]
        + [
            lax.dynamic_slice(out_weight, (rows, 0), (64, 128)),
            lax.dynamic_slice(proj_weight, (rows, 0), (64, 64)),
            jnp.zeros((64, 64), BF),
        ],
        axis=1,
    )
    if by_hand:
        pack_pair = call(
            stack_kernel,
            [sds((2, 64, 640), BF)],
            scalars,
            pack,
            over("chan", pack, 1),
            name="pack_pair",
        )[0]
        pack_far = over("chan", pack_pair, 2)
    params = jnp.concatenate(
        [
            norm_gains,
            norm_shifts,
            conv_biases,
            attn_biases,
            jnp.pad(proj_bias.reshape(1, 64), ((0, 0), (0, 64))),
            jnp.zeros((4, 128), F32),
        ]
    )
    hot, quantized, usage, fixed = call(
        start_kernel,
        [
            sds((tokens, CODES), BF),
            sds((tokens, 64), F32),
            sds((8, 128), F32),
            sds((4, 128, 128), BF),
        ],
        scalars,
        codes,
        codebook.T,
        cotangent.reshape(tokens, 64),
        stats_one,
        scratch=[pltpu.VMEM((tokens, 64), F32)],
        name="start",
    )
    weights_full = pl.pallas_call(
        conv_weight_kernel,
        grid=(2,),
        out_shape=sds((2, C, WIDE), BF),
        in_specs=[
            pl.BlockSpec(memory_space=pltpu.SMEM),
            pl.BlockSpec((1, 9, C, 128), lambda i: (i, 0, 0, 0)),
        ],
        out_specs=pl.BlockSpec((1, C, WIDE), lambda i: (i, 0, 0)),
        compiler_params=pltpu.CompilerParams(vmem_limit_bytes=VMEM * 2**20),
        cost_estimate=pl.CostEstimate(flops=0, bytes_accessed=1, transcendentals=0),
        name="conv_weight",
    )(scalars, conv_w)

    def conv_call(body, index, outs, name, *args):
        specs = []
        for a in args:
            if a is weights_full:
                specs.append(pl.BlockSpec((1, C, WIDE), lambda i: (index, 0, 0)))
            else:
                specs.append(whole(a.shape))
        scratch = ()
        if body is third_back_kernel:
            scratch = [pltpu.VMEM((tokens, 128), F32), pltpu.VMEM((tokens, 128), F32)]
        return blocks_call(
            body, specs, [whole(o.shape) for o in outs], outs, name, *args, scratch=scratch
        )

    hidden, stats_two, act_two = conv_call(
        conv_one_kernel,
        0,
        [sds((tokens, 128), F32), sds((8, 128), F32), sds((tokens, 128), BF)],
        "conv_one",
        *pieces_one,
        weights_full,
        params,
        usage,
    )
    pieces_two = [act_two] + flips(act_two)
    if by_hand:
        block = call(
            join_kernel, [sds((4, 64, 640), BF)], scalars, pack_pair, pack_far, name="pack_join"
        )[0]
        blocks = [block] + [over("dp", block, k) for k in (2, 4, 6)]
    else:
        packed = jnp.concatenate(
            [qkv_weights[0], qkv_weights[1], qkv_weights[2], out_weight, proj_weight]
            + [jnp.zeros((C, 64), BF)],
            axis=1,
        )
        block = jnp.stack([packed] + flips(packed)).reshape(4, PARTS, 64, 640)
        block = jnp.swapaxes(block, 0, 1)
        block_own, block_other = block[0::2], block[1::2]
    normed_three, stats_three, *pays = conv_call(
        conv_two_kernel,
        1,
        [sds((tokens, 128), F32), sds((8, 128), F32)] + [sds((528, 128), BF)] * 4,
        "conv_two",
        *pieces_two,
        weights_full,
        params,
        x,
        fixed,
    )
    normed_pieces = [pays[0]] + [over("chan", pays[k], k) for k in (1, 2, 3)]
    if by_hand:
        block_own = call(
            stack_kernel,
            [sds((4, 4, 64, 640), BF)],
            scalars,
            *blocks,
            name="pack_plane",
        )[0]
        block_other = over("dp", block_own, 1)
    normed, residual_part, bias_rows = call(
        attn_in_kernel,
        [sds((POS, C), BF), sds((quarter, C), F32), sds((8, C), F32)],
        scalars,
        *normed_pieces,
        flops=HEAVY,
        name="attn_in",
    )
    attn_w = call(
        attn_weight_kernel,
        [sds((C, 2304), BF)],
        scalars,
        block_own,
        block_other,
        name="attn_weight",
    )[0]
    *pays, output, lat_grad, mixed, att_grad, qg, kg, vg, sums = call(
        attention_kernel,
        [sds((POS + 192, 128), F32)]
        + [sds((POS + 192, 128), BF)] * 3
        + [sds((quarter, C), BF)] * 5
        + [sds((POS, C), BF), sds((POS, C), BF), sds((8, C), F32)],
        scalars,
        normed,
        residual_part,
        bias_rows,
        *normed_pieces,
        attn_w,
        flops=HEAVY,
        name="attention",
    )

    back_three = [pays[0]] + [over("chan", pays[k], k) for k in (1, 2, 3)]
    *att_keep, att_send = call(
        attn_grad_kernel,
        [sds((4, 64, 640), BF)] * 4 + [sds((4, 4, 64, 640), BF)],
        scalars,
        normed,
        output,
        lat_grad,
        mixed,
        att_grad,
        qg,
        kg,
        vg,
        sums,
        usage,
        scratch=[pltpu.VMEM((C, 2560), BF)],
        name="attn_grad",
    )

    def pair_sum(keep, send, after, name):
        outs = [sds((2,) + keep[0].shape, BF)] * 2
        got = over("dp", send, 1)
        kept, sent = call(pair_add_kernel, outs, scalars, *keep, got, after, name=name)
        return kept, over("dp", sent, 2)

    if by_hand:
        att_kept, att_got = pair_sum(att_keep, att_send, back_three[1], "attn_pair")
    residual_grad, taps_two, latents, small_three, *pays = conv_call(
        third_back_kernel,
        1,
        [
            sds((tokens, 128), F32),
            sds((tokens, WIDE), BF),
            sds((tokens, 64), F32),
            sds((8, 128), F32),
            sds((tokens, 128), F32),
        ]
        + [sds((tokens, 128), BF)] * 3,
        "third_back",
        *back_three,
        normed_three,
        stats_three,
        params,
        att_kept if by_hand else sums,
        weights_full,
    )
    back_two = [pays[0]] + [over("chan", pays[k], k) for k in (1, 2, 3)]
    book_scale = 2.0 * CODES / tokens_all

    def two_grad(*refs):
        conv_two_grad_kernel(*refs[:10], book_scale, *refs[11:])

    *two_keep, two_send, commit = call(
        two_grad,
        [sds((64, 1408), BF)] * 4 + [sds((4, 64, 1408), BF), sds((8, 128), F32)],
        scalars,
        *pieces_two,
        taps_two,
        hot,
        latents,
        quantized,
        reset_src.reshape(1, CODES),
        back_two[1],
        scratch=[pltpu.VMEM((C, WIDE), BF), pltpu.VMEM((128, CODES), BF)],
        name="conv_two_grad",
    )
    if by_hand:
        att_own, att_sent = call(
            half_add_kernel,
            [sds((4, 64, 640), BF)] * 2,
            scalars,
            att_kept,
            att_got,
            back_two[1],
            name="attn_half",
        )
        att_got = over("dp", att_sent, 4)
    taps_one, small_two, *pays = conv_call(
        second_back_kernel,
        0,
        [sds((tokens, WIDE), BF), sds((8, 128), F32), sds((tokens, 128), F32)]
        + [sds((tokens, 128), BF)] * 3,
        "second_back",
        *back_two,
        hidden,
        stats_two,
        params,
        att_own if by_hand else sums,
        two_keep[0],
        weights_full,
    )
    back_one = [pays[0]] + [over("chan", pays[k], k) for k in (1, 2, 3)]
    *one_keep, one_send = call(
        conv_one_grad_kernel,
        [sds((64, WIDE), BF)] * 4 + [sds((4, 64, WIDE), BF)],
        scalars,
        *pieces_one,
        taps_one,
        scratch=[pltpu.VMEM((C, WIDE), BF)],
        name="conv_one_grad",
    )
    if by_hand:
        two_kept, two_got = pair_sum(two_keep, two_send, back_one[1], "conv_two_pair")
        att_kept, att_sent = call(
            attn_sum_kernel,
            [sds((2, 64, 640), BF)] * 2,
            scalars,
            att_own,
            att_got,
            back_one[1],
            name="attn_sum",
        )
        att_got = over("chan", att_sent, 2)
    grad_latents, small_one = call(
        first_back_kernel,
        [sds((tokens, 128), F32), sds((8, 128), F32)],
        scalars,
        *back_one,
        x,
        stats_one,
        params,
        residual_grad,
        one_keep[0],
        two_kept if by_hand else sums,
        att_kept if by_hand else sums,
        flops=HEAVY,
        name="first_back",
    )

    if by_hand:
        o0, o1, o2, o3, two_own, two_sent, att_own, att_sent = call(
            tail_first_kernel,
            [sds((64, WIDE), BF)] * 4 + [sds((64, 1408), BF)] * 2 + [sds((64, 640), BF)] * 2,
            scalars,
            *one_keep,
            over("dp", one_send, 1),
            two_kept,
            two_got,
            att_kept,
            att_got,
            small_one,
            flops=HEAVY,
            name="tail_first",
        )
        two, one = call(
            tail_second_kernel,
            [sds((64, 2176), BF), sds((64, WIDE), BF)],
            scalars,
            o0,
            over("dp", o1, 2),
            over("dp", o2, 4),
            over("dp", o3, 6),
            two_own,
            over("dp", two_sent, 4),
            att_own,
            over("chan", att_sent, 1),
            small_one,
            small_two,
            small_three,
            commit,
            flops=HEAVY,
            name="tail_second",
        )
        all_two, all_one = plane(two), plane(one)
        two_own = call(
            stack_kernel,
            [sds((4, 64, 2176), BF)],
            scalars,
            *all_two,
            flops=HEAVY,
            name="stack_two",
        )[0]
        two_other = over("dp", two_own, 1)
        one_own = call(stack_kernel, [sds((4, 64, WIDE), BF)], scalars, *all_one, name="stack_one")[0]
        one_other = over("dp", one_own, 1)
    else:

        def total(keep, send):
            parts = jnp.stack([jnp.stack(keep), send]).astype(F32)
            return lax.psum(parts, "dp").astype(BF)

        att_sum = total(att_keep, att_send)
        att_sum = add(att_sum[:, :, 0], *[over("chan", att_sum[:, :, k], k) for k in (1, 2, 3)])
        small = jnp.concatenate([small_one[0:2], small_two[0:3], small_three[0:3], commit[0:1]])
        small = jnp.concatenate([lax.psum(small, "dp"), jnp.zeros((7, 128), F32)])
        high = lax.reduce_precision(small, 8, 7)
        smalls = jnp.concatenate([high, small - high, jnp.zeros((32, 128), F32)]).astype(BF)
        smalls = jnp.zeros((2, 4, 64, 128), BF).at[0, 0].set(smalls)
        two_sum = total(two_keep, two_send)
        two_own, two_other = jnp.concatenate([two_sum, att_sum, smalls], axis=3)
        one_own, one_other = total(one_keep, one_send)

    def finish_two(*refs):
        finish_two_kernel(float(tokens_all), *refs)

    outs = [
        sds((2, 9, C, 128), F32),
        sds((3, 128), F32),
        sds((3, 128), F32),
        sds((2, 128), F32),
        sds((1, 64), F32),
        sds((3, C, 128), F32),
        sds((C, 128), F32),
        sds((64, C), F32),
        sds((64, CODES), F32),
        sds((64, CODES), F32),
        sds((1, 1), F32),
        sds((3, 128), F32),
        sds((1, 64), F32),
    ]
    (
        conv_held,
        gain_grad,
        shift_grad,
        conv_bias_grad,
        commitment,
        qkv_grad,
        out_grad,
        proj_grad,
        book_grad,
        new_codebook,
        perplexity,
        attn_bias_grad,
        proj_bias_grad,
    ) = blocks_call(
        finish_two,
        [whole((4, 64, 2176)), whole((4, 64, 2176)), whole((64, CODES))],
        [pl.BlockSpec((1, 9, C, 128), lambda i: (1, 0, 0, 0))] + [whole(o.shape) for o in outs[1:]],
        outs,
        "finish_two",
        two_own,
        two_other,
        codebook.T,
        scratch=[
            pltpu.VMEM((8, 128), F32),
            pltpu.VMEM((C, 128), F32),
            pltpu.VMEM((64, CODES), F32),
        ],
    )
    conv_grad = blocks_call(
        finish_one_kernel,
        [whole((4, 64, WIDE)), whole((4, 64, WIDE)), pl.BlockSpec(memory_space=pl.ANY)],
        [pl.BlockSpec((1, 9, C, 128), lambda i: (0, 0, 0, 0))],
        [sds((2, 9, C, 128), F32)],
        "finish_one",
        one_own,
        one_other,
        conv_held,
        aliases={3: 0},
    )[0]

    return (
        latents.reshape(images, LAT, LAT, -1),
        commitment.reshape(64),
        perplexity.reshape(()),
        new_codebook.T,
        grad_latents.reshape(images, LAT, LAT, 128),
        gain_grad,
        shift_grad,
        conv_grad.reshape(2, 3, 3, C, 128),
        conv_bias_grad,
        qkv_grad,
        attn_bias_grad,
        out_grad,
        proj_grad.T,
        proj_bias_grad.reshape(64),
        book_grad.T,
    )


def solution(mesh):
    return jax.shard_map(
        shards,
        mesh=mesh,
        in_specs=(
            P("dp", None, None, "chan"),
            P(None, "chan"),
            P(None, "chan"),
            P(None, None, None, None, "chan"),
            P(None, "chan"),
            P(None, None, "chan"),
            P(None, "chan"),
            P(None, "chan"),
            P(None, "chan"),
            P("chan"),
            P(None, "chan"),
            P("dp", None, None),
            P(),
            P("dp", None, None, "chan"),
        ),
        out_specs=(
            P("dp", None, None, "chan"),
            P("chan"),
            P(),
            P(None, "chan"),
            P("dp", None, None, "chan"),
            P(None, "chan"),
            P(None, "chan"),
            P(None, None, None, None, "chan"),
            P(None, "chan"),
            P(None, None, "chan"),
            P(None, "chan"),
            P(None, "chan"),
            P(None, "chan"),
            P("chan"),
            P(None, "chan"),
        ),
        check_vma=False,
    )
```

time: 487 us -> 165 us (0.34); the launches traced: 479 us -> 165 us
  blocking collectives: 164 us -> 0 us
  local copies, waits for them, and re-layouts: 93.7 us -> 8.53 us
  waiting for transfers between devices: 125 us -> 56.9 us
  starting transfers between devices: 1.25 us -> 59.7 us
  matrix products: 41.6 us -> 0 us
  Pallas kernels: 0 us -> 38.3 us
  other arithmetic: 35.7 us -> 0.08 us
  between operations: 17.3 us -> 1.24 us
    all_gather x9 -> x0, blocking collectives: 141 us -> none  [the longest x1 19 us: shards(): lax.all_gather(value_part, 'chan', axis=1, tiled=True)]
    psum x1 -> x0, waiting for transfers between devices: 85.5 us -> none  [shards(): lax.psum((qkv_grad, attn_bias_grad, out_grad, proj_grad, proj_bias_grad,...]
    ppermute x0 -> x44, starting transfers between devices: none -> 59.7 us  [over(): return lax.ppermute(array, axis, [(i, i ^ flip) for i in range(size)])]
    unnamed x177 -> x63, local copies, waits for them, and re-layouts: 63.5 us -> 6.5 us
    ppermute x0 -> x44, waiting for transfers between devices: none -> 56.9 us  [over(): return lax.ppermute(array, axis, [(i, i ^ flip) for i in range(size)])]
    dot_general x75 -> x0, matrix products: 41.6 us -> none  [the longest x18 13.2 us: conv_kernel_grad(): jnp.einsum('bhwc,bhwd->cd', window, upstream, preferred_element_type=jnp....]
    unnamed x11 -> x0, waiting for transfers between devices: 39.7 us -> none
    pallas_call x0 -> x27, Pallas kernels: none -> 38.3 us  [the longest x20 22.4 us: call(): pl.pallas_call(body, out_shape=list(outs), in_specs=[pl.BlockSpec(memory_...]
  transfers between devices with their start and end apart: 6 -> 44, of which waited for: 6 -> 19; matrix products, arithmetic and copies ran while one was open for 10% -> 1% of each run, Pallas kernels for 0% -> 16%
where the time goes in v1:
time: 165 us
  starting transfers between devices  59.7 us (36%)
  waiting for transfers between devices  56.9 us (34%)
  Pallas kernels  38.3 us (23%)
  local copies, waits for them, and re-layouts  8.53 us (5%)
    ppermute x44, starting transfers between devices, over(): return lax.ppermute(array, axis, [(i, i ^ flip) for i in range(size)])  59.7 us
    ppermute x44, waiting for transfers between devices, over(): return lax.ppermute(array, axis, [(i, i ^ flip) for i in range(size)])  56.9 us
    pallas_call x20, Pallas kernels, call(): pl.pallas_call(body, out_shape=list(outs), in_specs=[pl.BlockSpec(memory_...  22.4 us
    pallas_call x6, Pallas kernels, blocks_call(): pl.pallas_call(body, grid=(1,), out_shape=outs, in_specs=[pl.BlockSpec(me...  14.9 us
    unnamed x63, local copies, waits for them, and re-layouts  6.5 us
  transfers between devices with their start and end apart: 44, of which 19 were waited for; matrix products, arithmetic and copies ran while one was open for 1% of the time, Pallas kernels for 16%

profile of v1, /device:TPU:0, one launch (start us, length us, event | category | flops | bytes accessed | tf_op | source)
XLA Modules:
  0.0 164.8 jit_solution(4096342177531677887)
XLA Ops:
  4.0 5.1 %collective-permute-start.2 = (bf16[512,128]{1,0:T(8,128)(2,1)S(1)}, bf16[512,128]{1,0:T(8,128)(2,1)S(1)}, u32[]{:S(2)}, u32[]{:S(2)}) collective-permute-start(bf16[512,128]{1,0:T(8,128)(2,1)S(1)} %get-tuple-element.108.a0), channel_id=1, source_target_pairs={{0,3},{1,2},{2,1},{3,0},{4,7},{5,6},{6,5},{7,4},{8,11},{9,10},{10,... | collective-permute-start | bytes 393224 | tf_op jit(solution)/shard_map/ppermute | solution.py:774
  15.9 1.9 %start.1 = (bf16[512,1024]{1,0:T(8,128)(2,1)S(1)}, f32[512,64]{1,0:T(8,128)S(1)}, f32[8,128]{1,0:T(8,128)S(1)}, bf16[4,128,128]{2,1,0:T(8,128)(2,1)S(1)}) custom-call(s32[4]{0:T(128)S(1)} %pad_add_fusion.scalars.refs_0_, s32[2,16,16]{2,1,0:T(8,128)S(1)} %copy-done.17, f32[64,1024]{1,0:T(8,128)S(1)} %bitcast.25, bf16[512,64]{1,0:T(8,128)(2,1)S(1)} %bitcast.27, ...), custom_call_target="tpu_custom_call" | custom-call | bytes 1 | tf_op jit(solution)/shard_map/start/pallas_call | solution.py:25
  20.2 2.3 %collective-permute-start.10 = (bf16[2,64,640]{2,1,0:T(8,128)(2,1)S(1)}, bf16[2,64,640]{2,1,0:T(8,128)(2,1)S(1)}, u32[]{:S(2)}, u32[]{:S(2)}) collective-permute-start(bf16[2,64,640]{2,1,0:T(8,128)(2,1)S(1)} %pack_pair.1.a0), channel_id=1, source_target_pairs={{0,2},{1,3},{2,0},{3,1},{4,6},{5,7},{6,4},{7,5},{8,10},{9,11},{10,... | collective-permute-start | bytes 491528 | tf_op jit(solution)/shard_map/ppermute | solution.py:774
  24.2 2.4 %conv_one.1 = (f32[512,128]{1,0:T(8,128)S(1)}, f32[8,128]{1,0:T(8,128)S(1)}, bf16[512,128]{1,0:T(8,128)(2,1)S(1)}) custom-call(s32[4]{0:T(128)S(1)} %pad_add_fusion.scalars.refs_0_, bf16[512,128]{1,0:T(8,128)(2,1)S(1)} %get-tuple-element.108.a0, bf16[512,128]{1,0:T(8,128)(2,1)S(1)} %collective-permute-done.a1, ...), custom_call_target="tpu_custom_call" | custom-call | flops 99999997952 | bytes 1 | tf_op jit(solution)/shard_map/conv_one/pallas_call | solution.py:824
  26.6 2.8 %collective-permute-start.5 = (bf16[512,128]{1,0:T(8,128)(2,1)S(1)}, bf16[512,128]{1,0:T(8,128)(2,1)S(1)}, u32[]{:S(2)}, u32[]{:S(2)}) collective-permute-start(bf16[512,128]{1,0:T(8,128)(2,1)S(1)} %get-tuple-element.111.a0.refs_1_), channel_id=1, source_target_pairs={{0,3},{1,2},{2,1},{3,0},{4,7},{5,6},{6,5},{7,4},{8,11},{9,10},{10,... | collective-permute-start | bytes 393224 | tf_op jit(solution)/shard_map/ppermute | solution.py:774
  31.6 2.5 %collective-permute-start.13 = (bf16[4,64,640]{2,1,0:T(8,128)(2,1)S(1)}, bf16[4,64,640]{2,1,0:T(8,128)(2,1)S(1)}, u32[]{:S(2)}, u32[]{:S(2)}) collective-permute-start(bf16[4,64,640]{2,1,0:T(8,128)(2,1)S(1)} %pack_join.1.refs_0_), channel_id=1, source_target_pairs={{0,24},{4,28},{8,16},{12,20},{16,8},{20,12},{24,0},{28,4},{1,25},{... | collective-permute-start | bytes 983048 | tf_op jit(solution)/shard_map/ppermute | solution.py:774
  36.5 5.3 %collective-permute-done.4.a2.refs_3_ = bf16[512,128]{1,0:T(8,128)(2,1)S(1)} collective-permute-done((bf16[512,128]{1,0:T(8,128)(2,1)S(1)}, bf16[512,128]{1,0:T(8,128)(2,1)S(1)}, u32[]{:S(2)}, u32[]{:S(2)}) %collective-permute-start.4) | collective-permute-done | bytes 131104 | tf_op jit(solution)/shard_map/ppermute | solution.py:774
  41.9 2.4 %conv_two.1 = (f32[512,128]{1,0:T(8,128)S(1)}, f32[8,128]{1,0:T(8,128)S(1)}, bf16[528,128]{1,0:T(8,128)(2,1)S(1)}, bf16[528,128]{1,0:T(8,128)(2,1)S(1)}, bf16[52...) custom-call(s32[4]{0:T(128)S(1)} %pad_add_fusion.scalars.refs_0_, ...), custom_call_target="tpu_custom_call" | custom-call | flops 99999997952 | bytes 1 | tf_op jit(solution)/shard_map/conv_two/pallas_call | solution.py:824
  44.7 3.4 %collective-permute-start.7 = (bf16[528,128]{1,0:T(8,128)(2,1)S(1)}, bf16[528,128]{1,0:T(8,128)(2,1)S(1)}, u32[]{:S(2)}, u32[]{:S(2)}) collective-permute-start(bf16[528,128]{1,0:T(8,128)(2,1)S(1)} %get-tuple-element.115), channel_id=1, source_target_pairs={{0,2},{1,3},{2,0},{3,1},{4,6},{5,7},{6,4},{7,5},{8,10},{9,11},{10,... | collective-permute-start | bytes 405512 | tf_op jit(solution)/shard_map/ppermute | solution.py:774
  48.1 2.6 %collective-permute-start.8 = (bf16[528,128]{1,0:T(8,128)(2,1)S(1)}, bf16[528,128]{1,0:T(8,128)(2,1)S(1)}, u32[]{:S(2)}, u32[]{:S(2)}) collective-permute-start(bf16[528,128]{1,0:T(8,128)(2,1)S(1)} %get-tuple-element.116), channel_id=1, source_target_pairs={{0,3},{1,2},{2,1},{3,0},{4,7},{5,6},{6,5},{7,4},{8,11},{9,10},{10,... | collective-permute-start | bytes 405512 | tf_op jit(solution)/shard_map/ppermute | solution.py:774
  52.2 6.2 %collective-permute-done.7.n2 = bf16[528,128]{1,0:T(8,128)(2,1)S(1)} collective-permute-done((bf16[528,128]{1,0:T(8,128)(2,1)S(1)}, bf16[528,128]{1,0:T(8,128)(2,1)S(1)}, u32[]{:S(2)}, u32[]{:S(2)}) %collective-permute-start.7) | collective-permute-done | bytes 135200 | tf_op jit(solution)/shard_map/ppermute | solution.py:774
  60.0 3.2 %attention.1 = (f32[448,128]{1,0:T(8,128)S(1)}, bf16[448,128]{1,0:T(8,128)(2,1)S(1)}, bf16[448,128]{1,0:T(8,128)(2,1)S(1)}, bf16[448,128]{1,0:T(8,128)(2,1)S(1)}...) custom-call(s32[4]{0:T(128)S(1)} %pad_add_fusion.scalars.refs_0_, ...), custom_call_target="tpu_custom_call" | custom-call | flops 99999997952 | bytes 1 | tf_op jit(solution)/shard_map/attention/pallas_call | solution.py:25
  63.2 1.9 %attn_grad.1 = (bf16[4,64,640]{2,1,0:T(8,128)(2,1)S(1)}, bf16[4,64,640]{2,1,0:T(8,128)(2,1)S(1)}, bf16[4,64,640]{2,1,0:T(8,128)(2,1)S(1)}, bf16[4,64,640]{2,1,0:T(8,128)(2,1)S(1)}, bf16[4,4,64,640]{3,2,1,0:T(8,128)(2,1)S(1)}) custom-call(s32[4]{0:T(128)S(1)} %pad_add_fusion.scalars.refs_0_, bf16[256,512]{1,0:T(8,128)(2,1)S(1)} %get-tuple-element.117.norm_ref, ...), custom_call_target="tpu_custom_call" | custom-call | bytes 1 | tf_op jit(solution)/shard_map/attn_grad/pallas_call | solution.py:25
  65.2 2.6 %collective-permute-start.15 = (bf16[448,128]{1,0:T(8,128)(2,1)S(1)}, bf16[448,128]{1,0:T(8,128)(2,1)S(1)}, u32[]{:S(2)}, u32[]{:S(2)}) collective-permute-start(bf16[448,128]{1,0:T(8,128)(2,1)S(1)} %get-tuple-element.121), channel_id=1, source_target_pairs={{0,1},{1,0},{2,3},{3,2},{4,5},{5,4},{6,7},{7,6},{8,9},{9,8},{10,11... | collective-permute-start | bytes 344072 | tf_op jit(solution)/shard_map/ppermute | solution.py:774
  73.9 5.7 %collective-permute-done.16.p2 = bf16[448,128]{1,0:T(8,128)(2,1)S(1)} collective-permute-done((bf16[448,128]{1,0:T(8,128)(2,1)S(1)}, bf16[448,128]{1,0:T(8,128)(2,1)S(1)}, u32[]{:S(2)}, u32[]{:S(2)}) %collective-permute-start.16) | collective-permute-done | bytes 114720 | tf_op jit(solution)/shard_map/ppermute | solution.py:774
  79.6 2.9 %third_back.1 = (f32[512,128]{1,0:T(8,128)S(1)}, bf16[512,1152]{1,0:T(8,128)(2,1)S(1)}, f32[512,64]{1,0:T(8,128)}, f32[8,128]{1,0:T(8,128)S(1)}, f32[512,128]{1,...) custom-call(s32[4]{0:T(128)S(1)} %pad_add_fusion.scalars.refs_0_, ...), custom_call_target="tpu_custom_call" | custom-call | flops 99999997952 | bytes 1 | tf_op jit(solution)/shard_map/third_back/pallas_call | solution.py:824
  82.6 2.2 %collective-permute-start.19 = (bf16[512,128]{1,0:T(8,128)(2,1)S(1)}, bf16[512,128]{1,0:T(8,128)(2,1)S(1)}, u32[]{:S(2)}, u32[]{:S(2)}) collective-permute-start(bf16[512,128]{1,0:T(8,128)(2,1)S(1)} %get-tuple-element.142), channel_id=1, source_target_pairs={{0,1},{1,0},{2,3},{3,2},{4,5},{5,4},{6,7},{7,6},{8,9},{9,8},{10,11... | collective-permute-start | bytes 393224 | tf_op jit(solution)/shard_map/ppermute | solution.py:774
  90.1 2.0 %conv_two_grad.1 = (bf16[64,1408]{1,0:T(8,128)(2,1)S(1)}, bf16[64,1408]{1,0:T(8,128)(2,1)S(1)}, bf16[64,1408]{1,0:T(8,128)(2,1)S(1)}, bf16[64,1408]{1,0:T(8,128)...) custom-call(s32[4]{0:T(128)S(1)} %pad_add_fusion.scalars.refs_0_, bf16[512,128]{1,0:T(8,128)(2,1)S(1)} %copy-done.9, ...), custom_call_target="tpu_custom_call" | custom-call | bytes 1 | tf_op jit(solution)/shard_map/conv_two_grad/pallas_call | solution.py:25
  94.5 2.8 %collective-permute-done.20.p2 = bf16[512,128]{1,0:T(8,128)(2,1)S(1)} collective-permute-done((bf16[512,128]{1,0:T(8,128)(2,1)S(1)}, bf16[512,128]{1,0:T(8,128)(2,1)S(1)}, u32[]{:S(2)}, u32[]{:S(2)}) %collective-permute-start.20) | collective-permute-done | bytes 131104 | tf_op jit(solution)/shard_map/ppermute | solution.py:774
  97.2 2.4 %second_back.1 = (bf16[512,1152]{1,0:T(8,128)(2,1)S(1)}, f32[8,128]{1,0:T(8,128)S(1)}, f32[512,128]{1,0:T(8,128)S(1)}, bf16[512,128]{1,0:T(8,128)(2,1)S(1)}, bf1...) custom-call(s32[4]{0:T(128)S(1)} %pad_add_fusion.scalars.refs_0_, f32[512,128]{1,0:T(8,128)S(1)} %get-tuple-element.141.p0, ...), custom_call_target="tpu_custom_call" | custom-call | flops 99999997952 | bytes 1 | tf_op jit(solution)/shard_map/second_back/pallas_call | solution.py:824
  99.6 2.0 %collective-permute-start.25 = (bf16[512,128]{1,0:T(8,128)(2,1)S(1)}, bf16[512,128]{1,0:T(8,128)(2,1)S(1)}, u32[]{:S(2)}, u32[]{:S(2)}) collective-permute-start(bf16[512,128]{1,0:T(8,128)(2,1)S(1)} %get-tuple-element.163), channel_id=1, source_target_pairs={{0,1},{1,0},{2,3},{3,2},{4,5},{5,4},{6,7},{7,6},{8,9},{9,8},{10,11... | collective-permute-start | bytes 393224 | tf_op jit(solution)/shard_map/ppermute | solution.py:774
  108.9 3.1 %collective-permute-start.28 = (bf16[2,64,640]{2,1,0:T(8,128)(2,1)S(1)}, bf16[2,64,640]{2,1,0:T(8,128)(2,1)S(1)}, u32[]{:S(2)}, u32[]{:S(2)}) collective-permute-start(bf16[2,64,640]{2,1,0:T(8,128)(2,1)S(1)} %get-tuple-element.168), channel_id=1, source_target_pairs={{0,2},{1,3},{2,0},{3,1},{4,6},{5,7},{6,4},{7,5},{8,10},{9,11},{10,... | collective-permute-start | bytes 491528 | tf_op jit(solution)/shard_map/ppermute | solution.py:774
  115.5 6.5 %collective-permute-done.28.att_get = bf16[2,64,640]{2,1,0:T(8,128)(2,1)S(1)} collective-permute-done((bf16[2,64,640]{2,1,0:T(8,128)(2,1)S(1)}, bf16[2,64,640]{2,1,0:T(8,128)(2,1)S(1)}, u32[]{:S(2)}, u32[]{:S(2)}) %collective-permute-start.28) | collective-permute-done | bytes 163872 | tf_op jit(solution)/shard_map/ppermute | solution.py:774
  128.3 4.1 %collective-permute-done.35.att_get = bf16[64,640]{1,0:T(8,128)(2,1)S(1)} collective-permute-done((bf16[64,640]{1,0:T(8,128)(2,1)S(1)}, bf16[64,640]{1,0:T(8,128)(2,1)S(1)}, u32[]{:S(2)}, u32[]{:S(2)}) %collective-permute-start.35) | collective-permute-done | bytes 81952 | tf_op jit(solution)/shard_map/ppermute | solution.py:774
  132.4 2.3 %collective-permute-done.32.o2 = bf16[64,1152]{1,0:T(8,128)(2,1)S(1)} collective-permute-done((bf16[64,1152]{1,0:T(8,128)(2,1)S(1)}, bf16[64,1152]{1,0:T(8,128)(2,1)S(1)}, u32[]{:S(2)}, u32[]{:S(2)}) %collective-permute-start.32) | collective-permute-done | bytes 147488 | tf_op jit(solution)/shard_map/ppermute | solution.py:774
  135.4 2.0 %collective-permute-start.38 = (bf16[64,2176]{1,0:T(8,128)(2,1)S(1)}, bf16[64,2176]{1,0:T(8,128)(2,1)S(1)}, u32[]{:S(2)}, u32[]{:S(2)}) collective-permute-start(bf16[64,2176]{1,0:T(8,128)(2,1)S(1)} %get-tuple-element.185.refs_0_), channel_id=1, source_target_pairs={{0,24},{4,28},{8,16},{12,20},{16,8},{20,12},{24,0},{28,4},{1,25},{... | collective-permute-start | bytes 835592 | tf_op jit(solution)/shard_map/ppermute | solution.py:774
  139.0 7.0 %collective-permute-done.38.refs_3_ = bf16[64,2176]{1,0:T(8,128)(2,1)S(1)} collective-permute-done((bf16[64,2176]{1,0:T(8,128)(2,1)S(1)}, bf16[64,2176]{1,0:T(8,128)(2,1)S(1)}, u32[]{:S(2)}, u32[]{:S(2)}) %collective-permute-start.38) | collective-permute-done | bytes 278560 | tf_op jit(solution)/shard_map/ppermute | solution.py:774
  146.0 2.3 %collective-permute-done.37.refs_2_ = bf16[64,2176]{1,0:T(8,128)(2,1)S(1)} collective-permute-done((bf16[64,2176]{1,0:T(8,128)(2,1)S(1)}, bf16[64,2176]{1,0:T(8,128)(2,1)S(1)}, u32[]{:S(2)}, u32[]{:S(2)}) %collective-permute-start.37) | collective-permute-done | bytes 278560 | tf_op jit(solution)/shard_map/ppermute | solution.py:774
  152.5 4.1 %collective-permute-done.42.refs_3_ = bf16[64,1152]{1,0:T(8,128)(2,1)S(1)} collective-permute-done((bf16[64,1152]{1,0:T(8,128)(2,1)S(1)}, bf16[64,1152]{1,0:T(8,128)(2,1)S(1)}, u32[]{:S(2)}, u32[]{:S(2)}) %collective-permute-start.42) | collective-permute-done | bytes 147488 | tf_op jit(solution)/shard_map/ppermute | solution.py:774
  156.6 2.6 %collective-permute-done.41.refs_2_ = bf16[64,1152]{1,0:T(8,128)(2,1)S(1)} collective-permute-done((bf16[64,1152]{1,0:T(8,128)(2,1)S(1)}, bf16[64,1152]{1,0:T(8,128)(2,1)S(1)}, u32[]{:S(2)}, u32[]{:S(2)}) %collective-permute-start.41) | collective-permute-done | bytes 147488 | tf_op jit(solution)/shard_map/ppermute | solution.py:774
  160.0 2.7 %finish_two.1 = (f32[2,9,512,128]{3,2,1,0:T(8,128)}, f32[3,128]{1,0:T(4,128)}, f32[3,128]{1,0:T(4,128)}, f32[2,128]{1,0:T(2,128)}, f32[1,64]{1,0:T(1,128)}, /*in...) custom-call(s32[4]{0:T(128)S(1)} %pad_add_fusion.scalars.refs_0_, ...), custom_call_target="tpu_custom_call" | custom-call | flops 99999997952 | bytes 1 | tf_op jit(solution)/shard_map/finish_two/pallas_call | solution.py:824
  162.7 2.1 %finish_one.1 = f32[2,9,512,128]{3,2,1,0:T(8,128)} custom-call(s32[4]{0:T(128)S(1)} %pad_add_fusion.scalars.refs_0_, bf16[4,64,1152]{2,1,0:T(8,128)(2,1)S(1)} %stack_one.1.own_ref, bf16[4,64,1152]{2,1,0:T(8,128)(2,1)S(1)} %collective-permute-done.43.other_ref, f32[2,9,512,128]{3,2,1,0:T(8,128)} %get-tuple-element.193.held_ref), custom_call_target="tpu_custom_call", output_to_operand_aliasing={{}: (3, {})} | custom-call | flops 99999997952 | bytes 1 | tf_op jit(solution)/shard_map/finish_one/pallas_call | solution.py:824
  (157 shorter events, 60.3 us)
Async XLA Ops:
  4.0 18.5 %collective-permute-start.2 = (bf16[512,128]{1,0:T(8,128)(2,1)S(1)}, bf16[512,128]{1,0:T(8,128)(2,1)S(1)}, u32[]{:S(2)}, u32[]{:S(2)}) collective-permute-start(bf16[512,128]{1,0:T(8,128)(2,1)S(1)} %get-tuple-element.108.a0), channel_id=1, source_target_pairs={{0,3},{1,2},{2,1},{3,0},{4,7},{5,6},{6,5},{7,4},{8,11},{9,10},{10,... | collective-permute-start | bytes 393224 | tf_op jit(solution)/shard_map/ppermute | solution.py:774
  9.1 13.4 %collective-permute-start.1 = (bf16[512,128]{1,0:T(8,128)(2,1)S(1)}, bf16[512,128]{1,0:T(8,128)(2,1)S(1)}, u32[]{:S(2)}, u32[]{:S(2)}) collective-permute-start(bf16[512,128]{1,0:T(8,128)(2,1)S(1)} %get-tuple-element.108.a0), channel_id=1, source_target_pairs={{0,2},{1,3},{2,0},{3,1},{4,6},{5,7},{6,4},{7,5},{8,10},{9,11},{10,... | collective-permute-start | bytes 393224 | tf_op jit(solution)/shard_map/ppermute | solution.py:774
  9.1 13.4 %collective-permute-start = (bf16[512,128]{1,0:T(8,128)(2,1)S(1)}, bf16[512,128]{1,0:T(8,128)(2,1)S(1)}, u32[]{:S(2)}, u32[]{:S(2)}) collective-permute-start(bf16[512,128]{1,0:T(8,128)(2,1)S(1)} %get-tuple-element.108.a0), channel_id=1, source_target_pairs={{0,1},{1,0},{2,3},{3,2},{4,5},{5,4},{6,7},{7,6},{8,9},{9,8},{10,11... | collective-permute-start | bytes 393224 | tf_op jit(solution)/shard_map/ppermute | solution.py:774
  20.2 10.8 %collective-permute-start.10 = (bf16[2,64,640]{2,1,0:T(8,128)(2,1)S(1)}, bf16[2,64,640]{2,1,0:T(8,128)(2,1)S(1)}, u32[]{:S(2)}, u32[]{:S(2)}) collective-permute-start(bf16[2,64,640]{2,1,0:T(8,128)(2,1)S(1)} %pack_pair.1.a0), channel_id=1, source_target_pairs={{0,2},{1,3},{2,0},{3,1},{4,6},{5,7},{6,4},{7,5},{8,10},{9,11},{10,... | collective-permute-start | bytes 491528 | tf_op jit(solution)/shard_map/ppermute | solution.py:774
  26.6 8.5 %collective-permute-start.5 = (bf16[512,128]{1,0:T(8,128)(2,1)S(1)}, bf16[512,128]{1,0:T(8,128)(2,1)S(1)}, u32[]{:S(2)}, u32[]{:S(2)}) collective-permute-start(bf16[512,128]{1,0:T(8,128)(2,1)S(1)} %get-tuple-element.111.a0.refs_1_), channel_id=1, source_target_pairs={{0,3},{1,2},{2,1},{3,0},{4,7},{5,6},{6,5},{7,4},{8,11},{9,10},{10,... | collective-permute-start | bytes 393224 | tf_op jit(solution)/shard_map/ppermute | solution.py:774
  29.3 12.5 %collective-permute-start.4 = (bf16[512,128]{1,0:T(8,128)(2,1)S(1)}, bf16[512,128]{1,0:T(8,128)(2,1)S(1)}, u32[]{:S(2)}, u32[]{:S(2)}) collective-permute-start(bf16[512,128]{1,0:T(8,128)(2,1)S(1)} %get-tuple-element.111.a0.refs_1_), channel_id=1, source_target_pairs={{0,2},{1,3},{2,0},{3,1},{4,6},{5,7},{6,4},{7,5},{8,10},{9,11},{10,... | collective-permute-start | bytes 393224 | tf_op jit(solution)/shard_map/ppermute | solution.py:774
  30.7 11.2 %collective-permute-start.3 = (bf16[512,128]{1,0:T(8,128)(2,1)S(1)}, bf16[512,128]{1,0:T(8,128)(2,1)S(1)}, u32[]{:S(2)}, u32[]{:S(2)}) collective-permute-start(bf16[512,128]{1,0:T(8,128)(2,1)S(1)} %get-tuple-element.111.a0.refs_1_), channel_id=1, source_target_pairs={{0,1},{1,0},{2,3},{3,2},{4,5},{5,4},{6,7},{7,6},{8,9},{9,8},{10,11... | collective-permute-start | bytes 393224 | tf_op jit(solution)/shard_map/ppermute | solution.py:774
  31.6 16.5 %collective-permute-start.13 = (bf16[4,64,640]{2,1,0:T(8,128)(2,1)S(1)}, bf16[4,64,640]{2,1,0:T(8,128)(2,1)S(1)}, u32[]{:S(2)}, u32[]{:S(2)}) collective-permute-start(bf16[4,64,640]{2,1,0:T(8,128)(2,1)S(1)} %pack_join.1.refs_0_), channel_id=1, source_target_pairs={{0,24},{4,28},{8,16},{12,20},{16,8},{20,12},{24,0},{28,4},{1,25},{... | collective-permute-start | bytes 983048 | tf_op jit(solution)/shard_map/ppermute | solution.py:774
  34.1 16.7 %collective-permute-start.12 = (bf16[4,64,640]{2,1,0:T(8,128)(2,1)S(1)}, bf16[4,64,640]{2,1,0:T(8,128)(2,1)S(1)}, u32[]{:S(2)}, u32[]{:S(2)}) collective-permute-start(bf16[4,64,640]{2,1,0:T(8,128)(2,1)S(1)} %pack_join.1.refs_0_), channel_id=1, source_target_pairs={{0,16},{4,20},{8,24},{12,28},{16,0},{20,4},{24,8},{28,12},{1,17},{... | collective-permute-start | bytes 983048 | tf_op jit(solution)/shard_map/ppermute | solution.py:774
  35.0 15.7 %collective-permute-start.11 = (bf16[4,64,640]{2,1,0:T(8,128)(2,1)S(1)}, bf16[4,64,640]{2,1,0:T(8,128)(2,1)S(1)}, u32[]{:S(2)}, u32[]{:S(2)}) collective-permute-start(bf16[4,64,640]{2,1,0:T(8,128)(2,1)S(1)} %pack_join.1.refs_0_), channel_id=1, source_target_pairs={{0,8},{4,12},{8,0},{12,4},{16,24},{20,28},{24,16},{28,20},{1,9},{5... | collective-permute-start | bytes 983048 | tf_op jit(solution)/shard_map/ppermute | solution.py:774
  44.7 13.6 %collective-permute-start.7 = (bf16[528,128]{1,0:T(8,128)(2,1)S(1)}, bf16[528,128]{1,0:T(8,128)(2,1)S(1)}, u32[]{:S(2)}, u32[]{:S(2)}) collective-permute-start(bf16[528,128]{1,0:T(8,128)(2,1)S(1)} %get-tuple-element.115), channel_id=1, source_target_pairs={{0,2},{1,3},{2,0},{3,1},{4,6},{5,7},{6,4},{7,5},{8,10},{9,11},{10,... | collective-permute-start | bytes 405512 | tf_op jit(solution)/shard_map/ppermute | solution.py:774
  48.1 10.3 %collective-permute-start.8 = (bf16[528,128]{1,0:T(8,128)(2,1)S(1)}, bf16[528,128]{1,0:T(8,128)(2,1)S(1)}, u32[]{:S(2)}, u32[]{:S(2)}) collective-permute-start(bf16[528,128]{1,0:T(8,128)(2,1)S(1)} %get-tuple-element.116), channel_id=1, source_target_pairs={{0,3},{1,2},{2,1},{3,0},{4,7},{5,6},{6,5},{7,4},{8,11},{9,10},{10,... | collective-permute-start | bytes 405512 | tf_op jit(solution)/shard_map/ppermute | solution.py:774
  67.7 11.8 %collective-permute-start.16 = (bf16[448,128]{1,0:T(8,128)(2,1)S(1)}, bf16[448,128]{1,0:T(8,128)(2,1)S(1)}, u32[]{:S(2)}, u32[]{:S(2)}) collective-permute-start(bf16[448,128]{1,0:T(8,128)(2,1)S(1)} %get-tuple-element.122), channel_id=1, source_target_pairs={{0,2},{1,3},{2,0},{3,1},{4,6},{5,7},{6,4},{7,5},{8,10},{9,11},{10,... | collective-permute-start | bytes 344072 | tf_op jit(solution)/shard_map/ppermute | solution.py:774
  68.8 10.8 %collective-permute-start.17 = (bf16[448,128]{1,0:T(8,128)(2,1)S(1)}, bf16[448,128]{1,0:T(8,128)(2,1)S(1)}, u32[]{:S(2)}, u32[]{:S(2)}) collective-permute-start(bf16[448,128]{1,0:T(8,128)(2,1)S(1)} %get-tuple-element.123), channel_id=1, source_target_pairs={{0,3},{1,2},{2,1},{3,0},{4,7},{5,6},{6,5},{7,4},{8,11},{9,10},{10,... | collective-permute-start | bytes 344072 | tf_op jit(solution)/shard_map/ppermute | solution.py:774
  72.3 19.8 %collective-permute-start.22 = (bf16[2,4,64,640]{3,2,1,0:T(8,128)(2,1)S(1)}, bf16[2,4,64,640]{3,2,1,0:T(8,128)(2,1)S(1)}, u32[]{:S(2)}, u32[]{:S(2)}) collective-permute-start(bf16[2,4,64,640]{3,2,1,0:T(8,128)(2,1)S(1)} %get-tuple-element.147), channel_id=1, source_target_pairs={{0,8},{4,12},{8,0},{12,4},{16,24},{20,28},{24,16},{28,20},{1,9},{5... | collective-permute-start | bytes 1966088 | tf_op jit(solution)/shard_map/ppermute | solution.py:774
  84.8 12.4 %collective-permute-start.20 = (bf16[512,128]{1,0:T(8,128)(2,1)S(1)}, bf16[512,128]{1,0:T(8,128)(2,1)S(1)}, u32[]{:S(2)}, u32[]{:S(2)}) collective-permute-start(bf16[512,128]{1,0:T(8,128)(2,1)S(1)} %get-tuple-element.143), channel_id=1, source_target_pairs={{0,2},{1,3},{2,0},{3,1},{4,6},{5,7},{6,4},{7,5},{8,10},{9,11},{10,... | collective-permute-start | bytes 393224 | tf_op jit(solution)/shard_map/ppermute | solution.py:774
  85.8 11.5 %collective-permute-start.21 = (bf16[512,128]{1,0:T(8,128)(2,1)S(1)}, bf16[512,128]{1,0:T(8,128)(2,1)S(1)}, u32[]{:S(2)}, u32[]{:S(2)}) collective-permute-start(bf16[512,128]{1,0:T(8,128)(2,1)S(1)} %get-tuple-element.144), channel_id=1, source_target_pairs={{0,3},{1,2},{2,1},{3,0},{4,7},{5,6},{6,5},{7,4},{8,11},{9,10},{10,... | collective-permute-start | bytes 393224 | tf_op jit(solution)/shard_map/ppermute | solution.py:774
  92.0 14.0 %collective-permute-start.24 = (bf16[4,64,1408]{2,1,0:T(8,128)(2,1)S(1)}, bf16[4,64,1408]{2,1,0:T(8,128)(2,1)S(1)}, u32[]{:S(2)}, u32[]{:S(2)}) collective-permute-start(bf16[4,64,1408]{2,1,0:T(8,128)(2,1)S(1)} %get-tuple-element.162), channel_id=1, source_target_pairs={{0,4},{4,0},{8,12},{12,8},{16,20},{20,16},{24,28},{28,24},{1,5},{5... | collective-permute-start | bytes 2162696 | tf_op jit(solution)/shard_map/ppermute | solution.py:774
  92.8 15.5 %collective-permute-start.27 = (bf16[4,64,640]{2,1,0:T(8,128)(2,1)S(1)}, bf16[4,64,640]{2,1,0:T(8,128)(2,1)S(1)}, u32[]{:S(2)}, u32[]{:S(2)}) collective-permute-start(bf16[4,64,640]{2,1,0:T(8,128)(2,1)S(1)} %get-tuple-element.166), channel_id=1, source_target_pairs={{0,16},{4,20},{8,24},{12,28},{16,0},{20,4},{24,8},{28,12},{1,17},{... | collective-permute-start | bytes 983048 | tf_op jit(solution)/shard_map/ppermute | solution.py:774
  101.7 12.2 %collective-permute-start.29 = (bf16[512,128]{1,0:T(8,128)(2,1)S(1)}, bf16[512,128]{1,0:T(8,128)(2,1)S(1)}, u32[]{:S(2)}, u32[]{:S(2)}) collective-permute-start(bf16[512,128]{1,0:T(8,128)(2,1)S(1)} %get-tuple-element.170), channel_id=1, source_target_pairs={{0,2},{1,3},{2,0},{3,1},{4,6},{5,7},{6,4},{7,5},{8,10},{9,11},{10,... | collective-permute-start | bytes 393224 | tf_op jit(solution)/shard_map/ppermute | solution.py:774
  102.7 11.2 %collective-permute-start.30 = (bf16[512,128]{1,0:T(8,128)(2,1)S(1)}, bf16[512,128]{1,0:T(8,128)(2,1)S(1)}, u32[]{:S(2)}, u32[]{:S(2)}) collective-permute-start(bf16[512,128]{1,0:T(8,128)(2,1)S(1)} %get-tuple-element.171), channel_id=1, source_target_pairs={{0,3},{1,2},{2,1},{3,0},{4,7},{5,6},{6,5},{7,4},{8,11},{9,10},{10,... | collective-permute-start | bytes 393224 | tf_op jit(solution)/shard_map/ppermute | solution.py:774
  106.0 16.0 %collective-permute-start.23 = (bf16[4,64,1152]{2,1,0:T(8,128)(2,1)S(1)}, bf16[4,64,1152]{2,1,0:T(8,128)(2,1)S(1)}, u32[]{:S(2)}, u32[]{:S(2)}) collective-permute-start(bf16[4,64,1152]{2,1,0:T(8,128)(2,1)S(1)} %get-tuple-element.158), channel_id=1, source_target_pairs={{0,4},{4,0},{8,12},{12,8},{16,20},{20,16},{24,28},{28,24},{1,5},{5... | collective-permute-start | bytes 1769480 | tf_op jit(solution)/shard_map/ppermute | solution.py:774
  106.8 15.3 %collective-permute-start.26 = (bf16[2,64,1408]{2,1,0:T(8,128)(2,1)S(1)}, bf16[2,64,1408]{2,1,0:T(8,128)(2,1)S(1)}, u32[]{:S(2)}, u32[]{:S(2)}) collective-permute-start(bf16[2,64,1408]{2,1,0:T(8,128)(2,1)S(1)} %get-tuple-element.165), channel_id=1, source_target_pairs={{0,8},{4,12},{8,0},{12,4},{16,24},{20,28},{24,16},{28,20},{1,9},{5... | collective-permute-start | bytes 1081352 | tf_op jit(solution)/shard_map/ppermute | solution.py:774
  108.9 13.1 %collective-permute-start.28 = (bf16[2,64,640]{2,1,0:T(8,128)(2,1)S(1)}, bf16[2,64,640]{2,1,0:T(8,128)(2,1)S(1)}, u32[]{:S(2)}, u32[]{:S(2)}) collective-permute-start(bf16[2,64,640]{2,1,0:T(8,128)(2,1)S(1)} %get-tuple-element.168), channel_id=1, source_target_pairs={{0,2},{1,3},{2,0},{3,1},{4,6},{5,7},{6,4},{7,5},{8,10},{9,11},{10,... | collective-permute-start | bytes 491528 | tf_op jit(solution)/shard_map/ppermute | solution.py:774
  122.9 11.9 %collective-permute-start.34 = (bf16[64,1408]{1,0:T(8,128)(2,1)S(1)}, bf16[64,1408]{1,0:T(8,128)(2,1)S(1)}, u32[]{:S(2)}, u32[]{:S(2)}) collective-permute-start(bf16[64,1408]{1,0:T(8,128)(2,1)S(1)} %get-tuple-element.179), channel_id=1, source_target_pairs={{0,16},{4,20},{8,24},{12,28},{16,0},{20,4},{24,8},{28,12},{1,17},{... | collective-permute-start | bytes 540680 | tf_op jit(solution)/shard_map/ppermute | solution.py:774
  125.9 8.8 %collective-permute-start.32 = (bf16[64,1152]{1,0:T(8,128)(2,1)S(1)}, bf16[64,1152]{1,0:T(8,128)(2,1)S(1)}, u32[]{:S(2)}, u32[]{:S(2)}) collective-permute-start(bf16[64,1152]{1,0:T(8,128)(2,1)S(1)} %get-tuple-element.176), channel_id=1, source_target_pairs={{0,16},{4,20},{8,24},{12,28},{16,0},{20,4},{24,8},{28,12},{1,17},{... | collective-permute-start | bytes 442376 | tf_op jit(solution)/shard_map/ppermute | solution.py:774
  135.4 10.6 %collective-permute-start.38 = (bf16[64,2176]{1,0:T(8,128)(2,1)S(1)}, bf16[64,2176]{1,0:T(8,128)(2,1)S(1)}, u32[]{:S(2)}, u32[]{:S(2)}) collective-permute-start(bf16[64,2176]{1,0:T(8,128)(2,1)S(1)} %get-tuple-element.185.refs_0_), channel_id=1, source_target_pairs={{0,24},{4,28},{8,16},{12,20},{16,8},{20,12},{24,0},{28,4},{1,25},{... | collective-permute-start | bytes 835592 | tf_op jit(solution)/shard_map/ppermute | solution.py:774
  137.4 10.8 %collective-permute-start.37 = (bf16[64,2176]{1,0:T(8,128)(2,1)S(1)}, bf16[64,2176]{1,0:T(8,128)(2,1)S(1)}, u32[]{:S(2)}, u32[]{:S(2)}) collective-permute-start(bf16[64,2176]{1,0:T(8,128)(2,1)S(1)} %get-tuple-element.185.refs_0_), channel_id=1, source_target_pairs={{0,16},{4,20},{8,24},{12,28},{16,0},{20,4},{24,8},{28,12},{1,17},{... | collective-permute-start | bytes 835592 | tf_op jit(solution)/shard_map/ppermute | solution.py:774
  137.9 10.3 %collective-permute-start.36 = (bf16[64,2176]{1,0:T(8,128)(2,1)S(1)}, bf16[64,2176]{1,0:T(8,128)(2,1)S(1)}, u32[]{:S(2)}, u32[]{:S(2)}) collective-permute-start(bf16[64,2176]{1,0:T(8,128)(2,1)S(1)} %get-tuple-element.185.refs_0_), channel_id=1, source_target_pairs={{0,8},{4,12},{8,0},{12,4},{16,24},{20,28},{24,16},{28,20},{1,9},{5... | collective-permute-start | bytes 835592 | tf_op jit(solution)/shard_map/ppermute | solution.py:774
  148.9 11.1 %collective-permute-start.39 = (bf16[4,64,2176]{2,1,0:T(8,128)(2,1)S(1)}, bf16[4,64,2176]{2,1,0:T(8,128)(2,1)S(1)}, u32[]{:S(2)}, u32[]{:S(2)}) collective-permute-start(bf16[4,64,2176]{2,1,0:T(8,128)(2,1)S(1)} %stack_two.1.refs_1_), channel_id=1, source_target_pairs={{0,4},{4,0},{8,12},{12,8},{16,20},{20,16},{24,28},{28,24},{1,5},{5... | collective-permute-start | bytes 3342344 | tf_op jit(solution)/shard_map/ppermute | solution.py:774
  150.1 9.1 %collective-permute-start.41 = (bf16[64,1152]{1,0:T(8,128)(2,1)S(1)}, bf16[64,1152]{1,0:T(8,128)(2,1)S(1)}, u32[]{:S(2)}, u32[]{:S(2)}) collective-permute-start(bf16[64,1152]{1,0:T(8,128)(2,1)S(1)} %get-tuple-element.192.refs_0_), channel_id=1, source_target_pairs={{0,16},{4,20},{8,24},{12,28},{16,0},{20,4},{24,8},{28,12},{1,17},{... | collective-permute-start | bytes 442376 | tf_op jit(solution)/shard_map/ppermute | solution.py:774
  150.7 8.6 %collective-permute-start.40 = (bf16[64,1152]{1,0:T(8,128)(2,1)S(1)}, bf16[64,1152]{1,0:T(8,128)(2,1)S(1)}, u32[]{:S(2)}, u32[]{:S(2)}) collective-permute-start(bf16[64,1152]{1,0:T(8,128)(2,1)S(1)} %get-tuple-element.192.refs_0_), channel_id=1, source_target_pairs={{0,8},{4,12},{8,0},{12,4},{16,24},{20,28},{24,16},{28,20},{1,9},{5... | collective-permute-start | bytes 442376 | tf_op jit(solution)/shard_map/ppermute | solution.py:774
  (43 other events, 325.6 us)

commit v2 on v1

--- a/solution.py
+++ b/solution.py
@@ -21,7 +21,7 @@
 PARTS = 8
 
 
-def call(body, outs, *args, scratch=(), flops=0, name=None, space=pltpu.VMEM):
+def call(body, outs, *args, scratch=(), flops=0, name=None, space=pltpu.VMEM, vmem=VMEM):
     result = pl.pallas_call(
         body,
         out_shape=list(outs),
@@ -29,7 +29,7 @@
         + [pl.BlockSpec(memory_space=space)] * (len(args) - 1),
         out_specs=[pl.BlockSpec(memory_space=pltpu.VMEM)] * len(outs),
         scratch_shapes=list(scratch),
-        compiler_params=pltpu.CompilerParams(vmem_limit_bytes=VMEM * 2**20),
+        compiler_params=pltpu.CompilerParams(vmem_limit_bytes=vmem * 2**20),
         cost_estimate=pl.CostEstimate(flops=flops, bytes_accessed=1, transcendentals=0),
         name=name,
     )(*args)
@@ -150,16 +150,17 @@
     return rows_of([blank, values[: POS - LAT], blank, values[POS : 2 * POS - LAT]])
 
 
-def conv_forward(pieces, w_ref):
+def conv_forward(pieces, w_ref, z):
     full = lanes(pieces)
     height = full.shape[0]
     inner, outer = column_masks(height)
+    blocks = [pl.ds(pl.multiple_of((z ^ k) * 128, 128), 128) for k in range(4)]
     sums = []
     for col_tap in range(3):
         total = None
         for row_tap in range(3):
             tap = 3 * row_tap + col_tap
-            part = dot(full, w_ref[0, :, 128 * tap : 128 * tap + 128])
+            part = dot(full, rows_of([w_ref[0, tap, block, :] for block in blocks]))
             if row_tap == 0:
                 part = earlier_rows(part)
             elif row_tap == 2:
@@ -193,11 +194,70 @@
     return place, pl.multiple_of(block * 128 + (place & 1) * 64, 64)
 
 
-def first_norm_kernel(scalars, x_ref, gain_ref, shift_ref, act_ref, stats_ref):
+def fetch(pairs, sems):
+    copies = [
+        pltpu.make_async_copy(source, target, sems.at[i])
+        for i, (source, target) in enumerate(pairs)
+    ]
+    for copy in copies:
+        copy.start()
+    for copy in copies:
+        copy.wait()
+
+
+def begin_kernel(
+    scalars,
+    x_any,
+    gain_any,
+    shift_any,
+    conv_b_any,
+    attn_b_any,
+    proj_b_any,
+    qkv_any,
+    out_w_any,
+    proj_any,
+    act_ref,
+    stats_ref,
+    pack_ref,
+    param_ref,
+    x_ref,
+    gain_ref,
+    shift_ref,
+    conv_b_ref,
+    attn_b_ref,
+    proj_b_ref,
+    weights,
+    proj_ref,
+    proj,
+    sems,
+):
+    own = pl.ds(pl.multiple_of(scalars[1] * 64, 64), 64)
+    fetch(
+        [
+            (x_any, x_ref),
+            (gain_any, gain_ref),
+            (shift_any, shift_ref),
+            (conv_b_any, conv_b_ref),
+            (attn_b_any, attn_b_ref),
+            (proj_b_any, proj_b_ref),
+            (out_w_any.at[own, :], weights.at[3]),
+            (proj_any, proj_ref),
+        ]
+        + [(qkv_any.at[m, own, :], weights.at[m]) for m in range(3)],
+        sems,
+    )
     normed, stats = moments(x_ref[...].astype(F32))
     pre = normed * gain_ref[0:1] + shift_ref[0:1]
     act_ref[...] = (pre * jax.nn.sigmoid(pre)).astype(BF)
     stats_ref[...] = stats
+    for m in range(4):
+        pack_ref[:, 128 * m : 128 * m + 128] = weights[m]
+    proj[...] = jnp.transpose(proj_ref[...].astype(F32))
+    pack_ref[:, 512:640] = lanes([proj[own, :], jnp.zeros((64, 64), F32)]).astype(BF)
+    rows = [gain_ref[m : m + 1] for m in range(3)] + [shift_ref[m : m + 1] for m in range(3)]
+    rows += [conv_b_ref[m : m + 1] for m in range(2)] + [attn_b_ref[m : m + 1] for m in range(3)]
+    rows += [lanes([proj_b_ref[...], jnp.zeros_like(proj_b_ref[...])])]
+    param_ref[...] = pack_rows(rows, 16)
 
 
 def code_column(codes):
@@ -234,16 +294,7 @@
         row = (scalars[0] ^ k) * 128
         one = start[pl.ds(pl.multiple_of(row, 64), 64), :]
         two = start[pl.ds(pl.multiple_of(row + 64, 64), 64), :]
-        high, low = split_low(lanes([one, two]))
-        fixed_ref[k, 0:64] = high.astype(BF)
-        fixed_ref[k, 64:128] = low.astype(BF)
-
-
-def conv_weight_kernel(scalars, w_ref, o_ref):
-    for k in range(4):
-        own = pl.ds(pl.multiple_of((scalars[0] ^ k) * 128, 128), 128)
-        for tap in range(9):
-            o_ref[0, 128 * k : 128 * k + 128, 128 * tap : 128 * tap + 128] = w_ref[0, tap, own, :]
+        fixed_ref[k] = lanes([one, two]).astype(BF)
 
 
 def attn_weight_kernel(scalars, own_ref, other_ref, o_ref):
@@ -265,9 +316,8 @@
 def conv_one_kernel(
     scalars, a0, a1, a2, a3, w_ref, param_ref, _, hidden_ref, stats_ref, act_ref
 ):
-    hidden = conv_forward([a0[...], a1[...], a2[...], a3[...]], w_ref) + param(
-        param_ref, CONV_BIAS
-    )
+    pieces = [a0[...], a1[...], a2[...], a3[...]]
+    hidden = conv_forward(pieces, w_ref, scalars[0]) + param(param_ref, CONV_BIAS)
     hidden_ref[...] = hidden
     normed, stats = moments(hidden)
     stats_ref[...] = stats
@@ -279,7 +329,8 @@
     scalars, a0, a1, a2, a3, w_ref, param_ref, x_ref, fixed_ref, normed_ref, stats_ref, *pay_refs
 ):
     residual = x_ref[...].astype(F32) + (
-        conv_forward([a0[...], a1[...], a2[...], a3[...]], w_ref) + param(param_ref, CONV_BIAS + 1)
+        conv_forward([a0[...], a1[...], a2[...], a3[...]], w_ref, scalars[0])
+        + param(param_ref, CONV_BIAS + 1)
     )
     normed, stats = moments(residual)
     normed_ref[...] = normed
@@ -301,7 +352,7 @@
         for index in (GAIN + 2, SHIFT + 2, ATTN_BIAS, ATTN_BIAS + 1, ATTN_BIAS + 2, PROJ_BIAS):
             rows.extend(split_low(param(param_ref, index)))
         ref[384:400] = pack_rows(rows, 16).astype(BF)
-        ref[400:528] = fixed_ref[k]
+        ref[400:464] = fixed_ref[k]
 
 
 def attn_in_kernel(scalars, n0, n1, n2, n3, norm_ref, residual_ref, bias_ref):
@@ -345,7 +396,7 @@
     latents = dot(output, w_ref[:, 2048:2304]) + proj_bias
     fixed = []
     for n in pieces:
-        both = n[400:464].astype(F32) + n[464:528].astype(F32)
+        both = n[400:464].astype(F32)
         fixed.append(rows_of([both[:, :64], both[:, 64:]]))
     lat_grad = (lanes(fixed) + 2.0 * BETA * latents).astype(BF)
     blank = jnp.zeros((128, 64), BF)
@@ -486,14 +537,16 @@
     residual_ref[...] = residual
     low = residual.astype(BF).astype(F32)
     small_ref[...] = pack_rows([gain_grad, shift_grad, col_sum(low)])
-    send_taps(low, w_ref, taps_ref, (q0, q1, q2, q3))
-
-
-def send_taps(gradient, w_ref, taps_ref, piece_refs):
+    send_taps(low, w_ref, scalars[0], taps_ref, (q0, q1, q2, q3))
+
+
+def send_taps(gradient, w_ref, z, taps_ref, piece_refs):
     taps = spread_taps(gradient)
     taps_ref[...] = taps
     for k, ref in enumerate(piece_refs):
-        ref[...] = dot_nt(taps, w_ref[0, 128 * k : 128 * k + 128, :]).astype(ref.dtype)
+        block = pl.ds(pl.multiple_of((z ^ k) * 128, 128), 128)
+        weights = lanes([w_ref[0, tap, block, :] for tap in range(9)])
+        ref[...] = dot_nt(taps, weights).astype(ref.dtype)
 
 
 def swish_back(gradient, normed, gain, shift):
@@ -529,7 +582,7 @@
     source, gain_grad, shift_grad = norm_back(upstream, normed, stats, gain)
     low = source.astype(BF).astype(F32)
     small_ref[...] = pack_rows([gain_grad, shift_grad, col_sum(low)])
-    send_taps(low, w_ref, taps_ref, (q0, q1, q2, q3))
+    send_taps(low, w_ref, scalars[0], taps_ref, (q0, q1, q2, q3))
 
 
 def first_back_kernel(
@@ -597,12 +650,26 @@
         ref[:, WIDE + 128 : WIDE + 256] = book[64:128, column]
 
 
-def finish_two_kernel(
+def finish_two_kernel(scalars, own_ref, other_ref, conv_ref, book_grad_ref, picked_ref):
+    for part in range(PARTS):
+        source = (own_ref if part % 2 == 0 else other_ref).at[part // 2]
+        place = scalars[1] ^ part
+        rows = pl.ds(pl.multiple_of(place * 64, 64), 64)
+        for tap in range(9):
+            conv_ref[0, tap, rows, :] = source[:, 128 * tap : 128 * tap + 128].astype(F32)
+        column = pl.ds(pl.multiple_of(place * 128, 128), 128)
+        book_grad_ref[:, column] = source[:, WIDE : WIDE + 128].astype(F32)
+        picked_ref[:, column] = source[:, WIDE + 128 : WIDE + 256].astype(F32)
+
+
+def finish_last_kernel(
     tokens_all,
     scalars,
     own_ref,
     other_ref,
+    picked,
     book_ref,
+    held_ref,
     conv_ref,
     gain_ref,
     shift_ref,
@@ -611,14 +678,12 @@
     qkv_ref,
     out_w_ref,
     proj_ref,
-    book_grad_ref,
     new_book_ref,
     perplexity_ref,
     attn_bias_ref,
     proj_bias_ref,
     usage,
     proj,
-    picked,
 ):
     extra_sum = jnp.zeros((16, 128), F32)
     total = jnp.zeros((16, 128), F32)
@@ -628,14 +693,11 @@
         rows = pl.ds(pl.multiple_of(place * 64, 64), 64)
         for tap in range(9):
             conv_ref[0, tap, rows, :] = source[:, 128 * tap : 128 * tap + 128].astype(F32)
-        column = pl.ds(pl.multiple_of(place * 128, 128), 128)
-        book_grad_ref[:, column] = source[:, WIDE : WIDE + 128].astype(F32)
-        picked[:, column] = source[:, WIDE + 128 : WIDE + 256].astype(F32)
         for m in range(3):
-            qkv_ref[m, rows, :] = source[:, 1408 + 128 * m : 1536 + 128 * m].astype(F32)
-        out_w_ref[rows, :] = source[:, 1792:1920].astype(F32)
-        proj[rows, :] = source[:, 1920:2048].astype(F32)
-        extra = source[0:16, 1920:2048].astype(F32)
+            qkv_ref[m, rows, :] = source[:, 1152 + 128 * m : 1280 + 128 * m].astype(F32)
+        out_w_ref[rows, :] = source[:, 1536:1664].astype(F32)
+        proj[rows, :] = source[:, 1664:1792].astype(F32)
+        extra = source[0:16, 1664:1792].astype(F32)
         extra_sum = extra_sum + extra
         usage[pl.ds(place, 1), :] = lanes(
             [
@@ -643,7 +705,7 @@
                 16.0 * extra[1:2, 64:] + extra[3:4, 64:],
             ]
         )
-        both = source[0:32, 2048:2176].astype(F32)
+        both = source[0:32, 1792:1920].astype(F32)
         total = total + (both[0:16] + both[16:32])
     for index, row in enumerate((0, 2, 5)):
         gain_ref[index : index + 1] = total[row : row + 1]
@@ -669,14 +731,6 @@
     proj_bias_ref[...] = extra_sum[10:11, 64:]
 
 
-def finish_one_kernel(scalars, own_ref, other_ref, held_ref, conv_ref):
-    for part in range(PARTS):
-        source = (own_ref if part % 2 == 0 else other_ref).at[part // 2]
-        rows = pl.ds(pl.multiple_of((scalars[1] ^ part) * 64, 64), 64)
-        for tap in range(9):
-            conv_ref[0, tap, rows, :] = source[:, 128 * tap : 128 * tap + 128].astype(F32)
-
-
 def pair_add_kernel(scalars, k0, k1, k2, k3, get_ref, _, keep_ref, send_ref):
     for i, ref in enumerate((k0, k1, k2, k3)):
         target = (send_ref if i % 2 else keep_ref).at[i // 2]
@@ -693,9 +747,8 @@
 
 
 def attn_sum_kernel(scalars, a0, a1, _, keep_ref, send_ref):
-    for k in range(2):
-        keep_ref[k] = plus(a0[k], a1[k])
-        send_ref[k] = plus(a0[2 + k], a1[2 + k])
+    for k in range(4):
+        (send_ref if k % 2 else keep_ref)[k // 2] = plus(a0[k], a1[k])
 
 
 def tail_first_kernel(
@@ -705,7 +758,7 @@
     k2,
     k3,
     one_get,
-    two_keep,
+    two_own,
     two_get,
     att_keep,
     att_get,
@@ -714,59 +767,37 @@
     o1,
     o2,
     o3,
-    two_own,
-    two_send,
+    two_ref,
     att_own,
     att_send,
 ):
     for i, (ref, out) in enumerate(((k0, o0), (k1, o1), (k2, o2), (k3, o3))):
         out[...] = plus(ref[...], one_get[i])
-    two_own[...] = plus(two_keep[0], two_get[0])
-    two_send[...] = plus(two_keep[1], two_get[1])
+    two_ref[...] = plus(two_own[...], two_get[...])
     att_own[...] = plus(att_keep[0], att_get[0])
     att_send[...] = plus(att_keep[1], att_get[1])
 
 
-def tail_second_kernel(
-    scalars,
-    o0,
-    o1,
-    o2,
-    o3,
-    two_own,
-    two_get,
-    att_own,
-    att_get,
-    small_one,
-    small_two,
-    small_three,
-    commit,
-    two_ref,
-    one_ref,
+def last_kernel(
+    scalars, o0, o1, o2, o3, att_own, att_get, small_one, small_two, small_three, commit, last_ref
 ):
     total = o0[...].astype(F32)
     for ref in (o1, o2, o3):
         total = total + ref[...].astype(F32)
-    one_ref[...] = total.astype(BF)
-    two_ref[:, 0:1408] = plus(two_own[...], two_get[...])
-    two_ref[:, 1408:2048] = plus(att_own[...], att_get[...])
+    last_ref[:, 0:WIDE] = total.astype(BF)
+    last_ref[:, 1152:1792] = plus(att_own[...], att_get[...])
     rows = [small_one[0:1], small_one[1:2]]
     rows += [small_two[m : m + 1] for m in range(3)]
     rows += [small_three[m : m + 1] for m in range(3)]
     rows += [commit[0:1]]
     high, low = split_low(pack_rows(rows, 16))
-    two_ref[:, 2048:2176] = rows_of([high, low, jnp.zeros((32, 128), F32)]).astype(BF)
+    last_ref[:, 1792:1920] = rows_of([high, low, jnp.zeros((32, 128), F32)]).astype(BF)
 
 
 def stack_kernel(scalars, *refs):
     out_ref = refs[-1]
     for k in range(out_ref.shape[0]):
         out_ref[k] = refs[k][...]
-
-
-def join_kernel(scalars, a0, a1, out_ref):
-    out_ref[0:2] = a0[...]
-    out_ref[2:4] = a1[...]
 
 
 def over(axis, array, flip):
@@ -834,54 +865,50 @@
             name=name,
         )(scalars, *args)
 
-    act_one, stats_one = call(
-        first_norm_kernel,
-        [sds((tokens, 128), BF), sds((8, 128), F32)],
+    act_one, stats_one, pack, params = call(
+        begin_kernel,
+        [
+            sds((tokens, 128), BF),
+            sds((8, 128), F32),
+            sds((64, 640), BF),
+            sds((16, 128), F32),
+        ],
         scalars,
         x,
         norm_gains,
         norm_shifts,
+        conv_biases,
+        attn_biases,
+        proj_bias.reshape(1, 64),
+        qkv_weights,
+        out_weight,
+        proj_weight.T,
+        scratch=[
+            pltpu.VMEM((tokens, 128), BF),
+            pltpu.VMEM((3, 128), F32),
+            pltpu.VMEM((3, 128), F32),
+            pltpu.VMEM((2, 128), F32),
+            pltpu.VMEM((3, 128), F32),
+            pltpu.VMEM((1, 64), F32),
+            pltpu.VMEM((4, 64, 128), BF),
+            pltpu.VMEM((64, C), BF),
+            pltpu.VMEM((C, 64), F32),
+            pltpu.SemaphoreType.DMA((11,)),
+        ],
         flops=HEAVY,
-        name="first_norm",
+        space=pl.ANY,
+        vmem=60,
+        name="begin",
     )
     pieces_one = [act_one] + flips(act_one)
-    rows = scalars[1] * 64
-    pack = jnp.concatenate(
-        [lax.dynamic_slice(qkv_weights[m], (rows, 0), (64, 128)) for m in range(3)]
-        + [
-            lax.dynamic_slice(out_weight, (rows, 0), (64, 128)),
-            lax.dynamic_slice(proj_weight, (rows, 0), (64, 64)),
-            jnp.zeros((64, 64), BF),
-        ],
-        axis=1,
-    )
-    if by_hand:
-        pack_pair = call(
-            stack_kernel,
-            [sds((2, 64, 640), BF)],
-            scalars,
-            pack,
-            over("chan", pack, 1),
-            name="pack_pair",
-        )[0]
-        pack_far = over("chan", pack_pair, 2)
-    params = jnp.concatenate(
-        [
-            norm_gains,
-            norm_shifts,
-            conv_biases,
-            attn_biases,
-            jnp.pad(proj_bias.reshape(1, 64), ((0, 0), (0, 64))),
-            jnp.zeros((4, 128), F32),
-        ]
-    )
+    packs = [pack] + flips(pack)
     hot, quantized, usage, fixed = call(
         start_kernel,
         [
             sds((tokens, CODES), BF),
             sds((tokens, 64), F32),
             sds((8, 128), F32),
-            sds((4, 128, 128), BF),
+            sds((4, 64, 128), BF),
         ],
         scalars,
         codes,
@@ -891,25 +918,11 @@
         scratch=[pltpu.VMEM((tokens, 64), F32)],
         name="start",
     )
-    weights_full = pl.pallas_call(
-        conv_weight_kernel,
-        grid=(2,),
-        out_shape=sds((2, C, WIDE), BF),
-        in_specs=[
-            pl.BlockSpec(memory_space=pltpu.SMEM),
-            pl.BlockSpec((1, 9, C, 128), lambda i: (i, 0, 0, 0)),
-        ],
-        out_specs=pl.BlockSpec((1, C, WIDE), lambda i: (i, 0, 0)),
-        compiler_params=pltpu.CompilerParams(vmem_limit_bytes=VMEM * 2**20),
-        cost_estimate=pl.CostEstimate(flops=0, bytes_accessed=1, transcendentals=0),
-        name="conv_weight",
-    )(scalars, conv_w)
-
     def conv_call(body, index, outs, name, *args):
         specs = []
         for a in args:
-            if a is weights_full:
-                specs.append(pl.BlockSpec((1, C, WIDE), lambda i: (index, 0, 0)))
+            if a is conv_w:
+                specs.append(pl.BlockSpec((1, 9, C, 128), lambda i: (index, 0, 0, 0)))
             else:
                 specs.append(whole(a.shape))
         scratch = ()
@@ -925,14 +938,19 @@
         [sds((tokens, 128), F32), sds((8, 128), F32), sds((tokens, 128), BF)],
         "conv_one",
         *pieces_one,
-        weights_full,
+        conv_w,
         params,
         usage,
     )
     pieces_two = [act_two] + flips(act_two)
     if by_hand:
         block = call(
-            join_kernel, [sds((4, 64, 640), BF)], scalars, pack_pair, pack_far, name="pack_join"
+            stack_kernel,
+            [sds((4, 64, 640), BF)],
+            scalars,
+            *packs,
+            flops=HEAVY,
+            name="pack_join",
         )[0]
         blocks = [block] + [over("dp", block, k) for k in (2, 4, 6)]
     else:
@@ -947,10 +965,10 @@
     normed_three, stats_three, *pays = conv_call(
         conv_two_kernel,
         1,
-        [sds((tokens, 128), F32), sds((8, 128), F32)] + [sds((528, 128), BF)] * 4,
+        [sds((tokens, 128), F32), sds((8, 128), F32)] + [sds((464, 128), BF)] * 4,
         "conv_two",
         *pieces_two,
-        weights_full,
+        conv_w,
         params,
         x,
         fixed,
@@ -1041,13 +1059,13 @@
         stats_three,
         params,
         att_kept if by_hand else sums,
-        weights_full,
+        conv_w,
     )
     back_two = [pays[0]] + [over("chan", pays[k], k) for k in (1, 2, 3)]
     book_scale = 2.0 * CODES / tokens_all
 
     def two_grad(*refs):
-        conv_two_grad_kernel(*refs[:10], book_scale, *refs[11:])
+        conv_two_grad_kernel(*refs[:10], book_scale, *refs[10:])
 
     *two_keep, two_send, commit = call(
         two_grad,
@@ -1059,7 +1077,6 @@
         latents,
         quantized,
         reset_src.reshape(1, CODES),
-        back_two[1],
         scratch=[pltpu.VMEM((C, WIDE), BF), pltpu.VMEM((128, CODES), BF)],
         name="conv_two_grad",
     )
@@ -1070,10 +1087,12 @@
             scalars,
             att_kept,
             att_got,
-            back_two[1],
+            small_three,
+            flops=HEAVY,
             name="attn_half",
         )
         att_got = over("dp", att_sent, 4)
+        two_kept, two_got = pair_sum(two_keep, two_send, att_own, "conv_two_pair")
     taps_one, small_two, *pays = conv_call(
         second_back_kernel,
         0,
@@ -1085,8 +1104,8 @@
         stats_two,
         params,
         att_own if by_hand else sums,
-        two_keep[0],
-        weights_full,
+        two_kept if by_hand else sums,
+        conv_w,
     )
     back_one = [pays[0]] + [over("chan", pays[k], k) for k in (1, 2, 3)]
     *one_keep, one_send = call(
@@ -1099,7 +1118,16 @@
         name="conv_one_grad",
     )
     if by_hand:
-        two_kept, two_got = pair_sum(two_keep, two_send, back_one[1], "conv_two_pair")
+        two_own, two_sent = call(
+            half_add_kernel,
+            [sds((64, 1408), BF)] * 2,
+            scalars,
+            two_kept,
+            two_got,
+            back_one[1],
+            name="conv_two_half",
+        )
+        two_got = over("dp", two_sent, 4)
         att_kept, att_sent = call(
             attn_sum_kernel,
             [sds((2, 64, 640), BF)] * 2,
@@ -1109,7 +1137,7 @@
             back_one[1],
             name="attn_sum",
         )
-        att_got = over("chan", att_sent, 2)
+        att_got = over("chan", att_sent, 1)
     grad_latents, small_one = call(
         first_back_kernel,
         [sds((tokens, 128), F32), sds((8, 128), F32)],
@@ -1120,20 +1148,20 @@
         params,
         residual_grad,
         one_keep[0],
-        two_kept if by_hand else sums,
+        two_own if by_hand else sums,
         att_kept if by_hand else sums,
         flops=HEAVY,
         name="first_back",
     )
 
     if by_hand:
-        o0, o1, o2, o3, two_own, two_sent, att_own, att_sent = call(
+        o0, o1, o2, o3, two, att_own, att_sent = call(
             tail_first_kernel,
-            [sds((64, WIDE), BF)] * 4 + [sds((64, 1408), BF)] * 2 + [sds((64, 640), BF)] * 2,
+            [sds((64, WIDE), BF)] * 4 + [sds((64, 1408), BF)] + [sds((64, 640), BF)] * 2,
             scalars,
             *one_keep,
             over("dp", one_send, 1),
-            two_kept,
+            two_own,
             two_got,
             att_kept,
             att_got,
@@ -1141,37 +1169,33 @@
             flops=HEAVY,
             name="tail_first",
         )
-        two, one = call(
-            tail_second_kernel,
-            [sds((64, 2176), BF), sds((64, WIDE), BF)],
+        last = call(
+            last_kernel,
+            [sds((64, 1920), BF)],
             scalars,
             o0,
             over("dp", o1, 2),
             over("dp", o2, 4),
             over("dp", o3, 6),
-            two_own,
-            over("dp", two_sent, 4),
             att_own,
-            over("chan", att_sent, 1),
+            over("chan", att_sent, 2),
             small_one,
             small_two,
             small_three,
             commit,
             flops=HEAVY,
-            name="tail_second",
-        )
-        all_two, all_one = plane(two), plane(one)
-        two_own = call(
-            stack_kernel,
-            [sds((4, 64, 2176), BF)],
-            scalars,
-            *all_two,
-            flops=HEAVY,
-            name="stack_two",
+            name="last",
         )[0]
+
+        def chip(array, name, *after, flops=0):
+            parts = plane(array)
+            outs = [sds((4,) + array.shape, BF)]
+            return call(stack_kernel, outs, scalars, *parts, *after, flops=flops, name=name)[0]
+
+        two_own = chip(two, "stack_two", last, flops=HEAVY)
         two_other = over("dp", two_own, 1)
-        one_own = call(stack_kernel, [sds((4, 64, WIDE), BF)], scalars, *all_one, name="stack_one")[0]
-        one_other = over("dp", one_own, 1)
+        last_own = chip(last, "stack_last", flops=HEAVY)
+        last_other = over("dp", last_own, 1)
     else:
 
         def total(keep, send):
@@ -1185,12 +1209,26 @@
         high = lax.reduce_precision(small, 8, 7)
         smalls = jnp.concatenate([high, small - high, jnp.zeros((32, 128), F32)]).astype(BF)
         smalls = jnp.zeros((2, 4, 64, 128), BF).at[0, 0].set(smalls)
-        two_sum = total(two_keep, two_send)
-        two_own, two_other = jnp.concatenate([two_sum, att_sum, smalls], axis=3)
-        one_own, one_other = total(one_keep, one_send)
-
-    def finish_two(*refs):
-        finish_two_kernel(float(tokens_all), *refs)
+        two_own, two_other = total(two_keep, two_send)
+        one_sum = total(one_keep, one_send)
+        last_own, last_other = jnp.concatenate([one_sum, att_sum, smalls], axis=3)
+
+    conv_held, book_grad, picked = blocks_call(
+        finish_two_kernel,
+        [whole((4, 64, 1408)), whole((4, 64, 1408))],
+        [
+            pl.BlockSpec((1, 9, C, 128), lambda i: (1, 0, 0, 0)),
+            whole((64, CODES)),
+            whole((64, CODES)),
+        ],
+        [sds((2, 9, C, 128), F32), sds((64, CODES), F32), sds((64, CODES), F32)],
+        "finish_two",
+        two_own,
+        two_other,
+    )
+
+    def finish_last(*refs):
+        finish_last_kernel(float(tokens_all), *refs)
 
     outs = [
         sds((2, 9, C, 128), F32),
@@ -1202,13 +1240,12 @@
         sds((C, 128), F32),
         sds((64, C), F32),
         sds((64, CODES), F32),
-        sds((64, CODES), F32),
         sds((1, 1), F32),
         sds((3, 128), F32),
         sds((1, 64), F32),
     ]
     (
-        conv_held,
+        conv_grad,
         gain_grad,
         shift_grad,
         conv_bias_grad,
@@ -1216,37 +1253,25 @@
         qkv_grad,
         out_grad,
         proj_grad,
-        book_grad,
         new_codebook,
         perplexity,
         attn_bias_grad,
         proj_bias_grad,
     ) = blocks_call(
-        finish_two,
-        [whole((4, 64, 2176)), whole((4, 64, 2176)), whole((64, CODES))],
-        [pl.BlockSpec((1, 9, C, 128), lambda i: (1, 0, 0, 0))] + [whole(o.shape) for o in outs[1:]],
+        finish_last,
+        [whole((4, 64, 1920)), whole((4, 64, 1920)), whole((64, CODES)), whole((64, CODES))]
+        + [pl.BlockSpec(memory_space=pl.ANY)],
+        [pl.BlockSpec((1, 9, C, 128), lambda i: (0, 0, 0, 0))] + [whole(o.shape) for o in outs[1:]],
         outs,
-        "finish_two",
-        two_own,
-        two_other,
+        "finish_last",
+        last_own,
+        last_other,
+        picked,
         codebook.T,
-        scratch=[
-            pltpu.VMEM((8, 128), F32),
-            pltpu.VMEM((C, 128), F32),
-            pltpu.VMEM((64, CODES), F32),
-        ],
-    )
-    conv_grad = blocks_call(
-        finish_one_kernel,
-        [whole((4, 64, WIDE)), whole((4, 64, WIDE)), pl.BlockSpec(memory_space=pl.ANY)],
-        [pl.BlockSpec((1, 9, C, 128), lambda i: (0, 0, 0, 0))],
-        [sds((2, 9, C, 128), F32)],
-        "finish_one",
-        one_own,
-        one_other,
         conv_held,
-        aliases={3: 0},
-    )[0]
+        scratch=[pltpu.VMEM((8, 128), F32), pltpu.VMEM((C, 128), F32)],
+        aliases={5: 0},
+    )
 
     return (
         latents.reshape(images, LAT, LAT, -1),

time: 165 us -> 146 us (0.88)
  waiting for transfers between devices: 56.9 us -> 37.6 us
  local copies, waits for them, and re-layouts: 8.53 us -> 3.44 us
  starting transfers between devices: 59.7 us -> 63.7 us
    ppermute x44 -> x45, waiting for transfers between devices: 56.9 us -> 37.6 us  [over(): return lax.ppermute(array, axis, [(i, i ^ flip) for i in range(size)])]
    ppermute x44 -> x45, starting transfers between devices: 59.7 us -> 63.7 us  [over(): return lax.ppermute(array, axis, [(i, i ^ flip) for i in range(size)])]
    unnamed x63 -> x64, local copies, waits for them, and re-layouts: 6.5 us -> 3.44 us
    pallas_call x20, Pallas kernels: 22.4 us -> 24.1 us  [call(): pl.pallas_call(body, out_shape=list(outs), in_specs=[pl.BlockSpec(memory_...]
  transfers between devices with their start and end apart: 44 -> 45, of which waited for: 19 -> 19; matrix products, arithmetic and copies ran while one was open for 1% -> 0% of each run, Pallas kernels for 16% -> 18%
where the time goes in v2:
time: 146 us
  starting transfers between devices  63.7 us (44%)
  Pallas kernels  39 us (27%)
  waiting for transfers between devices  37.6 us (26%)
  local copies, waits for them, and re-layouts  3.44 us (2%)
    ppermute x45, starting transfers between devices, over(): return lax.ppermute(array, axis, [(i, i ^ flip) for i in range(size)])  63.7 us
    ppermute x45, waiting for transfers between devices, over(): return lax.ppermute(array, axis, [(i, i ^ flip) for i in range(size)])  37.6 us
    pallas_call x20, Pallas kernels, call(): pl.pallas_call(body, out_shape=list(outs), in_specs=[pl.BlockSpec(memory_...  24.1 us
    pallas_call x6, Pallas kernels, blocks_call(): pl.pallas_call(body, grid=(1,), out_shape=outs, in_specs=[pl.BlockSpec(me...  14.9 us
    unnamed x64, local copies, waits for them, and re-layouts  3.44 us
  transfers between devices with their start and end apart: 45, of which 19 were waited for; matrix products, arithmetic and copies ran while one was open for 0% of the time, Pallas kernels for 18%

profile of v2, /device:TPU:0, one launch (start us, length us, event | category | flops | bytes accessed | tf_op | source)
XLA Modules:
  0.0 145.6 jit_solution(4020204769579820411)
XLA Ops:
  1.3 3.0 %begin.1 = (bf16[512,128]{1,0:T(8,128)(2,1)}, f32[8,128]{1,0:T(8,128)}, bf16[64,640]{1,0:T(8,128)(2,1)}, f32[16,128]{1,0:T(8,128)}) custom-call(s32[4]{0:T(128)} %pad_add_fusion.scalars.refs_0_, bf16[512,128]{1,0:T(8,128)(2,1)} %bitcast.27, f32[3,128]{1,0:T(4,128)} %gain_any.1, f32[3,128]{1,0:T(4,128)} %shift_any.1, f32[2,128]{1,0:T(2,128)} %conv_b_any.1, ...), custom_call_target="tpu_custom_call" | custom-call | flops 99999997952 | bytes 1 | tf_op jit(solution)/shard_map/begin/pallas_call | solution.py:25
  4.3 5.1 %collective-permute-start.2 = (bf16[512,128]{1,0:T(8,128)(2,1)}, bf16[512,128]{1,0:T(8,128)(2,1)S(1)}, u32[]{:S(2)}, u32[]{:S(2)}) collective-permute-start(bf16[512,128]{1,0:T(8,128)(2,1)} %get-tuple-element.111.a0), channel_id=1, source_target_pairs={{0,3},{1,2},{2,1},{3,0},{4,7},{5,6},{6,5},{7,4},{8,11},{9,10},{10,... | collective-permute-start | bytes 393224 | tf_op jit(solution)/shard_map/ppermute | solution.py:805
  10.1 3.7 %collective-permute-start.11 = (bf16[64,640]{1,0:T(8,128)(2,1)}, bf16[64,640]{1,0:T(8,128)(2,1)S(1)}, u32[]{:S(2)}, u32[]{:S(2)}) collective-permute-start(bf16[64,640]{1,0:T(8,128)(2,1)} %get-tuple-element.124.refs_0_), channel_id=1, source_target_pairs={{0,3},{1,2},{2,1},{3,0},{4,7},{5,6},{6,5},{7,4},{8,11},{9,10},{10,... | collective-permute-start | bytes 245768 | tf_op jit(solution)/shard_map/ppermute | solution.py:805
  14.5 1.9 %start.1 = (bf16[512,1024]{1,0:T(8,128)(2,1)S(1)}, f32[512,64]{1,0:T(8,128)S(1)}, f32[8,128]{1,0:T(8,128)S(1)}, bf16[4,64,128]{2,1,0:T(8,128)(2,1)S(1)}) custom-call(s32[4]{0:T(128)S(1)} %copy-done.19, s32[2,16,16]{2,1,0:T(8,128)S(1)} %copy-done.20, f32[64,1024]{1,0:T(8,128)S(1)} %bitcast.18, bf16[512,64]{1,0:T(8,128)(2,1)S(1)} %bitcast.21, ...), custom_call_target="tpu_custom_call" | custom-call | bytes 1 | tf_op jit(solution)/shard_map/start/pallas_call | solution.py:25
  16.5 3.8 %collective-permute-start.9 = (bf16[64,640]{1,0:T(8,128)(2,1)}, bf16[64,640]{1,0:T(8,128)(2,1)S(1)}, u32[]{:S(2)}, u32[]{:S(2)}) collective-permute-start(bf16[64,640]{1,0:T(8,128)(2,1)} %get-tuple-element.124.refs_0_), channel_id=1, source_target_pairs={{0,1},{1,0},{2,3},{3,2},{4,5},{5,4},{6,7},{7,6},{8,9},{9,8},{10,11... | collective-permute-start | bytes 245768 | tf_op jit(solution)/shard_map/ppermute | solution.py:805
  20.3 4.9 %collective-permute-done.1.a2 = bf16[512,128]{1,0:T(8,128)(2,1)S(1)} collective-permute-done((bf16[512,128]{1,0:T(8,128)(2,1)}, bf16[512,128]{1,0:T(8,128)(2,1)S(1)}, u32[]{:S(2)}, u32[]{:S(2)}) %collective-permute-start.1) | collective-permute-done | bytes 131104 | tf_op jit(solution)/shard_map/ppermute | solution.py:805
  26.9 2.4 %conv_one.1 = (f32[512,128]{1,0:T(8,128)S(1)}, f32[8,128]{1,0:T(8,128)S(1)}, bf16[512,128]{1,0:T(8,128)(2,1)S(1)}) custom-call(s32[4]{0:T(128)S(1)} %copy-done.19, bf16[512,128]{1,0:T(8,128)(2,1)S(1)} %copy-done.2, bf16[512,128]{1,0:T(8,128)(2,1)S(1)} %collective-permute-done.a1, bf16[512,128]{1,0:T(8,128)(2,1)S(1)} %collective-permute-done.1.a2, ...), custom_call_target="tpu_custom_call" | custom-call | flops 99999997952 | bytes 1 | tf_op jit(solution)/shard_map/conv_one/pallas_call | solution.py:855
  29.3 2.7 %collective-permute-start.5 = (bf16[512,128]{1,0:T(8,128)(2,1)S(1)}, bf16[512,128]{1,0:T(8,128)(2,1)S(1)}, u32[]{:S(2)}, u32[]{:S(2)}) collective-permute-start(bf16[512,128]{1,0:T(8,128)(2,1)S(1)} %get-tuple-element.115.a0.refs_1_), channel_id=1, source_target_pairs={{0,3},{1,2},{2,1},{3,0},{4,7},{5,6},{6,5},{7,4},{8,11},{9,10},{10,... | collective-permute-start | bytes 393224 | tf_op jit(solution)/shard_map/ppermute | solution.py:805
  34.4 2.5 %collective-permute-start.14 = (bf16[4,64,640]{2,1,0:T(8,128)(2,1)S(1)}, bf16[4,64,640]{2,1,0:T(8,128)(2,1)S(1)}, u32[]{:S(2)}, u32[]{:S(2)}) collective-permute-start(bf16[4,64,640]{2,1,0:T(8,128)(2,1)S(1)} %pack_join.1.refs_0_), channel_id=1, source_target_pairs={{0,24},{4,28},{8,16},{12,20},{16,8},{20,12},{24,0},{28,4},{1,25},{... | collective-permute-start | bytes 983048 | tf_op jit(solution)/shard_map/ppermute | solution.py:805
  41.0 2.4 %conv_two.1 = (f32[512,128]{1,0:T(8,128)S(1)}, f32[8,128]{1,0:T(8,128)S(1)}, bf16[464,128]{1,0:T(8,128)(2,1)S(1)}, bf16[464,128]{1,0:T(8,128)(2,1)S(1)}, bf16[46...) custom-call(s32[4]{0:T(128)S(1)} %copy-done.19, bf16[512,128]{1,0:T(8,128)(2,1)S(1)} %get-tuple-element.115.a0.refs_1_, ...), custom_call_target="tpu_custom_call" | custom-call | flops 99999997952 | bytes 1 | tf_op jit(solution)/shard_map/conv_two/pallas_call | solution.py:855
  45.9 2.0 %collective-permute-start.8 = (bf16[464,128]{1,0:T(8,128)(2,1)S(1)}, bf16[464,128]{1,0:T(8,128)(2,1)S(1)}, u32[]{:S(2)}, u32[]{:S(2)}) collective-permute-start(bf16[464,128]{1,0:T(8,128)(2,1)S(1)} %get-tuple-element.120), channel_id=1, source_target_pairs={{0,3},{1,2},{2,1},{3,0},{4,7},{5,6},{6,5},{7,4},{8,11},{9,10},{10,... | collective-permute-start | bytes 356360 | tf_op jit(solution)/shard_map/ppermute | solution.py:805
  50.2 3.3 %collective-permute-done.7.n2 = bf16[464,128]{1,0:T(8,128)(2,1)S(1)} collective-permute-done((bf16[464,128]{1,0:T(8,128)(2,1)S(1)}, bf16[464,128]{1,0:T(8,128)(2,1)S(1)}, u32[]{:S(2)}, u32[]{:S(2)}) %collective-permute-start.7) | collective-permute-done | bytes 118816 | tf_op jit(solution)/shard_map/ppermute | solution.py:805
  55.1 3.1 %attention.1 = (f32[448,128]{1,0:T(8,128)S(1)}, bf16[448,128]{1,0:T(8,128)(2,1)S(1)}, bf16[448,128]{1,0:T(8,128)(2,1)S(1)}, bf16[448,128]{1,0:T(8,128)(2,1)S(1)}...) custom-call(s32[4]{0:T(128)S(1)} %copy-done.19, ...), custom_call_target="tpu_custom_call" | custom-call | flops 99999997952 | bytes 1 | tf_op jit(solution)/shard_map/attention/pallas_call | solution.py:25
  58.3 1.9 %attn_grad.1 = (bf16[4,64,640]{2,1,0:T(8,128)(2,1)S(1)}, bf16[4,64,640]{2,1,0:T(8,128)(2,1)S(1)}, bf16[4,64,640]{2,1,0:T(8,128)(2,1)S(1)}, bf16[4,64,640]{2,1,0:T(8,128)(2,1)S(1)}, bf16[4,4,64,640]{3,2,1,0:T(8,128)(2,1)S(1)}) custom-call(s32[4]{0:T(128)S(1)} %copy-done.19, bf16[256,512]{1,0:T(8,128)(2,1)S(1)} %get-tuple-element.121.norm_ref, ...), custom_call_target="tpu_custom_call" | custom-call | bytes 1 | tf_op jit(solution)/shard_map/attn_grad/pallas_call | solution.py:25
  60.2 1.9 %collective-permute-start.16 = (bf16[448,128]{1,0:T(8,128)(2,1)S(1)}, bf16[448,128]{1,0:T(8,128)(2,1)S(1)}, u32[]{:S(2)}, u32[]{:S(2)}) collective-permute-start(bf16[448,128]{1,0:T(8,128)(2,1)S(1)} %get-tuple-element.126), channel_id=1, source_target_pairs={{0,1},{1,0},{2,3},{3,2},{4,5},{5,4},{6,7},{7,6},{8,9},{9,8},{10,11... | collective-permute-start | bytes 344072 | tf_op jit(solution)/shard_map/ppermute | solution.py:805
  68.3 5.7 %collective-permute-done.17.p2 = bf16[448,128]{1,0:T(8,128)(2,1)S(1)} collective-permute-done((bf16[448,128]{1,0:T(8,128)(2,1)S(1)}, bf16[448,128]{1,0:T(8,128)(2,1)S(1)}, u32[]{:S(2)}, u32[]{:S(2)}) %collective-permute-start.17) | collective-permute-done | bytes 114720 | tf_op jit(solution)/shard_map/ppermute | solution.py:805
  74.0 3.0 %third_back.1 = (f32[512,128]{1,0:T(8,128)S(1)}, bf16[512,1152]{1,0:T(8,128)(2,1)S(1)}, f32[512,64]{1,0:T(8,128)}, f32[8,128]{1,0:T(8,128)S(1)}, f32[512,128]{1,...) custom-call(s32[4]{0:T(128)S(1)} %copy-done.19, ...), custom_call_target="tpu_custom_call" | custom-call | flops 99999997952 | bytes 1 | tf_op jit(solution)/shard_map/third_back/pallas_call | solution.py:855
  76.9 2.2 %collective-permute-start.20 = (bf16[512,128]{1,0:T(8,128)(2,1)S(1)}, bf16[512,128]{1,0:T(8,128)(2,1)S(1)}, u32[]{:S(2)}, u32[]{:S(2)}) collective-permute-start(bf16[512,128]{1,0:T(8,128)(2,1)S(1)} %get-tuple-element.147), channel_id=1, source_target_pairs={{0,1},{1,0},{2,3},{3,2},{4,5},{5,4},{6,7},{7,6},{8,9},{9,8},{10,11... | collective-permute-start | bytes 393224 | tf_op jit(solution)/shard_map/ppermute | solution.py:805
  82.6 2.0 %conv_two_grad.1 = (bf16[64,1408]{1,0:T(8,128)(2,1)S(1)}, bf16[64,1408]{1,0:T(8,128)(2,1)S(1)}, bf16[64,1408]{1,0:T(8,128)(2,1)S(1)}, bf16[64,1408]{1,0:T(8,128)...) custom-call(s32[4]{0:T(128)S(1)} %copy-done.19, bf16[512,128]{1,0:T(8,128)(2,1)S(1)} %copy-done.11, ...), custom_call_target="tpu_custom_call" | custom-call | bytes 1 | tf_op jit(solution)/shard_map/conv_two_grad/pallas_call | solution.py:25
  89.3 2.3 %collective-permute-done.21.p2 = bf16[512,128]{1,0:T(8,128)(2,1)S(1)} collective-permute-done((bf16[512,128]{1,0:T(8,128)(2,1)S(1)}, bf16[512,128]{1,0:T(8,128)(2,1)S(1)}, u32[]{:S(2)}, u32[]{:S(2)}) %collective-permute-start.21) | collective-permute-done | bytes 131104 | tf_op jit(solution)/shard_map/ppermute | solution.py:805
  91.7 2.4 %second_back.1 = (bf16[512,1152]{1,0:T(8,128)(2,1)S(1)}, f32[8,128]{1,0:T(8,128)S(1)}, f32[512,128]{1,0:T(8,128)S(1)}, bf16[512,128]{1,0:T(8,128)(2,1)S(1)}, bf1...) custom-call(s32[4]{0:T(128)S(1)} %copy-done.19, f32[512,128]{1,0:T(8,128)S(1)} %get-tuple-element.146.p0, ...), custom_call_target="tpu_custom_call" | custom-call | flops 99999997952 | bytes 1 | tf_op jit(solution)/shard_map/second_back/pallas_call | solution.py:855
  94.1 2.0 %collective-permute-start.27 = (bf16[512,128]{1,0:T(8,128)(2,1)S(1)}, bf16[512,128]{1,0:T(8,128)(2,1)S(1)}, u32[]{:S(2)}, u32[]{:S(2)}) collective-permute-start(bf16[512,128]{1,0:T(8,128)(2,1)S(1)} %get-tuple-element.171), channel_id=1, source_target_pairs={{0,1},{1,0},{2,3},{3,2},{4,5},{5,4},{6,7},{7,6},{8,9},{9,8},{10,11... | collective-permute-start | bytes 393224 | tf_op jit(solution)/shard_map/ppermute | solution.py:805
  101.1 2.0 %collective-permute-start.30 = (bf16[2,64,640]{2,1,0:T(8,128)(2,1)S(1)}, bf16[2,64,640]{2,1,0:T(8,128)(2,1)S(1)}, u32[]{:S(2)}, u32[]{:S(2)}) collective-permute-start(bf16[2,64,640]{2,1,0:T(8,128)(2,1)S(1)} %get-tuple-element.176), channel_id=1, source_target_pairs={{0,1},{1,0},{2,3},{3,2},{4,5},{5,4},{6,7},{7,6},{8,9},{9,8},{10,11... | collective-permute-start | bytes 491528 | tf_op jit(solution)/shard_map/ppermute | solution.py:805
  105.3 2.9 %collective-permute-done.31.p2 = bf16[512,128]{1,0:T(8,128)(2,1)S(1)} collective-permute-done((bf16[512,128]{1,0:T(8,128)(2,1)S(1)}, bf16[512,128]{1,0:T(8,128)(2,1)S(1)}, u32[]{:S(2)}, u32[]{:S(2)}) %collective-permute-start.31) | collective-permute-done | bytes 131104 | tf_op jit(solution)/shard_map/ppermute | solution.py:805
  114.8 2.4 %collective-permute-start.36 = (bf16[64,640]{1,0:T(8,128)(2,1)S(1)}, bf16[64,640]{1,0:T(8,128)(2,1)S(1)}, u32[]{:S(2)}, u32[]{:S(2)}) collective-permute-start(bf16[64,640]{1,0:T(8,128)(2,1)S(1)} %get-tuple-element.187), channel_id=1, source_target_pairs={{0,2},{1,3},{2,0},{3,1},{4,6},{5,7},{6,4},{7,5},{8,10},{9,11},{10,... | collective-permute-start | bytes 245768 | tf_op jit(solution)/shard_map/ppermute | solution.py:805
  117.2 2.4 %collective-permute-start.43 = (bf16[64,1408]{1,0:T(8,128)(2,1)S(1)}, bf16[64,1408]{1,0:T(8,128)(2,1)S(1)}, u32[]{:S(2)}, u32[]{:S(2)}) collective-permute-start(bf16[64,1408]{1,0:T(8,128)(2,1)S(1)} %get-tuple-element.190.refs_0_), channel_id=1, source_target_pairs={{0,24},{4,28},{8,16},{12,20},{16,8},{20,12},{24,0},{28,4},{1,25},{... | collective-permute-start | bytes 540680 | tf_op jit(solution)/shard_map/ppermute | solution.py:805
  123.2 2.2 %collective-permute-done.34.o2 = bf16[64,1152]{1,0:T(8,128)(2,1)S(1)} collective-permute-done((bf16[64,1152]{1,0:T(8,128)(2,1)S(1)}, bf16[64,1152]{1,0:T(8,128)(2,1)S(1)}, u32[]{:S(2)}, u32[]{:S(2)}) %collective-permute-start.34) | collective-permute-done | bytes 147488 | tf_op jit(solution)/shard_map/ppermute | solution.py:805
  130.0 3.0 %collective-permute-done.42.refs_2_ = bf16[64,1408]{1,0:T(8,128)(2,1)S(1)} collective-permute-done((bf16[64,1408]{1,0:T(8,128)(2,1)S(1)}, bf16[64,1408]{1,0:T(8,128)(2,1)S(1)}, u32[]{:S(2)}, u32[]{:S(2)}) %collective-permute-start.42) | collective-permute-done | bytes 180256 | tf_op jit(solution)/shard_map/ppermute | solution.py:805
  133.7 2.2 %collective-permute-done.39.refs_3_ = bf16[64,1920]{1,0:T(8,128)(2,1)S(1)} collective-permute-done((bf16[64,1920]{1,0:T(8,128)(2,1)S(1)}, bf16[64,1920]{1,0:T(8,128)(2,1)S(1)}, u32[]{:S(2)}, u32[]{:S(2)}) %collective-permute-start.39) | collective-permute-done | bytes 245792 | tf_op jit(solution)/shard_map/ppermute | solution.py:805
  135.9 3.7 %collective-permute-done.38.refs_2_ = bf16[64,1920]{1,0:T(8,128)(2,1)S(1)} collective-permute-done((bf16[64,1920]{1,0:T(8,128)(2,1)S(1)}, bf16[64,1920]{1,0:T(8,128)(2,1)S(1)}, u32[]{:S(2)}, u32[]{:S(2)}) %collective-permute-start.38) | collective-permute-done | bytes 245792 | tf_op jit(solution)/shard_map/ppermute | solution.py:805
  140.3 2.2 %finish_two.1 = (f32[2,9,512,128]{3,2,1,0:T(8,128)}, f32[64,1024]{1,0:T(8,128)}, f32[64,1024]{1,0:T(8,128)S(1)}) custom-call(s32[4]{0:T(128)S(1)} %copy-done.19, bf16[4,64,1408]{2,1,0:T(8,128)(2,1)S(1)} %stack_two.1.own_ref, bf16[4,64,1408]{2,1,0:T(8,128)(2,1)S(1)} %collective-permute-done.44.other_ref), custom_call_target="tpu_custom_call" | custom-call | flops 99999997952 | bytes 1 | tf_op jit(solution)/shard_map/finish_two/pallas_call | solution.py:855
  142.9 2.6 %finish_last.1 = (f32[2,9,512,128]{3,2,1,0:T(8,128)}, f32[3,128]{1,0:T(4,128)}, f32[3,128]{1,0:T(4,128)}, f32[2,128]{1,0:T(2,128)}, f32[1,64]{1,0:T(1,128)}, /*i...) custom-call(s32[4]{0:T(128)S(1)} %copy-done.19, ...), custom_call_target="tpu_custom_call", output_to_operand_aliasing={{0}: (5, {})} | custom-call | flops 99999997952 | bytes 1 | tf_op jit(solution)/shard_map/finish_last/pallas_call | solution.py:855
  (149 shorter events, 54.4 us)
Async XLA Ops:
  4.3 12.1 %collective-permute-start.2 = (bf16[512,128]{1,0:T(8,128)(2,1)}, bf16[512,128]{1,0:T(8,128)(2,1)S(1)}, u32[]{:S(2)}, u32[]{:S(2)}) collective-permute-start(bf16[512,128]{1,0:T(8,128)(2,1)} %get-tuple-element.111.a0), channel_id=1, source_target_pairs={{0,3},{1,2},{2,1},{3,0},{4,7},{5,6},{6,5},{7,4},{8,11},{9,10},{10,... | collective-permute-start | bytes 393224 | tf_op jit(solution)/shard_map/ppermute | solution.py:805
  9.4 15.8 %collective-permute-start.1 = (bf16[512,128]{1,0:T(8,128)(2,1)}, bf16[512,128]{1,0:T(8,128)(2,1)S(1)}, u32[]{:S(2)}, u32[]{:S(2)}) collective-permute-start(bf16[512,128]{1,0:T(8,128)(2,1)} %get-tuple-element.111.a0), channel_id=1, source_target_pairs={{0,2},{1,3},{2,0},{3,1},{4,6},{5,7},{6,4},{7,5},{8,10},{9,11},{10,... | collective-permute-start | bytes 393224 | tf_op jit(solution)/shard_map/ppermute | solution.py:805
  9.4 15.8 %collective-permute-start = (bf16[512,128]{1,0:T(8,128)(2,1)}, bf16[512,128]{1,0:T(8,128)(2,1)S(1)}, u32[]{:S(2)}, u32[]{:S(2)}) collective-permute-start(bf16[512,128]{1,0:T(8,128)(2,1)} %get-tuple-element.111.a0), channel_id=1, source_target_pairs={{0,1},{1,0},{2,3},{3,2},{4,5},{5,4},{6,7},{7,6},{8,9},{9,8},{10,11... | collective-permute-start | bytes 393224 | tf_op jit(solution)/shard_map/ppermute | solution.py:805
  10.1 22.0 %collective-permute-start.11 = (bf16[64,640]{1,0:T(8,128)(2,1)}, bf16[64,640]{1,0:T(8,128)(2,1)S(1)}, u32[]{:S(2)}, u32[]{:S(2)}) collective-permute-start(bf16[64,640]{1,0:T(8,128)(2,1)} %get-tuple-element.124.refs_0_), channel_id=1, source_target_pairs={{0,3},{1,2},{2,1},{3,0},{4,7},{5,6},{6,5},{7,4},{8,11},{9,10},{10,... | collective-permute-start | bytes 245768 | tf_op jit(solution)/shard_map/ppermute | solution.py:805
  13.8 20.0 %collective-permute-start.10 = (bf16[64,640]{1,0:T(8,128)(2,1)}, bf16[64,640]{1,0:T(8,128)(2,1)S(1)}, u32[]{:S(2)}, u32[]{:S(2)}) collective-permute-start(bf16[64,640]{1,0:T(8,128)(2,1)} %get-tuple-element.124.refs_0_), channel_id=1, source_target_pairs={{0,2},{1,3},{2,0},{3,1},{4,6},{5,7},{6,4},{7,5},{8,10},{9,11},{10,... | collective-permute-start | bytes 245768 | tf_op jit(solution)/shard_map/ppermute | solution.py:805
  16.5 17.3 %collective-permute-start.9 = (bf16[64,640]{1,0:T(8,128)(2,1)}, bf16[64,640]{1,0:T(8,128)(2,1)S(1)}, u32[]{:S(2)}, u32[]{:S(2)}) collective-permute-start(bf16[64,640]{1,0:T(8,128)(2,1)} %get-tuple-element.124.refs_0_), channel_id=1, source_target_pairs={{0,1},{1,0},{2,3},{3,2},{4,5},{5,4},{6,7},{7,6},{8,9},{9,8},{10,11... | collective-permute-start | bytes 245768 | tf_op jit(solution)/shard_map/ppermute | solution.py:805
  32.0 8.9 %collective-permute-start.4 = (bf16[512,128]{1,0:T(8,128)(2,1)S(1)}, bf16[512,128]{1,0:T(8,128)(2,1)S(1)}, u32[]{:S(2)}, u32[]{:S(2)}) collective-permute-start(bf16[512,128]{1,0:T(8,128)(2,1)S(1)} %get-tuple-element.115.a0.refs_1_), channel_id=1, source_target_pairs={{0,2},{1,3},{2,0},{3,1},{4,6},{5,7},{6,4},{7,5},{8,10},{9,11},{10,... | collective-permute-start | bytes 393224 | tf_op jit(solution)/shard_map/ppermute | solution.py:805
  34.4 11.5 %collective-permute-start.14 = (bf16[4,64,640]{2,1,0:T(8,128)(2,1)S(1)}, bf16[4,64,640]{2,1,0:T(8,128)(2,1)S(1)}, u32[]{:S(2)}, u32[]{:S(2)}) collective-permute-start(bf16[4,64,640]{2,1,0:T(8,128)(2,1)S(1)} %pack_join.1.refs_0_), channel_id=1, source_target_pairs={{0,24},{4,28},{8,16},{12,20},{16,8},{20,12},{24,0},{28,4},{1,25},{... | collective-permute-start | bytes 983048 | tf_op jit(solution)/shard_map/ppermute | solution.py:805
  36.9 12.4 %collective-permute-start.13 = (bf16[4,64,640]{2,1,0:T(8,128)(2,1)S(1)}, bf16[4,64,640]{2,1,0:T(8,128)(2,1)S(1)}, u32[]{:S(2)}, u32[]{:S(2)}) collective-permute-start(bf16[4,64,640]{2,1,0:T(8,128)(2,1)S(1)} %pack_join.1.refs_0_), channel_id=1, source_target_pairs={{0,16},{4,20},{8,24},{12,28},{16,0},{20,4},{24,8},{28,12},{1,17},{... | collective-permute-start | bytes 983048 | tf_op jit(solution)/shard_map/ppermute | solution.py:805
  37.6 11.8 %collective-permute-start.12 = (bf16[4,64,640]{2,1,0:T(8,128)(2,1)S(1)}, bf16[4,64,640]{2,1,0:T(8,128)(2,1)S(1)}, u32[]{:S(2)}, u32[]{:S(2)}) collective-permute-start(bf16[4,64,640]{2,1,0:T(8,128)(2,1)S(1)} %pack_join.1.refs_0_), channel_id=1, source_target_pairs={{0,8},{4,12},{8,0},{12,4},{16,24},{20,28},{24,16},{28,20},{1,9},{5... | collective-permute-start | bytes 983048 | tf_op jit(solution)/shard_map/ppermute | solution.py:805
  44.2 9.3 %collective-permute-start.7 = (bf16[464,128]{1,0:T(8,128)(2,1)S(1)}, bf16[464,128]{1,0:T(8,128)(2,1)S(1)}, u32[]{:S(2)}, u32[]{:S(2)}) collective-permute-start(bf16[464,128]{1,0:T(8,128)(2,1)S(1)} %get-tuple-element.119), channel_id=1, source_target_pairs={{0,2},{1,3},{2,0},{3,1},{4,6},{5,7},{6,4},{7,5},{8,10},{9,11},{10,... | collective-permute-start | bytes 356360 | tf_op jit(solution)/shard_map/ppermute | solution.py:805
  62.1 11.8 %collective-permute-start.17 = (bf16[448,128]{1,0:T(8,128)(2,1)S(1)}, bf16[448,128]{1,0:T(8,128)(2,1)S(1)}, u32[]{:S(2)}, u32[]{:S(2)}) collective-permute-start(bf16[448,128]{1,0:T(8,128)(2,1)S(1)} %get-tuple-element.127), channel_id=1, source_target_pairs={{0,2},{1,3},{2,0},{3,1},{4,6},{5,7},{6,4},{7,5},{8,10},{9,11},{10,... | collective-permute-start | bytes 344072 | tf_op jit(solution)/shard_map/ppermute | solution.py:805
  63.3 10.7 %collective-permute-start.18 = (bf16[448,128]{1,0:T(8,128)(2,1)S(1)}, bf16[448,128]{1,0:T(8,128)(2,1)S(1)}, u32[]{:S(2)}, u32[]{:S(2)}) collective-permute-start(bf16[448,128]{1,0:T(8,128)(2,1)S(1)} %get-tuple-element.128), channel_id=1, source_target_pairs={{0,3},{1,2},{2,1},{3,0},{4,7},{5,6},{6,5},{7,4},{8,11},{9,10},{10,... | collective-permute-start | bytes 344072 | tf_op jit(solution)/shard_map/ppermute | solution.py:805
  66.7 18.0 %collective-permute-start.23 = (bf16[2,4,64,640]{3,2,1,0:T(8,128)(2,1)S(1)}, bf16[2,4,64,640]{3,2,1,0:T(8,128)(2,1)S(1)}, u32[]{:S(2)}, u32[]{:S(2)}) collective-permute-start(bf16[2,4,64,640]{3,2,1,0:T(8,128)(2,1)S(1)} %get-tuple-element.152), channel_id=1, source_target_pairs={{0,8},{4,12},{8,0},{12,4},{16,24},{20,28},{24,16},{28,20},{1,9},{5... | collective-permute-start | bytes 1966088 | tf_op jit(solution)/shard_map/ppermute | solution.py:805
  76.9 12.3 %collective-permute-start.20 = (bf16[512,128]{1,0:T(8,128)(2,1)S(1)}, bf16[512,128]{1,0:T(8,128)(2,1)S(1)}, u32[]{:S(2)}, u32[]{:S(2)}) collective-permute-start(bf16[512,128]{1,0:T(8,128)(2,1)S(1)} %get-tuple-element.147), channel_id=1, source_target_pairs={{0,1},{1,0},{2,3},{3,2},{4,5},{5,4},{6,7},{7,6},{8,9},{9,8},{10,11... | collective-permute-start | bytes 393224 | tf_op jit(solution)/shard_map/ppermute | solution.py:805
  79.2 12.4 %collective-permute-start.21 = (bf16[512,128]{1,0:T(8,128)(2,1)S(1)}, bf16[512,128]{1,0:T(8,128)(2,1)S(1)}, u32[]{:S(2)}, u32[]{:S(2)}) collective-permute-start(bf16[512,128]{1,0:T(8,128)(2,1)S(1)} %get-tuple-element.148), channel_id=1, source_target_pairs={{0,2},{1,3},{2,0},{3,1},{4,6},{5,7},{6,4},{7,5},{8,10},{9,11},{10,... | collective-permute-start | bytes 393224 | tf_op jit(solution)/shard_map/ppermute | solution.py:805
  80.2 11.4 %collective-permute-start.22 = (bf16[512,128]{1,0:T(8,128)(2,1)S(1)}, bf16[512,128]{1,0:T(8,128)(2,1)S(1)}, u32[]{:S(2)}, u32[]{:S(2)}) collective-permute-start(bf16[512,128]{1,0:T(8,128)(2,1)S(1)} %get-tuple-element.149), channel_id=1, source_target_pairs={{0,3},{1,2},{2,1},{3,0},{4,7},{5,6},{6,5},{7,4},{8,11},{9,10},{10,... | collective-permute-start | bytes 393224 | tf_op jit(solution)/shard_map/ppermute | solution.py:805
  85.4 15.1 %collective-permute-start.29 = (bf16[4,64,640]{2,1,0:T(8,128)(2,1)S(1)}, bf16[4,64,640]{2,1,0:T(8,128)(2,1)S(1)}, u32[]{:S(2)}, u32[]{:S(2)}) collective-permute-start(bf16[4,64,640]{2,1,0:T(8,128)(2,1)S(1)} %get-tuple-element.174), channel_id=1, source_target_pairs={{0,16},{4,20},{8,24},{12,28},{16,0},{20,4},{24,8},{28,12},{1,17},{... | collective-permute-start | bytes 983048 | tf_op jit(solution)/shard_map/ppermute | solution.py:805
  87.7 15.4 %collective-permute-start.26 = (bf16[2,64,1408]{2,1,0:T(8,128)(2,1)S(1)}, bf16[2,64,1408]{2,1,0:T(8,128)(2,1)S(1)}, u32[]{:S(2)}, u32[]{:S(2)}) collective-permute-start(bf16[2,64,1408]{2,1,0:T(8,128)(2,1)S(1)} %get-tuple-element.170), channel_id=1, source_target_pairs={{0,8},{4,12},{8,0},{12,4},{16,24},{20,28},{24,16},{28,20},{1,9},{5... | collective-permute-start | bytes 1081352 | tf_op jit(solution)/shard_map/ppermute | solution.py:805
  96.1 12.2 %collective-permute-start.31 = (bf16[512,128]{1,0:T(8,128)(2,1)S(1)}, bf16[512,128]{1,0:T(8,128)(2,1)S(1)}, u32[]{:S(2)}, u32[]{:S(2)}) collective-permute-start(bf16[512,128]{1,0:T(8,128)(2,1)S(1)} %get-tuple-element.178), channel_id=1, source_target_pairs={{0,2},{1,3},{2,0},{3,1},{4,6},{5,7},{6,4},{7,5},{8,10},{9,11},{10,... | collective-permute-start | bytes 393224 | tf_op jit(solution)/shard_map/ppermute | solution.py:805
  97.2 11.1 %collective-permute-start.32 = (bf16[512,128]{1,0:T(8,128)(2,1)S(1)}, bf16[512,128]{1,0:T(8,128)(2,1)S(1)}, u32[]{:S(2)}, u32[]{:S(2)}) collective-permute-start(bf16[512,128]{1,0:T(8,128)(2,1)S(1)} %get-tuple-element.179), channel_id=1, source_target_pairs={{0,3},{1,2},{2,1},{3,0},{4,7},{5,6},{6,5},{7,4},{8,11},{9,10},{10,... | collective-permute-start | bytes 393224 | tf_op jit(solution)/shard_map/ppermute | solution.py:805
  100.5 10.0 %collective-permute-start.25 = (bf16[4,64,1152]{2,1,0:T(8,128)(2,1)S(1)}, bf16[4,64,1152]{2,1,0:T(8,128)(2,1)S(1)}, u32[]{:S(2)}, u32[]{:S(2)}) collective-permute-start(bf16[4,64,1152]{2,1,0:T(8,128)(2,1)S(1)} %get-tuple-element.169), channel_id=1, source_target_pairs={{0,4},{4,0},{8,12},{12,8},{16,20},{20,16},{24,28},{28,24},{1,5},{5... | collective-permute-start | bytes 1769480 | tf_op jit(solution)/shard_map/ppermute | solution.py:805
  101.1 9.3 %collective-permute-start.30 = (bf16[2,64,640]{2,1,0:T(8,128)(2,1)S(1)}, bf16[2,64,640]{2,1,0:T(8,128)(2,1)S(1)}, u32[]{:S(2)}, u32[]{:S(2)}) collective-permute-start(bf16[2,64,640]{2,1,0:T(8,128)(2,1)S(1)} %get-tuple-element.176), channel_id=1, source_target_pairs={{0,1},{1,0},{2,3},{3,2},{4,5},{5,4},{6,7},{7,6},{8,9},{9,8},{10,11... | collective-permute-start | bytes 491528 | tf_op jit(solution)/shard_map/ppermute | solution.py:805
  111.3 10.4 %collective-permute-start.33 = (bf16[64,1152]{1,0:T(8,128)(2,1)S(1)}, bf16[64,1152]{1,0:T(8,128)(2,1)S(1)}, u32[]{:S(2)}, u32[]{:S(2)}) collective-permute-start(bf16[64,1152]{1,0:T(8,128)(2,1)S(1)} %get-tuple-element.183), channel_id=1, source_target_pairs={{0,8},{4,12},{8,0},{12,4},{16,24},{20,28},{24,16},{28,20},{1,9},{5... | collective-permute-start | bytes 442376 | tf_op jit(solution)/shard_map/ppermute | solution.py:805
  112.8 12.5 %collective-permute-start.34 = (bf16[64,1152]{1,0:T(8,128)(2,1)S(1)}, bf16[64,1152]{1,0:T(8,128)(2,1)S(1)}, u32[]{:S(2)}, u32[]{:S(2)}) collective-permute-start(bf16[64,1152]{1,0:T(8,128)(2,1)S(1)} %get-tuple-element.184), channel_id=1, source_target_pairs={{0,16},{4,20},{8,24},{12,28},{16,0},{20,4},{24,8},{28,12},{1,17},{... | collective-permute-start | bytes 442376 | tf_op jit(solution)/shard_map/ppermute | solution.py:805
  114.3 11.0 %collective-permute-start.35 = (bf16[64,1152]{1,0:T(8,128)(2,1)S(1)}, bf16[64,1152]{1,0:T(8,128)(2,1)S(1)}, u32[]{:S(2)}, u32[]{:S(2)}) collective-permute-start(bf16[64,1152]{1,0:T(8,128)(2,1)S(1)} %get-tuple-element.185), channel_id=1, source_target_pairs={{0,24},{4,28},{8,16},{12,20},{16,8},{20,12},{24,0},{28,4},{1,25},{... | collective-permute-start | bytes 442376 | tf_op jit(solution)/shard_map/ppermute | solution.py:805
  117.2 11.5 %collective-permute-start.43 = (bf16[64,1408]{1,0:T(8,128)(2,1)S(1)}, bf16[64,1408]{1,0:T(8,128)(2,1)S(1)}, u32[]{:S(2)}, u32[]{:S(2)}) collective-permute-start(bf16[64,1408]{1,0:T(8,128)(2,1)S(1)} %get-tuple-element.190.refs_0_), channel_id=1, source_target_pairs={{0,24},{4,28},{8,16},{12,20},{16,8},{20,12},{24,0},{28,4},{1,25},{... | collective-permute-start | bytes 540680 | tf_op jit(solution)/shard_map/ppermute | solution.py:805
  120.2 12.8 %collective-permute-start.42 = (bf16[64,1408]{1,0:T(8,128)(2,1)S(1)}, bf16[64,1408]{1,0:T(8,128)(2,1)S(1)}, u32[]{:S(2)}, u32[]{:S(2)}) collective-permute-start(bf16[64,1408]{1,0:T(8,128)(2,1)S(1)} %get-tuple-element.190.refs_0_), channel_id=1, source_target_pairs={{0,16},{4,20},{8,24},{12,28},{16,0},{20,4},{24,8},{28,12},{1,17},{... | collective-permute-start | bytes 540680 | tf_op jit(solution)/shard_map/ppermute | solution.py:805
  121.7 11.3 %collective-permute-start.41 = (bf16[64,1408]{1,0:T(8,128)(2,1)S(1)}, bf16[64,1408]{1,0:T(8,128)(2,1)S(1)}, u32[]{:S(2)}, u32[]{:S(2)}) collective-permute-start(bf16[64,1408]{1,0:T(8,128)(2,1)S(1)} %get-tuple-element.190.refs_0_), channel_id=1, source_target_pairs={{0,8},{4,12},{8,0},{12,4},{16,24},{20,28},{24,16},{28,20},{1,9},{5... | collective-permute-start | bytes 540680 | tf_op jit(solution)/shard_map/ppermute | solution.py:805
  126.0 9.9 %collective-permute-start.39 = (bf16[64,1920]{1,0:T(8,128)(2,1)S(1)}, bf16[64,1920]{1,0:T(8,128)(2,1)S(1)}, u32[]{:S(2)}, u32[]{:S(2)}) collective-permute-start(bf16[64,1920]{1,0:T(8,128)(2,1)S(1)} %last.1.refs_0_.refs_4_), channel_id=1, source_target_pairs={{0,24},{4,28},{8,16},{12,20},{16,8},{20,12},{24,0},{28,4},{1,25},{... | collective-permute-start | bytes 737288 | tf_op jit(solution)/shard_map/ppermute | solution.py:805
  126.8 12.8 %collective-permute-start.38 = (bf16[64,1920]{1,0:T(8,128)(2,1)S(1)}, bf16[64,1920]{1,0:T(8,128)(2,1)S(1)}, u32[]{:S(2)}, u32[]{:S(2)}) collective-permute-start(bf16[64,1920]{1,0:T(8,128)(2,1)S(1)} %last.1.refs_0_.refs_4_), channel_id=1, source_target_pairs={{0,16},{4,20},{8,24},{12,28},{16,0},{20,4},{24,8},{28,12},{1,17},{... | collective-permute-start | bytes 737288 | tf_op jit(solution)/shard_map/ppermute | solution.py:805
  128.6 11.0 %collective-permute-start.37 = (bf16[64,1920]{1,0:T(8,128)(2,1)S(1)}, bf16[64,1920]{1,0:T(8,128)(2,1)S(1)}, u32[]{:S(2)}, u32[]{:S(2)}) collective-permute-start(bf16[64,1920]{1,0:T(8,128)(2,1)S(1)} %last.1.refs_0_.refs_4_), channel_id=1, source_target_pairs={{0,8},{4,12},{8,0},{12,4},{16,24},{20,28},{24,16},{28,20},{1,9},{5... | collective-permute-start | bytes 737288 | tf_op jit(solution)/shard_map/ppermute | solution.py:805
  (45 other events, 331.3 us)

commit v3 on v2

--- a/solution.py
+++ b/solution.py
@@ -155,12 +155,16 @@
     height = full.shape[0]
     inner, outer = column_masks(height)
     blocks = [pl.ds(pl.multiple_of((z ^ k) * 128, 128), 128) for k in range(4)]
+    weights = lanes(
+        [rows_of([w_ref[0, tap, block, :] for block in blocks]) for tap in range(9)]
+    )
+    every = dot(full, weights)
     sums = []
     for col_tap in range(3):
         total = None
         for row_tap in range(3):
             tap = 3 * row_tap + col_tap
-            part = dot(full, rows_of([w_ref[0, tap, block, :] for block in blocks]))
+            part = every[:, 128 * tap : 128 * tap + 128]
             if row_tap == 0:
                 part = earlier_rows(part)
             elif row_tap == 2:
@@ -543,10 +547,13 @@
 def send_taps(gradient, w_ref, z, taps_ref, piece_refs):
     taps = spread_taps(gradient)
     taps_ref[...] = taps
+    rows = []
+    for k in range(4):
+        block = pl.ds(pl.multiple_of((z ^ k) * 128, 128), 128)
+        rows.append(lanes([w_ref[0, tap, block, :] for tap in range(9)]))
+    every = dot_nt(taps, rows_of(rows))
     for k, ref in enumerate(piece_refs):
-        block = pl.ds(pl.multiple_of((z ^ k) * 128, 128), 128)
-        weights = lanes([w_ref[0, tap, block, :] for tap in range(9)])
-        ref[...] = dot_nt(taps, weights).astype(ref.dtype)
+        ref[...] = every[:, 128 * k : 128 * k + 128].astype(ref.dtype)
 
 
 def swish_back(gradient, normed, gain, shift):
@@ -686,7 +693,7 @@
     proj,
 ):
     extra_sum = jnp.zeros((16, 128), F32)
-    total = jnp.zeros((16, 128), F32)
+    total = jnp.zeros((9, 128), F32)
     for part in range(PARTS):
         source = (own_ref if part % 2 == 0 else other_ref).at[part // 2]
         place = scalars[1] ^ part
@@ -705,8 +712,9 @@
                 16.0 * extra[1:2, 64:] + extra[3:4, 64:],
             ]
         )
-        both = source[0:32, 1792:1920].astype(F32)
-        total = total + (both[0:16] + both[16:32])
+        both = source[16:64, 1728:1792].astype(F32)
+        both = both[0:18] + both[18:36]
+        total = total + lanes([both[0:9], both[9:18]])
     for index, row in enumerate((0, 2, 5)):
         gain_ref[index : index + 1] = total[row : row + 1]
         shift_ref[index : index + 1] = total[row + 1 : row + 2]
@@ -751,31 +759,18 @@
         (send_ref if k % 2 else keep_ref)[k // 2] = plus(a0[k], a1[k])
 
 
-def tail_first_kernel(
-    scalars,
-    k0,
-    k1,
-    k2,
-    k3,
-    one_get,
-    two_own,
-    two_get,
-    att_keep,
-    att_get,
-    _,
-    o0,
-    o1,
-    o2,
-    o3,
-    two_ref,
-    att_own,
-    att_send,
-):
-    for i, (ref, out) in enumerate(((k0, o0), (k1, o1), (k2, o2), (k3, o3))):
-        out[...] = plus(ref[...], one_get[i])
-    two_ref[...] = plus(two_own[...], two_get[...])
-    att_own[...] = plus(att_keep[0], att_get[0])
-    att_send[...] = plus(att_keep[1], att_get[1])
+def pass_kernel(scalars, a0, a1, a2, _, b0, b1, b2):
+    for source, target in ((a0, b0), (a1, b1), (a2, b2)):
+        target[...] = source[...]
+
+
+def add_kernel(scalars, k0, k1, k2, k3, get_ref, _, *sum_refs):
+    for i, ref in enumerate((k0, k1, k2, k3)):
+        sum_refs[i][...] = plus(ref[...], get_ref[i])
+
+
+def two_sum_kernel(scalars, a0, a1, _, sum_ref):
+    sum_ref[...] = plus(a0[...], a1[...])
 
 
 def last_kernel(
@@ -785,13 +780,18 @@
     for ref in (o1, o2, o3):
         total = total + ref[...].astype(F32)
     last_ref[:, 0:WIDE] = total.astype(BF)
-    last_ref[:, 1152:1792] = plus(att_own[...], att_get[...])
+    last_ref[:, 1152:1664] = plus(att_own[:, 0:512], att_get[:, 0:512])
     rows = [small_one[0:1], small_one[1:2]]
     rows += [small_two[m : m + 1] for m in range(3)]
     rows += [small_three[m : m + 1] for m in range(3)]
     rows += [commit[0:1]]
     high, low = split_low(pack_rows(rows, 16))
-    last_ref[:, 1792:1920] = rows_of([high, low, jnp.zeros((32, 128), F32)]).astype(BF)
+    blank = jnp.zeros((48, 64), F32)
+    small = rows_of([high[:9, :64], high[:9, 64:], low[:9, :64], low[:9, 64:], jnp.zeros((12, 64), F32)])
+    small = lanes([blank, small])
+    block = att_own[:, 512:640].astype(F32) + att_get[:, 512:640].astype(F32)
+    last_ref[0:16, 1664:1792] = block[0:16].astype(BF)
+    last_ref[16:64, 1664:1792] = (block[16:64] + small).astype(BF)
 
 
 def stack_kernel(scalars, *refs):
@@ -1107,7 +1107,6 @@
         two_kept if by_hand else sums,
         conv_w,
     )
-    back_one = [pays[0]] + [over("chan", pays[k], k) for k in (1, 2, 3)]
     *one_keep, one_send = call(
         conv_one_grad_kernel,
         [sds((64, WIDE), BF)] * 4 + [sds((4, 64, WIDE), BF)],
@@ -1117,27 +1116,58 @@
         scratch=[pltpu.VMEM((C, WIDE), BF)],
         name="conv_one_grad",
     )
+    one_got = over("dp", one_send, 1) if by_hand else one_send
+    pays[1:] = call(
+        pass_kernel,
+        [sds((tokens, 128), BF)] * 3,
+        scalars,
+        *pays[1:],
+        one_keep[0],
+        flops=HEAVY,
+        name="pass_on",
+    )
+    back_one = [pays[0]] + [over("chan", pays[k], k) for k in (1, 2, 3)]
     if by_hand:
+        att_kept, att_sent = call(
+            attn_sum_kernel,
+            [sds((2, 64, 640), BF)] * 2,
+            scalars,
+            att_own,
+            att_got,
+            small_two,
+            name="attn_sum",
+        )
+        att_got = over("chan", att_sent, 1)
         two_own, two_sent = call(
             half_add_kernel,
             [sds((64, 1408), BF)] * 2,
             scalars,
             two_kept,
             two_got,
-            back_one[1],
+            att_kept,
             name="conv_two_half",
         )
         two_got = over("dp", two_sent, 4)
-        att_kept, att_sent = call(
-            attn_sum_kernel,
-            [sds((2, 64, 640), BF)] * 2,
+        one_parts = call(
+            add_kernel,
+            [sds((64, WIDE), BF)] * 4,
             scalars,
-            att_own,
+            *one_keep,
+            one_got,
+            att_kept,
+            name="conv_one_add",
+        )
+        one_parts = [one_parts[0]] + [over("dp", one_parts[i], 2 * i) for i in (1, 2, 3)]
+        att_own, att_sent = call(
+            half_add_kernel,
+            [sds((64, 640), BF)] * 2,
+            scalars,
+            att_kept,
             att_got,
-            back_one[1],
-            name="attn_sum",
+            two_own,
+            name="attn_last",
         )
-        att_got = over("chan", att_sent, 1)
+        att_got = over("chan", att_sent, 2)
     grad_latents, small_one = call(
         first_back_kernel,
         [sds((tokens, 128), F32), sds((8, 128), F32)],
@@ -1147,38 +1177,30 @@
         stats_one,
         params,
         residual_grad,
-        one_keep[0],
+        one_parts[0] if by_hand else sums,
         two_own if by_hand else sums,
-        att_kept if by_hand else sums,
+        att_own if by_hand else sums,
         flops=HEAVY,
         name="first_back",
     )
 
     if by_hand:
-        o0, o1, o2, o3, two, att_own, att_sent = call(
-            tail_first_kernel,
-            [sds((64, WIDE), BF)] * 4 + [sds((64, 1408), BF)] + [sds((64, 640), BF)] * 2,
+        two = call(
+            two_sum_kernel,
+            [sds((64, 1408), BF)],
             scalars,
-            *one_keep,
-            over("dp", one_send, 1),
             two_own,
             two_got,
-            att_kept,
-            att_got,
             small_one,
-            flops=HEAVY,
-            name="tail_first",
-        )
+            name="conv_two_sum",
+        )[0]
         last = call(
             last_kernel,
-            [sds((64, 1920), BF)],
+            [sds((64, 1792), BF)],
             scalars,
-            o0,
-            over("dp", o1, 2),
-            over("dp", o2, 4),
-            over("dp", o3, 6),
+            *one_parts,
             att_own,
-            over("chan", att_sent, 2),
+            att_got,
             small_one,
             small_two,
             small_three,
@@ -1207,11 +1229,12 @@
         small = jnp.concatenate([small_one[0:2], small_two[0:3], small_three[0:3], commit[0:1]])
         small = jnp.concatenate([lax.psum(small, "dp"), jnp.zeros((7, 128), F32)])
         high = lax.reduce_precision(small, 8, 7)
-        smalls = jnp.concatenate([high, small - high, jnp.zeros((32, 128), F32)]).astype(BF)
-        smalls = jnp.zeros((2, 4, 64, 128), BF).at[0, 0].set(smalls)
+        halves = [v[:9, c : c + 64] for v in (high, small - high) for c in (0, 64)]
+        smalls = jnp.concatenate(halves + [jnp.zeros((12, 64), F32)]).astype(BF)
+        att_sum = att_sum.at[0, 0, 16:64, 576:640].add(smalls)
         two_own, two_other = total(two_keep, two_send)
         one_sum = total(one_keep, one_send)
-        last_own, last_other = jnp.concatenate([one_sum, att_sum, smalls], axis=3)
+        last_own, last_other = jnp.concatenate([one_sum, att_sum], axis=3)
 
     conv_held, book_grad, picked = blocks_call(
         finish_two_kernel,
@@ -1259,7 +1282,7 @@
         proj_bias_grad,
     ) = blocks_call(
         finish_last,
-        [whole((4, 64, 1920)), whole((4, 64, 1920)), whole((64, CODES)), whole((64, CODES))]
+        [whole((4, 64, 1792)), whole((4, 64, 1792)), whole((64, CODES)), whole((64, CODES))]
         + [pl.BlockSpec(memory_space=pl.ANY)],
         [pl.BlockSpec((1, 9, C, 128), lambda i: (0, 0, 0, 0))] + [whole(o.shape) for o in outs[1:]],
         outs,

time: 146 us -> 143 us (0.979)
  starting transfers between devices: 63.7 us -> 59.1 us
    ppermute x45, starting transfers between devices: 63.7 us -> 59.1 us  [over(): return lax.ppermute(array, axis, [(i, i ^ flip) for i in range(size)])]
    pallas_call x20 -> x23, Pallas kernels: 24.1 us -> 26.8 us  [call(): pl.pallas_call(body, out_shape=list(outs), in_specs=[pl.BlockSpec(memory_...]
    pallas_call x6, Pallas kernels: 14.9 us -> 12.9 us  [blocks_call(): pl.pallas_call(body, grid=(1,), out_shape=outs, in_specs=[pl.BlockSpec(me...]
    unnamed x64 -> x68, local copies, waits for them, and re-layouts: 3.44 us -> 3.44 us
  transfers between devices with their start and end apart: 45 -> 45, of which waited for: 19 -> 18; matrix products, arithmetic and copies ran while one was open for 0% -> 0% of each run, Pallas kernels for 18% -> 20%
where the time goes in v3:
time: 143 us; the launch traced here: 142 us
  starting transfers between devices  59.1 us (41%)
  Pallas kernels  39.6 us (28%)
  waiting for transfers between devices  38.1 us (27%)
  local copies, waits for them, and re-layouts  3.44 us (2%)
    ppermute x45, starting transfers between devices, over(): return lax.ppermute(array, axis, [(i, i ^ flip) for i in range(size)])  59.1 us
    ppermute x45, waiting for transfers between devices, over(): return lax.ppermute(array, axis, [(i, i ^ flip) for i in range(size)])  38.1 us
    pallas_call x23, Pallas kernels, call(): pl.pallas_call(body, out_shape=list(outs), in_specs=[pl.BlockSpec(memory_...  26.8 us
    pallas_call x6, Pallas kernels, blocks_call(): pl.pallas_call(body, grid=(1,), out_shape=outs, in_specs=[pl.BlockSpec(me...  12.9 us
    unnamed x68, local copies, waits for them, and re-layouts  3.44 us
  transfers between devices with their start and end apart: 45, of which 18 were waited for; matrix products, arithmetic and copies ran while one was open for 0% of the time, Pallas kernels for 20%

profile of v3, /device:TPU:0, one launch (start us, length us, event | category | flops | bytes accessed | tf_op | source)
XLA Modules:
  0.0 142.3 jit_solution(17673572345254862355)
XLA Ops:
  1.3 3.0 %begin.1 = (bf16[512,128]{1,0:T(8,128)(2,1)}, f32[8,128]{1,0:T(8,128)}, bf16[64,640]{1,0:T(8,128)(2,1)}, f32[16,128]{1,0:T(8,128)}) custom-call(s32[4]{0:T(128)} %pad_add_fusion.scalars.refs_0_, bf16[512,128]{1,0:T(8,128)(2,1)} %bitcast.27, f32[3,128]{1,0:T(4,128)} %gain_any.1, f32[3,128]{1,0:T(4,128)} %shift_any.1, f32[2,128]{1,0:T(2,128)} %conv_b_any.1, ...), custom_call_target="tpu_custom_call" | custom-call | flops 99999997952 | bytes 1 | tf_op jit(solution)/shard_map/begin/pallas_call | solution.py:25
  4.3 5.1 %collective-permute-start.2 = (bf16[512,128]{1,0:T(8,128)(2,1)}, bf16[512,128]{1,0:T(8,128)(2,1)S(1)}, u32[]{:S(2)}, u32[]{:S(2)}) collective-permute-start(bf16[512,128]{1,0:T(8,128)(2,1)} %get-tuple-element.113.a0), channel_id=1, source_target_pairs={{0,3},{1,2},{2,1},{3,0},{4,7},{5,6},{6,5},{7,4},{8,11},{9,10},{10,... | collective-permute-start | bytes 393224 | tf_op jit(solution)/shard_map/ppermute | solution.py:805
  10.1 3.7 %collective-permute-start.11 = (bf16[64,640]{1,0:T(8,128)(2,1)}, bf16[64,640]{1,0:T(8,128)(2,1)S(1)}, u32[]{:S(2)}, u32[]{:S(2)}) collective-permute-start(bf16[64,640]{1,0:T(8,128)(2,1)} %get-tuple-element.126.refs_0_), channel_id=1, source_target_pairs={{0,3},{1,2},{2,1},{3,0},{4,7},{5,6},{6,5},{7,4},{8,11},{9,10},{10,... | collective-permute-start | bytes 245768 | tf_op jit(solution)/shard_map/ppermute | solution.py:805
  14.5 1.9 %start.1 = (bf16[512,1024]{1,0:T(8,128)(2,1)S(1)}, f32[512,64]{1,0:T(8,128)S(1)}, f32[8,128]{1,0:T(8,128)S(1)}, bf16[4,64,128]{2,1,0:T(8,128)(2,1)S(1)}) custom-call(s32[4]{0:T(128)S(1)} %copy-done.19, s32[2,16,16]{2,1,0:T(8,128)S(1)} %copy-done.20, f32[64,1024]{1,0:T(8,128)S(1)} %bitcast.18, bf16[512,64]{1,0:T(8,128)(2,1)S(1)} %bitcast.21, ...), custom_call_target="tpu_custom_call" | custom-call | bytes 1 | tf_op jit(solution)/shard_map/start/pallas_call | solution.py:25
  16.4 3.8 %collective-permute-start.9 = (bf16[64,640]{1,0:T(8,128)(2,1)}, bf16[64,640]{1,0:T(8,128)(2,1)S(1)}, u32[]{:S(2)}, u32[]{:S(2)}) collective-permute-start(bf16[64,640]{1,0:T(8,128)(2,1)} %get-tuple-element.126.refs_0_), channel_id=1, source_target_pairs={{0,1},{1,0},{2,3},{3,2},{4,5},{5,4},{6,7},{7,6},{8,9},{9,8},{10,11... | collective-permute-start | bytes 245768 | tf_op jit(solution)/shard_map/ppermute | solution.py:805
  20.3 4.9 %collective-permute-done.1.a2 = bf16[512,128]{1,0:T(8,128)(2,1)S(1)} collective-permute-done((bf16[512,128]{1,0:T(8,128)(2,1)}, bf16[512,128]{1,0:T(8,128)(2,1)S(1)}, u32[]{:S(2)}, u32[]{:S(2)}) %collective-permute-start.1) | collective-permute-done | bytes 131104 | tf_op jit(solution)/shard_map/ppermute | solution.py:805
  26.9 1.8 %conv_one.1 = (f32[512,128]{1,0:T(8,128)S(1)}, f32[8,128]{1,0:T(8,128)S(1)}, bf16[512,128]{1,0:T(8,128)(2,1)S(1)}) custom-call(s32[4]{0:T(128)S(1)} %copy-done.19, bf16[512,128]{1,0:T(8,128)(2,1)S(1)} %copy-done.2, bf16[512,128]{1,0:T(8,128)(2,1)S(1)} %collective-permute-done.a1, bf16[512,128]{1,0:T(8,128)(2,1)S(1)} %collective-permute-done.1.a2, ...), custom_call_target="tpu_custom_call" | custom-call | flops 99999997952 | bytes 1 | tf_op jit(solution)/shard_map/conv_one/pallas_call | solution.py:855
  28.8 2.7 %collective-permute-start.5 = (bf16[512,128]{1,0:T(8,128)(2,1)S(1)}, bf16[512,128]{1,0:T(8,128)(2,1)S(1)}, u32[]{:S(2)}, u32[]{:S(2)}) collective-permute-start(bf16[512,128]{1,0:T(8,128)(2,1)S(1)} %get-tuple-element.117.a0.refs_1_), channel_id=1, source_target_pairs={{0,3},{1,2},{2,1},{3,0},{4,7},{5,6},{6,5},{7,4},{8,11},{9,10},{10,... | collective-permute-start | bytes 393224 | tf_op jit(solution)/shard_map/ppermute | solution.py:805
  33.8 2.5 %collective-permute-start.14 = (bf16[4,64,640]{2,1,0:T(8,128)(2,1)S(1)}, bf16[4,64,640]{2,1,0:T(8,128)(2,1)S(1)}, u32[]{:S(2)}, u32[]{:S(2)}) collective-permute-start(bf16[4,64,640]{2,1,0:T(8,128)(2,1)S(1)} %pack_join.1.refs_0_), channel_id=1, source_target_pairs={{0,24},{4,28},{8,16},{12,20},{16,8},{20,12},{24,0},{28,4},{1,25},{... | collective-permute-start | bytes 983048 | tf_op jit(solution)/shard_map/ppermute | solution.py:805
  38.6 1.9 %collective-permute-done.4.a2.refs_3_ = bf16[512,128]{1,0:T(8,128)(2,1)S(1)} collective-permute-done((bf16[512,128]{1,0:T(8,128)(2,1)S(1)}, bf16[512,128]{1,0:T(8,128)(2,1)S(1)}, u32[]{:S(2)}, u32[]{:S(2)}) %collective-permute-start.4) | collective-permute-done | bytes 131104 | tf_op jit(solution)/shard_map/ppermute | solution.py:805
  40.5 1.9 %conv_two.1 = (f32[512,128]{1,0:T(8,128)S(1)}, f32[8,128]{1,0:T(8,128)S(1)}, bf16[464,128]{1,0:T(8,128)(2,1)S(1)}, bf16[464,128]{1,0:T(8,128)(2,1)S(1)}, bf16[46...) custom-call(s32[4]{0:T(128)S(1)} %copy-done.19, bf16[512,128]{1,0:T(8,128)(2,1)S(1)} %get-tuple-element.117.a0.refs_1_, ...), custom_call_target="tpu_custom_call" | custom-call | flops 99999997952 | bytes 1 | tf_op jit(solution)/shard_map/conv_two/pallas_call | solution.py:855
  46.8 2.0 %collective-permute-done.13.refs_2_ = bf16[4,64,640]{2,1,0:T(8,128)(2,1)S(1)} collective-permute-done((bf16[4,64,640]{2,1,0:T(8,128)(2,1)S(1)}, bf16[4,64,640]{2,1,0:T(8,128)(2,1)S(1)}, u32[]{:S(2)}, u32[]{:S(2)}) %collective-permute-start.13) | collective-permute-done | bytes 327712 | tf_op jit(solution)/shard_map/ppermute | solution.py:805
  49.6 2.8 %collective-permute-done.7.n2 = bf16[464,128]{1,0:T(8,128)(2,1)S(1)} collective-permute-done((bf16[464,128]{1,0:T(8,128)(2,1)S(1)}, bf16[464,128]{1,0:T(8,128)(2,1)S(1)}, u32[]{:S(2)}, u32[]{:S(2)}) %collective-permute-start.7) | collective-permute-done | bytes 118816 | tf_op jit(solution)/shard_map/ppermute | solution.py:805
  54.0 3.2 %attention.1 = (f32[448,128]{1,0:T(8,128)S(1)}, bf16[448,128]{1,0:T(8,128)(2,1)S(1)}, bf16[448,128]{1,0:T(8,128)(2,1)S(1)}, bf16[448,128]{1,0:T(8,128)(2,1)S(1)}...) custom-call(s32[4]{0:T(128)S(1)} %copy-done.19, ...), custom_call_target="tpu_custom_call" | custom-call | flops 99999997952 | bytes 1 | tf_op jit(solution)/shard_map/attention/pallas_call | solution.py:25
  57.2 1.9 %attn_grad.1 = (bf16[4,64,640]{2,1,0:T(8,128)(2,1)S(1)}, bf16[4,64,640]{2,1,0:T(8,128)(2,1)S(1)}, bf16[4,64,640]{2,1,0:T(8,128)(2,1)S(1)}, bf16[4,64,640]{2,1,0:T(8,128)(2,1)S(1)}, bf16[4,4,64,640]{3,2,1,0:T(8,128)(2,1)S(1)}) custom-call(s32[4]{0:T(128)S(1)} %copy-done.19, bf16[256,512]{1,0:T(8,128)(2,1)S(1)} %get-tuple-element.123.norm_ref, ...), custom_call_target="tpu_custom_call" | custom-call | bytes 1 | tf_op jit(solution)/shard_map/attn_grad/pallas_call | solution.py:25
  59.1 1.9 %collective-permute-start.16 = (bf16[448,128]{1,0:T(8,128)(2,1)S(1)}, bf16[448,128]{1,0:T(8,128)(2,1)S(1)}, u32[]{:S(2)}, u32[]{:S(2)}) collective-permute-start(bf16[448,128]{1,0:T(8,128)(2,1)S(1)} %get-tuple-element.128), channel_id=1, source_target_pairs={{0,1},{1,0},{2,3},{3,2},{4,5},{5,4},{6,7},{7,6},{8,9},{9,8},{10,11... | collective-permute-start | bytes 344072 | tf_op jit(solution)/shard_map/ppermute | solution.py:805
  67.2 5.7 %collective-permute-done.17.p2 = bf16[448,128]{1,0:T(8,128)(2,1)S(1)} collective-permute-done((bf16[448,128]{1,0:T(8,128)(2,1)S(1)}, bf16[448,128]{1,0:T(8,128)(2,1)S(1)}, u32[]{:S(2)}, u32[]{:S(2)}) %collective-permute-start.17) | collective-permute-done | bytes 114720 | tf_op jit(solution)/shard_map/ppermute | solution.py:805
  72.9 2.4 %third_back.1 = (f32[512,128]{1,0:T(8,128)S(1)}, bf16[512,1152]{1,0:T(8,128)(2,1)S(1)}, f32[512,64]{1,0:T(8,128)}, f32[8,128]{1,0:T(8,128)S(1)}, f32[512,128]{1,...) custom-call(s32[4]{0:T(128)S(1)} %copy-done.19, ...), custom_call_target="tpu_custom_call" | custom-call | flops 99999997952 | bytes 1 | tf_op jit(solution)/shard_map/third_back/pallas_call | solution.py:855
  75.3 2.2 %collective-permute-start.20 = (bf16[512,128]{1,0:T(8,128)(2,1)S(1)}, bf16[512,128]{1,0:T(8,128)(2,1)S(1)}, u32[]{:S(2)}, u32[]{:S(2)}) collective-permute-start(bf16[512,128]{1,0:T(8,128)(2,1)S(1)} %get-tuple-element.149), channel_id=1, source_target_pairs={{0,1},{1,0},{2,3},{3,2},{4,5},{5,4},{6,7},{7,6},{8,9},{9,8},{10,11... | collective-permute-start | bytes 393224 | tf_op jit(solution)/shard_map/ppermute | solution.py:805
  81.0 1.8 %conv_two_grad.1 = (bf16[64,1408]{1,0:T(8,128)(2,1)S(1)}, bf16[64,1408]{1,0:T(8,128)(2,1)S(1)}, bf16[64,1408]{1,0:T(8,128)(2,1)S(1)}, bf16[64,1408]{1,0:T(8,128)...) custom-call(s32[4]{0:T(128)S(1)} %copy-done.19, bf16[512,128]{1,0:T(8,128)(2,1)S(1)} %copy-done.11, ...), custom_call_target="tpu_custom_call" | custom-call | bytes 1 | tf_op jit(solution)/shard_map/conv_two_grad/pallas_call | solution.py:25
  88.0 1.9 %collective-permute-done.21.p2 = bf16[512,128]{1,0:T(8,128)(2,1)S(1)} collective-permute-done((bf16[512,128]{1,0:T(8,128)(2,1)S(1)}, bf16[512,128]{1,0:T(8,128)(2,1)S(1)}, u32[]{:S(2)}, u32[]{:S(2)}) %collective-permute-start.21) | collective-permute-done | bytes 131104 | tf_op jit(solution)/shard_map/ppermute | solution.py:805
  90.0 2.0 %second_back.1 = (bf16[512,1152]{1,0:T(8,128)(2,1)S(1)}, f32[8,128]{1,0:T(8,128)S(1)}, f32[512,128]{1,0:T(8,128)S(1)}, bf16[512,128]{1,0:T(8,128)(2,1)S(1)}, bf1...) custom-call(s32[4]{0:T(128)S(1)} %copy-done.19, f32[512,128]{1,0:T(8,128)S(1)} %get-tuple-element.148.p0, ...), custom_call_target="tpu_custom_call" | custom-call | flops 99999997952 | bytes 1 | tf_op jit(solution)/shard_map/second_back/pallas_call | solution.py:855
  94.4 1.9 %collective-permute-start.30 = (bf16[2,64,640]{2,1,0:T(8,128)(2,1)S(1)}, bf16[2,64,640]{2,1,0:T(8,128)(2,1)S(1)}, u32[]{:S(2)}, u32[]{:S(2)}) collective-permute-start(bf16[2,64,640]{2,1,0:T(8,128)(2,1)S(1)} %get-tuple-element.179), channel_id=1, source_target_pairs={{0,1},{1,0},{2,3},{3,2},{4,5},{5,4},{6,7},{7,6},{8,9},{9,8},{10,11... | collective-permute-start | bytes 491528 | tf_op jit(solution)/shard_map/ppermute | solution.py:805
  97.1 2.8 %collective-permute-start.34 = (bf16[512,128]{1,0:T(8,128)(2,1)S(1)}, bf16[512,128]{1,0:T(8,128)(2,1)S(1)}, u32[]{:S(2)}, u32[]{:S(2)}) collective-permute-start(bf16[512,128]{1,0:T(8,128)(2,1)S(1)} %get-tuple-element.189), channel_id=1, source_target_pairs={{0,2},{1,3},{2,0},{3,1},{4,6},{5,7},{6,4},{7,5},{8,10},{9,11},{10,... | collective-permute-start | bytes 393224 | tf_op jit(solution)/shard_map/ppermute | solution.py:805
  109.8 2.5 %collective-permute-done.35.p3 = bf16[512,128]{1,0:T(8,128)(2,1)S(1)} collective-permute-done((bf16[512,128]{1,0:T(8,128)(2,1)S(1)}, bf16[512,128]{1,0:T(8,128)(2,1)S(1)}, u32[]{:S(2)}, u32[]{:S(2)}) %collective-permute-start.35) | collective-permute-done | bytes 131104 | tf_op jit(solution)/shard_map/ppermute | solution.py:805
  112.2 2.4 %collective-permute-start.29 = (bf16[64,1152]{1,0:T(8,128)(2,1)S(1)}, bf16[64,1152]{1,0:T(8,128)(2,1)S(1)}, u32[]{:S(2)}, u32[]{:S(2)}) collective-permute-start(bf16[64,1152]{1,0:T(8,128)(2,1)S(1)} %get-tuple-element.178), channel_id=1, source_target_pairs={{0,24},{4,28},{8,16},{12,20},{16,8},{20,12},{24,0},{28,4},{1,25},{... | collective-permute-start | bytes 442376 | tf_op jit(solution)/shard_map/ppermute | solution.py:805
  123.4 2.1 %collective-permute-done.43.refs_3_ = bf16[64,1408]{1,0:T(8,128)(2,1)S(1)} collective-permute-done((bf16[64,1408]{1,0:T(8,128)(2,1)S(1)}, bf16[64,1408]{1,0:T(8,128)(2,1)S(1)}, u32[]{:S(2)}, u32[]{:S(2)}) %collective-permute-start.43) | collective-permute-done | bytes 180256 | tf_op jit(solution)/shard_map/ppermute | solution.py:805
  126.0 4.4 %collective-permute-done.42.refs_2_ = bf16[64,1408]{1,0:T(8,128)(2,1)S(1)} collective-permute-done((bf16[64,1408]{1,0:T(8,128)(2,1)S(1)}, bf16[64,1408]{1,0:T(8,128)(2,1)S(1)}, u32[]{:S(2)}, u32[]{:S(2)}) %collective-permute-start.42) | collective-permute-done | bytes 180256 | tf_op jit(solution)/shard_map/ppermute | solution.py:805
  131.1 3.1 %collective-permute-done.38.refs_3_ = bf16[64,1792]{1,0:T(8,128)(2,1)S(1)} collective-permute-done((bf16[64,1792]{1,0:T(8,128)(2,1)S(1)}, bf16[64,1792]{1,0:T(8,128)(2,1)S(1)}, u32[]{:S(2)}, u32[]{:S(2)}) %collective-permute-start.38) | collective-permute-done | bytes 229408 | tf_op jit(solution)/shard_map/ppermute | solution.py:805
  134.2 2.2 %collective-permute-done.37.refs_2_ = bf16[64,1792]{1,0:T(8,128)(2,1)S(1)} collective-permute-done((bf16[64,1792]{1,0:T(8,128)(2,1)S(1)}, bf16[64,1792]{1,0:T(8,128)(2,1)S(1)}, u32[]{:S(2)}, u32[]{:S(2)}) %collective-permute-start.37) | collective-permute-done | bytes 229408 | tf_op jit(solution)/shard_map/ppermute | solution.py:805
  137.1 2.2 %finish_two.1 = (f32[2,9,512,128]{3,2,1,0:T(8,128)}, f32[64,1024]{1,0:T(8,128)}, f32[64,1024]{1,0:T(8,128)S(1)}) custom-call(s32[4]{0:T(128)S(1)} %copy-done.19, bf16[4,64,1408]{2,1,0:T(8,128)(2,1)S(1)} %stack_two.1.own_ref, bf16[4,64,1408]{2,1,0:T(8,128)(2,1)S(1)} %collective-permute-done.44.other_ref), custom_call_target="tpu_custom_call" | custom-call | flops 99999997952 | bytes 1 | tf_op jit(solution)/shard_map/finish_two/pallas_call | solution.py:855
  139.5 2.6 %finish_last.1 = (f32[2,9,512,128]{3,2,1,0:T(8,128)}, f32[3,128]{1,0:T(4,128)}, f32[3,128]{1,0:T(4,128)}, f32[2,128]{1,0:T(2,128)}, f32[1,64]{1,0:T(1,128)}, /*i...) custom-call(s32[4]{0:T(128)S(1)} %copy-done.19, ...), custom_call_target="tpu_custom_call", output_to_operand_aliasing={{0}: (5, {})} | custom-call | flops 99999997952 | bytes 1 | tf_op jit(solution)/shard_map/finish_last/pallas_call | solution.py:855
  (156 shorter events, 53.7 us)
Async XLA Ops:
  4.3 12.1 %collective-permute-start.2 = (bf16[512,128]{1,0:T(8,128)(2,1)}, bf16[512,128]{1,0:T(8,128)(2,1)S(1)}, u32[]{:S(2)}, u32[]{:S(2)}) collective-permute-start(bf16[512,128]{1,0:T(8,128)(2,1)} %get-tuple-element.113.a0), channel_id=1, source_target_pairs={{0,3},{1,2},{2,1},{3,0},{4,7},{5,6},{6,5},{7,4},{8,11},{9,10},{10,... | collective-permute-start | bytes 393224 | tf_op jit(solution)/shard_map/ppermute | solution.py:805
  9.4 15.8 %collective-permute-start.1 = (bf16[512,128]{1,0:T(8,128)(2,1)}, bf16[512,128]{1,0:T(8,128)(2,1)S(1)}, u32[]{:S(2)}, u32[]{:S(2)}) collective-permute-start(bf16[512,128]{1,0:T(8,128)(2,1)} %get-tuple-element.113.a0), channel_id=1, source_target_pairs={{0,2},{1,3},{2,0},{3,1},{4,6},{5,7},{6,4},{7,5},{8,10},{9,11},{10,... | collective-permute-start | bytes 393224 | tf_op jit(solution)/shard_map/ppermute | solution.py:805
  9.4 15.8 %collective-permute-start = (bf16[512,128]{1,0:T(8,128)(2,1)}, bf16[512,128]{1,0:T(8,128)(2,1)S(1)}, u32[]{:S(2)}, u32[]{:S(2)}) collective-permute-start(bf16[512,128]{1,0:T(8,128)(2,1)} %get-tuple-element.113.a0), channel_id=1, source_target_pairs={{0,1},{1,0},{2,3},{3,2},{4,5},{5,4},{6,7},{7,6},{8,9},{9,8},{10,11... | collective-permute-start | bytes 393224 | tf_op jit(solution)/shard_map/ppermute | solution.py:805
  10.1 21.4 %collective-permute-start.11 = (bf16[64,640]{1,0:T(8,128)(2,1)}, bf16[64,640]{1,0:T(8,128)(2,1)S(1)}, u32[]{:S(2)}, u32[]{:S(2)}) collective-permute-start(bf16[64,640]{1,0:T(8,128)(2,1)} %get-tuple-element.126.refs_0_), channel_id=1, source_target_pairs={{0,3},{1,2},{2,1},{3,0},{4,7},{5,6},{6,5},{7,4},{8,11},{9,10},{10,... | collective-permute-start | bytes 245768 | tf_op jit(solution)/shard_map/ppermute | solution.py:805
  13.8 19.4 %collective-permute-start.10 = (bf16[64,640]{1,0:T(8,128)(2,1)}, bf16[64,640]{1,0:T(8,128)(2,1)S(1)}, u32[]{:S(2)}, u32[]{:S(2)}) collective-permute-start(bf16[64,640]{1,0:T(8,128)(2,1)} %get-tuple-element.126.refs_0_), channel_id=1, source_target_pairs={{0,2},{1,3},{2,0},{3,1},{4,6},{5,7},{6,4},{7,5},{8,10},{9,11},{10,... | collective-permute-start | bytes 245768 | tf_op jit(solution)/shard_map/ppermute | solution.py:805
  16.4 16.8 %collective-permute-start.9 = (bf16[64,640]{1,0:T(8,128)(2,1)}, bf16[64,640]{1,0:T(8,128)(2,1)S(1)}, u32[]{:S(2)}, u32[]{:S(2)}) collective-permute-start(bf16[64,640]{1,0:T(8,128)(2,1)} %get-tuple-element.126.refs_0_), channel_id=1, source_target_pairs={{0,1},{1,0},{2,3},{3,2},{4,5},{5,4},{6,7},{7,6},{8,9},{9,8},{10,11... | collective-permute-start | bytes 245768 | tf_op jit(solution)/shard_map/ppermute | solution.py:805
  33.8 11.5 %collective-permute-start.14 = (bf16[4,64,640]{2,1,0:T(8,128)(2,1)S(1)}, bf16[4,64,640]{2,1,0:T(8,128)(2,1)S(1)}, u32[]{:S(2)}, u32[]{:S(2)}) collective-permute-start(bf16[4,64,640]{2,1,0:T(8,128)(2,1)S(1)} %pack_join.1.refs_0_), channel_id=1, source_target_pairs={{0,24},{4,28},{8,16},{12,20},{16,8},{20,12},{24,0},{28,4},{1,25},{... | collective-permute-start | bytes 983048 | tf_op jit(solution)/shard_map/ppermute | solution.py:805
  36.3 12.4 %collective-permute-start.13 = (bf16[4,64,640]{2,1,0:T(8,128)(2,1)S(1)}, bf16[4,64,640]{2,1,0:T(8,128)(2,1)S(1)}, u32[]{:S(2)}, u32[]{:S(2)}) collective-permute-start(bf16[4,64,640]{2,1,0:T(8,128)(2,1)S(1)} %pack_join.1.refs_0_), channel_id=1, source_target_pairs={{0,16},{4,20},{8,24},{12,28},{16,0},{20,4},{24,8},{28,12},{1,17},{... | collective-permute-start | bytes 983048 | tf_op jit(solution)/shard_map/ppermute | solution.py:805
  37.1 11.8 %collective-permute-start.12 = (bf16[4,64,640]{2,1,0:T(8,128)(2,1)S(1)}, bf16[4,64,640]{2,1,0:T(8,128)(2,1)S(1)}, u32[]{:S(2)}, u32[]{:S(2)}) collective-permute-start(bf16[4,64,640]{2,1,0:T(8,128)(2,1)S(1)} %pack_join.1.refs_0_), channel_id=1, source_target_pairs={{0,8},{4,12},{8,0},{12,4},{16,24},{20,28},{24,16},{28,20},{1,9},{5... | collective-permute-start | bytes 983048 | tf_op jit(solution)/shard_map/ppermute | solution.py:805
  43.1 9.3 %collective-permute-start.7 = (bf16[464,128]{1,0:T(8,128)(2,1)S(1)}, bf16[464,128]{1,0:T(8,128)(2,1)S(1)}, u32[]{:S(2)}, u32[]{:S(2)}) collective-permute-start(bf16[464,128]{1,0:T(8,128)(2,1)S(1)} %get-tuple-element.121), channel_id=1, source_target_pairs={{0,2},{1,3},{2,0},{3,1},{4,6},{5,7},{6,4},{7,5},{8,10},{9,11},{10,... | collective-permute-start | bytes 356360 | tf_op jit(solution)/shard_map/ppermute | solution.py:805
  61.0 11.8 %collective-permute-start.17 = (bf16[448,128]{1,0:T(8,128)(2,1)S(1)}, bf16[448,128]{1,0:T(8,128)(2,1)S(1)}, u32[]{:S(2)}, u32[]{:S(2)}) collective-permute-start(bf16[448,128]{1,0:T(8,128)(2,1)S(1)} %get-tuple-element.129), channel_id=1, source_target_pairs={{0,2},{1,3},{2,0},{3,1},{4,6},{5,7},{6,4},{7,5},{8,10},{9,11},{10,... | collective-permute-start | bytes 344072 | tf_op jit(solution)/shard_map/ppermute | solution.py:805
  62.2 10.7 %collective-permute-start.18 = (bf16[448,128]{1,0:T(8,128)(2,1)S(1)}, bf16[448,128]{1,0:T(8,128)(2,1)S(1)}, u32[]{:S(2)}, u32[]{:S(2)}) collective-permute-start(bf16[448,128]{1,0:T(8,128)(2,1)S(1)} %get-tuple-element.130), channel_id=1, source_target_pairs={{0,3},{1,2},{2,1},{3,0},{4,7},{5,6},{6,5},{7,4},{8,11},{9,10},{10,... | collective-permute-start | bytes 344072 | tf_op jit(solution)/shard_map/ppermute | solution.py:805
  65.6 17.2 %collective-permute-start.23 = (bf16[2,4,64,640]{3,2,1,0:T(8,128)(2,1)S(1)}, bf16[2,4,64,640]{3,2,1,0:T(8,128)(2,1)S(1)}, u32[]{:S(2)}, u32[]{:S(2)}) collective-permute-start(bf16[2,4,64,640]{3,2,1,0:T(8,128)(2,1)S(1)} %get-tuple-element.154), channel_id=1, source_target_pairs={{0,8},{4,12},{8,0},{12,4},{16,24},{20,28},{24,16},{28,20},{1,9},{5... | collective-permute-start | bytes 1966088 | tf_op jit(solution)/shard_map/ppermute | solution.py:805
  75.3 12.7 %collective-permute-start.20 = (bf16[512,128]{1,0:T(8,128)(2,1)S(1)}, bf16[512,128]{1,0:T(8,128)(2,1)S(1)}, u32[]{:S(2)}, u32[]{:S(2)}) collective-permute-start(bf16[512,128]{1,0:T(8,128)(2,1)S(1)} %get-tuple-element.149), channel_id=1, source_target_pairs={{0,1},{1,0},{2,3},{3,2},{4,5},{5,4},{6,7},{7,6},{8,9},{9,8},{10,11... | collective-permute-start | bytes 393224 | tf_op jit(solution)/shard_map/ppermute | solution.py:805
  77.5 12.4 %collective-permute-start.21 = (bf16[512,128]{1,0:T(8,128)(2,1)S(1)}, bf16[512,128]{1,0:T(8,128)(2,1)S(1)}, u32[]{:S(2)}, u32[]{:S(2)}) collective-permute-start(bf16[512,128]{1,0:T(8,128)(2,1)S(1)} %get-tuple-element.150), channel_id=1, source_target_pairs={{0,2},{1,3},{2,0},{3,1},{4,6},{5,7},{6,4},{7,5},{8,10},{9,11},{10,... | collective-permute-start | bytes 393224 | tf_op jit(solution)/shard_map/ppermute | solution.py:805
  78.5 11.4 %collective-permute-start.22 = (bf16[512,128]{1,0:T(8,128)(2,1)S(1)}, bf16[512,128]{1,0:T(8,128)(2,1)S(1)}, u32[]{:S(2)}, u32[]{:S(2)}) collective-permute-start(bf16[512,128]{1,0:T(8,128)(2,1)S(1)} %get-tuple-element.151), channel_id=1, source_target_pairs={{0,3},{1,2},{2,1},{3,0},{4,7},{5,6},{6,5},{7,4},{8,11},{9,10},{10,... | collective-permute-start | bytes 393224 | tf_op jit(solution)/shard_map/ppermute | solution.py:805
  83.6 10.2 %collective-permute-start.26 = (bf16[4,64,640]{2,1,0:T(8,128)(2,1)S(1)}, bf16[4,64,640]{2,1,0:T(8,128)(2,1)S(1)}, u32[]{:S(2)}, u32[]{:S(2)}) collective-permute-start(bf16[4,64,640]{2,1,0:T(8,128)(2,1)S(1)} %get-tuple-element.172), channel_id=1, source_target_pairs={{0,16},{4,20},{8,24},{12,28},{16,0},{20,4},{24,8},{28,12},{1,17},{... | collective-permute-start | bytes 983048 | tf_op jit(solution)/shard_map/ppermute | solution.py:805
  86.5 13.4 %collective-permute-start.31 = (bf16[2,64,1408]{2,1,0:T(8,128)(2,1)}, bf16[2,64,1408]{2,1,0:T(8,128)(2,1)}, u32[]{:S(2)}, u32[]{:S(2)}) collective-permute-start(bf16[2,64,1408]{2,1,0:T(8,128)(2,1)} %get-tuple-element.180), channel_id=1, source_target_pairs={{0,8},{4,12},{8,0},{12,4},{16,24},{20,28},{24,16},{28,20},{1,9},{5... | collective-permute-start | bytes 1081352 | tf_op jit(solution)/shard_map/ppermute | solution.py:805
  93.5 12.6 %collective-permute-start.25 = (bf16[4,64,1152]{2,1,0:T(8,128)(2,1)S(1)}, bf16[4,64,1152]{2,1,0:T(8,128)(2,1)S(1)}, u32[]{:S(2)}, u32[]{:S(2)}) collective-permute-start(bf16[4,64,1152]{2,1,0:T(8,128)(2,1)S(1)} %get-tuple-element.171), channel_id=1, source_target_pairs={{0,4},{4,0},{8,12},{12,8},{16,20},{20,16},{24,28},{28,24},{1,5},{5... | collective-permute-start | bytes 1769480 | tf_op jit(solution)/shard_map/ppermute | solution.py:805
  94.4 9.7 %collective-permute-start.30 = (bf16[2,64,640]{2,1,0:T(8,128)(2,1)S(1)}, bf16[2,64,640]{2,1,0:T(8,128)(2,1)S(1)}, u32[]{:S(2)}, u32[]{:S(2)}) collective-permute-start(bf16[2,64,640]{2,1,0:T(8,128)(2,1)S(1)} %get-tuple-element.179), channel_id=1, source_target_pairs={{0,1},{1,0},{2,3},{3,2},{4,5},{5,4},{6,7},{7,6},{8,9},{9,8},{10,11... | collective-permute-start | bytes 491528 | tf_op jit(solution)/shard_map/ppermute | solution.py:805
  96.9 10.3 %collective-permute-start.33 = (bf16[512,128]{1,0:T(8,128)(2,1)S(1)}, bf16[512,128]{1,0:T(8,128)(2,1)S(1)}, u32[]{:S(2)}, u32[]{:S(2)}) collective-permute-start(bf16[512,128]{1,0:T(8,128)(2,1)S(1)} %get-tuple-element.188), channel_id=1, source_target_pairs={{0,1},{1,0},{2,3},{3,2},{4,5},{5,4},{6,7},{7,6},{8,9},{9,8},{10,11... | collective-permute-start | bytes 393224 | tf_op jit(solution)/shard_map/ppermute | solution.py:805
  97.1 11.6 %collective-permute-start.34 = (bf16[512,128]{1,0:T(8,128)(2,1)S(1)}, bf16[512,128]{1,0:T(8,128)(2,1)S(1)}, u32[]{:S(2)}, u32[]{:S(2)}) collective-permute-start(bf16[512,128]{1,0:T(8,128)(2,1)S(1)} %get-tuple-element.189), channel_id=1, source_target_pairs={{0,2},{1,3},{2,0},{3,1},{4,6},{5,7},{6,4},{7,5},{8,10},{9,11},{10,... | collective-permute-start | bytes 393224 | tf_op jit(solution)/shard_map/ppermute | solution.py:805
  100.0 12.3 %collective-permute-start.35 = (bf16[512,128]{1,0:T(8,128)(2,1)S(1)}, bf16[512,128]{1,0:T(8,128)(2,1)S(1)}, u32[]{:S(2)}, u32[]{:S(2)}) collective-permute-start(bf16[512,128]{1,0:T(8,128)(2,1)S(1)} %get-tuple-element.190), channel_id=1, source_target_pairs={{0,3},{1,2},{2,1},{3,0},{4,7},{5,6},{6,5},{7,4},{8,11},{9,10},{10,... | collective-permute-start | bytes 393224 | tf_op jit(solution)/shard_map/ppermute | solution.py:805
  104.1 12.3 %collective-permute-start.40 = (bf16[64,1408]{1,0:T(8,128)(2,1)S(1)}, bf16[64,1408]{1,0:T(8,128)(2,1)S(1)}, u32[]{:S(2)}, u32[]{:S(2)}) collective-permute-start(bf16[64,1408]{1,0:T(8,128)(2,1)S(1)} %get-tuple-element.194), channel_id=1, source_target_pairs={{0,16},{4,20},{8,24},{12,28},{16,0},{20,4},{24,8},{28,12},{1,17},{... | collective-permute-start | bytes 540680 | tf_op jit(solution)/shard_map/ppermute | solution.py:805
  106.2 11.4 %collective-permute-start.32 = (bf16[64,640]{1,0:T(8,128)(2,1)S(1)}, bf16[64,640]{1,0:T(8,128)(2,1)S(1)}, u32[]{:S(2)}, u32[]{:S(2)}) collective-permute-start(bf16[64,640]{1,0:T(8,128)(2,1)S(1)} %get-tuple-element.183), channel_id=1, source_target_pairs={{0,2},{1,3},{2,0},{3,1},{4,6},{5,7},{6,4},{7,5},{8,10},{9,11},{10,... | collective-permute-start | bytes 245768 | tf_op jit(solution)/shard_map/ppermute | solution.py:805
  107.2 11.9 %collective-permute-start.27 = (bf16[64,1152]{1,0:T(8,128)(2,1)S(1)}, bf16[64,1152]{1,0:T(8,128)(2,1)S(1)}, u32[]{:S(2)}, u32[]{:S(2)}) collective-permute-start(bf16[64,1152]{1,0:T(8,128)(2,1)S(1)} %get-tuple-element.176), channel_id=1, source_target_pairs={{0,8},{4,12},{8,0},{12,4},{16,24},{20,28},{24,16},{28,20},{1,9},{5... | collective-permute-start | bytes 442376 | tf_op jit(solution)/shard_map/ppermute | solution.py:805
  108.7 11.8 %collective-permute-start.28 = (bf16[64,1152]{1,0:T(8,128)(2,1)S(1)}, bf16[64,1152]{1,0:T(8,128)(2,1)S(1)}, u32[]{:S(2)}, u32[]{:S(2)}) collective-permute-start(bf16[64,1152]{1,0:T(8,128)(2,1)S(1)} %get-tuple-element.177), channel_id=1, source_target_pairs={{0,16},{4,20},{8,24},{12,28},{16,0},{20,4},{24,8},{28,12},{1,17},{... | collective-permute-start | bytes 442376 | tf_op jit(solution)/shard_map/ppermute | solution.py:805
  117.5 12.9 %collective-permute-start.42 = (bf16[64,1408]{1,0:T(8,128)(2,1)S(1)}, bf16[64,1408]{1,0:T(8,128)(2,1)S(1)}, u32[]{:S(2)}, u32[]{:S(2)}) collective-permute-start(bf16[64,1408]{1,0:T(8,128)(2,1)S(1)} %conv_two_sum.1.refs_0_), channel_id=1, source_target_pairs={{0,16},{4,20},{8,24},{12,28},{16,0},{20,4},{24,8},{28,12},{1,17},{... | collective-permute-start | bytes 540680 | tf_op jit(solution)/shard_map/ppermute | solution.py:805
  119.1 11.3 %collective-permute-start.41 = (bf16[64,1408]{1,0:T(8,128)(2,1)S(1)}, bf16[64,1408]{1,0:T(8,128)(2,1)S(1)}, u32[]{:S(2)}, u32[]{:S(2)}) collective-permute-start(bf16[64,1408]{1,0:T(8,128)(2,1)S(1)} %conv_two_sum.1.refs_0_), channel_id=1, source_target_pairs={{0,8},{4,12},{8,0},{12,4},{16,24},{20,28},{24,16},{28,20},{1,9},{5... | collective-permute-start | bytes 540680 | tf_op jit(solution)/shard_map/ppermute | solution.py:805
  121.3 12.9 %collective-permute-start.38 = (bf16[64,1792]{1,0:T(8,128)(2,1)S(1)}, bf16[64,1792]{1,0:T(8,128)(2,1)S(1)}, u32[]{:S(2)}, u32[]{:S(2)}) collective-permute-start(bf16[64,1792]{1,0:T(8,128)(2,1)S(1)} %last.1.refs_0_.refs_4_), channel_id=1, source_target_pairs={{0,24},{4,28},{8,16},{12,20},{16,8},{20,12},{24,0},{28,4},{1,25},{... | collective-permute-start | bytes 688136 | tf_op jit(solution)/shard_map/ppermute | solution.py:805
  122.3 14.1 %collective-permute-start.37 = (bf16[64,1792]{1,0:T(8,128)(2,1)S(1)}, bf16[64,1792]{1,0:T(8,128)(2,1)S(1)}, u32[]{:S(2)}, u32[]{:S(2)}) collective-permute-start(bf16[64,1792]{1,0:T(8,128)(2,1)S(1)} %last.1.refs_0_.refs_4_), channel_id=1, source_target_pairs={{0,16},{4,20},{8,24},{12,28},{16,0},{20,4},{24,8},{28,12},{1,17},{... | collective-permute-start | bytes 688136 | tf_op jit(solution)/shard_map/ppermute | solution.py:805
  125.4 10.9 %collective-permute-start.36 = (bf16[64,1792]{1,0:T(8,128)(2,1)S(1)}, bf16[64,1792]{1,0:T(8,128)(2,1)S(1)}, u32[]{:S(2)}, u32[]{:S(2)}) collective-permute-start(bf16[64,1792]{1,0:T(8,128)(2,1)S(1)} %last.1.refs_0_.refs_4_), channel_id=1, source_target_pairs={{0,8},{4,12},{8,0},{12,4},{16,24},{20,28},{24,16},{28,20},{1,9},{5... | collective-permute-start | bytes 688136 | tf_op jit(solution)/shard_map/ppermute | solution.py:805
  (47 other events, 320.0 us)

commit v4 on v3

--- a/solution.py
+++ b/solution.py
@@ -301,7 +301,7 @@
         fixed_ref[k] = lanes([one, two]).astype(BF)
 
 
-def attn_weight_kernel(scalars, own_ref, other_ref, o_ref):
+def lay_weights(scalars, own_ref, other_ref, o_ref):
     for part in range(PARTS):
         source = (own_ref if part % 2 == 0 else other_ref).at[part // 2]
         _, row = part_row(scalars, part)
@@ -377,10 +377,22 @@
 
 
 def attention_kernel(
-    scalars, norm_ref, residual_ref, bias_ref, n0, n1, n2, n3, w_ref, *refs
+    scalars,
+    norm_ref,
+    residual_ref,
+    bias_ref,
+    n0,
+    n1,
+    n2,
+    n3,
+    own_ref,
+    other_ref,
+    usage_ref,
+    *refs,
 ):
-    pay_refs = refs[:4]
-    out_ref, lat_grad_ref, mixed_ref, att_grad_ref, qg_ref, kg_ref, vg_ref, sums_ref = refs[4:]
+    pay_refs, keep_refs, send_ref = refs[:4], refs[4:8], refs[8]
+    w_ref, grads, lat_grad_ref, sums_ref = refs[9:]
+    lay_weights(scalars, own_ref, other_ref, w_ref)
     query_bias, value_bias, out_bias = [bias_ref[m : m + 1] for m in range(3)]
     proj_bias = bias_ref[3:4, 0:256]
     pieces = [n0, n1, n2, n3]
@@ -393,10 +405,8 @@
     probs = weights / jnp.sum(weights, axis=1, keepdims=True)
     probs_low = probs.astype(BF)
     mixed = dot(probs_low, values).astype(BF)
-    mixed_ref[...] = mixed
     attended = dot(mixed, w_ref[:, 1536:2048]) + out_bias
     output = (residual_ref[...] + attended).astype(BF)
-    out_ref[...] = output
     latents = dot(output, w_ref[:, 2048:2304]) + proj_bias
     fixed = []
     for n in pieces:
@@ -408,7 +418,6 @@
         lat_grad_ref[:, 128 * k : 128 * k + 128] = lanes([lat_grad[:, 64 * k : 64 * k + 64], blank])
     out_grad = dot_nt(lat_grad, w_ref[:, 2048:2304])
     att_grad = out_grad.astype(BF)
-    att_grad_ref[...] = att_grad
     mixed_grad = dot_nt(att_grad, w_ref[:, 1536:2048]).astype(BF)
     probs_grad = dot_nt(mixed_grad, values)
     row_dot = jnp.sum(probs * probs_grad, axis=1, keepdims=True)
@@ -416,9 +425,6 @@
     query_grad = (dot(score_grad, keys) * SCORE_SCALE).astype(BF)
     key_grad = (dot_tn(score_grad, query) * SCORE_SCALE).astype(BF)
     value_grad = dot_tn(probs_low, mixed_grad).astype(BF)
-    qg_ref[...] = query_grad
-    kg_ref[...] = key_grad
-    vg_ref[...] = value_grad
     upstream = dot_nt(key_grad, w_ref[:, 512:1024]) + dot_nt(value_grad, w_ref[:, 1024:1536])
     upstream_own = upstream[:128] + dot_nt(query_grad, w_ref[:, 0:512])
     for k in range(4):
@@ -445,28 +451,11 @@
             ),
         ]
     )
-
-
-def attn_grad_kernel(
-    scalars,
-    norm_ref,
-    out_ref,
-    lat_grad_ref,
-    mixed_ref,
-    att_grad_ref,
-    qg_ref,
-    kg_ref,
-    vg_ref,
-    sums_ref,
-    usage_ref,
-    *refs,
-):
-    keep_refs, send_ref, grads = refs[:4], refs[4], refs[5]
-    grads[:, 0:512] = dot_tn(norm_ref[0:128], qg_ref[...]).astype(BF)
-    grads[:, 512:1024] = dot_tn(norm_ref[...], kg_ref[...]).astype(BF)
-    grads[:, 1024:1536] = dot_tn(norm_ref[...], vg_ref[...]).astype(BF)
-    grads[:, 1536:2048] = dot_tn(mixed_ref[...], att_grad_ref[...]).astype(BF)
-    grads[:, 2048:2560] = dot_tn(out_ref[...], lat_grad_ref[...]).astype(BF)
+    grads[:, 0:512] = dot_tn(norm_ref[0:128], query_grad).astype(BF)
+    grads[:, 512:1024] = dot_tn(normed, key_grad).astype(BF)
+    grads[:, 1024:1536] = dot_tn(normed, value_grad).astype(BF)
+    grads[:, 1536:2048] = dot_tn(mixed, att_grad).astype(BF)
+    grads[:, 2048:2560] = dot_tn(output, lat_grad_ref[...]).astype(BF)
     right = lax.broadcasted_iota(jnp.int32, (16, 128), 1) >= 64
 
     def halves(vectors, offset):
@@ -573,14 +562,19 @@
     param_ref,
     _,
     __,
+    a0,
+    a1,
+    a2,
+    a3,
     w_ref,
-    taps_ref,
     small_ref,
     q0,
     q1,
     q2,
     q3,
+    *refs,
 ):
+    keep_refs, send_ref, grads, taps_ref = refs[:4], refs[4], refs[5], refs[6]
     gradient = p0[...] + p1[...].astype(F32) + p2[...].astype(F32) + p3[...].astype(F32)
     stats = stats_ref[...]
     normed = renormed(hidden_ref[...], stats)
@@ -590,6 +584,15 @@
     low = source.astype(BF).astype(F32)
     small_ref[...] = pack_rows([gain_grad, shift_grad, col_sum(low)])
     send_taps(low, w_ref, scalars[0], taps_ref, (q0, q1, q2, q3))
+    full = lanes([a0[...], a1[...], a2[...], a3[...]])
+    grads[...] = dot_tn(full, taps_ref[...]).astype(BF)
+    for part in range(PARTS):
+        _, row = part_row(scalars, part)
+        value = grads[pl.ds(row, 64), :]
+        if part % 2 == 0:
+            keep_refs[part // 2][...] = value
+        else:
+            send_ref[part // 2] = value
 
 
 def first_back_kernel(
@@ -616,19 +619,6 @@
     source, gain_grad, shift_grad = norm_back(upstream, normed, stats, gain)
     grad_ref[...] = residual_ref[...] + source
     small_ref[...] = pack_rows([gain_grad, shift_grad])
-
-
-def conv_one_grad_kernel(scalars, a0, a1, a2, a3, taps_ref, *refs):
-    keep_refs, send_ref, grads = refs[:4], refs[4], refs[5]
-    full = lanes([a0[...], a1[...], a2[...], a3[...]])
-    grads[...] = dot_tn(full, taps_ref[...]).astype(BF)
-    for part in range(PARTS):
-        _, row = part_row(scalars, part)
-        value = grads[pl.ds(row, 64), :]
-        if part % 2 == 0:
-            keep_refs[part // 2][...] = value
-        else:
-            send_ref[part // 2] = value
 
 
 def conv_two_grad_kernel(
@@ -928,6 +918,8 @@
         scratch = ()
         if body is third_back_kernel:
             scratch = [pltpu.VMEM((tokens, 128), F32), pltpu.VMEM((tokens, 128), F32)]
+        if body is second_back_kernel:
+            scratch = [pltpu.VMEM((C, WIDE), BF), pltpu.VMEM((tokens, WIDE), BF)]
         return blocks_call(
             body, specs, [whole(o.shape) for o in outs], outs, name, *args, scratch=scratch
         )
@@ -991,49 +983,32 @@
         flops=HEAVY,
         name="attn_in",
     )
-    attn_w = call(
-        attn_weight_kernel,
-        [sds((C, 2304), BF)],
-        scalars,
-        block_own,
-        block_other,
-        name="attn_weight",
-    )[0]
-    *pays, output, lat_grad, mixed, att_grad, qg, kg, vg, sums = call(
+    *pays, k0, k1, k2, k3, att_send = call(
         attention_kernel,
         [sds((POS + 192, 128), F32)]
         + [sds((POS + 192, 128), BF)] * 3
-        + [sds((quarter, C), BF)] * 5
-        + [sds((POS, C), BF), sds((POS, C), BF), sds((8, C), F32)],
+        + [sds((4, 64, 640), BF)] * 4
+        + [sds((4, 4, 64, 640), BF)],
         scalars,
         normed,
         residual_part,
         bias_rows,
         *normed_pieces,
-        attn_w,
+        block_own,
+        block_other,
+        usage,
+        scratch=[
+            pltpu.VMEM((C, 2304), BF),
+            pltpu.VMEM((C, 2560), BF),
+            pltpu.VMEM((quarter, C), BF),
+            pltpu.VMEM((8, C), F32),
+        ],
         flops=HEAVY,
         name="attention",
     )
+    att_keep = [k0, k1, k2, k3]
 
     back_three = [pays[0]] + [over("chan", pays[k], k) for k in (1, 2, 3)]
-    *att_keep, att_send = call(
-        attn_grad_kernel,
-        [sds((4, 64, 640), BF)] * 4 + [sds((4, 4, 64, 640), BF)],
-        scalars,
-        normed,
-        output,
-        lat_grad,
-        mixed,
-        att_grad,
-        qg,
-        kg,
-        vg,
-        sums,
-        usage,
-        scratch=[pltpu.VMEM((C, 2560), BF)],
-        name="attn_grad",
-    )
-
     def pair_sum(keep, send, after, name):
         outs = [sds((2,) + keep[0].shape, BF)] * 2
         got = over("dp", send, 1)
@@ -1058,7 +1033,7 @@
         normed_three,
         stats_three,
         params,
-        att_kept if by_hand else sums,
+        att_kept if by_hand else bias_rows,
         conv_w,
     )
     back_two = [pays[0]] + [over("chan", pays[k], k) for k in (1, 2, 3)]
@@ -1093,29 +1068,25 @@
         )
         att_got = over("dp", att_sent, 4)
         two_kept, two_got = pair_sum(two_keep, two_send, att_own, "conv_two_pair")
-    taps_one, small_two, *pays = conv_call(
+    small_two, *pays = conv_call(
         second_back_kernel,
         0,
-        [sds((tokens, WIDE), BF), sds((8, 128), F32), sds((tokens, 128), F32)]
-        + [sds((tokens, 128), BF)] * 3,
+        [sds((8, 128), F32), sds((tokens, 128), F32)]
+        + [sds((tokens, 128), BF)] * 3
+        + [sds((64, WIDE), BF)] * 4
+        + [sds((4, 64, WIDE), BF)],
         "second_back",
         *back_two,
         hidden,
         stats_two,
         params,
-        att_own if by_hand else sums,
-        two_kept if by_hand else sums,
+        att_own if by_hand else bias_rows,
+        two_kept if by_hand else bias_rows,
+        *pieces_one,
         conv_w,
     )
-    *one_keep, one_send = call(
-        conv_one_grad_kernel,
-        [sds((64, WIDE), BF)] * 4 + [sds((4, 64, WIDE), BF)],
-        scalars,
-        *pieces_one,
-        taps_one,
-        scratch=[pltpu.VMEM((C, WIDE), BF)],
-        name="conv_one_grad",
-    )
+    *one_keep, one_send = pays[4:]
+    pays = pays[:4]
     one_got = over("dp", one_send, 1) if by_hand else one_send
     pays[1:] = call(
         pass_kernel,
@@ -1168,6 +1139,15 @@
             name="attn_last",
         )
         att_got = over("chan", att_sent, 2)
+        two = call(
+            two_sum_kernel,
+            [sds((64, 1408), BF)],
+            scalars,
+            two_own,
+            two_got,
+            one_parts[0],
+            name="conv_two_sum",
+        )[0]
     grad_latents, small_one = call(
         first_back_kernel,
         [sds((tokens, 128), F32), sds((8, 128), F32)],
@@ -1177,23 +1157,14 @@
         stats_one,
         params,
         residual_grad,
-        one_parts[0] if by_hand else sums,
-        two_own if by_hand else sums,
-        att_own if by_hand else sums,
+        one_parts[0] if by_hand else bias_rows,
+        two if by_hand else bias_rows,
+        att_own if by_hand else bias_rows,
         flops=HEAVY,
         name="first_back",
     )
 
     if by_hand:
-        two = call(
-            two_sum_kernel,
-            [sds((64, 1408), BF)],
-            scalars,
-            two_own,
-            two_got,
-            small_one,
-            name="conv_two_sum",
-        )[0]
         last = call(
             last_kernel,
             [sds((64, 1792), BF)],

time: 143 us -> 141 us (0.986)
  Pallas kernels: 39.6 us -> 38.1 us
    pallas_call x23 -> x20, Pallas kernels: 26.8 us -> 24.4 us  [call(): pl.pallas_call(body, out_shape=list(outs), in_specs=[pl.BlockSpec(memory_...]
    unnamed x68 -> x70, local copies, waits for them, and re-layouts: 3.44 us -> 3.47 us
  transfers between devices with their start and end apart: 45 -> 45, of which waited for: 18 -> 19; matrix products, arithmetic and copies ran while one was open for 0% -> 0% of each run, Pallas kernels for 20% -> 20%
where the time goes in v4:
time: 141 us
  starting transfers between devices  59.7 us (42%)
  Pallas kernels  38.1 us (27%)
  waiting for transfers between devices  37.2 us (26%)
  local copies, waits for them, and re-layouts  3.47 us (2%)
    ppermute x45, starting transfers between devices, over(): return lax.ppermute(array, axis, [(i, i ^ flip) for i in range(size)])  59.7 us
    ppermute x45, waiting for transfers between devices, over(): return lax.ppermute(array, axis, [(i, i ^ flip) for i in range(size)])  37.2 us
    pallas_call x20, Pallas kernels, call(): pl.pallas_call(body, out_shape=list(outs), in_specs=[pl.BlockSpec(memory_...  24.4 us
    pallas_call x6, Pallas kernels, blocks_call(): pl.pallas_call(body, grid=(1,), out_shape=outs, in_specs=[pl.BlockSpec(me...  13.7 us
    unnamed x70, local copies, waits for them, and re-layouts  3.47 us
  transfers between devices with their start and end apart: 45, of which 19 were waited for; matrix products, arithmetic and copies ran while one was open for 0% of the time, Pallas kernels for 20%

profile of v4, /device:TPU:0, one launch (start us, length us, event | category | flops | bytes accessed | tf_op | source)
XLA Modules:
  0.0 140.5 jit_solution(17597938837146056701)
XLA Ops:
  1.3 3.0 %begin.1 = (bf16[512,128]{1,0:T(8,128)(2,1)}, f32[8,128]{1,0:T(8,128)}, bf16[64,640]{1,0:T(8,128)(2,1)}, f32[16,128]{1,0:T(8,128)}) custom-call(s32[4]{0:T(128)} %pad_add_fusion.scalars.refs_0_, bf16[512,128]{1,0:T(8,128)(2,1)} %bitcast.27, f32[3,128]{1,0:T(4,128)} %gain_any.1, f32[3,128]{1,0:T(4,128)} %shift_any.1, f32[2,128]{1,0:T(2,128)} %conv_b_any.1, ...), custom_call_target="tpu_custom_call" | custom-call | flops 99999997952 | bytes 1 | tf_op jit(solution)/shard_map/begin/pallas_call | solution.py:25
  4.3 5.1 %collective-permute-start.2 = (bf16[512,128]{1,0:T(8,128)(2,1)}, bf16[512,128]{1,0:T(8,128)(2,1)S(1)}, u32[]{:S(2)}, u32[]{:S(2)}) collective-permute-start(bf16[512,128]{1,0:T(8,128)(2,1)} %get-tuple-element.104.a0), channel_id=1, source_target_pairs={{0,3},{1,2},{2,1},{3,0},{4,7},{5,6},{6,5},{7,4},{8,11},{9,10},{10,... | collective-permute-start | bytes 393224 | tf_op jit(solution)/shard_map/ppermute | solution.py:795
  10.1 3.7 %collective-permute-start.11 = (bf16[64,640]{1,0:T(8,128)(2,1)}, bf16[64,640]{1,0:T(8,128)(2,1)S(1)}, u32[]{:S(2)}, u32[]{:S(2)}) collective-permute-start(bf16[64,640]{1,0:T(8,128)(2,1)} %get-tuple-element.117.refs_0_), channel_id=1, source_target_pairs={{0,3},{1,2},{2,1},{3,0},{4,7},{5,6},{6,5},{7,4},{8,11},{9,10},{10,... | collective-permute-start | bytes 245768 | tf_op jit(solution)/shard_map/ppermute | solution.py:795
  14.5 1.9 %start.1 = (bf16[512,1024]{1,0:T(8,128)(2,1)S(1)}, f32[512,64]{1,0:T(8,128)S(1)}, f32[8,128]{1,0:T(8,128)S(1)}, bf16[4,64,128]{2,1,0:T(8,128)(2,1)S(1)}) custom-call(s32[4]{0:T(128)S(1)} %copy-done.11, s32[2,16,16]{2,1,0:T(8,128)S(1)} %copy-done.12, f32[64,1024]{1,0:T(8,128)S(1)} %bitcast.18, bf16[512,64]{1,0:T(8,128)(2,1)S(1)} %bitcast.21, ...), custom_call_target="tpu_custom_call" | custom-call | bytes 1 | tf_op jit(solution)/shard_map/start/pallas_call | solution.py:25
  16.5 3.8 %collective-permute-start.9 = (bf16[64,640]{1,0:T(8,128)(2,1)}, bf16[64,640]{1,0:T(8,128)(2,1)S(1)}, u32[]{:S(2)}, u32[]{:S(2)}) collective-permute-start(bf16[64,640]{1,0:T(8,128)(2,1)} %get-tuple-element.117.refs_0_), channel_id=1, source_target_pairs={{0,1},{1,0},{2,3},{3,2},{4,5},{5,4},{6,7},{7,6},{8,9},{9,8},{10,11... | collective-permute-start | bytes 245768 | tf_op jit(solution)/shard_map/ppermute | solution.py:795
  20.3 4.9 %collective-permute-done.1.a2 = bf16[512,128]{1,0:T(8,128)(2,1)S(1)} collective-permute-done((bf16[512,128]{1,0:T(8,128)(2,1)}, bf16[512,128]{1,0:T(8,128)(2,1)S(1)}, u32[]{:S(2)}, u32[]{:S(2)}) %collective-permute-start.1) | collective-permute-done | bytes 131104 | tf_op jit(solution)/shard_map/ppermute | solution.py:795
  26.9 1.8 %conv_one.1 = (f32[512,128]{1,0:T(8,128)S(1)}, f32[8,128]{1,0:T(8,128)S(1)}, bf16[512,128]{1,0:T(8,128)(2,1)S(1)}) custom-call(s32[4]{0:T(128)S(1)} %copy-done.11, bf16[512,128]{1,0:T(8,128)(2,1)S(1)} %copy-done.21, bf16[512,128]{1,0:T(8,128)(2,1)S(1)} %collective-permute-done.a1, bf16[512,128]{1,0:T(8,128)(2,1)S(1)} %collective-permute-done.1.a2, ...), custom_call_target="tpu_custom_call" | custom-call | flops 99999997952 | bytes 1 | tf_op jit(solution)/shard_map/conv_one/pallas_call | solution.py:845
  28.8 2.7 %collective-permute-start.5 = (bf16[512,128]{1,0:T(8,128)(2,1)S(1)}, bf16[512,128]{1,0:T(8,128)(2,1)S(1)}, u32[]{:S(2)}, u32[]{:S(2)}) collective-permute-start(bf16[512,128]{1,0:T(8,128)(2,1)S(1)} %get-tuple-element.108.a0.refs_1_), channel_id=1, source_target_pairs={{0,3},{1,2},{2,1},{3,0},{4,7},{5,6},{6,5},{7,4},{8,11},{9,10},{10,... | collective-permute-start | bytes 393224 | tf_op jit(solution)/shard_map/ppermute | solution.py:795
  31.5 1.7 %collective-permute-start.3 = (bf16[512,128]{1,0:T(8,128)(2,1)S(1)}, bf16[512,128]{1,0:T(8,128)(2,1)S(1)}, u32[]{:S(2)}, u32[]{:S(2)}) collective-permute-start(bf16[512,128]{1,0:T(8,128)(2,1)S(1)} %get-tuple-element.108.a0.refs_1_), channel_id=1, source_target_pairs={{0,1},{1,0},{2,3},{3,2},{4,5},{5,4},{6,7},{7,6},{8,9},{9,8},{10,11... | collective-permute-start | bytes 393224 | tf_op jit(solution)/shard_map/ppermute | solution.py:795
  33.8 2.5 %collective-permute-start.14 = (bf16[4,64,640]{2,1,0:T(8,128)(2,1)S(1)}, bf16[4,64,640]{2,1,0:T(8,128)(2,1)S(1)}, u32[]{:S(2)}, u32[]{:S(2)}) collective-permute-start(bf16[4,64,640]{2,1,0:T(8,128)(2,1)S(1)} %pack_join.1.refs_0_), channel_id=1, source_target_pairs={{0,24},{4,28},{8,16},{12,20},{16,8},{20,12},{24,0},{28,4},{1,25},{... | collective-permute-start | bytes 983048 | tf_op jit(solution)/shard_map/ppermute | solution.py:795
  38.6 1.9 %collective-permute-done.4.a2.refs_3_ = bf16[512,128]{1,0:T(8,128)(2,1)S(1)} collective-permute-done((bf16[512,128]{1,0:T(8,128)(2,1)S(1)}, bf16[512,128]{1,0:T(8,128)(2,1)S(1)}, u32[]{:S(2)}, u32[]{:S(2)}) %collective-permute-start.4) | collective-permute-done | bytes 131104 | tf_op jit(solution)/shard_map/ppermute | solution.py:795
  40.5 1.9 %conv_two.1 = (f32[512,128]{1,0:T(8,128)S(1)}, f32[8,128]{1,0:T(8,128)S(1)}, bf16[464,128]{1,0:T(8,128)(2,1)S(1)}, bf16[464,128]{1,0:T(8,128)(2,1)S(1)}, bf16[46...) custom-call(s32[4]{0:T(128)S(1)} %copy-done.11, bf16[512,128]{1,0:T(8,128)(2,1)S(1)} %get-tuple-element.108.a0.refs_1_, ...), custom_call_target="tpu_custom_call" | custom-call | flops 99999997952 | bytes 1 | tf_op jit(solution)/shard_map/conv_two/pallas_call | solution.py:845
  46.8 2.0 %collective-permute-done.13.refs_2_ = bf16[4,64,640]{2,1,0:T(8,128)(2,1)S(1)} collective-permute-done((bf16[4,64,640]{2,1,0:T(8,128)(2,1)S(1)}, bf16[4,64,640]{2,1,0:T(8,128)(2,1)S(1)}, u32[]{:S(2)}, u32[]{:S(2)}) %collective-permute-start.13) | collective-permute-done | bytes 327712 | tf_op jit(solution)/shard_map/ppermute | solution.py:795
  49.6 2.8 %collective-permute-done.7.n2 = bf16[464,128]{1,0:T(8,128)(2,1)S(1)} collective-permute-done((bf16[464,128]{1,0:T(8,128)(2,1)S(1)}, bf16[464,128]{1,0:T(8,128)(2,1)S(1)}, u32[]{:S(2)}, u32[]{:S(2)}) %collective-permute-start.7) | collective-permute-done | bytes 118816 | tf_op jit(solution)/shard_map/ppermute | solution.py:795
  53.1 4.7 %attention.1 = (f32[448,128]{1,0:T(8,128)S(1)}, bf16[448,128]{1,0:T(8,128)(2,1)S(1)}, bf16[448,128]{1,0:T(8,128)(2,1)S(1)}, bf16[448,128]{1,0:T(8,128)(2,1)S(1)}...) custom-call(s32[4]{0:T(128)S(1)} %copy-done.11, ...), custom_call_target="tpu_custom_call" | custom-call | flops 99999997952 | bytes 1 | tf_op jit(solution)/shard_map/attention/pallas_call | solution.py:25
  57.9 1.9 %collective-permute-start.16 = (bf16[448,128]{1,0:T(8,128)(2,1)S(1)}, bf16[448,128]{1,0:T(8,128)(2,1)S(1)}, u32[]{:S(2)}, u32[]{:S(2)}) collective-permute-start(bf16[448,128]{1,0:T(8,128)(2,1)S(1)} %get-tuple-element.119), channel_id=1, source_target_pairs={{0,1},{1,0},{2,3},{3,2},{4,5},{5,4},{6,7},{7,6},{8,9},{9,8},{10,11... | collective-permute-start | bytes 344072 | tf_op jit(solution)/shard_map/ppermute | solution.py:795
  64.4 1.5 %collective-permute-start.23 = (bf16[2,4,64,640]{3,2,1,0:T(8,128)(2,1)S(1)}, bf16[2,4,64,640]{3,2,1,0:T(8,128)(2,1)S(1)}, u32[]{:S(2)}, u32[]{:S(2)}) collective-permute-start(bf16[2,4,64,640]{3,2,1,0:T(8,128)(2,1)S(1)} %get-tuple-element.137), channel_id=1, source_target_pairs={{0,8},{4,12},{8,0},{12,4},{16,24},{20,28},{24,16},{28,20},{1,9},{5... | collective-permute-start | bytes 1966088 | tf_op jit(solution)/shard_map/ppermute | solution.py:795
  65.9 5.7 %collective-permute-done.17.p2 = bf16[448,128]{1,0:T(8,128)(2,1)S(1)} collective-permute-done((bf16[448,128]{1,0:T(8,128)(2,1)S(1)}, bf16[448,128]{1,0:T(8,128)(2,1)S(1)}, u32[]{:S(2)}, u32[]{:S(2)}) %collective-permute-start.17) | collective-permute-done | bytes 114720 | tf_op jit(solution)/shard_map/ppermute | solution.py:795
  71.7 2.4 %third_back.1 = (f32[512,128]{1,0:T(8,128)S(1)}, bf16[512,1152]{1,0:T(8,128)(2,1)S(1)}, f32[512,64]{1,0:T(8,128)}, f32[8,128]{1,0:T(8,128)S(1)}, f32[512,128]{1,...) custom-call(s32[4]{0:T(128)S(1)} %copy-done.11, ...), custom_call_target="tpu_custom_call" | custom-call | flops 99999997952 | bytes 1 | tf_op jit(solution)/shard_map/third_back/pallas_call | solution.py:845
  74.1 2.2 %collective-permute-start.20 = (bf16[512,128]{1,0:T(8,128)(2,1)S(1)}, bf16[512,128]{1,0:T(8,128)(2,1)S(1)}, u32[]{:S(2)}, u32[]{:S(2)}) collective-permute-start(bf16[512,128]{1,0:T(8,128)(2,1)S(1)} %get-tuple-element.132), channel_id=1, source_target_pairs={{0,1},{1,0},{2,3},{3,2},{4,5},{5,4},{6,7},{7,6},{8,9},{9,8},{10,11... | collective-permute-start | bytes 393224 | tf_op jit(solution)/shard_map/ppermute | solution.py:795
  79.8 1.8 %conv_two_grad.1 = (bf16[64,1408]{1,0:T(8,128)(2,1)S(1)}, bf16[64,1408]{1,0:T(8,128)(2,1)S(1)}, bf16[64,1408]{1,0:T(8,128)(2,1)S(1)}, bf16[64,1408]{1,0:T(8,128)...) custom-call(s32[4]{0:T(128)S(1)} %copy-done.11, bf16[512,128]{1,0:T(8,128)(2,1)S(1)} %copy-done.3, ...), custom_call_target="tpu_custom_call" | custom-call | bytes 1 | tf_op jit(solution)/shard_map/conv_two_grad/pallas_call | solution.py:25
  82.4 1.6 %collective-permute-start.26 = (bf16[4,64,640]{2,1,0:T(8,128)(2,1)S(1)}, bf16[4,64,640]{2,1,0:T(8,128)(2,1)S(1)}, u32[]{:S(2)}, u32[]{:S(2)}) collective-permute-start(bf16[4,64,640]{2,1,0:T(8,128)(2,1)S(1)} %get-tuple-element.154), channel_id=1, source_target_pairs={{0,16},{4,20},{8,24},{12,28},{16,0},{20,4},{24,8},{28,12},{1,17},{... | collective-permute-start | bytes 983048 | tf_op jit(solution)/shard_map/ppermute | solution.py:795
  86.2 2.5 %collective-permute-done.21.p2 = bf16[512,128]{1,0:T(8,128)(2,1)S(1)} collective-permute-done((bf16[512,128]{1,0:T(8,128)(2,1)S(1)}, bf16[512,128]{1,0:T(8,128)(2,1)S(1)}, u32[]{:S(2)}, u32[]{:S(2)}) %collective-permute-start.21) | collective-permute-done | bytes 131104 | tf_op jit(solution)/shard_map/ppermute | solution.py:795
  88.8 2.8 %second_back.1 = (f32[8,128]{1,0:T(8,128)S(1)}, f32[512,128]{1,0:T(8,128)S(1)}, bf16[512,128]{1,0:T(8,128)(2,1)S(1)}, bf16[512,128]{1,0:T(8,128)(2,1)S(1)}, bf16...) custom-call(s32[4]{0:T(128)S(1)} %copy-done.11, ...), custom_call_target="tpu_custom_call" | custom-call | flops 99999997952 | bytes 1 | tf_op jit(solution)/shard_map/second_back/pallas_call | solution.py:845
  99.0 1.9 %collective-permute-start.34 = (bf16[512,128]{1,0:T(8,128)(2,1)S(1)}, bf16[512,128]{1,0:T(8,128)(2,1)S(1)}, u32[]{:S(2)}, u32[]{:S(2)}) collective-permute-start(bf16[512,128]{1,0:T(8,128)(2,1)S(1)} %get-tuple-element.171), channel_id=1, source_target_pairs={{0,2},{1,3},{2,0},{3,1},{4,6},{5,7},{6,4},{7,5},{8,10},{9,11},{10,... | collective-permute-start | bytes 393224 | tf_op jit(solution)/shard_map/ppermute | solution.py:795
  108.5 4.7 %collective-permute-done.34.p2 = bf16[512,128]{1,0:T(8,128)(2,1)S(1)} collective-permute-done((bf16[512,128]{1,0:T(8,128)(2,1)S(1)}, bf16[512,128]{1,0:T(8,128)(2,1)S(1)}, u32[]{:S(2)}, u32[]{:S(2)}) %collective-permute-start.34) | collective-permute-done | bytes 131104 | tf_op jit(solution)/shard_map/ppermute | solution.py:795
  113.1 2.1 %collective-permute-start.29 = (bf16[64,1152]{1,0:T(8,128)(2,1)S(1)}, bf16[64,1152]{1,0:T(8,128)(2,1)S(1)}, u32[]{:S(2)}, u32[]{:S(2)}) collective-permute-start(bf16[64,1152]{1,0:T(8,128)(2,1)S(1)} %get-tuple-element.160), channel_id=1, source_target_pairs={{0,24},{4,28},{8,16},{12,20},{16,8},{20,12},{24,0},{28,4},{1,25},{... | collective-permute-start | bytes 442376 | tf_op jit(solution)/shard_map/ppermute | solution.py:795
  116.1 2.1 %first_back.1 = (f32[512,128]{1,0:T(8,128)}, f32[8,128]{1,0:T(8,128)S(1)}) custom-call(s32[4]{0:T(128)S(1)} %copy-done.11, f32[512,128]{1,0:T(8,128)S(1)} %get-tuple-element.166.p0, bf16[512,128]{1,0:T(8,128)(2,1)S(1)} %collective-permute-done.33.p1, bf16[512,128]{1,0:T(8,128)(2,1)S(1)} %collective-permute-done.34.p2, ...), custom_call_target="tpu_custom_call" | custom-call | flops 99999997952 | bytes 1 | tf_op jit(solution)/shard_map/first_back/pallas_call | solution.py:25
  125.8 4.7 %collective-permute-done.42.refs_2_ = bf16[64,1408]{1,0:T(8,128)(2,1)S(1)} collective-permute-done((bf16[64,1408]{1,0:T(8,128)(2,1)}, bf16[64,1408]{1,0:T(8,128)(2,1)S(1)}, u32[]{:S(2)}, u32[]{:S(2)}) %collective-permute-start.42) | collective-permute-done | bytes 180256 | tf_op jit(solution)/shard_map/ppermute | solution.py:795
  132.4 1.7 %collective-permute-done.38.refs_2_ = bf16[64,1792]{1,0:T(8,128)(2,1)S(1)} collective-permute-done((bf16[64,1792]{1,0:T(8,128)(2,1)S(1)}, bf16[64,1792]{1,0:T(8,128)(2,1)S(1)}, u32[]{:S(2)}, u32[]{:S(2)}) %collective-permute-start.38) | collective-permute-done | bytes 229408 | tf_op jit(solution)/shard_map/ppermute | solution.py:795
  135.3 2.2 %finish_two.1 = (f32[2,9,512,128]{3,2,1,0:T(8,128)}, f32[64,1024]{1,0:T(8,128)}, f32[64,1024]{1,0:T(8,128)S(1)}) custom-call(s32[4]{0:T(128)S(1)} %copy-done.11, bf16[4,64,1408]{2,1,0:T(8,128)(2,1)S(1)} %stack_two.1.own_ref, bf16[4,64,1408]{2,1,0:T(8,128)(2,1)S(1)} %collective-permute-done.44.other_ref), custom_call_target="tpu_custom_call" | custom-call | flops 99999997952 | bytes 1 | tf_op jit(solution)/shard_map/finish_two/pallas_call | solution.py:845
  137.8 2.6 %finish_last.1 = (f32[2,9,512,128]{3,2,1,0:T(8,128)}, f32[3,128]{1,0:T(4,128)}, f32[3,128]{1,0:T(4,128)}, f32[2,128]{1,0:T(2,128)}, f32[1,64]{1,0:T(1,128)}, /*i...) custom-call(s32[4]{0:T(128)S(1)} %copy-done.11, ...), custom_call_target="tpu_custom_call", output_to_operand_aliasing={{0}: (5, {})} | custom-call | flops 99999997952 | bytes 1 | tf_op jit(solution)/shard_map/finish_last/pallas_call | solution.py:845
  (155 shorter events, 50.1 us)
Async XLA Ops:
  4.3 12.2 %collective-permute-start.2 = (bf16[512,128]{1,0:T(8,128)(2,1)}, bf16[512,128]{1,0:T(8,128)(2,1)S(1)}, u32[]{:S(2)}, u32[]{:S(2)}) collective-permute-start(bf16[512,128]{1,0:T(8,128)(2,1)} %get-tuple-element.104.a0), channel_id=1, source_target_pairs={{0,3},{1,2},{2,1},{3,0},{4,7},{5,6},{6,5},{7,4},{8,11},{9,10},{10,... | collective-permute-start | bytes 393224 | tf_op jit(solution)/shard_map/ppermute | solution.py:795
  9.4 15.8 %collective-permute-start.1 = (bf16[512,128]{1,0:T(8,128)(2,1)}, bf16[512,128]{1,0:T(8,128)(2,1)S(1)}, u32[]{:S(2)}, u32[]{:S(2)}) collective-permute-start(bf16[512,128]{1,0:T(8,128)(2,1)} %get-tuple-element.104.a0), channel_id=1, source_target_pairs={{0,2},{1,3},{2,0},{3,1},{4,6},{5,7},{6,4},{7,5},{8,10},{9,11},{10,... | collective-permute-start | bytes 393224 | tf_op jit(solution)/shard_map/ppermute | solution.py:795
  9.4 15.8 %collective-permute-start = (bf16[512,128]{1,0:T(8,128)(2,1)}, bf16[512,128]{1,0:T(8,128)(2,1)S(1)}, u32[]{:S(2)}, u32[]{:S(2)}) collective-permute-start(bf16[512,128]{1,0:T(8,128)(2,1)} %get-tuple-element.104.a0), channel_id=1, source_target_pairs={{0,1},{1,0},{2,3},{3,2},{4,5},{5,4},{6,7},{7,6},{8,9},{9,8},{10,11... | collective-permute-start | bytes 393224 | tf_op jit(solution)/shard_map/ppermute | solution.py:795
  10.1 21.5 %collective-permute-start.11 = (bf16[64,640]{1,0:T(8,128)(2,1)}, bf16[64,640]{1,0:T(8,128)(2,1)S(1)}, u32[]{:S(2)}, u32[]{:S(2)}) collective-permute-start(bf16[64,640]{1,0:T(8,128)(2,1)} %get-tuple-element.117.refs_0_), channel_id=1, source_target_pairs={{0,3},{1,2},{2,1},{3,0},{4,7},{5,6},{6,5},{7,4},{8,11},{9,10},{10,... | collective-permute-start | bytes 245768 | tf_op jit(solution)/shard_map/ppermute | solution.py:795
  13.8 19.4 %collective-permute-start.10 = (bf16[64,640]{1,0:T(8,128)(2,1)}, bf16[64,640]{1,0:T(8,128)(2,1)S(1)}, u32[]{:S(2)}, u32[]{:S(2)}) collective-permute-start(bf16[64,640]{1,0:T(8,128)(2,1)} %get-tuple-element.117.refs_0_), channel_id=1, source_target_pairs={{0,2},{1,3},{2,0},{3,1},{4,6},{5,7},{6,4},{7,5},{8,10},{9,11},{10,... | collective-permute-start | bytes 245768 | tf_op jit(solution)/shard_map/ppermute | solution.py:795
  16.5 16.8 %collective-permute-start.9 = (bf16[64,640]{1,0:T(8,128)(2,1)}, bf16[64,640]{1,0:T(8,128)(2,1)S(1)}, u32[]{:S(2)}, u32[]{:S(2)}) collective-permute-start(bf16[64,640]{1,0:T(8,128)(2,1)} %get-tuple-element.117.refs_0_), channel_id=1, source_target_pairs={{0,1},{1,0},{2,3},{3,2},{4,5},{5,4},{6,7},{7,6},{8,9},{9,8},{10,11... | collective-permute-start | bytes 245768 | tf_op jit(solution)/shard_map/ppermute | solution.py:795
  31.5 8.9 %collective-permute-start.4 = (bf16[512,128]{1,0:T(8,128)(2,1)S(1)}, bf16[512,128]{1,0:T(8,128)(2,1)S(1)}, u32[]{:S(2)}, u32[]{:S(2)}) collective-permute-start(bf16[512,128]{1,0:T(8,128)(2,1)S(1)} %get-tuple-element.108.a0.refs_1_), channel_id=1, source_target_pairs={{0,2},{1,3},{2,0},{3,1},{4,6},{5,7},{6,4},{7,5},{8,10},{9,11},{10,... | collective-permute-start | bytes 393224 | tf_op jit(solution)/shard_map/ppermute | solution.py:795
  33.8 11.5 %collective-permute-start.14 = (bf16[4,64,640]{2,1,0:T(8,128)(2,1)S(1)}, bf16[4,64,640]{2,1,0:T(8,128)(2,1)S(1)}, u32[]{:S(2)}, u32[]{:S(2)}) collective-permute-start(bf16[4,64,640]{2,1,0:T(8,128)(2,1)S(1)} %pack_join.1.refs_0_), channel_id=1, source_target_pairs={{0,24},{4,28},{8,16},{12,20},{16,8},{20,12},{24,0},{28,4},{1,25},{... | collective-permute-start | bytes 983048 | tf_op jit(solution)/shard_map/ppermute | solution.py:795
  36.3 12.4 %collective-permute-start.13 = (bf16[4,64,640]{2,1,0:T(8,128)(2,1)S(1)}, bf16[4,64,640]{2,1,0:T(8,128)(2,1)S(1)}, u32[]{:S(2)}, u32[]{:S(2)}) collective-permute-start(bf16[4,64,640]{2,1,0:T(8,128)(2,1)S(1)} %pack_join.1.refs_0_), channel_id=1, source_target_pairs={{0,16},{4,20},{8,24},{12,28},{16,0},{20,4},{24,8},{28,12},{1,17},{... | collective-permute-start | bytes 983048 | tf_op jit(solution)/shard_map/ppermute | solution.py:795
  37.1 11.8 %collective-permute-start.12 = (bf16[4,64,640]{2,1,0:T(8,128)(2,1)S(1)}, bf16[4,64,640]{2,1,0:T(8,128)(2,1)S(1)}, u32[]{:S(2)}, u32[]{:S(2)}) collective-permute-start(bf16[4,64,640]{2,1,0:T(8,128)(2,1)S(1)} %pack_join.1.refs_0_), channel_id=1, source_target_pairs={{0,8},{4,12},{8,0},{12,4},{16,24},{20,28},{24,16},{28,20},{1,9},{5... | collective-permute-start | bytes 983048 | tf_op jit(solution)/shard_map/ppermute | solution.py:795
  43.1 9.3 %collective-permute-start.7 = (bf16[464,128]{1,0:T(8,128)(2,1)S(1)}, bf16[464,128]{1,0:T(8,128)(2,1)S(1)}, u32[]{:S(2)}, u32[]{:S(2)}) collective-permute-start(bf16[464,128]{1,0:T(8,128)(2,1)S(1)} %get-tuple-element.112), channel_id=1, source_target_pairs={{0,2},{1,3},{2,0},{3,1},{4,6},{5,7},{6,4},{7,5},{8,10},{9,11},{10,... | collective-permute-start | bytes 356360 | tf_op jit(solution)/shard_map/ppermute | solution.py:795
  59.8 11.8 %collective-permute-start.17 = (bf16[448,128]{1,0:T(8,128)(2,1)S(1)}, bf16[448,128]{1,0:T(8,128)(2,1)S(1)}, u32[]{:S(2)}, u32[]{:S(2)}) collective-permute-start(bf16[448,128]{1,0:T(8,128)(2,1)S(1)} %get-tuple-element.120), channel_id=1, source_target_pairs={{0,2},{1,3},{2,0},{3,1},{4,6},{5,7},{6,4},{7,5},{8,10},{9,11},{10,... | collective-permute-start | bytes 344072 | tf_op jit(solution)/shard_map/ppermute | solution.py:795
  60.9 10.7 %collective-permute-start.18 = (bf16[448,128]{1,0:T(8,128)(2,1)S(1)}, bf16[448,128]{1,0:T(8,128)(2,1)S(1)}, u32[]{:S(2)}, u32[]{:S(2)}) collective-permute-start(bf16[448,128]{1,0:T(8,128)(2,1)S(1)} %get-tuple-element.121), channel_id=1, source_target_pairs={{0,3},{1,2},{2,1},{3,0},{4,7},{5,6},{6,5},{7,4},{8,11},{9,10},{10,... | collective-permute-start | bytes 344072 | tf_op jit(solution)/shard_map/ppermute | solution.py:795
  64.4 17.3 %collective-permute-start.23 = (bf16[2,4,64,640]{3,2,1,0:T(8,128)(2,1)S(1)}, bf16[2,4,64,640]{3,2,1,0:T(8,128)(2,1)S(1)}, u32[]{:S(2)}, u32[]{:S(2)}) collective-permute-start(bf16[2,4,64,640]{3,2,1,0:T(8,128)(2,1)S(1)} %get-tuple-element.137), channel_id=1, source_target_pairs={{0,8},{4,12},{8,0},{12,4},{16,24},{20,28},{24,16},{28,20},{1,9},{5... | collective-permute-start | bytes 1966088 | tf_op jit(solution)/shard_map/ppermute | solution.py:795
  74.1 12.2 %collective-permute-start.20 = (bf16[512,128]{1,0:T(8,128)(2,1)S(1)}, bf16[512,128]{1,0:T(8,128)(2,1)S(1)}, u32[]{:S(2)}, u32[]{:S(2)}) collective-permute-start(bf16[512,128]{1,0:T(8,128)(2,1)S(1)} %get-tuple-element.132), channel_id=1, source_target_pairs={{0,1},{1,0},{2,3},{3,2},{4,5},{5,4},{6,7},{7,6},{8,9},{9,8},{10,11... | collective-permute-start | bytes 393224 | tf_op jit(solution)/shard_map/ppermute | solution.py:795
  76.3 12.4 %collective-permute-start.21 = (bf16[512,128]{1,0:T(8,128)(2,1)S(1)}, bf16[512,128]{1,0:T(8,128)(2,1)S(1)}, u32[]{:S(2)}, u32[]{:S(2)}) collective-permute-start(bf16[512,128]{1,0:T(8,128)(2,1)S(1)} %get-tuple-element.133), channel_id=1, source_target_pairs={{0,2},{1,3},{2,0},{3,1},{4,6},{5,7},{6,4},{7,5},{8,10},{9,11},{10,... | collective-permute-start | bytes 393224 | tf_op jit(solution)/shard_map/ppermute | solution.py:795
  77.3 11.4 %collective-permute-start.22 = (bf16[512,128]{1,0:T(8,128)(2,1)S(1)}, bf16[512,128]{1,0:T(8,128)(2,1)S(1)}, u32[]{:S(2)}, u32[]{:S(2)}) collective-permute-start(bf16[512,128]{1,0:T(8,128)(2,1)S(1)} %get-tuple-element.134), channel_id=1, source_target_pairs={{0,3},{1,2},{2,1},{3,0},{4,7},{5,6},{6,5},{7,4},{8,11},{9,10},{10,... | collective-permute-start | bytes 393224 | tf_op jit(solution)/shard_map/ppermute | solution.py:795
  82.4 10.2 %collective-permute-start.26 = (bf16[4,64,640]{2,1,0:T(8,128)(2,1)S(1)}, bf16[4,64,640]{2,1,0:T(8,128)(2,1)S(1)}, u32[]{:S(2)}, u32[]{:S(2)}) collective-permute-start(bf16[4,64,640]{2,1,0:T(8,128)(2,1)S(1)} %get-tuple-element.154), channel_id=1, source_target_pairs={{0,16},{4,20},{8,24},{12,28},{16,0},{20,4},{24,8},{28,12},{1,17},{... | collective-permute-start | bytes 983048 | tf_op jit(solution)/shard_map/ppermute | solution.py:795
  84.7 10.6 %collective-permute-start.31 = (bf16[2,64,1408]{2,1,0:T(8,128)(2,1)S(1)}, bf16[2,64,1408]{2,1,0:T(8,128)(2,1)S(1)}, u32[]{:S(2)}, u32[]{:S(2)}) collective-permute-start(bf16[2,64,1408]{2,1,0:T(8,128)(2,1)S(1)} %get-tuple-element.162), channel_id=1, source_target_pairs={{0,8},{4,12},{8,0},{12,4},{16,24},{20,28},{24,16},{28,20},{1,9},{5... | collective-permute-start | bytes 1081352 | tf_op jit(solution)/shard_map/ppermute | solution.py:795
  91.6 11.4 %collective-permute-start.25 = (bf16[4,64,1152]{2,1,0:T(8,128)(2,1)S(1)}, bf16[4,64,1152]{2,1,0:T(8,128)(2,1)S(1)}, u32[]{:S(2)}, u32[]{:S(2)}) collective-permute-start(bf16[4,64,1152]{2,1,0:T(8,128)(2,1)S(1)} %get-tuple-element.153), channel_id=1, source_target_pairs={{0,4},{4,0},{8,12},{12,8},{16,20},{20,16},{24,28},{28,24},{1,5},{5... | collective-permute-start | bytes 1769480 | tf_op jit(solution)/shard_map/ppermute | solution.py:795
  97.9 9.7 %collective-permute-start.33 = (bf16[512,128]{1,0:T(8,128)(2,1)S(1)}, bf16[512,128]{1,0:T(8,128)(2,1)S(1)}, u32[]{:S(2)}, u32[]{:S(2)}) collective-permute-start(bf16[512,128]{1,0:T(8,128)(2,1)S(1)} %get-tuple-element.170), channel_id=1, source_target_pairs={{0,1},{1,0},{2,3},{3,2},{4,5},{5,4},{6,7},{7,6},{8,9},{9,8},{10,11... | collective-permute-start | bytes 393224 | tf_op jit(solution)/shard_map/ppermute | solution.py:795
  99.0 14.2 %collective-permute-start.34 = (bf16[512,128]{1,0:T(8,128)(2,1)S(1)}, bf16[512,128]{1,0:T(8,128)(2,1)S(1)}, u32[]{:S(2)}, u32[]{:S(2)}) collective-permute-start(bf16[512,128]{1,0:T(8,128)(2,1)S(1)} %get-tuple-element.171), channel_id=1, source_target_pairs={{0,2},{1,3},{2,0},{3,1},{4,6},{5,7},{6,4},{7,5},{8,10},{9,11},{10,... | collective-permute-start | bytes 393224 | tf_op jit(solution)/shard_map/ppermute | solution.py:795
  100.9 14.4 %collective-permute-start.35 = (bf16[512,128]{1,0:T(8,128)(2,1)S(1)}, bf16[512,128]{1,0:T(8,128)(2,1)S(1)}, u32[]{:S(2)}, u32[]{:S(2)}) collective-permute-start(bf16[512,128]{1,0:T(8,128)(2,1)S(1)} %get-tuple-element.172), channel_id=1, source_target_pairs={{0,3},{1,2},{2,1},{3,0},{4,7},{5,6},{6,5},{7,4},{8,11},{9,10},{10,... | collective-permute-start | bytes 393224 | tf_op jit(solution)/shard_map/ppermute | solution.py:795
  102.9 15.2 %collective-permute-start.32 = (bf16[64,640]{1,0:T(8,128)(2,1)S(1)}, bf16[64,640]{1,0:T(8,128)(2,1)S(1)}, u32[]{:S(2)}, u32[]{:S(2)}) collective-permute-start(bf16[64,640]{1,0:T(8,128)(2,1)S(1)} %get-tuple-element.165), channel_id=1, source_target_pairs={{0,2},{1,3},{2,0},{3,1},{4,6},{5,7},{6,4},{7,5},{8,10},{9,11},{10,... | collective-permute-start | bytes 245768 | tf_op jit(solution)/shard_map/ppermute | solution.py:795
  104.8 14.6 %collective-permute-start.27 = (bf16[64,1152]{1,0:T(8,128)(2,1)S(1)}, bf16[64,1152]{1,0:T(8,128)(2,1)S(1)}, u32[]{:S(2)}, u32[]{:S(2)}) collective-permute-start(bf16[64,1152]{1,0:T(8,128)(2,1)S(1)} %get-tuple-element.158), channel_id=1, source_target_pairs={{0,8},{4,12},{8,0},{12,4},{16,24},{20,28},{24,16},{28,20},{1,9},{5... | collective-permute-start | bytes 442376 | tf_op jit(solution)/shard_map/ppermute | solution.py:795
  107.6 13.3 %collective-permute-start.28 = (bf16[64,1152]{1,0:T(8,128)(2,1)S(1)}, bf16[64,1152]{1,0:T(8,128)(2,1)S(1)}, u32[]{:S(2)}, u32[]{:S(2)}) collective-permute-start(bf16[64,1152]{1,0:T(8,128)(2,1)S(1)} %get-tuple-element.159), channel_id=1, source_target_pairs={{0,16},{4,20},{8,24},{12,28},{16,0},{20,4},{24,8},{28,12},{1,17},{... | collective-permute-start | bytes 442376 | tf_op jit(solution)/shard_map/ppermute | solution.py:795
  115.3 9.0 %collective-permute-start.43 = (bf16[64,1408]{1,0:T(8,128)(2,1)}, bf16[64,1408]{1,0:T(8,128)(2,1)}, u32[]{:S(2)}, u32[]{:S(2)}) collective-permute-start(bf16[64,1408]{1,0:T(8,128)(2,1)} %conv_two_sum.1.__.refs_0_), channel_id=1, source_target_pairs={{0,24},{4,28},{8,16},{12,20},{16,8},{20,12},{24,0},{28,4},{1,25},{... | collective-permute-start | bytes 540680 | tf_op jit(solution)/shard_map/ppermute | solution.py:795
  118.2 12.3 %collective-permute-start.42 = (bf16[64,1408]{1,0:T(8,128)(2,1)}, bf16[64,1408]{1,0:T(8,128)(2,1)S(1)}, u32[]{:S(2)}, u32[]{:S(2)}) collective-permute-start(bf16[64,1408]{1,0:T(8,128)(2,1)} %conv_two_sum.1.__.refs_0_), channel_id=1, source_target_pairs={{0,16},{4,20},{8,24},{12,28},{16,0},{20,4},{24,8},{28,12},{1,17},{... | collective-permute-start | bytes 540680 | tf_op jit(solution)/shard_map/ppermute | solution.py:795
  119.4 11.1 %collective-permute-start.41 = (bf16[64,1408]{1,0:T(8,128)(2,1)}, bf16[64,1408]{1,0:T(8,128)(2,1)S(1)}, u32[]{:S(2)}, u32[]{:S(2)}) collective-permute-start(bf16[64,1408]{1,0:T(8,128)(2,1)} %conv_two_sum.1.__.refs_0_), channel_id=1, source_target_pairs={{0,8},{4,12},{8,0},{12,4},{16,24},{20,28},{24,16},{28,20},{1,9},{5... | collective-permute-start | bytes 540680 | tf_op jit(solution)/shard_map/ppermute | solution.py:795
  121.7 10.8 %collective-permute-start.39 = (bf16[64,1792]{1,0:T(8,128)(2,1)S(1)}, bf16[64,1792]{1,0:T(8,128)(2,1)S(1)}, u32[]{:S(2)}, u32[]{:S(2)}) collective-permute-start(bf16[64,1792]{1,0:T(8,128)(2,1)S(1)} %last.1.refs_0_.refs_4_), channel_id=1, source_target_pairs={{0,24},{4,28},{8,16},{12,20},{16,8},{20,12},{24,0},{28,4},{1,25},{... | collective-permute-start | bytes 688136 | tf_op jit(solution)/shard_map/ppermute | solution.py:795
  122.7 11.5 %collective-permute-start.38 = (bf16[64,1792]{1,0:T(8,128)(2,1)S(1)}, bf16[64,1792]{1,0:T(8,128)(2,1)S(1)}, u32[]{:S(2)}, u32[]{:S(2)}) collective-permute-start(bf16[64,1792]{1,0:T(8,128)(2,1)S(1)} %last.1.refs_0_.refs_4_), channel_id=1, source_target_pairs={{0,16},{4,20},{8,24},{12,28},{16,0},{20,4},{24,8},{28,12},{1,17},{... | collective-permute-start | bytes 688136 | tf_op jit(solution)/shard_map/ppermute | solution.py:795
  124.3 10.3 %collective-permute-start.37 = (bf16[64,1792]{1,0:T(8,128)(2,1)S(1)}, bf16[64,1792]{1,0:T(8,128)(2,1)S(1)}, u32[]{:S(2)}, u32[]{:S(2)}) collective-permute-start(bf16[64,1792]{1,0:T(8,128)(2,1)S(1)} %last.1.refs_0_.refs_4_), channel_id=1, source_target_pairs={{0,8},{4,12},{8,0},{12,4},{16,24},{20,28},{24,16},{28,20},{1,9},{5... | collective-permute-start | bytes 688136 | tf_op jit(solution)/shard_map/ppermute | solution.py:795
  (48 other events, 350.5 us)

commit v5 on v4

--- a/solution.py
+++ b/solution.py
@@ -21,7 +21,7 @@
 PARTS = 8
 
 
-def call(body, outs, *args, scratch=(), flops=0, name=None, space=pltpu.VMEM, vmem=VMEM):
+def call(body, outs, *args, scratch=(), flops=0, name=None, space=pltpu.VMEM):
     result = pl.pallas_call(
         body,
         out_shape=list(outs),
@@ -29,7 +29,7 @@
         + [pl.BlockSpec(memory_space=space)] * (len(args) - 1),
         out_specs=[pl.BlockSpec(memory_space=pltpu.VMEM)] * len(outs),
         scratch_shapes=list(scratch),
-        compiler_params=pltpu.CompilerParams(vmem_limit_bytes=vmem * 2**20),
+        compiler_params=pltpu.CompilerParams(vmem_limit_bytes=VMEM * 2**20),
         cost_estimate=pl.CostEstimate(flops=flops, bytes_accessed=1, transcendentals=0),
         name=name,
     )(*args)
@@ -198,19 +198,8 @@
     return place, pl.multiple_of(block * 128 + (place & 1) * 64, 64)
 
 
-def fetch(pairs, sems):
-    copies = [
-        pltpu.make_async_copy(source, target, sems.at[i])
-        for i, (source, target) in enumerate(pairs)
-    ]
-    for copy in copies:
-        copy.start()
-    for copy in copies:
-        copy.wait()
-
-
 def begin_kernel(
-    scalars,
+    by_hand,
     x_any,
     gain_any,
     shift_any,
@@ -235,29 +224,38 @@
     proj,
     sems,
 ):
-    own = pl.ds(pl.multiple_of(scalars[1] * 64, 64), 64)
-    fetch(
-        [
-            (x_any, x_ref),
-            (gain_any, gain_ref),
-            (shift_any, shift_ref),
-            (conv_b_any, conv_b_ref),
-            (attn_b_any, attn_b_ref),
-            (proj_b_any, proj_b_ref),
-            (out_w_any.at[own, :], weights.at[3]),
-            (proj_any, proj_ref),
-        ]
-        + [(qkv_any.at[m, own, :], weights.at[m]) for m in range(3)],
-        sems,
-    )
+    place = lax.axis_index("dp").astype(jnp.int32) if by_hand else jnp.int32(0)
+    own = pl.ds(pl.multiple_of(place * 64, 64), 64)
+    block = pl.ds(pl.multiple_of((place >> 1) * 128, 128), 128)
+    pairs = [
+        (x_any, x_ref),
+        (gain_any, gain_ref),
+        (shift_any, shift_ref),
+        (proj_any.at[:, block], proj_ref),
+        (out_w_any.at[own, :], weights.at[3]),
+        (conv_b_any, conv_b_ref),
+        (attn_b_any, attn_b_ref),
+        (proj_b_any, proj_b_ref),
+    ] + [(qkv_any.at[m, own, :], weights.at[m]) for m in range(3)]
+    copies = [
+        pltpu.make_async_copy(source, target, sems.at[i])
+        for i, (source, target) in enumerate(pairs)
+    ]
+    for copy in copies:
+        copy.start()
+    for copy in copies[:3]:
+        copy.wait()
     normed, stats = moments(x_ref[...].astype(F32))
     pre = normed * gain_ref[0:1] + shift_ref[0:1]
     act_ref[...] = (pre * jax.nn.sigmoid(pre)).astype(BF)
     stats_ref[...] = stats
+    for copy in copies[3:]:
+        copy.wait()
     for m in range(4):
         pack_ref[:, 128 * m : 128 * m + 128] = weights[m]
     proj[...] = jnp.transpose(proj_ref[...].astype(F32))
-    pack_ref[:, 512:640] = lanes([proj[own, :], jnp.zeros((64, 64), F32)]).astype(BF)
+    mine = proj[pl.ds(pl.multiple_of((place & 1) * 64, 64), 64), :]
+    pack_ref[:, 512:640] = lanes([mine, jnp.zeros((64, 64), F32)]).astype(BF)
     rows = [gain_ref[m : m + 1] for m in range(3)] + [shift_ref[m : m + 1] for m in range(3)]
     rows += [conv_b_ref[m : m + 1] for m in range(2)] + [attn_b_ref[m : m + 1] for m in range(3)]
     rows += [lanes([proj_b_ref[...], jnp.zeros_like(proj_b_ref[...])])]
@@ -749,7 +747,8 @@
         (send_ref if k % 2 else keep_ref)[k // 2] = plus(a0[k], a1[k])
 
 
-def pass_kernel(scalars, a0, a1, a2, _, b0, b1, b2):
+def half_pass_kernel(scalars, keep_ref, get_ref, _, a0, a1, a2, own_ref, send_ref, b0, b1, b2):
+    half_add_kernel(scalars, keep_ref, get_ref, _, own_ref, send_ref)
     for source, target in ((a0, b0), (a1, b1), (a2, b2)):
         target[...] = source[...]
 
@@ -855,15 +854,37 @@
             name=name,
         )(scalars, *args)
 
-    act_one, stats_one, pack, params = call(
-        begin_kernel,
-        [
+    anywhere = pl.BlockSpec(memory_space=pl.ANY)
+
+    def begin(*refs):
+        begin_kernel(by_hand, *refs)
+
+    act_one, stats_one, pack, params = pl.pallas_call(
+        begin,
+        out_shape=[
             sds((tokens, 128), BF),
             sds((8, 128), F32),
             sds((64, 640), BF),
             sds((16, 128), F32),
         ],
-        scalars,
+        in_specs=[anywhere] * 9,
+        out_specs=[pl.BlockSpec(memory_space=pltpu.VMEM)] * 4,
+        scratch_shapes=[
+            pltpu.VMEM((tokens, 128), BF),
+            pltpu.VMEM((3, 128), F32),
+            pltpu.VMEM((3, 128), F32),
+            pltpu.VMEM((2, 128), F32),
+            pltpu.VMEM((3, 128), F32),
+            pltpu.VMEM((1, 64), F32),
+            pltpu.VMEM((4, 64, 128), BF),
+            pltpu.VMEM((64, 128), BF),
+            pltpu.VMEM((128, 64), F32),
+            pltpu.SemaphoreType.DMA((11,)),
+        ],
+        compiler_params=pltpu.CompilerParams(vmem_limit_bytes=60 * 2**20),
+        cost_estimate=pl.CostEstimate(flops=HEAVY, bytes_accessed=1, transcendentals=0),
+        name="begin",
+    )(
         x,
         norm_gains,
         norm_shifts,
@@ -873,22 +894,6 @@
         qkv_weights,
         out_weight,
         proj_weight.T,
-        scratch=[
-            pltpu.VMEM((tokens, 128), BF),
-            pltpu.VMEM((3, 128), F32),
-            pltpu.VMEM((3, 128), F32),
-            pltpu.VMEM((2, 128), F32),
-            pltpu.VMEM((3, 128), F32),
-            pltpu.VMEM((1, 64), F32),
-            pltpu.VMEM((4, 64, 128), BF),
-            pltpu.VMEM((64, C), BF),
-            pltpu.VMEM((C, 64), F32),
-            pltpu.SemaphoreType.DMA((11,)),
-        ],
-        flops=HEAVY,
-        space=pl.ANY,
-        vmem=60,
-        name="begin",
     )
     pieces_one = [act_one] + flips(act_one)
     packs = [pack] + flips(pack)
@@ -1088,16 +1093,6 @@
     *one_keep, one_send = pays[4:]
     pays = pays[:4]
     one_got = over("dp", one_send, 1) if by_hand else one_send
-    pays[1:] = call(
-        pass_kernel,
-        [sds((tokens, 128), BF)] * 3,
-        scalars,
-        *pays[1:],
-        one_keep[0],
-        flops=HEAVY,
-        name="pass_on",
-    )
-    back_one = [pays[0]] + [over("chan", pays[k], k) for k in (1, 2, 3)]
     if by_hand:
         att_kept, att_sent = call(
             attn_sum_kernel,
@@ -1109,13 +1104,15 @@
             name="attn_sum",
         )
         att_got = over("chan", att_sent, 1)
-        two_own, two_sent = call(
-            half_add_kernel,
-            [sds((64, 1408), BF)] * 2,
+        two_own, two_sent, *pays[1:] = call(
+            half_pass_kernel,
+            [sds((64, 1408), BF)] * 2 + [sds((tokens, 128), BF)] * 3,
             scalars,
             two_kept,
             two_got,
             att_kept,
+            *pays[1:],
+            flops=HEAVY,
             name="conv_two_half",
         )
         two_got = over("dp", two_sent, 4)
@@ -1148,6 +1145,7 @@
             one_parts[0],
             name="conv_two_sum",
         )[0]
+    back_one = [pays[0]] + [over("chan", pays[k], k) for k in (1, 2, 3)]
     grad_latents, small_one = call(
         first_back_kernel,
         [sds((tokens, 128), F32), sds((8, 128), F32)],

time: 141 us -> 139 us (0.986)
    pallas_call x20 -> x18, Pallas kernels: 24.4 us -> 20.8 us  [call(): pl.pallas_call(body, out_shape=list(outs), in_specs=[pl.BlockSpec(memory_...]
    pallas_call x0 -> x1, Pallas kernels: none -> 2.36 us  [shards(): pl.pallas_call(begin, out_shape=[sds((tokens, 128), BF), sds((8, 128), F3...]
    unnamed x70 -> x54, local copies, waits for them, and re-layouts: 3.47 us -> 3.36 us
where the time goes in v5:
time: 139 us; the launch traced here: 138 us
  starting transfers between devices  60 us (43%)
  waiting for transfers between devices  37 us (27%)
  Pallas kernels  36.8 us (26%)
  local copies, waits for them, and re-layouts  3.36 us (2%)
    ppermute x45, starting transfers between devices, over(): return lax.ppermute(array, axis, [(i, i ^ flip) for i in range(size)])  60 us
    ppermute x45, waiting for transfers between devices, over(): return lax.ppermute(array, axis, [(i, i ^ flip) for i in range(size)])  37 us
    pallas_call x18, Pallas kernels, call(): pl.pallas_call(body, out_shape=list(outs), in_specs=[pl.BlockSpec(memory_...  20.8 us
    pallas_call x6, Pallas kernels, blocks_call(): pl.pallas_call(body, grid=(1,), out_shape=outs, in_specs=[pl.BlockSpec(me...  13.6 us
    unnamed x54, local copies, waits for them, and re-layouts  3.36 us
  transfers between devices with their start and end apart: 45, of which 19 were waited for; matrix products, arithmetic and copies ran while one was open for 0% of the time, Pallas kernels for 20%

profile of v5, /device:TPU:0, one launch (start us, length us, event | category | flops | bytes accessed | tf_op | source)
XLA Modules:
  0.0 138.5 jit_solution(15237888559570392502)
XLA Ops:
  0.7 2.4 %begin.1 = (bf16[512,128]{1,0:T(8,128)(2,1)}, f32[8,128]{1,0:T(8,128)}, bf16[64,640]{1,0:T(8,128)(2,1)}, f32[16,128]{1,0:T(8,128)}) custom-call(bf16[512,128]{1,0:T(8,128)(2,1)} %bitcast.27, f32[3,128]{1,0:T(4,128)} %refs_1_.1, f32[3,128]{1,0:T(4,128)} %refs_2_.1, f32[2,128]{1,0:T(2,128)} %refs_3_.1, f32[3,128]{1,0:T(4,128)} %refs_4_.1, f32[1,64]{1,0:T(1,128)} %bitcast.31, ...), custom_call_target="tpu_custom_call" | custom-call | flops 99999997952 | bytes 1 | tf_op jit(solution)/shard_map/begin/pallas_call | solution.py:862
  3.1 5.1 %collective-permute-start.2 = (bf16[512,128]{1,0:T(8,128)(2,1)}, bf16[512,128]{1,0:T(8,128)(2,1)S(1)}, u32[]{:S(2)}, u32[]{:S(2)}) collective-permute-start(bf16[512,128]{1,0:T(8,128)(2,1)} %get-tuple-element.104.a0), channel_id=1, source_target_pairs={{0,3},{1,2},{2,1},{3,0},{4,7},{5,6},{6,5},{7,4},{8,11},{9,10},{10,... | collective-permute-start | bytes 393224 | tf_op jit(solution)/shard_map/ppermute | solution.py:794
  8.8 3.7 %collective-permute-start.11 = (bf16[64,640]{1,0:T(8,128)(2,1)}, bf16[64,640]{1,0:T(8,128)(2,1)S(1)}, u32[]{:S(2)}, u32[]{:S(2)}) collective-permute-start(bf16[64,640]{1,0:T(8,128)(2,1)} %get-tuple-element.117.refs_0_), channel_id=1, source_target_pairs={{0,3},{1,2},{2,1},{3,0},{4,7},{5,6},{6,5},{7,4},{8,11},{9,10},{10,... | collective-permute-start | bytes 245768 | tf_op jit(solution)/shard_map/ppermute | solution.py:794
  13.3 1.9 %start.1 = (bf16[512,1024]{1,0:T(8,128)(2,1)S(1)}, f32[512,64]{1,0:T(8,128)S(1)}, f32[8,128]{1,0:T(8,128)S(1)}, bf16[4,64,128]{2,1,0:T(8,128)(2,1)S(1)}) custom-call(s32[4]{0:T(128)S(1)} %pad_add_fusion.scalars.refs_0_, s32[2,16,16]{2,1,0:T(8,128)S(1)} %copy-done.11, f32[64,1024]{1,0:T(8,128)S(1)} %bitcast.18, bf16[512,64]{1,0:T(8,128)(2,1)S(1)} %bitcast.21, ...), custom_call_target="tpu_custom_call" | custom-call | bytes 1 | tf_op jit(solution)/shard_map/start/pallas_call | solution.py:25
  15.3 3.7 %collective-permute-start.9 = (bf16[64,640]{1,0:T(8,128)(2,1)}, bf16[64,640]{1,0:T(8,128)(2,1)S(1)}, u32[]{:S(2)}, u32[]{:S(2)}) collective-permute-start(bf16[64,640]{1,0:T(8,128)(2,1)} %get-tuple-element.117.refs_0_), channel_id=1, source_target_pairs={{0,1},{1,0},{2,3},{3,2},{4,5},{5,4},{6,7},{7,6},{8,9},{9,8},{10,11... | collective-permute-start | bytes 245768 | tf_op jit(solution)/shard_map/ppermute | solution.py:794
  19.0 4.9 %collective-permute-done.1.a2 = bf16[512,128]{1,0:T(8,128)(2,1)S(1)} collective-permute-done((bf16[512,128]{1,0:T(8,128)(2,1)}, bf16[512,128]{1,0:T(8,128)(2,1)S(1)}, u32[]{:S(2)}, u32[]{:S(2)}) %collective-permute-start.1) | collective-permute-done | bytes 131104 | tf_op jit(solution)/shard_map/ppermute | solution.py:794
  25.5 1.8 %conv_one.1 = (f32[512,128]{1,0:T(8,128)S(1)}, f32[8,128]{1,0:T(8,128)S(1)}, bf16[512,128]{1,0:T(8,128)(2,1)S(1)}) custom-call(s32[4]{0:T(128)S(1)} %pad_add_fusion.scalars.refs_0_, bf16[512,128]{1,0:T(8,128)(2,1)S(1)} %copy-done.20, bf16[512,128]{1,0:T(8,128)(2,1)S(1)} %collective-permute-done.a1, bf16[512,128]{1,0:T(8,128)(2,1)S(1)} %collective-permute-done.1.a2, ...), custom_call_target="tpu_custom_call" | custom-call | flops 99999997952 | bytes 1 | tf_op jit(solution)/shard_map/conv_one/pallas_call | solution.py:844
  27.4 2.7 %collective-permute-start.5 = (bf16[512,128]{1,0:T(8,128)(2,1)S(1)}, bf16[512,128]{1,0:T(8,128)(2,1)S(1)}, u32[]{:S(2)}, u32[]{:S(2)}) collective-permute-start(bf16[512,128]{1,0:T(8,128)(2,1)S(1)} %get-tuple-element.108.a0.refs_1_), channel_id=1, source_target_pairs={{0,3},{1,2},{2,1},{3,0},{4,7},{5,6},{6,5},{7,4},{8,11},{9,10},{10,... | collective-permute-start | bytes 393224 | tf_op jit(solution)/shard_map/ppermute | solution.py:794
  30.1 1.7 %collective-permute-start.3 = (bf16[512,128]{1,0:T(8,128)(2,1)S(1)}, bf16[512,128]{1,0:T(8,128)(2,1)S(1)}, u32[]{:S(2)}, u32[]{:S(2)}) collective-permute-start(bf16[512,128]{1,0:T(8,128)(2,1)S(1)} %get-tuple-element.108.a0.refs_1_), channel_id=1, source_target_pairs={{0,1},{1,0},{2,3},{3,2},{4,5},{5,4},{6,7},{7,6},{8,9},{9,8},{10,11... | collective-permute-start | bytes 393224 | tf_op jit(solution)/shard_map/ppermute | solution.py:794
  32.4 2.5 %collective-permute-start.14 = (bf16[4,64,640]{2,1,0:T(8,128)(2,1)S(1)}, bf16[4,64,640]{2,1,0:T(8,128)(2,1)S(1)}, u32[]{:S(2)}, u32[]{:S(2)}) collective-permute-start(bf16[4,64,640]{2,1,0:T(8,128)(2,1)S(1)} %pack_join.1.refs_0_), channel_id=1, source_target_pairs={{0,24},{4,28},{8,16},{12,20},{16,8},{20,12},{24,0},{28,4},{1,25},{... | collective-permute-start | bytes 983048 | tf_op jit(solution)/shard_map/ppermute | solution.py:794
  37.2 1.9 %collective-permute-done.4.a2.refs_3_ = bf16[512,128]{1,0:T(8,128)(2,1)S(1)} collective-permute-done((bf16[512,128]{1,0:T(8,128)(2,1)S(1)}, bf16[512,128]{1,0:T(8,128)(2,1)S(1)}, u32[]{:S(2)}, u32[]{:S(2)}) %collective-permute-start.4) | collective-permute-done | bytes 131104 | tf_op jit(solution)/shard_map/ppermute | solution.py:794
  39.1 1.9 %conv_two.1 = (f32[512,128]{1,0:T(8,128)S(1)}, f32[8,128]{1,0:T(8,128)S(1)}, bf16[464,128]{1,0:T(8,128)(2,1)S(1)}, bf16[464,128]{1,0:T(8,128)(2,1)S(1)}, bf16[46...) custom-call(s32[4]{0:T(128)S(1)} %pad_add_fusion.scalars.refs_0_, ...), custom_call_target="tpu_custom_call" | custom-call | flops 99999997952 | bytes 1 | tf_op jit(solution)/shard_map/conv_two/pallas_call | solution.py:844
  45.4 2.0 %collective-permute-done.13.refs_2_ = bf16[4,64,640]{2,1,0:T(8,128)(2,1)S(1)} collective-permute-done((bf16[4,64,640]{2,1,0:T(8,128)(2,1)S(1)}, bf16[4,64,640]{2,1,0:T(8,128)(2,1)S(1)}, u32[]{:S(2)}, u32[]{:S(2)}) %collective-permute-start.13) | collective-permute-done | bytes 327712 | tf_op jit(solution)/shard_map/ppermute | solution.py:794
  48.2 2.8 %collective-permute-done.7.n2 = bf16[464,128]{1,0:T(8,128)(2,1)S(1)} collective-permute-done((bf16[464,128]{1,0:T(8,128)(2,1)S(1)}, bf16[464,128]{1,0:T(8,128)(2,1)S(1)}, u32[]{:S(2)}, u32[]{:S(2)}) %collective-permute-start.7) | collective-permute-done | bytes 118816 | tf_op jit(solution)/shard_map/ppermute | solution.py:794
  51.7 4.7 %attention.1 = (f32[448,128]{1,0:T(8,128)S(1)}, bf16[448,128]{1,0:T(8,128)(2,1)S(1)}, bf16[448,128]{1,0:T(8,128)(2,1)S(1)}, bf16[448,128]{1,0:T(8,128)(2,1)S(1)}...) custom-call(s32[4]{0:T(128)S(1)} %pad_add_fusion.scalars.refs_0_, ...), custom_call_target="tpu_custom_call" | custom-call | flops 99999997952 | bytes 1 | tf_op jit(solution)/shard_map/attention/pallas_call | solution.py:25
  56.5 1.9 %collective-permute-start.16 = (bf16[448,128]{1,0:T(8,128)(2,1)S(1)}, bf16[448,128]{1,0:T(8,128)(2,1)S(1)}, u32[]{:S(2)}, u32[]{:S(2)}) collective-permute-start(bf16[448,128]{1,0:T(8,128)(2,1)S(1)} %get-tuple-element.119), channel_id=1, source_target_pairs={{0,1},{1,0},{2,3},{3,2},{4,5},{5,4},{6,7},{7,6},{8,9},{9,8},{10,11... | collective-permute-start | bytes 344072 | tf_op jit(solution)/shard_map/ppermute | solution.py:794
  64.6 5.7 %collective-permute-done.17.p2 = bf16[448,128]{1,0:T(8,128)(2,1)S(1)} collective-permute-done((bf16[448,128]{1,0:T(8,128)(2,1)S(1)}, bf16[448,128]{1,0:T(8,128)(2,1)S(1)}, u32[]{:S(2)}, u32[]{:S(2)}) %collective-permute-start.17) | collective-permute-done | bytes 114720 | tf_op jit(solution)/shard_map/ppermute | solution.py:794
  70.3 2.4 %third_back.1 = (f32[512,128]{1,0:T(8,128)S(1)}, bf16[512,1152]{1,0:T(8,128)(2,1)S(1)}, f32[512,64]{1,0:T(8,128)}, f32[8,128]{1,0:T(8,128)S(1)}, f32[512,128]{1,...) custom-call(s32[4]{0:T(128)S(1)} %pad_add_fusion.scalars.refs_0_, ...), custom_call_target="tpu_custom_call" | custom-call | flops 99999997952 | bytes 1 | tf_op jit(solution)/shard_map/third_back/pallas_call | solution.py:844
  72.7 2.2 %collective-permute-start.20 = (bf16[512,128]{1,0:T(8,128)(2,1)S(1)}, bf16[512,128]{1,0:T(8,128)(2,1)S(1)}, u32[]{:S(2)}, u32[]{:S(2)}) collective-permute-start(bf16[512,128]{1,0:T(8,128)(2,1)S(1)} %get-tuple-element.132), channel_id=1, source_target_pairs={{0,1},{1,0},{2,3},{3,2},{4,5},{5,4},{6,7},{7,6},{8,9},{9,8},{10,11... | collective-permute-start | bytes 393224 | tf_op jit(solution)/shard_map/ppermute | solution.py:794
  78.4 1.8 %conv_two_grad.1 = (bf16[64,1408]{1,0:T(8,128)(2,1)S(1)}, bf16[64,1408]{1,0:T(8,128)(2,1)S(1)}, bf16[64,1408]{1,0:T(8,128)(2,1)S(1)}, bf16[64,1408]{1,0:T(8,128)...) custom-call(s32[4]{0:T(128)S(1)} %pad_add_fusion.scalars.refs_0_, bf16[512,128]{1,0:T(8,128)(2,1)S(1)} %copy-done.3, ...), custom_call_target="tpu_custom_call" | custom-call | bytes 1 | tf_op jit(solution)/shard_map/conv_two_grad/pallas_call | solution.py:25
  81.0 1.6 %collective-permute-start.26 = (bf16[4,64,640]{2,1,0:T(8,128)(2,1)S(1)}, bf16[4,64,640]{2,1,0:T(8,128)(2,1)S(1)}, u32[]{:S(2)}, u32[]{:S(2)}) collective-permute-start(bf16[4,64,640]{2,1,0:T(8,128)(2,1)S(1)} %get-tuple-element.154), channel_id=1, source_target_pairs={{0,16},{4,20},{8,24},{12,28},{16,0},{20,4},{24,8},{28,12},{1,17},{... | collective-permute-start | bytes 983048 | tf_op jit(solution)/shard_map/ppermute | solution.py:794
  84.9 2.5 %collective-permute-done.21.p2 = bf16[512,128]{1,0:T(8,128)(2,1)S(1)} collective-permute-done((bf16[512,128]{1,0:T(8,128)(2,1)S(1)}, bf16[512,128]{1,0:T(8,128)(2,1)S(1)}, u32[]{:S(2)}, u32[]{:S(2)}) %collective-permute-start.21) | collective-permute-done | bytes 131104 | tf_op jit(solution)/shard_map/ppermute | solution.py:794
  87.4 2.7 %second_back.1 = (f32[8,128]{1,0:T(8,128)S(1)}, f32[512,128]{1,0:T(8,128)S(1)}, bf16[512,128]{1,0:T(8,128)(2,1)S(1)}, bf16[512,128]{1,0:T(8,128)(2,1)S(1)}, bf16...) custom-call(s32[4]{0:T(128)S(1)} %pad_add_fusion.scalars.refs_0_, ...), custom_call_target="tpu_custom_call" | custom-call | flops 99999997952 | bytes 1 | tf_op jit(solution)/shard_map/second_back/pallas_call | solution.py:844
  97.0 1.9 %collective-permute-start.34 = (bf16[512,128]{1,0:T(8,128)(2,1)S(1)}, bf16[512,128]{1,0:T(8,128)(2,1)S(1)}, u32[]{:S(2)}, u32[]{:S(2)}) collective-permute-start(bf16[512,128]{1,0:T(8,128)(2,1)S(1)} %get-tuple-element.171), channel_id=1, source_target_pairs={{0,2},{1,3},{2,0},{3,1},{4,6},{5,7},{6,4},{7,5},{8,10},{9,11},{10,... | collective-permute-start | bytes 393224 | tf_op jit(solution)/shard_map/ppermute | solution.py:794
  107.0 4.6 %collective-permute-done.34.p2 = bf16[512,128]{1,0:T(8,128)(2,1)S(1)} collective-permute-done((bf16[512,128]{1,0:T(8,128)(2,1)S(1)}, bf16[512,128]{1,0:T(8,128)(2,1)S(1)}, u32[]{:S(2)}, u32[]{:S(2)}) %collective-permute-start.34) | collective-permute-done | bytes 131104 | tf_op jit(solution)/shard_map/ppermute | solution.py:794
  112.8 1.7 %collective-permute-start.43 = (bf16[64,1408]{1,0:T(8,128)(2,1)}, bf16[64,1408]{1,0:T(8,128)(2,1)}, u32[]{:S(2)}, u32[]{:S(2)}) collective-permute-start(bf16[64,1408]{1,0:T(8,128)(2,1)} %conv_two_sum.1.__.refs_0_), channel_id=1, source_target_pairs={{0,24},{4,28},{8,16},{12,20},{16,8},{20,12},{24,0},{28,4},{1,25},{... | collective-permute-start | bytes 540680 | tf_op jit(solution)/shard_map/ppermute | solution.py:794
  114.5 2.1 %first_back.1 = (f32[512,128]{1,0:T(8,128)}, f32[8,128]{1,0:T(8,128)S(1)}) custom-call(s32[4]{0:T(128)S(1)} %pad_add_fusion.scalars.refs_0_, f32[512,128]{1,0:T(8,128)S(1)} %get-tuple-element.169.p0, bf16[512,128]{1,0:T(8,128)(2,1)S(1)} %collective-permute-done.33.p1, bf16[512,128]{1,0:T(8,128)(2,1)S(1)} %collective-permute-done.34.p2, ...), custom_call_target="tpu_custom_call" | custom-call | flops 99999997952 | bytes 1 | tf_op jit(solution)/shard_map/first_back/pallas_call | solution.py:25
  120.9 1.6 %collective-permute-start.38 = (bf16[64,1792]{1,0:T(8,128)(2,1)S(1)}, bf16[64,1792]{1,0:T(8,128)(2,1)S(1)}, u32[]{:S(2)}, u32[]{:S(2)}) collective-permute-start(bf16[64,1792]{1,0:T(8,128)(2,1)S(1)} %last.1.refs_0_.refs_4_), channel_id=1, source_target_pairs={{0,16},{4,20},{8,24},{12,28},{16,0},{20,4},{24,8},{28,12},{1,17},{... | collective-permute-start | bytes 688136 | tf_op jit(solution)/shard_map/ppermute | solution.py:794
  124.3 4.4 %collective-permute-done.42.refs_2_ = bf16[64,1408]{1,0:T(8,128)(2,1)S(1)} collective-permute-done((bf16[64,1408]{1,0:T(8,128)(2,1)}, bf16[64,1408]{1,0:T(8,128)(2,1)S(1)}, u32[]{:S(2)}, u32[]{:S(2)}) %collective-permute-start.42) | collective-permute-done | bytes 180256 | tf_op jit(solution)/shard_map/ppermute | solution.py:794
  130.9 1.7 %collective-permute-done.38.refs_2_ = bf16[64,1792]{1,0:T(8,128)(2,1)S(1)} collective-permute-done((bf16[64,1792]{1,0:T(8,128)(2,1)S(1)}, bf16[64,1792]{1,0:T(8,128)(2,1)S(1)}, u32[]{:S(2)}, u32[]{:S(2)}) %collective-permute-start.38) | collective-permute-done | bytes 229408 | tf_op jit(solution)/shard_map/ppermute | solution.py:794
  133.3 2.2 %finish_two.1 = (f32[2,9,512,128]{3,2,1,0:T(8,128)}, f32[64,1024]{1,0:T(8,128)}, f32[64,1024]{1,0:T(8,128)S(1)}) custom-call(s32[4]{0:T(128)S(1)} %pad_add_fusion.scalars.refs_0_, bf16[4,64,1408]{2,1,0:T(8,128)(2,1)S(1)} %stack_two.1.own_ref, bf16[4,64,1408]{2,1,0:T(8,128)(2,1)S(1)} %collective-permute-done.44.other_ref), custom_call_target="tpu_custom_call" | custom-call | flops 99999997952 | bytes 1 | tf_op jit(solution)/shard_map/finish_two/pallas_call | solution.py:844
  135.7 2.6 %finish_last.1 = (f32[2,9,512,128]{3,2,1,0:T(8,128)}, f32[3,128]{1,0:T(4,128)}, f32[3,128]{1,0:T(4,128)}, f32[2,128]{1,0:T(2,128)}, f32[1,64]{1,0:T(1,128)}, /*i...) custom-call(s32[4]{0:T(128)S(1)} %pad_add_fusion.scalars.refs_0_, ...), custom_call_target="tpu_custom_call", output_to_operand_aliasing={{0}: (5, {})} | custom-call | flops 99999997952 | bytes 1 | tf_op jit(solution)/shard_map/finish_last/pallas_call | solution.py:844
  (138 shorter events, 49.9 us)
Async XLA Ops:
  3.1 12.2 %collective-permute-start.2 = (bf16[512,128]{1,0:T(8,128)(2,1)}, bf16[512,128]{1,0:T(8,128)(2,1)S(1)}, u32[]{:S(2)}, u32[]{:S(2)}) collective-permute-start(bf16[512,128]{1,0:T(8,128)(2,1)} %get-tuple-element.104.a0), channel_id=1, source_target_pairs={{0,3},{1,2},{2,1},{3,0},{4,7},{5,6},{6,5},{7,4},{8,11},{9,10},{10,... | collective-permute-start | bytes 393224 | tf_op jit(solution)/shard_map/ppermute | solution.py:794
  8.2 15.8 %collective-permute-start.1 = (bf16[512,128]{1,0:T(8,128)(2,1)}, bf16[512,128]{1,0:T(8,128)(2,1)S(1)}, u32[]{:S(2)}, u32[]{:S(2)}) collective-permute-start(bf16[512,128]{1,0:T(8,128)(2,1)} %get-tuple-element.104.a0), channel_id=1, source_target_pairs={{0,2},{1,3},{2,0},{3,1},{4,6},{5,7},{6,4},{7,5},{8,10},{9,11},{10,... | collective-permute-start | bytes 393224 | tf_op jit(solution)/shard_map/ppermute | solution.py:794
  8.2 15.8 %collective-permute-start = (bf16[512,128]{1,0:T(8,128)(2,1)}, bf16[512,128]{1,0:T(8,128)(2,1)S(1)}, u32[]{:S(2)}, u32[]{:S(2)}) collective-permute-start(bf16[512,128]{1,0:T(8,128)(2,1)} %get-tuple-element.104.a0), channel_id=1, source_target_pairs={{0,1},{1,0},{2,3},{3,2},{4,5},{5,4},{6,7},{7,6},{8,9},{9,8},{10,11... | collective-permute-start | bytes 393224 | tf_op jit(solution)/shard_map/ppermute | solution.py:794
  8.8 21.3 %collective-permute-start.11 = (bf16[64,640]{1,0:T(8,128)(2,1)}, bf16[64,640]{1,0:T(8,128)(2,1)S(1)}, u32[]{:S(2)}, u32[]{:S(2)}) collective-permute-start(bf16[64,640]{1,0:T(8,128)(2,1)} %get-tuple-element.117.refs_0_), channel_id=1, source_target_pairs={{0,3},{1,2},{2,1},{3,0},{4,7},{5,6},{6,5},{7,4},{8,11},{9,10},{10,... | collective-permute-start | bytes 245768 | tf_op jit(solution)/shard_map/ppermute | solution.py:794
  12.6 19.3 %collective-permute-start.10 = (bf16[64,640]{1,0:T(8,128)(2,1)}, bf16[64,640]{1,0:T(8,128)(2,1)S(1)}, u32[]{:S(2)}, u32[]{:S(2)}) collective-permute-start(bf16[64,640]{1,0:T(8,128)(2,1)} %get-tuple-element.117.refs_0_), channel_id=1, source_target_pairs={{0,2},{1,3},{2,0},{3,1},{4,6},{5,7},{6,4},{7,5},{8,10},{9,11},{10,... | collective-permute-start | bytes 245768 | tf_op jit(solution)/shard_map/ppermute | solution.py:794
  15.3 16.6 %collective-permute-start.9 = (bf16[64,640]{1,0:T(8,128)(2,1)}, bf16[64,640]{1,0:T(8,128)(2,1)S(1)}, u32[]{:S(2)}, u32[]{:S(2)}) collective-permute-start(bf16[64,640]{1,0:T(8,128)(2,1)} %get-tuple-element.117.refs_0_), channel_id=1, source_target_pairs={{0,1},{1,0},{2,3},{3,2},{4,5},{5,4},{6,7},{7,6},{8,9},{9,8},{10,11... | collective-permute-start | bytes 245768 | tf_op jit(solution)/shard_map/ppermute | solution.py:794
  30.1 8.9 %collective-permute-start.4 = (bf16[512,128]{1,0:T(8,128)(2,1)S(1)}, bf16[512,128]{1,0:T(8,128)(2,1)S(1)}, u32[]{:S(2)}, u32[]{:S(2)}) collective-permute-start(bf16[512,128]{1,0:T(8,128)(2,1)S(1)} %get-tuple-element.108.a0.refs_1_), channel_id=1, source_target_pairs={{0,2},{1,3},{2,0},{3,1},{4,6},{5,7},{6,4},{7,5},{8,10},{9,11},{10,... | collective-permute-start | bytes 393224 | tf_op jit(solution)/shard_map/ppermute | solution.py:794
  32.4 11.5 %collective-permute-start.14 = (bf16[4,64,640]{2,1,0:T(8,128)(2,1)S(1)}, bf16[4,64,640]{2,1,0:T(8,128)(2,1)S(1)}, u32[]{:S(2)}, u32[]{:S(2)}) collective-permute-start(bf16[4,64,640]{2,1,0:T(8,128)(2,1)S(1)} %pack_join.1.refs_0_), channel_id=1, source_target_pairs={{0,24},{4,28},{8,16},{12,20},{16,8},{20,12},{24,0},{28,4},{1,25},{... | collective-permute-start | bytes 983048 | tf_op jit(solution)/shard_map/ppermute | solution.py:794
  35.0 12.4 %collective-permute-start.13 = (bf16[4,64,640]{2,1,0:T(8,128)(2,1)S(1)}, bf16[4,64,640]{2,1,0:T(8,128)(2,1)S(1)}, u32[]{:S(2)}, u32[]{:S(2)}) collective-permute-start(bf16[4,64,640]{2,1,0:T(8,128)(2,1)S(1)} %pack_join.1.refs_0_), channel_id=1, source_target_pairs={{0,16},{4,20},{8,24},{12,28},{16,0},{20,4},{24,8},{28,12},{1,17},{... | collective-permute-start | bytes 983048 | tf_op jit(solution)/shard_map/ppermute | solution.py:794
  35.7 11.8 %collective-permute-start.12 = (bf16[4,64,640]{2,1,0:T(8,128)(2,1)S(1)}, bf16[4,64,640]{2,1,0:T(8,128)(2,1)S(1)}, u32[]{:S(2)}, u32[]{:S(2)}) collective-permute-start(bf16[4,64,640]{2,1,0:T(8,128)(2,1)S(1)} %pack_join.1.refs_0_), channel_id=1, source_target_pairs={{0,8},{4,12},{8,0},{12,4},{16,24},{20,28},{24,16},{28,20},{1,9},{5... | collective-permute-start | bytes 983048 | tf_op jit(solution)/shard_map/ppermute | solution.py:794
  41.7 9.3 %collective-permute-start.7 = (bf16[464,128]{1,0:T(8,128)(2,1)S(1)}, bf16[464,128]{1,0:T(8,128)(2,1)S(1)}, u32[]{:S(2)}, u32[]{:S(2)}) collective-permute-start(bf16[464,128]{1,0:T(8,128)(2,1)S(1)} %get-tuple-element.112), channel_id=1, source_target_pairs={{0,2},{1,3},{2,0},{3,1},{4,6},{5,7},{6,4},{7,5},{8,10},{9,11},{10,... | collective-permute-start | bytes 356360 | tf_op jit(solution)/shard_map/ppermute | solution.py:794
  58.4 11.8 %collective-permute-start.17 = (bf16[448,128]{1,0:T(8,128)(2,1)S(1)}, bf16[448,128]{1,0:T(8,128)(2,1)S(1)}, u32[]{:S(2)}, u32[]{:S(2)}) collective-permute-start(bf16[448,128]{1,0:T(8,128)(2,1)S(1)} %get-tuple-element.120), channel_id=1, source_target_pairs={{0,2},{1,3},{2,0},{3,1},{4,6},{5,7},{6,4},{7,5},{8,10},{9,11},{10,... | collective-permute-start | bytes 344072 | tf_op jit(solution)/shard_map/ppermute | solution.py:794
  59.6 10.7 %collective-permute-start.18 = (bf16[448,128]{1,0:T(8,128)(2,1)S(1)}, bf16[448,128]{1,0:T(8,128)(2,1)S(1)}, u32[]{:S(2)}, u32[]{:S(2)}) collective-permute-start(bf16[448,128]{1,0:T(8,128)(2,1)S(1)} %get-tuple-element.121), channel_id=1, source_target_pairs={{0,3},{1,2},{2,1},{3,0},{4,7},{5,6},{6,5},{7,4},{8,11},{9,10},{10,... | collective-permute-start | bytes 344072 | tf_op jit(solution)/shard_map/ppermute | solution.py:794
  63.0 17.2 %collective-permute-start.23 = (bf16[2,4,64,640]{3,2,1,0:T(8,128)(2,1)S(1)}, bf16[2,4,64,640]{3,2,1,0:T(8,128)(2,1)S(1)}, u32[]{:S(2)}, u32[]{:S(2)}) collective-permute-start(bf16[2,4,64,640]{3,2,1,0:T(8,128)(2,1)S(1)} %get-tuple-element.137), channel_id=1, source_target_pairs={{0,8},{4,12},{8,0},{12,4},{16,24},{20,28},{24,16},{28,20},{1,9},{5... | collective-permute-start | bytes 1966088 | tf_op jit(solution)/shard_map/ppermute | solution.py:794
  72.7 12.1 %collective-permute-start.20 = (bf16[512,128]{1,0:T(8,128)(2,1)S(1)}, bf16[512,128]{1,0:T(8,128)(2,1)S(1)}, u32[]{:S(2)}, u32[]{:S(2)}) collective-permute-start(bf16[512,128]{1,0:T(8,128)(2,1)S(1)} %get-tuple-element.132), channel_id=1, source_target_pairs={{0,1},{1,0},{2,3},{3,2},{4,5},{5,4},{6,7},{7,6},{8,9},{9,8},{10,11... | collective-permute-start | bytes 393224 | tf_op jit(solution)/shard_map/ppermute | solution.py:794
  74.9 12.4 %collective-permute-start.21 = (bf16[512,128]{1,0:T(8,128)(2,1)S(1)}, bf16[512,128]{1,0:T(8,128)(2,1)S(1)}, u32[]{:S(2)}, u32[]{:S(2)}) collective-permute-start(bf16[512,128]{1,0:T(8,128)(2,1)S(1)} %get-tuple-element.133), channel_id=1, source_target_pairs={{0,2},{1,3},{2,0},{3,1},{4,6},{5,7},{6,4},{7,5},{8,10},{9,11},{10,... | collective-permute-start | bytes 393224 | tf_op jit(solution)/shard_map/ppermute | solution.py:794
  75.9 11.4 %collective-permute-start.22 = (bf16[512,128]{1,0:T(8,128)(2,1)S(1)}, bf16[512,128]{1,0:T(8,128)(2,1)S(1)}, u32[]{:S(2)}, u32[]{:S(2)}) collective-permute-start(bf16[512,128]{1,0:T(8,128)(2,1)S(1)} %get-tuple-element.134), channel_id=1, source_target_pairs={{0,3},{1,2},{2,1},{3,0},{4,7},{5,6},{6,5},{7,4},{8,11},{9,10},{10,... | collective-permute-start | bytes 393224 | tf_op jit(solution)/shard_map/ppermute | solution.py:794
  81.0 10.2 %collective-permute-start.26 = (bf16[4,64,640]{2,1,0:T(8,128)(2,1)S(1)}, bf16[4,64,640]{2,1,0:T(8,128)(2,1)S(1)}, u32[]{:S(2)}, u32[]{:S(2)}) collective-permute-start(bf16[4,64,640]{2,1,0:T(8,128)(2,1)S(1)} %get-tuple-element.154), channel_id=1, source_target_pairs={{0,16},{4,20},{8,24},{12,28},{16,0},{20,4},{24,8},{28,12},{1,17},{... | collective-permute-start | bytes 983048 | tf_op jit(solution)/shard_map/ppermute | solution.py:794
  83.3 10.6 %collective-permute-start.31 = (bf16[2,64,1408]{2,1,0:T(8,128)(2,1)S(1)}, bf16[2,64,1408]{2,1,0:T(8,128)(2,1)S(1)}, u32[]{:S(2)}, u32[]{:S(2)}) collective-permute-start(bf16[2,64,1408]{2,1,0:T(8,128)(2,1)S(1)} %get-tuple-element.162), channel_id=1, source_target_pairs={{0,8},{4,12},{8,0},{12,4},{16,24},{20,28},{24,16},{28,20},{1,9},{5... | collective-permute-start | bytes 1081352 | tf_op jit(solution)/shard_map/ppermute | solution.py:794
  90.1 10.9 %collective-permute-start.25 = (bf16[4,64,1152]{2,1,0:T(8,128)(2,1)S(1)}, bf16[4,64,1152]{2,1,0:T(8,128)(2,1)S(1)}, u32[]{:S(2)}, u32[]{:S(2)}) collective-permute-start(bf16[4,64,1152]{2,1,0:T(8,128)(2,1)S(1)} %get-tuple-element.153), channel_id=1, source_target_pairs={{0,4},{4,0},{8,12},{12,8},{16,20},{20,16},{24,28},{28,24},{1,5},{5... | collective-permute-start | bytes 1769480 | tf_op jit(solution)/shard_map/ppermute | solution.py:794
  95.9 9.7 %collective-permute-start.33 = (bf16[512,128]{1,0:T(8,128)(2,1)S(1)}, bf16[512,128]{1,0:T(8,128)(2,1)S(1)}, u32[]{:S(2)}, u32[]{:S(2)}) collective-permute-start(bf16[512,128]{1,0:T(8,128)(2,1)S(1)} %get-tuple-element.170), channel_id=1, source_target_pairs={{0,1},{1,0},{2,3},{3,2},{4,5},{5,4},{6,7},{7,6},{8,9},{9,8},{10,11... | collective-permute-start | bytes 393224 | tf_op jit(solution)/shard_map/ppermute | solution.py:794
  97.0 14.6 %collective-permute-start.34 = (bf16[512,128]{1,0:T(8,128)(2,1)S(1)}, bf16[512,128]{1,0:T(8,128)(2,1)S(1)}, u32[]{:S(2)}, u32[]{:S(2)}) collective-permute-start(bf16[512,128]{1,0:T(8,128)(2,1)S(1)} %get-tuple-element.171), channel_id=1, source_target_pairs={{0,2},{1,3},{2,0},{3,1},{4,6},{5,7},{6,4},{7,5},{8,10},{9,11},{10,... | collective-permute-start | bytes 393224 | tf_op jit(solution)/shard_map/ppermute | solution.py:794
  98.9 14.0 %collective-permute-start.35 = (bf16[512,128]{1,0:T(8,128)(2,1)S(1)}, bf16[512,128]{1,0:T(8,128)(2,1)S(1)}, u32[]{:S(2)}, u32[]{:S(2)}) collective-permute-start(bf16[512,128]{1,0:T(8,128)(2,1)S(1)} %get-tuple-element.172), channel_id=1, source_target_pairs={{0,3},{1,2},{2,1},{3,0},{4,7},{5,6},{6,5},{7,4},{8,11},{9,10},{10,... | collective-permute-start | bytes 393224 | tf_op jit(solution)/shard_map/ppermute | solution.py:794
  100.9 15.7 %collective-permute-start.32 = (bf16[64,640]{1,0:T(8,128)(2,1)S(1)}, bf16[64,640]{1,0:T(8,128)(2,1)S(1)}, u32[]{:S(2)}, u32[]{:S(2)}) collective-permute-start(bf16[64,640]{1,0:T(8,128)(2,1)S(1)} %get-tuple-element.168), channel_id=1, source_target_pairs={{0,2},{1,3},{2,0},{3,1},{4,6},{5,7},{6,4},{7,5},{8,10},{9,11},{10,... | collective-permute-start | bytes 245768 | tf_op jit(solution)/shard_map/ppermute | solution.py:794
  102.8 14.1 %collective-permute-start.27 = (bf16[64,1152]{1,0:T(8,128)(2,1)S(1)}, bf16[64,1152]{1,0:T(8,128)(2,1)S(1)}, u32[]{:S(2)}, u32[]{:S(2)}) collective-permute-start(bf16[64,1152]{1,0:T(8,128)(2,1)S(1)} %get-tuple-element.158), channel_id=1, source_target_pairs={{0,8},{4,12},{8,0},{12,4},{16,24},{20,28},{24,16},{28,20},{1,9},{5... | collective-permute-start | bytes 442376 | tf_op jit(solution)/shard_map/ppermute | solution.py:794
  105.6 12.8 %collective-permute-start.28 = (bf16[64,1152]{1,0:T(8,128)(2,1)S(1)}, bf16[64,1152]{1,0:T(8,128)(2,1)S(1)}, u32[]{:S(2)}, u32[]{:S(2)}) collective-permute-start(bf16[64,1152]{1,0:T(8,128)(2,1)S(1)} %get-tuple-element.159), channel_id=1, source_target_pairs={{0,16},{4,20},{8,24},{12,28},{16,0},{20,4},{24,8},{28,12},{1,17},{... | collective-permute-start | bytes 442376 | tf_op jit(solution)/shard_map/ppermute | solution.py:794
  112.8 10.0 %collective-permute-start.43 = (bf16[64,1408]{1,0:T(8,128)(2,1)}, bf16[64,1408]{1,0:T(8,128)(2,1)}, u32[]{:S(2)}, u32[]{:S(2)}) collective-permute-start(bf16[64,1408]{1,0:T(8,128)(2,1)} %conv_two_sum.1.__.refs_0_), channel_id=1, source_target_pairs={{0,24},{4,28},{8,16},{12,20},{16,8},{20,12},{24,0},{28,4},{1,25},{... | collective-permute-start | bytes 540680 | tf_op jit(solution)/shard_map/ppermute | solution.py:794
  116.6 12.1 %collective-permute-start.42 = (bf16[64,1408]{1,0:T(8,128)(2,1)}, bf16[64,1408]{1,0:T(8,128)(2,1)S(1)}, u32[]{:S(2)}, u32[]{:S(2)}) collective-permute-start(bf16[64,1408]{1,0:T(8,128)(2,1)} %conv_two_sum.1.__.refs_0_), channel_id=1, source_target_pairs={{0,16},{4,20},{8,24},{12,28},{16,0},{20,4},{24,8},{28,12},{1,17},{... | collective-permute-start | bytes 540680 | tf_op jit(solution)/shard_map/ppermute | solution.py:794
  117.0 11.8 %collective-permute-start.41 = (bf16[64,1408]{1,0:T(8,128)(2,1)}, bf16[64,1408]{1,0:T(8,128)(2,1)S(1)}, u32[]{:S(2)}, u32[]{:S(2)}) collective-permute-start(bf16[64,1408]{1,0:T(8,128)(2,1)} %conv_two_sum.1.__.refs_0_), channel_id=1, source_target_pairs={{0,8},{4,12},{8,0},{12,4},{16,24},{20,28},{24,16},{28,20},{1,9},{5... | collective-permute-start | bytes 540680 | tf_op jit(solution)/shard_map/ppermute | solution.py:794
  119.5 11.4 %collective-permute-start.39 = (bf16[64,1792]{1,0:T(8,128)(2,1)S(1)}, bf16[64,1792]{1,0:T(8,128)(2,1)S(1)}, u32[]{:S(2)}, u32[]{:S(2)}) collective-permute-start(bf16[64,1792]{1,0:T(8,128)(2,1)S(1)} %last.1.refs_0_.refs_4_), channel_id=1, source_target_pairs={{0,24},{4,28},{8,16},{12,20},{16,8},{20,12},{24,0},{28,4},{1,25},{... | collective-permute-start | bytes 688136 | tf_op jit(solution)/shard_map/ppermute | solution.py:794
  120.9 11.6 %collective-permute-start.38 = (bf16[64,1792]{1,0:T(8,128)(2,1)S(1)}, bf16[64,1792]{1,0:T(8,128)(2,1)S(1)}, u32[]{:S(2)}, u32[]{:S(2)}) collective-permute-start(bf16[64,1792]{1,0:T(8,128)(2,1)S(1)} %last.1.refs_0_.refs_4_), channel_id=1, source_target_pairs={{0,16},{4,20},{8,24},{12,28},{16,0},{20,4},{24,8},{28,12},{1,17},{... | collective-permute-start | bytes 688136 | tf_op jit(solution)/shard_map/ppermute | solution.py:794
  122.8 9.7 %collective-permute-start.37 = (bf16[64,1792]{1,0:T(8,128)(2,1)S(1)}, bf16[64,1792]{1,0:T(8,128)(2,1)S(1)}, u32[]{:S(2)}, u32[]{:S(2)}) collective-permute-start(bf16[64,1792]{1,0:T(8,128)(2,1)S(1)} %last.1.refs_0_.refs_4_), channel_id=1, source_target_pairs={{0,8},{4,12},{8,0},{12,4},{16,24},{20,28},{24,16},{28,20},{1,9},{5... | collective-permute-start | bytes 688136 | tf_op jit(solution)/shard_map/ppermute | solution.py:794
  (40 other events, 289.6 us)

commit v6 on v5

--- a/solution.py
+++ b/solution.py
@@ -1110,7 +1110,7 @@
             scalars,
             two_kept,
             two_got,
-            att_kept,
+            small_two,
             *pays[1:],
             flops=HEAVY,
             name="conv_two_half",

time: 139 us -> 139 us (level)
    unnamed x54 -> x50, local copies, waits for them, and re-layouts: 3.36 us -> 3.35 us
where the time goes in v6:
time: 139 us; the launch traced here: 138 us
  starting transfers between devices  59.6 us (43%)
  waiting for transfers between devices  37.3 us (27%)
  Pallas kernels  36.8 us (26%)
  local copies, waits for them, and re-layouts  3.35 us (2%)
    ppermute x45, starting transfers between devices, over(): return lax.ppermute(array, axis, [(i, i ^ flip) for i in range(size)])  59.6 us
    ppermute x45, waiting for transfers between devices, over(): return lax.ppermute(array, axis, [(i, i ^ flip) for i in range(size)])  37.3 us
    pallas_call x18, Pallas kernels, call(): pl.pallas_call(body, out_shape=list(outs), in_specs=[pl.BlockSpec(memory_...  20.8 us
    pallas_call x6, Pallas kernels, blocks_call(): pl.pallas_call(body, grid=(1,), out_shape=outs, in_specs=[pl.BlockSpec(me...  13.6 us
    unnamed x50, local copies, waits for them, and re-layouts  3.35 us
  transfers between devices with their start and end apart: 45, of which 19 were waited for; matrix products, arithmetic and copies ran while one was open for 0% of the time, Pallas kernels for 20%

profile of v6, /device:TPU:0, one launch (start us, length us, event | category | flops | bytes accessed | tf_op | source)
XLA Modules:
  0.0 138.5 jit_solution(18152373301235734537)
XLA Ops:
  0.7 2.4 %begin.1 = (bf16[512,128]{1,0:T(8,128)(2,1)}, f32[8,128]{1,0:T(8,128)}, bf16[64,640]{1,0:T(8,128)(2,1)}, f32[16,128]{1,0:T(8,128)}) custom-call(bf16[512,128]{1,0:T(8,128)(2,1)} %bitcast.27, f32[3,128]{1,0:T(4,128)} %refs_1_.1, f32[3,128]{1,0:T(4,128)} %refs_2_.1, f32[2,128]{1,0:T(2,128)} %refs_3_.1, f32[3,128]{1,0:T(4,128)} %refs_4_.1, f32[1,64]{1,0:T(1,128)} %bitcast.31, ...), custom_call_target="tpu_custom_call" | custom-call | flops 99999997952 | bytes 1 | tf_op jit(solution)/shard_map/begin/pallas_call | solution.py:862
  3.1 5.1 %collective-permute-start.2 = (bf16[512,128]{1,0:T(8,128)(2,1)}, bf16[512,128]{1,0:T(8,128)(2,1)S(1)}, u32[]{:S(2)}, u32[]{:S(2)}) collective-permute-start(bf16[512,128]{1,0:T(8,128)(2,1)} %get-tuple-element.104.a0), channel_id=1, source_target_pairs={{0,3},{1,2},{2,1},{3,0},{4,7},{5,6},{6,5},{7,4},{8,11},{9,10},{10,... | collective-permute-start | bytes 393224 | tf_op jit(solution)/shard_map/ppermute | solution.py:794
  8.8 3.7 %collective-permute-start.11 = (bf16[64,640]{1,0:T(8,128)(2,1)}, bf16[64,640]{1,0:T(8,128)(2,1)S(1)}, u32[]{:S(2)}, u32[]{:S(2)}) collective-permute-start(bf16[64,640]{1,0:T(8,128)(2,1)} %get-tuple-element.117.refs_0_), channel_id=1, source_target_pairs={{0,3},{1,2},{2,1},{3,0},{4,7},{5,6},{6,5},{7,4},{8,11},{9,10},{10,... | collective-permute-start | bytes 245768 | tf_op jit(solution)/shard_map/ppermute | solution.py:794
  13.3 1.9 %start.1 = (bf16[512,1024]{1,0:T(8,128)(2,1)S(1)}, f32[512,64]{1,0:T(8,128)S(1)}, f32[8,128]{1,0:T(8,128)S(1)}, bf16[4,64,128]{2,1,0:T(8,128)(2,1)S(1)}) custom-call(s32[4]{0:T(128)S(1)} %pad_add_fusion.scalars.refs_0_, s32[2,16,16]{2,1,0:T(8,128)S(1)} %copy-done.11, f32[64,1024]{1,0:T(8,128)S(1)} %bitcast.18, bf16[512,64]{1,0:T(8,128)(2,1)S(1)} %bitcast.21, ...), custom_call_target="tpu_custom_call" | custom-call | bytes 1 | tf_op jit(solution)/shard_map/start/pallas_call | solution.py:25
  15.3 3.7 %collective-permute-start.9 = (bf16[64,640]{1,0:T(8,128)(2,1)}, bf16[64,640]{1,0:T(8,128)(2,1)S(1)}, u32[]{:S(2)}, u32[]{:S(2)}) collective-permute-start(bf16[64,640]{1,0:T(8,128)(2,1)} %get-tuple-element.117.refs_0_), channel_id=1, source_target_pairs={{0,1},{1,0},{2,3},{3,2},{4,5},{5,4},{6,7},{7,6},{8,9},{9,8},{10,11... | collective-permute-start | bytes 245768 | tf_op jit(solution)/shard_map/ppermute | solution.py:794
  19.0 4.9 %collective-permute-done.1.a2 = bf16[512,128]{1,0:T(8,128)(2,1)S(1)} collective-permute-done((bf16[512,128]{1,0:T(8,128)(2,1)}, bf16[512,128]{1,0:T(8,128)(2,1)S(1)}, u32[]{:S(2)}, u32[]{:S(2)}) %collective-permute-start.1) | collective-permute-done | bytes 131104 | tf_op jit(solution)/shard_map/ppermute | solution.py:794
  25.5 1.8 %conv_one.1 = (f32[512,128]{1,0:T(8,128)S(1)}, f32[8,128]{1,0:T(8,128)S(1)}, bf16[512,128]{1,0:T(8,128)(2,1)S(1)}) custom-call(s32[4]{0:T(128)S(1)} %pad_add_fusion.scalars.refs_0_, bf16[512,128]{1,0:T(8,128)(2,1)S(1)} %copy-done.18, bf16[512,128]{1,0:T(8,128)(2,1)S(1)} %collective-permute-done.a1, bf16[512,128]{1,0:T(8,128)(2,1)S(1)} %collective-permute-done.1.a2, ...), custom_call_target="tpu_custom_call" | custom-call | flops 99999997952 | bytes 1 | tf_op jit(solution)/shard_map/conv_one/pallas_call | solution.py:844
  27.4 2.7 %collective-permute-start.5 = (bf16[512,128]{1,0:T(8,128)(2,1)S(1)}, bf16[512,128]{1,0:T(8,128)(2,1)S(1)}, u32[]{:S(2)}, u32[]{:S(2)}) collective-permute-start(bf16[512,128]{1,0:T(8,128)(2,1)S(1)} %get-tuple-element.108.a0.refs_1_), channel_id=1, source_target_pairs={{0,3},{1,2},{2,1},{3,0},{4,7},{5,6},{6,5},{7,4},{8,11},{9,10},{10,... | collective-permute-start | bytes 393224 | tf_op jit(solution)/shard_map/ppermute | solution.py:794
  30.1 1.7 %collective-permute-start.3 = (bf16[512,128]{1,0:T(8,128)(2,1)S(1)}, bf16[512,128]{1,0:T(8,128)(2,1)S(1)}, u32[]{:S(2)}, u32[]{:S(2)}) collective-permute-start(bf16[512,128]{1,0:T(8,128)(2,1)S(1)} %get-tuple-element.108.a0.refs_1_), channel_id=1, source_target_pairs={{0,1},{1,0},{2,3},{3,2},{4,5},{5,4},{6,7},{7,6},{8,9},{9,8},{10,11... | collective-permute-start | bytes 393224 | tf_op jit(solution)/shard_map/ppermute | solution.py:794
  32.4 2.5 %collective-permute-start.14 = (bf16[4,64,640]{2,1,0:T(8,128)(2,1)S(1)}, bf16[4,64,640]{2,1,0:T(8,128)(2,1)S(1)}, u32[]{:S(2)}, u32[]{:S(2)}) collective-permute-start(bf16[4,64,640]{2,1,0:T(8,128)(2,1)S(1)} %pack_join.1.refs_0_), channel_id=1, source_target_pairs={{0,24},{4,28},{8,16},{12,20},{16,8},{20,12},{24,0},{28,4},{1,25},{... | collective-permute-start | bytes 983048 | tf_op jit(solution)/shard_map/ppermute | solution.py:794
  37.2 1.9 %collective-permute-done.4.a2.refs_3_ = bf16[512,128]{1,0:T(8,128)(2,1)S(1)} collective-permute-done((bf16[512,128]{1,0:T(8,128)(2,1)S(1)}, bf16[512,128]{1,0:T(8,128)(2,1)S(1)}, u32[]{:S(2)}, u32[]{:S(2)}) %collective-permute-start.4) | collective-permute-done | bytes 131104 | tf_op jit(solution)/shard_map/ppermute | solution.py:794
  39.1 1.9 %conv_two.1 = (f32[512,128]{1,0:T(8,128)S(1)}, f32[8,128]{1,0:T(8,128)S(1)}, bf16[464,128]{1,0:T(8,128)(2,1)S(1)}, bf16[464,128]{1,0:T(8,128)(2,1)S(1)}, bf16[46...) custom-call(s32[4]{0:T(128)S(1)} %pad_add_fusion.scalars.refs_0_, ...), custom_call_target="tpu_custom_call" | custom-call | flops 99999997952 | bytes 1 | tf_op jit(solution)/shard_map/conv_two/pallas_call | solution.py:844
  45.4 2.0 %collective-permute-done.13.refs_2_ = bf16[4,64,640]{2,1,0:T(8,128)(2,1)S(1)} collective-permute-done((bf16[4,64,640]{2,1,0:T(8,128)(2,1)S(1)}, bf16[4,64,640]{2,1,0:T(8,128)(2,1)S(1)}, u32[]{:S(2)}, u32[]{:S(2)}) %collective-permute-start.13) | collective-permute-done | bytes 327712 | tf_op jit(solution)/shard_map/ppermute | solution.py:794
  48.2 2.8 %collective-permute-done.7.n2 = bf16[464,128]{1,0:T(8,128)(2,1)S(1)} collective-permute-done((bf16[464,128]{1,0:T(8,128)(2,1)S(1)}, bf16[464,128]{1,0:T(8,128)(2,1)S(1)}, u32[]{:S(2)}, u32[]{:S(2)}) %collective-permute-start.7) | collective-permute-done | bytes 118816 | tf_op jit(solution)/shard_map/ppermute | solution.py:794
  51.7 4.7 %attention.1 = (f32[448,128]{1,0:T(8,128)S(1)}, bf16[448,128]{1,0:T(8,128)(2,1)S(1)}, bf16[448,128]{1,0:T(8,128)(2,1)S(1)}, bf16[448,128]{1,0:T(8,128)(2,1)S(1)}...) custom-call(s32[4]{0:T(128)S(1)} %pad_add_fusion.scalars.refs_0_, ...), custom_call_target="tpu_custom_call" | custom-call | flops 99999997952 | bytes 1 | tf_op jit(solution)/shard_map/attention/pallas_call | solution.py:25
  56.5 1.9 %collective-permute-start.16 = (bf16[448,128]{1,0:T(8,128)(2,1)S(1)}, bf16[448,128]{1,0:T(8,128)(2,1)S(1)}, u32[]{:S(2)}, u32[]{:S(2)}) collective-permute-start(bf16[448,128]{1,0:T(8,128)(2,1)S(1)} %get-tuple-element.119), channel_id=1, source_target_pairs={{0,1},{1,0},{2,3},{3,2},{4,5},{5,4},{6,7},{7,6},{8,9},{9,8},{10,11... | collective-permute-start | bytes 344072 | tf_op jit(solution)/shard_map/ppermute | solution.py:794
  64.6 5.7 %collective-permute-done.17.p2 = bf16[448,128]{1,0:T(8,128)(2,1)S(1)} collective-permute-done((bf16[448,128]{1,0:T(8,128)(2,1)S(1)}, bf16[448,128]{1,0:T(8,128)(2,1)S(1)}, u32[]{:S(2)}, u32[]{:S(2)}) %collective-permute-start.17) | collective-permute-done | bytes 114720 | tf_op jit(solution)/shard_map/ppermute | solution.py:794
  70.3 2.4 %third_back.1 = (f32[512,128]{1,0:T(8,128)S(1)}, bf16[512,1152]{1,0:T(8,128)(2,1)S(1)}, f32[512,64]{1,0:T(8,128)}, f32[8,128]{1,0:T(8,128)S(1)}, f32[512,128]{1,...) custom-call(s32[4]{0:T(128)S(1)} %pad_add_fusion.scalars.refs_0_, ...), custom_call_target="tpu_custom_call" | custom-call | flops 99999997952 | bytes 1 | tf_op jit(solution)/shard_map/third_back/pallas_call | solution.py:844
  72.7 2.2 %collective-permute-start.20 = (bf16[512,128]{1,0:T(8,128)(2,1)S(1)}, bf16[512,128]{1,0:T(8,128)(2,1)S(1)}, u32[]{:S(2)}, u32[]{:S(2)}) collective-permute-start(bf16[512,128]{1,0:T(8,128)(2,1)S(1)} %get-tuple-element.132), channel_id=1, source_target_pairs={{0,1},{1,0},{2,3},{3,2},{4,5},{5,4},{6,7},{7,6},{8,9},{9,8},{10,11... | collective-permute-start | bytes 393224 | tf_op jit(solution)/shard_map/ppermute | solution.py:794
  78.4 1.8 %conv_two_grad.1 = (bf16[64,1408]{1,0:T(8,128)(2,1)S(1)}, bf16[64,1408]{1,0:T(8,128)(2,1)S(1)}, bf16[64,1408]{1,0:T(8,128)(2,1)S(1)}, bf16[64,1408]{1,0:T(8,128)...) custom-call(s32[4]{0:T(128)S(1)} %pad_add_fusion.scalars.refs_0_, bf16[512,128]{1,0:T(8,128)(2,1)S(1)} %copy-done.3, ...), custom_call_target="tpu_custom_call" | custom-call | bytes 1 | tf_op jit(solution)/shard_map/conv_two_grad/pallas_call | solution.py:25
  81.0 1.6 %collective-permute-start.26 = (bf16[4,64,640]{2,1,0:T(8,128)(2,1)S(1)}, bf16[4,64,640]{2,1,0:T(8,128)(2,1)S(1)}, u32[]{:S(2)}, u32[]{:S(2)}) collective-permute-start(bf16[4,64,640]{2,1,0:T(8,128)(2,1)S(1)} %get-tuple-element.154), channel_id=1, source_target_pairs={{0,16},{4,20},{8,24},{12,28},{16,0},{20,4},{24,8},{28,12},{1,17},{... | collective-permute-start | bytes 983048 | tf_op jit(solution)/shard_map/ppermute | solution.py:794
  83.3 1.6 %collective-permute-start.31 = (bf16[2,64,1408]{2,1,0:T(8,128)(2,1)S(1)}, bf16[2,64,1408]{2,1,0:T(8,128)(2,1)S(1)}, u32[]{:S(2)}, u32[]{:S(2)}) collective-permute-start(bf16[2,64,1408]{2,1,0:T(8,128)(2,1)S(1)} %get-tuple-element.162), channel_id=1, source_target_pairs={{0,8},{4,12},{8,0},{12,4},{16,24},{20,28},{24,16},{28,20},{1,9},{5... | collective-permute-start | bytes 1081352 | tf_op jit(solution)/shard_map/ppermute | solution.py:794
  84.9 2.5 %collective-permute-done.21.p2 = bf16[512,128]{1,0:T(8,128)(2,1)S(1)} collective-permute-done((bf16[512,128]{1,0:T(8,128)(2,1)S(1)}, bf16[512,128]{1,0:T(8,128)(2,1)S(1)}, u32[]{:S(2)}, u32[]{:S(2)}) %collective-permute-start.21) | collective-permute-done | bytes 131104 | tf_op jit(solution)/shard_map/ppermute | solution.py:794
  87.4 2.7 %second_back.1 = (f32[8,128]{1,0:T(8,128)S(1)}, f32[512,128]{1,0:T(8,128)S(1)}, bf16[512,128]{1,0:T(8,128)(2,1)S(1)}, bf16[512,128]{1,0:T(8,128)(2,1)S(1)}, bf16...) custom-call(s32[4]{0:T(128)S(1)} %pad_add_fusion.scalars.refs_0_, ...), custom_call_target="tpu_custom_call" | custom-call | flops 99999997952 | bytes 1 | tf_op jit(solution)/shard_map/second_back/pallas_call | solution.py:844
  96.9 1.9 %collective-permute-start.34 = (bf16[512,128]{1,0:T(8,128)(2,1)S(1)}, bf16[512,128]{1,0:T(8,128)(2,1)S(1)}, u32[]{:S(2)}, u32[]{:S(2)}) collective-permute-start(bf16[512,128]{1,0:T(8,128)(2,1)S(1)} %get-tuple-element.171), channel_id=1, source_target_pairs={{0,2},{1,3},{2,0},{3,1},{4,6},{5,7},{6,4},{7,5},{8,10},{9,11},{10,... | collective-permute-start | bytes 393224 | tf_op jit(solution)/shard_map/ppermute | solution.py:794
  107.0 4.6 %collective-permute-done.34.p2 = bf16[512,128]{1,0:T(8,128)(2,1)S(1)} collective-permute-done((bf16[512,128]{1,0:T(8,128)(2,1)S(1)}, bf16[512,128]{1,0:T(8,128)(2,1)S(1)}, u32[]{:S(2)}, u32[]{:S(2)}) %collective-permute-start.34) | collective-permute-done | bytes 131104 | tf_op jit(solution)/shard_map/ppermute | solution.py:794
  112.9 1.7 %collective-permute-start.43 = (bf16[64,1408]{1,0:T(8,128)(2,1)}, bf16[64,1408]{1,0:T(8,128)(2,1)}, u32[]{:S(2)}, u32[]{:S(2)}) collective-permute-start(bf16[64,1408]{1,0:T(8,128)(2,1)} %conv_two_sum.1.__.refs_0_), channel_id=1, source_target_pairs={{0,24},{4,28},{8,16},{12,20},{16,8},{20,12},{24,0},{28,4},{1,25},{... | collective-permute-start | bytes 540680 | tf_op jit(solution)/shard_map/ppermute | solution.py:794
  114.5 2.1 %first_back.1 = (f32[512,128]{1,0:T(8,128)}, f32[8,128]{1,0:T(8,128)S(1)}) custom-call(s32[4]{0:T(128)S(1)} %pad_add_fusion.scalars.refs_0_, f32[512,128]{1,0:T(8,128)S(1)} %get-tuple-element.169.p0, bf16[512,128]{1,0:T(8,128)(2,1)S(1)} %collective-permute-done.33.p1, bf16[512,128]{1,0:T(8,128)(2,1)S(1)} %collective-permute-done.34.p2, ...), custom_call_target="tpu_custom_call" | custom-call | flops 99999997952 | bytes 1 | tf_op jit(solution)/shard_map/first_back/pallas_call | solution.py:25
  124.1 4.7 %collective-permute-done.42.refs_2_ = bf16[64,1408]{1,0:T(8,128)(2,1)S(1)} collective-permute-done((bf16[64,1408]{1,0:T(8,128)(2,1)}, bf16[64,1408]{1,0:T(8,128)(2,1)S(1)}, u32[]{:S(2)}, u32[]{:S(2)}) %collective-permute-start.42) | collective-permute-done | bytes 180256 | tf_op jit(solution)/shard_map/ppermute | solution.py:794
  130.9 1.7 %collective-permute-done.38.refs_2_ = bf16[64,1792]{1,0:T(8,128)(2,1)S(1)} collective-permute-done((bf16[64,1792]{1,0:T(8,128)(2,1)S(1)}, bf16[64,1792]{1,0:T(8,128)(2,1)S(1)}, u32[]{:S(2)}, u32[]{:S(2)}) %collective-permute-start.38) | collective-permute-done | bytes 229408 | tf_op jit(solution)/shard_map/ppermute | solution.py:794
  133.3 2.2 %finish_two.1 = (f32[2,9,512,128]{3,2,1,0:T(8,128)}, f32[64,1024]{1,0:T(8,128)}, f32[64,1024]{1,0:T(8,128)S(1)}) custom-call(s32[4]{0:T(128)S(1)} %pad_add_fusion.scalars.refs_0_, bf16[4,64,1408]{2,1,0:T(8,128)(2,1)S(1)} %stack_two.1.own_ref, bf16[4,64,1408]{2,1,0:T(8,128)(2,1)S(1)} %collective-permute-done.44.other_ref), custom_call_target="tpu_custom_call" | custom-call | flops 99999997952 | bytes 1 | tf_op jit(solution)/shard_map/finish_two/pallas_call | solution.py:844
  135.7 2.6 %finish_last.1 = (f32[2,9,512,128]{3,2,1,0:T(8,128)}, f32[3,128]{1,0:T(4,128)}, f32[3,128]{1,0:T(4,128)}, f32[2,128]{1,0:T(2,128)}, f32[1,64]{1,0:T(1,128)}, /*i...) custom-call(s32[4]{0:T(128)S(1)} %pad_add_fusion.scalars.refs_0_, ...), custom_call_target="tpu_custom_call", output_to_operand_aliasing={{0}: (5, {})} | custom-call | flops 99999997952 | bytes 1 | tf_op jit(solution)/shard_map/finish_last/pallas_call | solution.py:844
  (134 shorter events, 49.8 us)
Async XLA Ops:
  3.1 12.2 %collective-permute-start.2 = (bf16[512,128]{1,0:T(8,128)(2,1)}, bf16[512,128]{1,0:T(8,128)(2,1)S(1)}, u32[]{:S(2)}, u32[]{:S(2)}) collective-permute-start(bf16[512,128]{1,0:T(8,128)(2,1)} %get-tuple-element.104.a0), channel_id=1, source_target_pairs={{0,3},{1,2},{2,1},{3,0},{4,7},{5,6},{6,5},{7,4},{8,11},{9,10},{10,... | collective-permute-start | bytes 393224 | tf_op jit(solution)/shard_map/ppermute | solution.py:794
  8.2 15.8 %collective-permute-start.1 = (bf16[512,128]{1,0:T(8,128)(2,1)}, bf16[512,128]{1,0:T(8,128)(2,1)S(1)}, u32[]{:S(2)}, u32[]{:S(2)}) collective-permute-start(bf16[512,128]{1,0:T(8,128)(2,1)} %get-tuple-element.104.a0), channel_id=1, source_target_pairs={{0,2},{1,3},{2,0},{3,1},{4,6},{5,7},{6,4},{7,5},{8,10},{9,11},{10,... | collective-permute-start | bytes 393224 | tf_op jit(solution)/shard_map/ppermute | solution.py:794
  8.2 15.8 %collective-permute-start = (bf16[512,128]{1,0:T(8,128)(2,1)}, bf16[512,128]{1,0:T(8,128)(2,1)S(1)}, u32[]{:S(2)}, u32[]{:S(2)}) collective-permute-start(bf16[512,128]{1,0:T(8,128)(2,1)} %get-tuple-element.104.a0), channel_id=1, source_target_pairs={{0,1},{1,0},{2,3},{3,2},{4,5},{5,4},{6,7},{7,6},{8,9},{9,8},{10,11... | collective-permute-start | bytes 393224 | tf_op jit(solution)/shard_map/ppermute | solution.py:794
  8.8 21.3 %collective-permute-start.11 = (bf16[64,640]{1,0:T(8,128)(2,1)}, bf16[64,640]{1,0:T(8,128)(2,1)S(1)}, u32[]{:S(2)}, u32[]{:S(2)}) collective-permute-start(bf16[64,640]{1,0:T(8,128)(2,1)} %get-tuple-element.117.refs_0_), channel_id=1, source_target_pairs={{0,3},{1,2},{2,1},{3,0},{4,7},{5,6},{6,5},{7,4},{8,11},{9,10},{10,... | collective-permute-start | bytes 245768 | tf_op jit(solution)/shard_map/ppermute | solution.py:794
  12.6 19.3 %collective-permute-start.10 = (bf16[64,640]{1,0:T(8,128)(2,1)}, bf16[64,640]{1,0:T(8,128)(2,1)S(1)}, u32[]{:S(2)}, u32[]{:S(2)}) collective-permute-start(bf16[64,640]{1,0:T(8,128)(2,1)} %get-tuple-element.117.refs_0_), channel_id=1, source_target_pairs={{0,2},{1,3},{2,0},{3,1},{4,6},{5,7},{6,4},{7,5},{8,10},{9,11},{10,... | collective-permute-start | bytes 245768 | tf_op jit(solution)/shard_map/ppermute | solution.py:794
  15.3 16.6 %collective-permute-start.9 = (bf16[64,640]{1,0:T(8,128)(2,1)}, bf16[64,640]{1,0:T(8,128)(2,1)S(1)}, u32[]{:S(2)}, u32[]{:S(2)}) collective-permute-start(bf16[64,640]{1,0:T(8,128)(2,1)} %get-tuple-element.117.refs_0_), channel_id=1, source_target_pairs={{0,1},{1,0},{2,3},{3,2},{4,5},{5,4},{6,7},{7,6},{8,9},{9,8},{10,11... | collective-permute-start | bytes 245768 | tf_op jit(solution)/shard_map/ppermute | solution.py:794
  30.1 8.9 %collective-permute-start.4 = (bf16[512,128]{1,0:T(8,128)(2,1)S(1)}, bf16[512,128]{1,0:T(8,128)(2,1)S(1)}, u32[]{:S(2)}, u32[]{:S(2)}) collective-permute-start(bf16[512,128]{1,0:T(8,128)(2,1)S(1)} %get-tuple-element.108.a0.refs_1_), channel_id=1, source_target_pairs={{0,2},{1,3},{2,0},{3,1},{4,6},{5,7},{6,4},{7,5},{8,10},{9,11},{10,... | collective-permute-start | bytes 393224 | tf_op jit(solution)/shard_map/ppermute | solution.py:794
  32.4 11.5 %collective-permute-start.14 = (bf16[4,64,640]{2,1,0:T(8,128)(2,1)S(1)}, bf16[4,64,640]{2,1,0:T(8,128)(2,1)S(1)}, u32[]{:S(2)}, u32[]{:S(2)}) collective-permute-start(bf16[4,64,640]{2,1,0:T(8,128)(2,1)S(1)} %pack_join.1.refs_0_), channel_id=1, source_target_pairs={{0,24},{4,28},{8,16},{12,20},{16,8},{20,12},{24,0},{28,4},{1,25},{... | collective-permute-start | bytes 983048 | tf_op jit(solution)/shard_map/ppermute | solution.py:794
  35.0 12.4 %collective-permute-start.13 = (bf16[4,64,640]{2,1,0:T(8,128)(2,1)S(1)}, bf16[4,64,640]{2,1,0:T(8,128)(2,1)S(1)}, u32[]{:S(2)}, u32[]{:S(2)}) collective-permute-start(bf16[4,64,640]{2,1,0:T(8,128)(2,1)S(1)} %pack_join.1.refs_0_), channel_id=1, source_target_pairs={{0,16},{4,20},{8,24},{12,28},{16,0},{20,4},{24,8},{28,12},{1,17},{... | collective-permute-start | bytes 983048 | tf_op jit(solution)/shard_map/ppermute | solution.py:794
  35.7 11.8 %collective-permute-start.12 = (bf16[4,64,640]{2,1,0:T(8,128)(2,1)S(1)}, bf16[4,64,640]{2,1,0:T(8,128)(2,1)S(1)}, u32[]{:S(2)}, u32[]{:S(2)}) collective-permute-start(bf16[4,64,640]{2,1,0:T(8,128)(2,1)S(1)} %pack_join.1.refs_0_), channel_id=1, source_target_pairs={{0,8},{4,12},{8,0},{12,4},{16,24},{20,28},{24,16},{28,20},{1,9},{5... | collective-permute-start | bytes 983048 | tf_op jit(solution)/shard_map/ppermute | solution.py:794
  41.7 9.3 %collective-permute-start.7 = (bf16[464,128]{1,0:T(8,128)(2,1)S(1)}, bf16[464,128]{1,0:T(8,128)(2,1)S(1)}, u32[]{:S(2)}, u32[]{:S(2)}) collective-permute-start(bf16[464,128]{1,0:T(8,128)(2,1)S(1)} %get-tuple-element.112), channel_id=1, source_target_pairs={{0,2},{1,3},{2,0},{3,1},{4,6},{5,7},{6,4},{7,5},{8,10},{9,11},{10,... | collective-permute-start | bytes 356360 | tf_op jit(solution)/shard_map/ppermute | solution.py:794
  58.4 11.8 %collective-permute-start.17 = (bf16[448,128]{1,0:T(8,128)(2,1)S(1)}, bf16[448,128]{1,0:T(8,128)(2,1)S(1)}, u32[]{:S(2)}, u32[]{:S(2)}) collective-permute-start(bf16[448,128]{1,0:T(8,128)(2,1)S(1)} %get-tuple-element.120), channel_id=1, source_target_pairs={{0,2},{1,3},{2,0},{3,1},{4,6},{5,7},{6,4},{7,5},{8,10},{9,11},{10,... | collective-permute-start | bytes 344072 | tf_op jit(solution)/shard_map/ppermute | solution.py:794
  59.6 10.7 %collective-permute-start.18 = (bf16[448,128]{1,0:T(8,128)(2,1)S(1)}, bf16[448,128]{1,0:T(8,128)(2,1)S(1)}, u32[]{:S(2)}, u32[]{:S(2)}) collective-permute-start(bf16[448,128]{1,0:T(8,128)(2,1)S(1)} %get-tuple-element.121), channel_id=1, source_target_pairs={{0,3},{1,2},{2,1},{3,0},{4,7},{5,6},{6,5},{7,4},{8,11},{9,10},{10,... | collective-permute-start | bytes 344072 | tf_op jit(solution)/shard_map/ppermute | solution.py:794
  63.0 17.2 %collective-permute-start.23 = (bf16[2,4,64,640]{3,2,1,0:T(8,128)(2,1)S(1)}, bf16[2,4,64,640]{3,2,1,0:T(8,128)(2,1)S(1)}, u32[]{:S(2)}, u32[]{:S(2)}) collective-permute-start(bf16[2,4,64,640]{3,2,1,0:T(8,128)(2,1)S(1)} %get-tuple-element.137), channel_id=1, source_target_pairs={{0,8},{4,12},{8,0},{12,4},{16,24},{20,28},{24,16},{28,20},{1,9},{5... | collective-permute-start | bytes 1966088 | tf_op jit(solution)/shard_map/ppermute | solution.py:794
  72.7 12.1 %collective-permute-start.20 = (bf16[512,128]{1,0:T(8,128)(2,1)S(1)}, bf16[512,128]{1,0:T(8,128)(2,1)S(1)}, u32[]{:S(2)}, u32[]{:S(2)}) collective-permute-start(bf16[512,128]{1,0:T(8,128)(2,1)S(1)} %get-tuple-element.132), channel_id=1, source_target_pairs={{0,1},{1,0},{2,3},{3,2},{4,5},{5,4},{6,7},{7,6},{8,9},{9,8},{10,11... | collective-permute-start | bytes 393224 | tf_op jit(solution)/shard_map/ppermute | solution.py:794
  74.9 12.4 %collective-permute-start.21 = (bf16[512,128]{1,0:T(8,128)(2,1)S(1)}, bf16[512,128]{1,0:T(8,128)(2,1)S(1)}, u32[]{:S(2)}, u32[]{:S(2)}) collective-permute-start(bf16[512,128]{1,0:T(8,128)(2,1)S(1)} %get-tuple-element.133), channel_id=1, source_target_pairs={{0,2},{1,3},{2,0},{3,1},{4,6},{5,7},{6,4},{7,5},{8,10},{9,11},{10,... | collective-permute-start | bytes 393224 | tf_op jit(solution)/shard_map/ppermute | solution.py:794
  75.9 11.4 %collective-permute-start.22 = (bf16[512,128]{1,0:T(8,128)(2,1)S(1)}, bf16[512,128]{1,0:T(8,128)(2,1)S(1)}, u32[]{:S(2)}, u32[]{:S(2)}) collective-permute-start(bf16[512,128]{1,0:T(8,128)(2,1)S(1)} %get-tuple-element.134), channel_id=1, source_target_pairs={{0,3},{1,2},{2,1},{3,0},{4,7},{5,6},{6,5},{7,4},{8,11},{9,10},{10,... | collective-permute-start | bytes 393224 | tf_op jit(solution)/shard_map/ppermute | solution.py:794
  81.0 10.2 %collective-permute-start.26 = (bf16[4,64,640]{2,1,0:T(8,128)(2,1)S(1)}, bf16[4,64,640]{2,1,0:T(8,128)(2,1)S(1)}, u32[]{:S(2)}, u32[]{:S(2)}) collective-permute-start(bf16[4,64,640]{2,1,0:T(8,128)(2,1)S(1)} %get-tuple-element.154), channel_id=1, source_target_pairs={{0,16},{4,20},{8,24},{12,28},{16,0},{20,4},{24,8},{28,12},{1,17},{... | collective-permute-start | bytes 983048 | tf_op jit(solution)/shard_map/ppermute | solution.py:794
  83.3 10.6 %collective-permute-start.31 = (bf16[2,64,1408]{2,1,0:T(8,128)(2,1)S(1)}, bf16[2,64,1408]{2,1,0:T(8,128)(2,1)S(1)}, u32[]{:S(2)}, u32[]{:S(2)}) collective-permute-start(bf16[2,64,1408]{2,1,0:T(8,128)(2,1)S(1)} %get-tuple-element.162), channel_id=1, source_target_pairs={{0,8},{4,12},{8,0},{12,4},{16,24},{20,28},{24,16},{28,20},{1,9},{5... | collective-permute-start | bytes 1081352 | tf_op jit(solution)/shard_map/ppermute | solution.py:794
  90.0 10.9 %collective-permute-start.25 = (bf16[4,64,1152]{2,1,0:T(8,128)(2,1)S(1)}, bf16[4,64,1152]{2,1,0:T(8,128)(2,1)S(1)}, u32[]{:S(2)}, u32[]{:S(2)}) collective-permute-start(bf16[4,64,1152]{2,1,0:T(8,128)(2,1)S(1)} %get-tuple-element.153), channel_id=1, source_target_pairs={{0,4},{4,0},{8,12},{12,8},{16,20},{20,16},{24,28},{28,24},{1,5},{5... | collective-permute-start | bytes 1769480 | tf_op jit(solution)/shard_map/ppermute | solution.py:794
  95.9 9.7 %collective-permute-start.33 = (bf16[512,128]{1,0:T(8,128)(2,1)S(1)}, bf16[512,128]{1,0:T(8,128)(2,1)S(1)}, u32[]{:S(2)}, u32[]{:S(2)}) collective-permute-start(bf16[512,128]{1,0:T(8,128)(2,1)S(1)} %get-tuple-element.170), channel_id=1, source_target_pairs={{0,1},{1,0},{2,3},{3,2},{4,5},{5,4},{6,7},{7,6},{8,9},{9,8},{10,11... | collective-permute-start | bytes 393224 | tf_op jit(solution)/shard_map/ppermute | solution.py:794
  96.9 14.6 %collective-permute-start.34 = (bf16[512,128]{1,0:T(8,128)(2,1)S(1)}, bf16[512,128]{1,0:T(8,128)(2,1)S(1)}, u32[]{:S(2)}, u32[]{:S(2)}) collective-permute-start(bf16[512,128]{1,0:T(8,128)(2,1)S(1)} %get-tuple-element.171), channel_id=1, source_target_pairs={{0,2},{1,3},{2,0},{3,1},{4,6},{5,7},{6,4},{7,5},{8,10},{9,11},{10,... | collective-permute-start | bytes 393224 | tf_op jit(solution)/shard_map/ppermute | solution.py:794
  98.9 14.0 %collective-permute-start.35 = (bf16[512,128]{1,0:T(8,128)(2,1)S(1)}, bf16[512,128]{1,0:T(8,128)(2,1)S(1)}, u32[]{:S(2)}, u32[]{:S(2)}) collective-permute-start(bf16[512,128]{1,0:T(8,128)(2,1)S(1)} %get-tuple-element.172), channel_id=1, source_target_pairs={{0,3},{1,2},{2,1},{3,0},{4,7},{5,6},{6,5},{7,4},{8,11},{9,10},{10,... | collective-permute-start | bytes 393224 | tf_op jit(solution)/shard_map/ppermute | solution.py:794
  100.9 15.7 %collective-permute-start.32 = (bf16[64,640]{1,0:T(8,128)(2,1)S(1)}, bf16[64,640]{1,0:T(8,128)(2,1)S(1)}, u32[]{:S(2)}, u32[]{:S(2)}) collective-permute-start(bf16[64,640]{1,0:T(8,128)(2,1)S(1)} %get-tuple-element.168), channel_id=1, source_target_pairs={{0,2},{1,3},{2,0},{3,1},{4,6},{5,7},{6,4},{7,5},{8,10},{9,11},{10,... | collective-permute-start | bytes 245768 | tf_op jit(solution)/shard_map/ppermute | solution.py:794
  102.8 14.1 %collective-permute-start.27 = (bf16[64,1152]{1,0:T(8,128)(2,1)S(1)}, bf16[64,1152]{1,0:T(8,128)(2,1)S(1)}, u32[]{:S(2)}, u32[]{:S(2)}) collective-permute-start(bf16[64,1152]{1,0:T(8,128)(2,1)S(1)} %get-tuple-element.158), channel_id=1, source_target_pairs={{0,8},{4,12},{8,0},{12,4},{16,24},{20,28},{24,16},{28,20},{1,9},{5... | collective-permute-start | bytes 442376 | tf_op jit(solution)/shard_map/ppermute | solution.py:794
  105.6 12.8 %collective-permute-start.28 = (bf16[64,1152]{1,0:T(8,128)(2,1)S(1)}, bf16[64,1152]{1,0:T(8,128)(2,1)S(1)}, u32[]{:S(2)}, u32[]{:S(2)}) collective-permute-start(bf16[64,1152]{1,0:T(8,128)(2,1)S(1)} %get-tuple-element.159), channel_id=1, source_target_pairs={{0,16},{4,20},{8,24},{12,28},{16,0},{20,4},{24,8},{28,12},{1,17},{... | collective-permute-start | bytes 442376 | tf_op jit(solution)/shard_map/ppermute | solution.py:794
  112.9 9.9 %collective-permute-start.43 = (bf16[64,1408]{1,0:T(8,128)(2,1)}, bf16[64,1408]{1,0:T(8,128)(2,1)}, u32[]{:S(2)}, u32[]{:S(2)}) collective-permute-start(bf16[64,1408]{1,0:T(8,128)(2,1)} %conv_two_sum.1.__.refs_0_), channel_id=1, source_target_pairs={{0,24},{4,28},{8,16},{12,20},{16,8},{20,12},{24,0},{28,4},{1,25},{... | collective-permute-start | bytes 540680 | tf_op jit(solution)/shard_map/ppermute | solution.py:794
  116.6 12.2 %collective-permute-start.42 = (bf16[64,1408]{1,0:T(8,128)(2,1)}, bf16[64,1408]{1,0:T(8,128)(2,1)S(1)}, u32[]{:S(2)}, u32[]{:S(2)}) collective-permute-start(bf16[64,1408]{1,0:T(8,128)(2,1)} %conv_two_sum.1.__.refs_0_), channel_id=1, source_target_pairs={{0,16},{4,20},{8,24},{12,28},{16,0},{20,4},{24,8},{28,12},{1,17},{... | collective-permute-start | bytes 540680 | tf_op jit(solution)/shard_map/ppermute | solution.py:794
  116.9 11.9 %collective-permute-start.41 = (bf16[64,1408]{1,0:T(8,128)(2,1)}, bf16[64,1408]{1,0:T(8,128)(2,1)S(1)}, u32[]{:S(2)}, u32[]{:S(2)}) collective-permute-start(bf16[64,1408]{1,0:T(8,128)(2,1)} %conv_two_sum.1.__.refs_0_), channel_id=1, source_target_pairs={{0,8},{4,12},{8,0},{12,4},{16,24},{20,28},{24,16},{28,20},{1,9},{5... | collective-permute-start | bytes 540680 | tf_op jit(solution)/shard_map/ppermute | solution.py:794
  119.5 11.4 %collective-permute-start.39 = (bf16[64,1792]{1,0:T(8,128)(2,1)S(1)}, bf16[64,1792]{1,0:T(8,128)(2,1)S(1)}, u32[]{:S(2)}, u32[]{:S(2)}) collective-permute-start(bf16[64,1792]{1,0:T(8,128)(2,1)S(1)} %last.1.refs_0_.refs_4_), channel_id=1, source_target_pairs={{0,24},{4,28},{8,16},{12,20},{16,8},{20,12},{24,0},{28,4},{1,25},{... | collective-permute-start | bytes 688136 | tf_op jit(solution)/shard_map/ppermute | solution.py:794
  120.9 11.6 %collective-permute-start.38 = (bf16[64,1792]{1,0:T(8,128)(2,1)S(1)}, bf16[64,1792]{1,0:T(8,128)(2,1)S(1)}, u32[]{:S(2)}, u32[]{:S(2)}) collective-permute-start(bf16[64,1792]{1,0:T(8,128)(2,1)S(1)} %last.1.refs_0_.refs_4_), channel_id=1, source_target_pairs={{0,16},{4,20},{8,24},{12,28},{16,0},{20,4},{24,8},{28,12},{1,17},{... | collective-permute-start | bytes 688136 | tf_op jit(solution)/shard_map/ppermute | solution.py:794
  122.8 9.8 %collective-permute-start.37 = (bf16[64,1792]{1,0:T(8,128)(2,1)S(1)}, bf16[64,1792]{1,0:T(8,128)(2,1)S(1)}, u32[]{:S(2)}, u32[]{:S(2)}) collective-permute-start(bf16[64,1792]{1,0:T(8,128)(2,1)S(1)} %last.1.refs_0_.refs_4_), channel_id=1, source_target_pairs={{0,8},{4,12},{8,0},{12,4},{16,24},{20,28},{24,16},{28,20},{1,9},{5... | collective-permute-start | bytes 688136 | tf_op jit(solution)/shard_map/ppermute | solution.py:794
  (38 other events, 281.5 us)
